TPU v7x, 32 devices: a whole 2x2x4 slice. The times are simulated.
32 devices in a mesh: cuts: 4 (over y, x), blk: 8 (over z, core).
Axes of the slice: x: 2, y: 2, z: 4, core: 2. Of those that a mesh axis runs over, the one named last changes fastest.
Arguments:
- gap_load: float32 [4, 16, 2, 256, 128], P('cuts', 'blk'), may hold values from -24 to 24
- offsets: int32 [4, 16, 2], P('cuts', 'blk'), may hold values from -1 to 255, as said below
- corner_map: int32 [4, 16, 4], P('cuts', 'blk'), may hold values from -1 to 63, as said below
- flexibility: float32 [4, 16, 1024, 1024], P('cuts', 'blk'), may hold values from -0.5 to 4.5, as said below
- coupling: float32 [4, 16, 12, 1024], P('cuts', 'blk'), may hold values from -1.25 to 1.25
- corner_rows: float32 [4, 16, 12, 192], P('cuts', 'blk'), may hold values from -0.1 to 1.1, as said below
Outputs:
- multipliers: float32 [4, 16, 2, 256, 128], P('cuts', 'blk')
- residual: float32 [4, 16, 2, 256, 128], P('cuts', 'blk')
Inputs may be any that keep to these rules, and one draw needn't show every extreme that they name: `offsets`: on an interface owned by a subdomain, the neighbour's dof k matches the owner's dof (k + offset) mod 256; -1 marks an interface without multipliers: the tunnel's far end, or one that touches an excavated subdomain. `corner_map`: entries k = 0, 1, 2, 3 are the corners at near-left, near-right, far-left, far-right. Entry 2 of subdomain (r, c) is never -1, and every node is entry 2 of exactly one subdomain; the same node is entry 3 of (r, (c - 1) mod 16) and, for r + 1 < 4, entries 0 of (r + 1, c) and 1 of (r + 1, (c - 1) mod 16), and no other entry. -1 marks a clamped corner at the tunnel's near end. `flexibility`: each block is symmetric positive definite. `corner_rows`: row 3 k + j of a subdomain is row 3 m + j of one symmetric positive definite matrix of order 3 * 64, with m = corner_map entry k; zero rows where that entry is -1.
All inputs are finite; a program needn't handle non-finite values.
Results may differ from a plain program's by a relative error of at most 0.00021.
Values sent between devices are 32-bit elements; how exact they have to be, the bound alone decides.
No kernel may reach another device: no remote copies, remote signals or barrier semaphores. Data moves between devices by JAX's collectives and lax.ppermute only.
A program may use at most 64 MiB of HBM per device.

v0:
```python
import jax
import jax.numpy as jnp
from jax import lax
from jax.sharding import PartitionSpec as P

ITERS = 3


HIGH = lax.Precision.HIGHEST


def from_behind(value, axis, steps):
    count = lax.axis_size(axis)
    first, last = (max(0, -steps), min(count, count - steps))
    return lax.ppermute(value, axis, [(source, source + steps) for source in range(first, last)])


def passed_along(value, axis, steps):
    count = lax.axis_size(axis)
    pairs = [(source, (source + steps) % count) for source in range(count)]
    return lax.ppermute(value, axis, pairs)


def rotate(values, amounts, orient):
    face_size = values.shape[-2]
    indices = (jnp.arange(face_size, dtype=jnp.int32) + orient * amounts[..., None]) % face_size
    return jnp.take_along_axis(values, indices[..., None], axis=-2)


def corner_indices(corner_map, dof_count):
    spread = 3 * corner_map[..., None] + jnp.arange(3, dtype=jnp.int32)
    spread = jnp.where(corner_map[..., None] >= 0, spread, dof_count)
    return spread.reshape(corner_map.shape[0], corner_map.shape[1], 12)


def inner_sum(first, second):
    return jnp.sum(first * second, axis=(0, 1, 2, 3))


def squares(residual):
    return lax.psum(inner_sum(residual, residual), ("cuts", "blk"))


def per_device(gap_load, offsets, corner_map, flexibility, coupling, corner_rows):
    cycle_count, circ_count, _, face_size, load_count = gap_load.shape
    dof_count = corner_rows.shape[-1]
    active = (offsets >= 0).astype(jnp.float32)[..., None, None]
    corner_dofs = corner_indices(corner_map, dof_count)
    every_dofs = lax.all_gather(corner_dofs, ("cuts", "blk"), axis=0, tiled=True)
    residual = gap_load * active
    multipliers = jnp.zeros_like(residual)
    direction = residual
    norm_now = squares(residual)
    for iteration in range(ITERS):
        sent_far = -rotate(direction[:, :, 0], offsets[:, :, 0], 1)
        sent_right = -rotate(direction[:, :, 1], offsets[:, :, 1], 1)
        edge_near = from_behind(sent_far[-1], "cuts", 1)
        edge_left = passed_along(sent_right[:, -1], "blk", 1)
        nearside = jnp.concatenate([edge_near[None], sent_far[:-1]], axis=0)
        leftside = jnp.concatenate([edge_left[:, None], sent_right[:, :-1]], axis=1)
        loads = jnp.stack([nearside, direction[:, :, 0], leftside, direction[:, :, 1]], axis=2)
        loads = loads.reshape(cycle_count, circ_count, 4 * face_size, load_count)
        operator_corner_terms = jnp.einsum("rcki,rcin->rckn", coupling, loads, precision=HIGH)
        every_terms = lax.all_gather(operator_corner_terms, ("cuts", "blk"), axis=0, tiled=True)
        whole = jnp.zeros((dof_count, load_count), jnp.float32)
        coarse = whole.at[every_dofs.reshape(-1)].add(
            every_terms.reshape(-1, load_count), mode="drop"
        )
        corner_values = jnp.einsum("rckm,mn->rckn", corner_rows, coarse, precision=HIGH)
        moved = jnp.einsum("rcij,rcjn->rcin", flexibility, loads, precision=HIGH)
        moved = moved + jnp.einsum("rcki,rckn->rcin", coupling, corner_values, precision=HIGH)
        moved = moved.reshape(cycle_count, circ_count, 4, face_size, load_count)
        from_far = from_behind(moved[0, :, 0], "cuts", -1)
        from_right = passed_along(moved[:, 0, 2], "blk", -1)
        far_near = jnp.concatenate([moved[1:, :, 0], from_far[None]], axis=0)
        right_left = jnp.concatenate([moved[:, 1:, 2], from_right[:, None]], axis=1)
        jump_far = moved[:, :, 1] - rotate(far_near, offsets[:, :, 0], -1)
        jump_right = moved[:, :, 3] - rotate(right_left, offsets[:, :, 1], -1)
        mapped = jnp.stack([jump_far, jump_right], axis=2) * active
        step_size = norm_now / lax.psum(inner_sum(direction, mapped), ("cuts", "blk"))
        multipliers = multipliers + step_size * direction
        residual = residual - step_size * mapped
        norm_next = squares(residual)
        direction = residual + norm_next / norm_now * direction
        norm_now = norm_next
    return (multipliers, residual)


def solution(mesh):
    in_specs = (
        P("cuts", "blk", None, None, None),
        P("cuts", "blk", None),
        P("cuts", "blk", None),
        P("cuts", "blk", None, None),
        P("cuts", "blk", None, None),
        P("cuts", "blk", None, None),
    )
    out_specs = (P("cuts", "blk", None, None, None), P("cuts", "blk", None, None, None))
    return jax.shard_map(
        per_device, mesh=mesh, in_specs=in_specs, out_specs=out_specs, check_vma=False
    )
```

profile of v0, /device:TPU:0, one launch (start us, length us, event | category | flops | bytes accessed | tf_op | source)
XLA Modules:
  0.0 544.3 jit_solution(15691530683097970761)
XLA Ops:
  3.9 3.7 gather_fusion.1
  8.4 3.7 gather_fusion
  12.2 4.4 collective-permute-start
  17.3 39.7 %all_gather.12 = s32[32,2,12]{2,1,0:T(2,128)S(1)} all-gather(s32[1,2,12]{2,1,0:T(2,128)S(1)} %add_select_fusion), channel_id=1, replica_groups=mesh['cuts'=4,'blk'=8] {'cuts','blk'}, dimensions={0}, use_global_device_ids=true | all-gather | bytes 3168 | tf_op jit(solution)/shard_map/all_gather | solution.py:49
  59.3 38.8 %all-gather = f32[64,12,128]{2,1,0:T(8,128)S(1)} all-gather(f32[2,12,128]{2,1,0:T(8,128)S(1)} %convolution_bitcast_fusion.5), channel_id=2, replica_groups=mesh['cuts'=4,'blk'=8] {'cuts','blk'}, dimensions={0}, use_global_device_ids=true | all-gather | bytes 405504 | tf_op jit(solution)/shard_map/all_gather | solution.py:64
  98.1 11.0 %fusion.4 = f32[2,128,1024]{2,1,0:T(8,128)S(1)} fusion(f32[2,1024,128]{1,2,0:T(8,128)S(1)} %reshape.750, f32[1,2,1024,1024]{3,2,1,0:T(8,128)} %param.11), kind=kOutput, calls=%fused_computation.19 | convolution fusion | flops 3221225472 | bytes 10485760 | tf_op jit(solution)/shard_map/rcij,rcjn->rcin/dot_general | solution.py:70
  109.2 6.5 %scatter_custom_fusion = f32[192,128]{1,0:T(8,128)S(1)} fusion(s32[768]{0:T(1024)S(1)} %fusion.36, f32[768,128]{1,0:T(8,128)S(1)} %reshape.875, f32[]{:T(128)} %constant.71.clone.1), kind=kCustom, calls=%fused_computation.95 | custom fusion | flops 98304 | bytes 98308 | tf_op jit(solution)/shard_map/scatter-add | solution.py:66
  122.7 3.7 gather_fusion.3
  126.5 4.9 collective-permute-done.2
  131.4 3.7 gather_fusion.2
  135.5 40.0 %all-reduce = (f32[128]{0:T(128)S(1)}, f32[128]{0:T(128)S(1)}) all-reduce(f32[128]{0:T(128)S(1)} %get-tuple-element.10, f32[128]{0:T(128)S(1)} %get-tuple-element.9), channel_id=1, replica_groups=mesh['cuts'=4,'blk'=8] {'cuts','blk'}, use_global_device_ids=true, to_apply=%region_1.2 | all-reduce | flops 256 | bytes 2048 | tf_op jit(solution)/shard_map/psum | solution.py:41
  175.7 40.4 %psum.44 = f32[128]{0:T(128)S(1)} all-reduce(f32[128]{0:T(128)S(1)} %multiply_reduce_fusion.3), channel_id=1, replica_groups=mesh['cuts'=4,'blk'=8] {'cuts','blk'}, use_global_device_ids=true, to_apply=%region_6.8 | all-reduce | flops 128 | bytes 1024 | tf_op jit(solution)/shard_map/psum | solution.py:41
  216.4 3.7 gather_fusion.5
  220.2 3.7 gather_fusion.4
  224.1 4.2 collective-permute-start.4
  228.5 6.2 %collective-permute-done.5 = f32[1,256,128]{2,1,0:T(8,128)S(1)} collective-permute-done((f32[1,256,128]{2,1,0:T(8,128)S(1)}, f32[1,256,128]{2,1,0:T(8,128)S(1)}, u32[]{:S(2)}, u32[]{:S(2)}) %collective-permute-start.5) | collective-permute-done | bytes 131104 | tf_op jit(solution)/shard_map/ppermute | solution.py:21
  238.9 11.1 %fusion.2 = f32[2,128,1024]{2,1,0:T(8,128)S(1)} fusion(f32[2,1024,128]{1,2,0:T(8,128)S(1)} %reshape.757, f32[1,2,1024,1024]{3,2,1,0:T(8,128)} %param.11), kind=kOutput, calls=%fused_computation.17 | convolution fusion | flops 3221225472 | bytes 10485760 | tf_op jit(solution)/shard_map/rcij,rcjn->rcin/dot_general | solution.py:70
  250.0 40.2 %all-gather.1 = f32[64,12,128]{2,1,0:T(8,128)S(1)} all-gather(f32[2,12,128]{2,1,0:T(8,128)S(1)} %convolution_bitcast_fusion.3), channel_id=3, replica_groups=mesh['cuts'=4,'blk'=8] {'cuts','blk'}, dimensions={0}, use_global_device_ids=true | all-gather | bytes 405504 | tf_op jit(solution)/shard_map/all_gather | solution.py:64
  290.3 6.1 %scatter_custom_fusion.1 = f32[192,128]{1,0:T(8,128)S(1)} fusion(s32[768]{0:T(1024)S(1)} %fusion.36, f32[768,128]{1,0:T(8,128)S(1)} %reshape.883, f32[]{:T(128)} %constant.71.clone.1), kind=kCustom, calls=%fused_computation.93 | custom fusion | flops 98304 | bytes 98308 | tf_op jit(solution)/shard_map/scatter-add | solution.py:66
  302.0 3.7 gather_fusion.7
  309.8 3.7 gather_fusion.6
  315.1 37.9 %psum.45 = f32[128]{0:T(128)S(1)} all-reduce(f32[128]{0:T(128)S(1)} %multiply_reduce_fusion.2), channel_id=1, replica_groups=mesh['cuts'=4,'blk'=8] {'cuts','blk'}, use_global_device_ids=true, to_apply=%region_9.11 | all-reduce | flops 128 | bytes 1024 | tf_op jit(solution)/shard_map/psum | solution.py:80
  353.9 40.5 %psum.46 = f32[128]{0:T(128)S(1)} all-reduce(f32[128]{0:T(128)S(1)} %get-tuple-element.17), channel_id=1, replica_groups=mesh['cuts'=4,'blk'=8] {'cuts','blk'}, use_global_device_ids=true, to_apply=%region_11.13 | all-reduce | flops 128 | bytes 1024 | tf_op jit(solution)/shard_map/psum | solution.py:41
  396.0 3.7 gather_fusion.9
  400.5 3.7 gather_fusion.8
  404.3 4.2 collective-permute-start.8
  408.6 6.2 %collective-permute-done.9 = f32[1,256,128]{2,1,0:T(8,128)S(1)} collective-permute-done((f32[1,256,128]{2,1,0:T(8,128)S(1)}, f32[1,256,128]{2,1,0:T(8,128)S(1)}, u32[]{:S(2)}, u32[]{:S(2)}) %collective-permute-start.9) | collective-permute-done | bytes 131104 | tf_op jit(solution)/shard_map/ppermute | solution.py:21
  419.0 12.0 %fusion = f32[2,128,1024]{2,1,0:T(8,128)} fusion(f32[2,1024,128]{1,2,0:T(8,128)S(1)} %reshape.760, f32[1,2,1024,1024]{3,2,1,0:T(8,128)} %param.11), kind=kOutput, calls=%fused_computation.15 | convolution fusion | flops 3221225472 | bytes 10485760 | tf_op jit(solution)/shard_map/rcij,rcjn->rcin/dot_general | solution.py:70
  431.0 40.7 %all-gather.2 = f32[64,12,128]{2,1,0:T(8,128)S(1)} all-gather(f32[2,12,128]{2,1,0:T(8,128)S(1)} %convolution_bitcast_fusion.1), channel_id=4, replica_groups=mesh['cuts'=4,'blk'=8] {'cuts','blk'}, dimensions={0}, use_global_device_ids=true | all-gather | bytes 405504 | tf_op jit(solution)/shard_map/all_gather | solution.py:64
  471.7 6.2 %scatter_custom_fusion.2 = f32[192,128]{1,0:T(8,128)S(1)} fusion(s32[768]{0:T(1024)} %copy-done.14, f32[768,128]{1,0:T(8,128)S(1)} %reshape.891, f32[]{:T(128)} %constant.71.clone.1), kind=kCustom, calls=%fused_computation.91 | custom fusion | flops 98304 | bytes 98816 | tf_op jit(solution)/shard_map/scatter-add | solution.py:66
  492.4 3.7 gather_fusion.11
  502.8 39.1 %psum.47 = f32[128]{0:T(128)S(1)} all-reduce(f32[128]{0:T(128)S(1)} %multiply_reduce_fusion), channel_id=1, replica_groups=mesh['cuts'=4,'blk'=8] {'cuts','blk'}, use_global_device_ids=true, to_apply=%region_14.16 | all-reduce | flops 128 | bytes 1024 | tf_op jit(solution)/shard_map/psum | solution.py:80
  (162 shorter events, 61.6 us)
Async XLA Ops:
  0.6 57.7 %copy-start = (f32[1,2,12,1024]{3,1,2,0:T(2,128)S(1)}, f32[1,2,12,1024]{3,1,2,0:T(2,128)}, u32[]{:S(2)}) copy-start(f32[1,2,12,1024]{3,1,2,0:T(2,128)} %param.12) | copy-start | bytes 294916
  0.6 16.0 %copy-start.15 = (s32[1,2,4]{2,1,0:T(2,128)S(1)}, s32[1,2,4]{2,1,0:T(2,128)}, u32[]{:S(2)}) copy-start(s32[1,2,4]{2,1,0:T(2,128)} %param.10) | copy-start | bytes 100
  2.5 217.6 %copy-start.9 = (pred[2,256]{1,0:T(4,128)(4,1)}, pred[2,256]{1,0:T(4,128)(4,1)S(1)}, u32[]{:S(2)}) copy-start(pred[2,256]{1,0:T(4,128)(4,1)S(1)} %and_bitcast_fusion.2) | copy-start | bytes 1540
  7.7 49.5 %collective-permute-start.1 = (f32[1,256,128]{2,1,0:T(8,128)S(1)}, f32[1,256,128]{2,1,0:T(8,128)S(1)}, u32[]{:S(2)}, u32[]{:S(2)}) collective-permute-start(f32[1,256,128]{2,1,0:T(8,128)S(1)} %get-tuple-element.50), channel_id=1, source_target_pairs={{0,1},{1,2},{2,3},{3,4},{4,5},{5,6},{6,7},{7,0},{8,9},{9,10},{10,1... | collective-permute-start | bytes 393224 | tf_op jit(solution)/shard_map/ppermute | solution.py:21
  8.4 215.5 %copy-start.10 = (pred[2,256]{1,0:T(4,128)(4,1)}, pred[2,256]{1,0:T(4,128)(4,1)S(1)}, u32[]{:S(2)}) copy-start(pred[2,256]{1,0:T(4,128)(4,1)S(1)} %and_bitcast_fusion.3) | copy-start | bytes 1540
  12.2 45.0 %collective-permute-start = (f32[2,256,128]{2,1,0:T(8,128)S(1)}, f32[2,256,128]{2,1,0:T(8,128)S(1)}, u32[]{:S(2)}, u32[]{:S(2)}) collective-permute-start(f32[2,256,128]{2,1,0:T(8,128)S(1)} %fusion.17), channel_id=1, source_target_pairs={{0,8},{8,16},{16,24},{1,9},{9,17},{17,25},{2,10},{10,18},{18,26},{... | collective-permute-start | bytes 786440 | tf_op jit(solution)/shard_map/ppermute | solution.py:15
  16.8 109.5 %copy-start.7 = (pred[2,256]{1,0:T(4,128)(4,1)}, pred[2,256]{1,0:T(4,128)(4,1)S(1)}, u32[]{:S(2)}) copy-start(pred[2,256]{1,0:T(4,128)(4,1)S(1)} %get-tuple-element.54) | copy-start | bytes 1540
  16.9 118.2 %copy-start.5 = (pred[2,256]{1,0:T(4,128)(4,1)}, pred[2,256]{1,0:T(4,128)(4,1)S(1)}, u32[]{:S(2)}) copy-start(pred[2,256]{1,0:T(4,128)(4,1)S(1)} %get-tuple-element.55) | copy-start | bytes 1540
  57.2 233.1 %copy-start.14 = (s32[768]{0:T(1024)}, s32[768]{0:T(1024)S(1)}, u32[]{:S(2)}) copy-start(s32[768]{0:T(1024)S(1)} %fusion.36) | copy-start | bytes 9220
  57.3 58.4 %copy-start.4 = (f32[1,2,12,192]{3,1,2,0:T(2,128)S(1)}, f32[1,2,12,192]{3,1,2,0:T(2,128)}, u32[]{:S(2)}) copy-start(f32[1,2,12,192]{3,1,2,0:T(2,128)} %param.13) | copy-start | bytes 55300
  109.2 26.0 %copy-start.1 = (f32[1,2,2,256,128]{4,3,2,1,0:T(8,128)S(1)}, f32[1,2,2,256,128]{4,3,2,1,0:T(8,128)}, u32[]{:S(2)}) copy-start(f32[1,2,2,256,128]{4,3,2,1,0:T(8,128)} %param.8) | copy-start | bytes 1572868
  120.1 2.6 collective-permute-start.3
  120.8 10.6 %collective-permute-start.2 = (f32[2,256,128]{2,1,0:T(8,128)S(1)}, f32[2,256,128]{2,1,0:T(8,128)S(1)}, u32[]{:S(2)}, u32[]{:S(2)}) collective-permute-start(f32[2,256,128]{2,1,0:T(8,128)S(1)} %bitcast.272), channel_id=1, source_target_pairs={{8,0},{16,8},{24,16},{9,1},{17,9},{25,17},{10,2},{18,10},{26,18},{... | collective-permute-start | bytes 786440 | tf_op jit(solution)/shard_map/ppermute | solution.py:15
  216.2 20.0 %copy-start.16 = (f32[128]{0:T(128)}, f32[128]{0:T(128)S(1)}, u32[]{:S(2)}) copy-start(f32[128]{0:T(128)S(1)} %psum.44) | copy-start | bytes 1540
  216.2 20.0 %copy-start.12 = (f32[128]{0:T(128)}, f32[128]{0:T(128)S(1)}, u32[]{:S(2)}) copy-start(f32[128]{0:T(128)S(1)} %div.16) | copy-start | bytes 1540
  224.1 10.7 %collective-permute-start.4 = (f32[2,256,128]{2,1,0:T(8,128)S(1)}, f32[2,256,128]{2,1,0:T(8,128)S(1)}, u32[]{:S(2)}, u32[]{:S(2)}) collective-permute-start(f32[2,256,128]{2,1,0:T(8,128)S(1)} %fusion.16), channel_id=1, source_target_pairs={{0,8},{8,16},{16,24},{1,9},{9,17},{17,25},{2,10},{10,18},{18,26},{... | collective-permute-start | bytes 786440 | tf_op jit(solution)/shard_map/ppermute | solution.py:15
  228.3 6.4 %collective-permute-start.5 = (f32[1,256,128]{2,1,0:T(8,128)S(1)}, f32[1,256,128]{2,1,0:T(8,128)S(1)}, u32[]{:S(2)}, u32[]{:S(2)}) collective-permute-start(f32[1,256,128]{2,1,0:T(8,128)S(1)} %get-tuple-element.48), channel_id=1, source_target_pairs={{0,1},{1,2},{2,3},{3,4},{4,5},{5,6},{6,7},{7,0},{8,9},{9,10},{10,1... | collective-permute-start | bytes 393224 | tf_op jit(solution)/shard_map/ppermute | solution.py:21
  298.5 2.7 collective-permute-start.7
  299.2 10.6 %collective-permute-start.6 = (f32[2,256,128]{2,1,0:T(8,128)S(1)}, f32[2,256,128]{2,1,0:T(8,128)S(1)}, u32[]{:S(2)}, u32[]{:S(2)}) collective-permute-start(f32[2,256,128]{2,1,0:T(8,128)S(1)} %bitcast.273), channel_id=1, source_target_pairs={{8,0},{16,8},{24,16},{9,1},{17,9},{25,17},{10,2},{18,10},{26,18},{... | collective-permute-start | bytes 786440 | tf_op jit(solution)/shard_map/ppermute | solution.py:15
  309.8 94.3 %copy-start.11 = (pred[2,256]{1,0:T(4,128)(4,1)S(1)}, pred[2,256]{1,0:T(4,128)(4,1)}, u32[]{:S(2)}) copy-start(pred[2,256]{1,0:T(4,128)(4,1)} %copy-done.10) | copy-start | bytes 1540
  353.9 41.2 %copy-start.2 = (f32[1,2,2,256,128]{4,3,1,2,0:T(8,128)}, f32[1,2,2,256,128]{4,3,1,2,0:T(8,128)S(1)}, u32[]{:S(2)}) copy-start(f32[1,2,2,256,128]{4,3,1,2,0:T(8,128)S(1)} %get-tuple-element.18) | copy-start | bytes 1572868
  404.3 10.5 %collective-permute-start.8 = (f32[2,256,128]{2,1,0:T(8,128)S(1)}, f32[2,256,128]{2,1,0:T(8,128)S(1)}, u32[]{:S(2)}, u32[]{:S(2)}) collective-permute-start(f32[2,256,128]{2,1,0:T(8,128)S(1)} %fusion.15), channel_id=1, source_target_pairs={{0,8},{8,16},{16,24},{1,9},{9,17},{17,25},{2,10},{10,18},{18,26},{... | collective-permute-start | bytes 786440 | tf_op jit(solution)/shard_map/ppermute | solution.py:15
  408.5 6.2 %collective-permute-start.9 = (f32[1,256,128]{2,1,0:T(8,128)S(1)}, f32[1,256,128]{2,1,0:T(8,128)S(1)}, u32[]{:S(2)}, u32[]{:S(2)}) collective-permute-start(f32[1,256,128]{2,1,0:T(8,128)S(1)} %get-tuple-element.46), channel_id=1, source_target_pairs={{0,1},{1,2},{2,3},{3,4},{4,5},{5,6},{6,7},{7,0},{8,9},{9,10},{10,1... | collective-permute-start | bytes 393224 | tf_op jit(solution)/shard_map/ppermute | solution.py:21
  431.0 65.0 %copy-start.8 = (pred[2,256]{1,0:T(4,128)(4,1)S(1)}, pred[2,256]{1,0:T(4,128)(4,1)}, u32[]{:S(2)}) copy-start(pred[2,256]{1,0:T(4,128)(4,1)} %copy-done.7) | copy-start | bytes 1540
  431.0 71.4 %copy-start.6 = (pred[2,256]{1,0:T(4,128)(4,1)S(1)}, pred[2,256]{1,0:T(4,128)(4,1)}, u32[]{:S(2)}) copy-start(pred[2,256]{1,0:T(4,128)(4,1)} %copy-done.5) | copy-start | bytes 1540
  478.1 63.8 %copy-start.3 = (f32[1,2,2,256,128]{4,3,1,2,0:T(8,128)S(1)}, f32[1,2,2,256,128]{4,3,1,2,0:T(8,128)}, u32[]{:S(2)}) copy-start(f32[1,2,2,256,128]{4,3,1,2,0:T(8,128)} %copy-done.2) | copy-start | bytes 1572868
  478.1 63.8 %copy-start.13 = (f32[128]{0:T(128)S(1)}, f32[128]{0:T(128)}, u32[]{:S(2)}) copy-start(f32[128]{0:T(128)} %copy-done.12) | copy-start | bytes 1540
  484.8 6.6 %collective-permute-start.11 = (f32[1,256,128]{2,1,0:T(8,128)}, f32[1,256,128]{2,1,0:T(8,128)}, u32[]{:S(2)}, u32[]{:S(2)}) collective-permute-start(f32[1,256,128]{2,1,0:T(8,128)} %bitcast.105), channel_id=1, source_target_pairs={{0,7},{1,0},{2,1},{3,2},{4,3},{5,4},{6,5},{7,6},{8,15},{9,8},{10,9... | collective-permute-start | bytes 393224 | tf_op jit(solution)/shard_map/ppermute | solution.py:21
  487.9 10.8 %collective-permute-start.10 = (f32[2,256,128]{2,1,0:T(8,128)}, f32[2,256,128]{2,1,0:T(8,128)S(1)}, u32[]{:S(2)}, u32[]{:S(2)}) collective-permute-start(f32[2,256,128]{2,1,0:T(8,128)} %bitcast.97), channel_id=1, source_target_pairs={{8,0},{16,8},{24,16},{9,1},{17,9},{25,17},{10,2},{18,10},{26,18},{... | collective-permute-start | bytes 786440 | tf_op jit(solution)/shard_map/ppermute | solution.py:15
where the time goes:
time: 553 us; the launch traced here: 544 us
  blocking collectives  357 us (65%)
  local copies, waits for them, and re-layouts  67.4 us (12%)
  matrix products  44.1 us (8%)
  other arithmetic  32.3 us (6%)
  waiting for transfers between devices  23.2 us (4%)
  starting transfers between devices  17.8 us (3%)
    psum x3, blocking collectives, squares(): return lax.psum(inner_sum(residual, residual), ('cuts', 'blk'))  121 us
    all_gather x3, blocking collectives, per_device(): lax.all_gather(operator_corner_terms, ('cuts', 'blk'), axis=0, tiled=True)  120 us
    psum x2, blocking collectives, per_device(): lax.psum(inner_sum(direction, mapped), ('cuts', 'blk'))  77.1 us
    gather x12, local copies, waits for them, and re-layouts, rotate(): return jnp.take_along_axis(values, indices[..., None], axis=-2)  43.9 us
    all_gather x1, blocking collectives, per_device(): lax.all_gather(corner_dofs, ('cuts', 'blk'), axis=0, tiled=True)  39.7 us
    dot_general x3, matrix products, per_device(): moved = jnp.einsum('rcij,rcjn->rcin', flexibility, loads, precision=HIGH)  34.1 us
    scatter-add x3, other arithmetic, per_device(): whole.at[every_dofs.reshape(-1)]  18.8 us
    ppermute x6, starting transfers between devices, from_behind(): lax.ppermute(value, axis, [(source, source + steps) for source in range(f...  16.9 us
  transfers between devices with their start and end apart: 12, of which 6 were waited for; matrix products, arithmetic and copies ran while one was open for 5% of the time, Pallas kernels for 0%

commit v1 on v0

v1 whole, which is shorter than its diff:
```python
import functools

import jax
import jax.numpy as jnp
from jax import lax
from jax.experimental import pallas as pl
from jax.experimental.pallas import tpu as pltpu
from jax.sharding import PartitionSpec as P

ITERS = 3
NEAR, FAR, LEFT, RIGHT = range(4)
VMEM = pl.BlockSpec(memory_space=pltpu.VMEM)
SMEM = pl.BlockSpec(memory_space=pltpu.SMEM)
ANY = pl.BlockSpec(memory_space=pl.ANY)
F32, BF16 = jnp.float32, jnp.bfloat16


def shifted(value, axis, steps, wrap):
    count = lax.axis_size(axis)
    if wrap:
        pairs = [(source, (source + steps) % count) for source in range(count)]
    else:
        pairs = [(source, source + steps) for source in range(count) if 0 <= source + steps < count]
    return lax.ppermute(value, axis, pairs)


def summed(value, axis):
    others = [shifted(value, axis, k, True) for k in range(1, lax.axis_size(axis))]
    return functools.reduce(jnp.add, others, value)


def collected(value, axis):
    count, stride = lax.axis_size(axis), 1
    parts = [value]
    while stride < count:
        radix = next((r for r in range(8, 1, -1) if (count // stride) % r == 0), count // stride)
        value = parts[0] if len(parts) == 1 else jnp.concatenate(parts, axis=0)
        parts = [value] + [shifted(value, axis, k * stride, True) for k in range(1, radix)]
        stride *= radix
    return parts


def halves(value):
    high = value.astype(BF16)
    return high, (value - high.astype(F32)).astype(BF16)


def kept_halves(value):
    high = lax.reduce_precision(value, 8, 7)
    return high.astype(BF16), (value - high).astype(BF16)


def dot(first, second):
    return lax.dot_general(first, second, (((1,), (0,)), ((), ())), preferred_element_type=F32)


def rotated(buffer, value, start):
    size = value.shape[0]
    buffer[0:size] = value
    buffer[size:] = value
    return buffer[pl.ds(start, size)]


def prepare_kernel(offsets, gap, residual, to_far, to_right, inner, buffer):
    count, _, size, _ = gap.shape
    for s in range(count):
        for face in range(2):
            shift = offsets[s, face]
            value = gap[s, face] * (shift >= 0).astype(F32)
            residual[s, face] = value
            turned = -rotated(buffer.at[s, face], value, jnp.maximum(shift, 0))
            if face == 0:
                to_far[s] = turned
            elif s == count - 1:
                to_right[...] = turned
            else:
                inner[s] = turned
    inner[count - 1] = jnp.zeros(inner.shape[1:], F32)


def split_kernel(block, high, low):
    high[...], low[...] = halves(block[...])


def apply_flexibility(loads, a_high, a_low, coupling, height, outs, scratch, rr_rows):
    near, far, sides, to_left, to_right, terms = outs
    split = scratch["split"]
    count, size = len(loads), loads[0][0].shape[0]
    for s in range(count):
        for face in range(4):
            high, low = halves(loads[s][face])
            split[s, face * size:(face + 1) * size, 0:128] = high
            split[s, face * size:(face + 1) * size, 128:256] = low
    terms[...] = jnp.zeros_like(terms)
    total = jnp.zeros((1, 128), F32)
    width = coupling.shape[1] // 2
    for s in range(count):
        both = dot(coupling[s], split[s])
        mine = both[0:width, 0:128] + both[0:width, 128:256] + both[width:, 0:128]
        terms[s * height:s * height + width] += mine
    for s in range(count):
        for face in range(4):
            scratch["wait"](s * 4 + face)
            rows = slice(face * size, (face + 1) * size)
            product = dot(a_high[s, rows], split[s])
            product = product[:, 0:128] + product[:, 128:256]
            product = product + dot(a_low[s, rows], split[s, :, 0:128])
            total = total + jnp.sum(product * loads[s][face], axis=0, keepdims=True)
            if face == NEAR:
                near[s] = product
            elif face == FAR:
                far[s] = product
            else:
                sides[s, face - 2] = product
                if face == LEFT and s == 0:
                    to_left[...] = product
                if face == RIGHT and s == count - 1:
                    to_right[...] = product
    squares = jnp.zeros((1, 128), F32)
    for s in range(count):
        for face in (FAR, RIGHT):
            squares = squares + jnp.sum(loads[s][face] * loads[s][face], axis=0, keepdims=True)
    terms[rr_rows:rr_rows + 1] = squares
    terms[rr_rows + 1:rr_rows + 2] = total


def finish_operator(offsets, terms, matrix, spread, product, received, height, rr_rows, scratch, faces):
    k_high, k_low = matrix
    ct_own, ct_left, ct_right = spread
    near, far, sides = product
    from_near, from_far, from_left, from_right = received
    count, size = near.shape[0], near.shape[1]
    blocks = len(terms)
    stacked = scratch["stack"]
    norm = functools.reduce(jnp.add, [t[rr_rows:rr_rows + 1] for t in terms])
    energy = functools.reduce(jnp.add, [t[rr_rows + 1:rr_rows + 2] for t in terms])
    span = count * height
    for k in range(blocks):
        stacked[k * span:(k + 1) * span] = terms[k][0:span]
        stacked[k * span:k * span + height] = (
            terms[k][0:height] + terms[(k + 1) % blocks][span:span + height]
        )
    coarse = stacked[...]
    high, low = halves(coarse)
    both = dot(k_high[...], jnp.concatenate([high, low], axis=1))
    values = both[:, 0:128] + both[:, 128:256] + dot(k_low[...], high)
    energy = energy + jnp.sum(coarse * values, axis=0, keepdims=True)

    def column(q):
        block = (-(q // count)) % blocks
        at = block * span + (q % count) * height
        return values[at:at + height]

    def tripled(q):
        high, low = halves(jnp.concatenate([column(q), column(q + 1)], axis=0))
        return jnp.concatenate([high, high, low], axis=0)

    own = [[None] * 4 for _ in range(count)]
    other = [[None] * 4 for _ in range(count)]
    for s in range(count):
        added = dot(ct_own[s], tripled(s))
        parts = [added[i * size:(i + 1) * size] for i in range(6)]
        raw = [near[s], far[s], sides[s, 0], sides[s, 1]]
        own[s] = [raw[i] + parts[i] for i in range(4)]
        other[s][FAR] = from_far[s] + parts[4]
        if NEAR in faces:
            other[s][NEAR] = from_near[s] + parts[5]
    other[count - 1][RIGHT] = from_right[...] + dot(ct_right[...], tripled(count))
    if LEFT in faces:
        other[0][LEFT] = from_left[...] + dot(ct_left[...], tripled(-1))
    for s in range(count):
        if s + 1 < count:
            other[s][RIGHT] = own[s + 1][LEFT]
        if s > 0:
            other[s][LEFT] = own[s - 1][RIGHT]
    result = [[None] * 4 for _ in range(count)]
    for s in range(count):
        for face in faces:
            shift = offsets[s, face]
            safe = jnp.maximum(shift, 0)
            start = safe if face in (NEAR, LEFT) else size - safe
            turned = rotated(scratch["turn"].at[s, face], other[s][face], start)
            result[s][face] = (own[s][face] - turned) * (shift >= 0).astype(F32)
    return result, norm, energy


def copies_of(high, low, high_buffer, low_buffer, sems, size):
    count = high.shape[0]
    pairs = []
    for s in range(count):
        for face in range(4):
            rows = pl.ds(face * size, size)
            index = s * 4 + face
            pairs.append((
                pltpu.make_async_copy(high.at[s, rows], high_buffer.at[s, rows], sems.at[0, index]),
                pltpu.make_async_copy(low.at[s, rows], low_buffer.at[s, rows], sems.at[1, index]),
            ))
    for pair in pairs:
        for copy in pair:
            copy.start()

    def wait(index):
        for copy in pairs[index]:
            copy.wait()

    return wait


def first_kernel(height, rr_rows, residual, from_near, from_left, inner, a_high, a_low, coupling, *rest):
    outs, loads_out = rest[0:6], rest[6]
    high_buffer, low_buffer, sems, split = rest[7:]
    count, size = residual.shape[0], residual.shape[2]
    scratch = dict(split=split, wait=copies_of(a_high, a_low, high_buffer, low_buffer, sems, size))
    loads = []
    for s in range(count):
        left = from_left[...] if s == 0 else inner[s - 1]
        loads.append([from_near[s], residual[s, 0], left, residual[s, 1]])
        for face in range(4):
            loads_out[s, face] = loads[s][face]
    apply_flexibility(loads, high_buffer, low_buffer, coupling, height, outs, scratch, rr_rows)


def step_kernel(which, pieces, height, rr_rows, *refs):
    refs = list(refs)
    take = lambda number: [refs.pop(0) for _ in range(number)]
    last = which == ITERS - 1
    (offsets,) = take(1)
    terms = take(pieces)
    matrix, spread, product, received = take(2), take(3), take(3), take(4)
    (loads,) = take(1)
    map_before, ways, found, scalars = (take(4) if which > 0 else [None] * 4)
    if not last:
        a_high, a_low, coupling = take(3)
        outs = take(6)
        loads_out, map_out = take(2)
        ways_out, found_out = take(2) if which > 0 else (None, None)
        (scalars_out,) = take(1)
        stack, turn, high_buffer, low_buffer, sems, split = take(6)
        faces = (NEAR, FAR, LEFT, RIGHT)
    else:
        found_out, residual_out = take(2)
        stack, turn = take(2)
        faces = (FAR, RIGHT)
    count, size = loads.shape[0], loads.shape[2]
    scratch = dict(stack=stack, turn=turn)
    if not last:
        scratch["split"] = split
        scratch["wait"] = copies_of(a_high, a_low, high_buffer, low_buffer, sems, size)
    span = (count + 1) * height
    terms = [t[i:i + span] for t in terms for i in range(0, t.shape[0], span)]
    mapped, norm, energy = finish_operator(
        offsets, terms, matrix, spread, product, received, height, rr_rows, scratch, faces
    )
    if which > 0:
        ratio = norm / scalars[0:1]
        energy = energy - ratio * norm / scalars[1:2]
    step = norm / energy
    fresh = [[None] * 4 for _ in range(count)]
    for s in range(count):
        for face in faces:
            here = mapped[s][face]
            now = loads[s, face]
            if which > 0:
                here = here + ratio * map_before[s, face]
            fresh[s][face] = now - step * here
            if not last:
                map_out[s, face] = here
                loads_out[s, face] = fresh[s][face]
            if face in (FAR, RIGHT):
                i = 0 if face == FAR else 1
                if which == 0:
                    continue
                if which == 1:
                    before = ways[s, face]
                    start = scalars[1:2] * before
                else:
                    before = ways[s, i]
                    start = found[s, i]
                way = now + ratio * before
                found_out[s, i] = start + step * way
                if last:
                    residual_out[s, i] = fresh[s][face]
                else:
                    ways_out[s, i] = way
    if not last:
        scalars_out[...] = jnp.concatenate([norm, step, jnp.zeros((6, 128), F32)], axis=0)
        apply_flexibility(fresh, high_buffer, low_buffer, coupling, height, outs, scratch, rr_rows)


def placed(rows, at, height):
    pad = [(0, 0)] * (rows.ndim - 2) + [(height, height), (0, 0)]
    return lax.dynamic_slice_in_dim(jnp.pad(rows, pad), height - 3 * (at - 1), height, axis=rows.ndim - 2)


def by_columns(coupling):
    lead, length = coupling.shape[:-2], coupling.shape[-1]
    split = coupling.reshape(lead + (2, 2, 3, length))
    return jnp.swapaxes(split, -4, -3).reshape(lead + (2, 6, length))


def spread_out(faces, at, height):
    wide = placed(by_columns(faces), at, height)
    wide = wide.reshape(wide.shape[:-3] + (2 * height, wide.shape[-1]))
    high, low = kept_halves(jnp.swapaxes(wide, -1, -2))
    return jnp.concatenate([high, low, high], axis=-1)


def per_device(gap_load, offsets, corner_map, flexibility, coupling, corner_rows):
    _, count, _, size, loads_n = gap_load.shape
    dofs = corner_rows.shape[-1]
    cuts, blocks = lax.axis_size("cuts"), lax.axis_size("blk")
    at = lax.axis_index("cuts")
    rr_rows = 3 * cuts
    height = -(-(rr_rows + 2) // 8) * 8
    gap, offsets, corner_map, flexibility, coupling, corner_rows = (
        x[0] for x in (gap_load, offsets, corner_map, flexibility, coupling, corner_rows)
    )
    shape = lambda *dims: jax.ShapeDtypeStruct(dims, F32)
    face = shape(size, loads_n)
    faces = shape(count, size, loads_n)
    pair = shape(count, 2, size, loads_n)
    four = shape(count, 4, size, loads_n)

    residual, to_far, to_right, inner = pl.pallas_call(
        prepare_kernel,
        out_shape=(pair, faces, face, faces),
        in_specs=[SMEM, VMEM],
        out_specs=(VMEM,) * 4,
        scratch_shapes=[pltpu.VMEM((count, 2, 2 * size, loads_n), F32)],
        name="prepare",
    )(offsets, gap)
    from_near = shifted(to_far, "cuts", 1, False)
    from_left = shifted(to_right, "blk", 1, True)

    tile = size
    total = flexibility.shape[1]
    block = pl.BlockSpec((1, tile, total), lambda s, i: (s, i, 0))
    a_high, a_low = pl.pallas_call(
        split_kernel,
        grid=(count, total // tile),
        out_shape=(jax.ShapeDtypeStruct(flexibility.shape, BF16),) * 2,
        in_specs=[block],
        out_specs=(block, block),
        name="split",
    )(flexibility)

    cface = lambda f: coupling[:, :, f * size:(f + 1) * size]
    note = lambda amounts: jnp.broadcast_to((amounts + 1).astype(F32)[:, None, None], (amounts.shape[0], 4, size))
    c_far = jnp.concatenate([cface(FAR), note(offsets[:, 0])], axis=1)
    c_right = jnp.concatenate([cface(RIGHT)[-1:], note(offsets[-1:, 1])], axis=1)
    c_from_near = shifted(c_far, "cuts", 1, False)
    c_from_far = shifted(cface(NEAR), "cuts", -1, False)
    c_from_left = shifted(c_right, "blk", 1, True)
    c_from_right = shifted(cface(LEFT)[:1], "blk", -1, True)
    near_offsets = c_from_near[:, 12, 0].astype(jnp.int32) - 1
    first_left = c_from_left[:, 12, 0].astype(jnp.int32) - 1
    left_offsets = jnp.concatenate([first_left, offsets[:-1, 1]])
    all_offsets = jnp.stack([near_offsets, offsets[:, 0], left_offsets, offsets[:, 1]], axis=1)
    wide = placed(by_columns(coupling), at, height).reshape(count, 2 * height, total)
    c_rows = jnp.concatenate(kept_halves(wide), axis=1)
    own = spread_out(coupling, at, height)
    far_part = spread_out(c_from_far, at + 1, height)
    near_part = spread_out(c_from_near[:, :12], at - 1, height)
    ct_own = jnp.concatenate([own, far_part, near_part], axis=1)
    ct_left = spread_out(c_from_left[0, :12], at, height)
    ct_right = spread_out(c_from_right[0], at, height)

    slots = jnp.zeros((count, height, dofs), F32)
    slots = lax.dynamic_update_slice(slots, corner_rows[:, 6:9], (0, 3 * at, 0))
    numbers = (corner_map[:, 2] + 1).astype(F32)[:, None, None]
    slots = lax.dynamic_update_slice(slots, numbers, (0, rr_rows, at))
    pieces = collected(summed(slots.reshape(count * height, dofs), "cuts"), "blk")
    numbers = jnp.concatenate([
        piece.reshape(-1, height, dofs)[:, rr_rows, :cuts].astype(jnp.int32) - 1 for piece in pieces
    ], axis=0)
    chosen = 3 * numbers[..., None] + jnp.arange(3, dtype=jnp.int32)
    chosen = jnp.pad(chosen.reshape(-1, rr_rows), ((0, 0), (0, height - rr_rows)), constant_values=-1).reshape(-1)
    pick = (jnp.arange(dofs, dtype=jnp.int32)[:, None] == chosen[None, :]).astype(BF16)
    used = (jnp.arange(pieces[0].shape[0]) % height < rr_rows)[:, None]
    k_parts = [kept_halves(jnp.where(used, piece, 0.0)) for piece in pieces]
    k_high, k_low = (
        jnp.concatenate([jnp.dot(part[i], pick, preferred_element_type=F32).astype(BF16) for part in k_parts], axis=0)
        for i in range(2)
    )

    flops = 2 * count * total * total * loads_n * 3
    moved = 4 * flexibility.size
    cost = pl.CostEstimate(flops=flops, bytes_accessed=moved, transcendentals=0)
    params = pltpu.CompilerParams(vmem_limit_bytes=40 * 1024 * 1024)
    terms_shape = shape((count + 1) * height, loads_n)
    sends = (faces, faces, pair, face, face, terms_shape)
    a_buffers = [
        pltpu.VMEM(flexibility.shape, BF16),
        pltpu.VMEM(flexibility.shape, BF16),
        pltpu.SemaphoreType.DMA((2, 4 * count)),
        pltpu.VMEM((count, total, 2 * loads_n), BF16),
    ]
    f_buffers = [
        pltpu.VMEM((blocks * count * height, loads_n), F32),
        pltpu.VMEM((count, 4, 2 * size, loads_n), F32),
    ]
    *out, loads = pl.pallas_call(
        functools.partial(first_kernel, height, rr_rows),
        out_shape=sends + (four,),
        in_specs=[VMEM] * 4 + [ANY] * 2 + [VMEM],
        out_specs=(VMEM,) * 7,
        scratch_shapes=a_buffers,
        compiler_params=params,
        cost_estimate=cost,
        name="first",
    )(residual, from_near, from_left, inner, a_high, a_low, c_rows)

    state = []
    for which in range(ITERS):
        last = which == ITERS - 1
        near, far, sides, to_left, to_right, terms = out
        gathered = collected(summed(terms, "cuts"), "blk")
        r_far = shifted(near, "cuts", -1, False)
        r_right = shifted(to_left, "blk", -1, True)
        if last:
            r_near, r_left = far, to_right
        else:
            r_near = shifted(far, "cuts", 1, False)
            r_left = shifted(to_right, "blk", 1, True)
        args = [all_offsets, *gathered, k_high, k_low, ct_own, ct_left, ct_right, near, far, sides,
                r_near, r_far, r_left, r_right, loads, *state]
        specs = [SMEM] + [VMEM] * (len(args) - 1)
        if last:
            outs, scratch = (pair, pair), f_buffers
        else:
            args += [a_high, a_low, c_rows]
            specs += [ANY, ANY, VMEM]
            outs = sends + (four, four) + ((pair, pair) if which > 0 else ()) + (shape(8, loads_n),)
            scratch = f_buffers + a_buffers
        result = pl.pallas_call(
            functools.partial(step_kernel, which, len(gathered), height, rr_rows),
            out_shape=outs,
            in_specs=specs,
            out_specs=(VMEM,) * len(outs),
            scratch_shapes=scratch,
            compiler_params=params,
            cost_estimate=None if last else cost,
            name=f"step{which}",
        )(*args)
        if last:
            multipliers, residual = result
            break
        out = result[0:6]
        before, loads = loads, result[6]
        if which == 0:
            state = [result[7], before, before, result[8]]
        else:
            state = [result[7], result[8], result[9], result[10]]
    return multipliers[None], residual[None]


def solution(mesh):
    spec5, spec4, spec3 = (P("cuts", "blk", *[None] * k) for k in (3, 2, 1))
    return jax.shard_map(
        per_device,
        mesh=mesh,
        in_specs=(spec5, spec3, spec3, spec4, spec4, spec4),
        out_specs=(spec5, spec5),
        check_vma=False,
    )
```

time: 553 us -> 174 us (0.31); the launches traced: 544 us -> 173 us
  blocking collectives: 357 us -> 0 us
  local copies, waits for them, and re-layouts: 67.4 us -> 13.2 us
  starting transfers between devices: 17.8 us -> 63.3 us
  matrix products: 44.1 us -> 6.1 us
  Pallas kernels: 0 us -> 31.5 us
  waiting for transfers between devices: 23.2 us -> 50.6 us
  other arithmetic: 32.3 us -> 5.32 us
    psum x5 -> x0, blocking collectives: 198 us -> none  [the longest x3 121 us: squares(): return lax.psum(inner_sum(residual, residual), ('cuts', 'blk'))]
    all_gather x4 -> x0, blocking collectives: 159 us -> none  [the longest x3 120 us: per_device(): lax.all_gather(operator_corner_terms, ('cuts', 'blk'), axis=0, tiled=True)]
    ppermute x12 -> x56, starting transfers between devices: 17.8 us -> 63.3 us  [shifted(): return lax.ppermute(value, axis, pairs)]
    gather x12 -> x0, local copies, waits for them, and re-layouts: 43.9 us -> none  [rotate(): return jnp.take_along_axis(values, indices[..., None], axis=-2)]
    dot_general x12 -> x16, matrix products: 44.1 us -> 6.1 us  [per_device(): jnp.dot(part[i], pick, preferred_element_type=F32).astype(BF16)]
    pallas_call x0 -> x6, Pallas kernels: none -> 31.5 us  [the longest x3 15.4 us: per_device(): pl.pallas_call(functools.partial(step_kernel, which, len(gathered), heigh...]
    ppermute x12 -> x56, waiting for transfers between devices: 23.2 us -> 50.6 us  [shifted(): return lax.ppermute(value, axis, pairs)]
    scatter-add x3 -> x0, other arithmetic: 18.8 us -> none  [per_device(): whole.at[every_dofs.reshape(-1)]]
  transfers between devices with their start and end apart: 12 -> 56, of which waited for: 6 -> 22; matrix products, arithmetic and copies ran while one was open for 5% -> 11% of each run, Pallas kernels for 0% -> 6%
where the time goes in v1:
time: 174 us; the launch traced here: 173 us
  starting transfers between devices  63.3 us (36%)
  waiting for transfers between devices  50.6 us (29%)
  Pallas kernels  31.5 us (18%)
  local copies, waits for them, and re-layouts  13.2 us (8%)
  matrix products  6.1 us (4%)
  other arithmetic  5.32 us (3%)
  between operations  2.61 us (2%)
    ppermute x56, starting transfers between devices, shifted(): return lax.ppermute(value, axis, pairs)  63.3 us
    ppermute x56, waiting for transfers between devices, shifted(): return lax.ppermute(value, axis, pairs)  50.6 us
    pallas_call x3, Pallas kernels, per_device(): pl.pallas_call(functools.partial(step_kernel, which, len(gathered), heigh...  15.4 us
    pallas_call x1, Pallas kernels, per_device(): pl.pallas_call(split_kernel, grid=(count, total // tile), out_shape=(jax....  9.03 us
    dot_general x16, matrix products, per_device(): jnp.dot(part[i], pick, preferred_element_type=F32).astype(BF16)  6.1 us
    unnamed x12, local copies, waits for them, and re-layouts  5.21 us
    pallas_call x1, Pallas kernels, per_device(): pl.pallas_call(functools.partial(first_kernel, height, rr_rows), out_shap...  4.94 us
  transfers between devices with their start and end apart: 56, of which 22 were waited for; matrix products, arithmetic and copies ran while one was open for 11% of the time, Pallas kernels for 6%

profile of v1, /device:TPU:0, one launch (start us, length us, event | category | flops | bytes accessed | tf_op | source)
XLA Modules:
  0.0 172.7 jit_solution(13848182804818859379)
XLA Ops:
  2.4 3.1 %collective-permute-start.15 = (f32[32,192]{1,0:T(8,128)S(1)}, f32[32,192]{1,0:T(8,128)S(1)}, u32[]{:S(2)}, u32[]{:S(2)}) collective-permute-start(f32[32,192]{1,0:T(8,128)S(1)} %bitcast.86), channel_id=1, source_target_pairs={{0,16},{8,24},{16,0},{24,8},{1,17},{9,25},{17,1},{25,9},{2,18},{10... | collective-permute-start | bytes 73736 | tf_op jit(solution)/shard_map/ppermute | solution.py:24
  8.3 2.3 %collective-permute-start.25 = (f32[1,12,256]{2,0,1:T(1,128)S(1)}, f32[1,12,256]{2,0,1:T(1,128)S(1)}, u32[]{:S(2)}, u32[]{:S(2)}) collective-permute-start(f32[1,12,256]{2,0,1:T(1,128)S(1)} %get-tuple-element.84), channel_id=1, source_target_pairs={{0,7},{1,0},{2,1},{3,2},{4,3},{5,4},{6,5},{7,6},{8,15},{9,8},{10,9... | collective-permute-start | bytes 36872 | tf_op jit(solution)/shard_map/ppermute | solution.py:24
  17.1 2.2 %prepare.1 = (f32[2,2,256,128]{3,2,1,0:T(8,128)}, f32[2,256,128]{2,1,0:T(8,128)}, f32[256,128]{1,0:T(8,128)}, f32[2,256,128]{2,1,0:T(8,128)}) custom-call(s32[2,2]{1,0:T(2,128)} %bitcast.103, f32[2,2,256,128]{3,2,1,0:T(8,128)} %bitcast.78), custom_call_target="tpu_custom_call" | custom-call | tf_op jit(solution)/shard_map/prepare/pallas_call | solution.py:324
  19.3 9.0 %split.1 = (bf16[2,1024,1024]{2,1,0:T(8,128)(2,1)}, bf16[2,1024,1024]{2,1,0:T(8,128)(2,1)}) custom-call(f32[2,1024,1024]{2,1,0:T(8,128)} %bitcast.76), custom_call_target="tpu_custom_call" | custom-call | tf_op jit(solution)/shard_map/split/pallas_call | solution.py:338
  29.7 4.9 %collective-permute-start = (f32[2,16,256]{2,0,1:T(2,128)S(1)}, f32[2,16,256]{2,0,1:T(2,128)S(1)}, u32[]{:S(2)}, u32[]{:S(2)}) collective-permute-start(f32[2,16,256]{2,0,1:T(2,128)S(1)} %pad_maximum_fusion.3), channel_id=1, source_target_pairs={{0,8},{8,16},{16,24},{1,9},{9,17},{17,25},{2,10},{10,18},{18,26},{... | collective-permute-start | bytes 98312 | tf_op jit(solution)/shard_map/ppermute | solution.py:24
  37.3 4.8 %collective-permute-start.2 = (f32[2,256,128]{2,1,0:T(8,128)}, f32[2,256,128]{2,1,0:T(8,128)S(1)}, u32[]{:S(2)}, u32[]{:S(2)}) collective-permute-start(f32[2,256,128]{2,1,0:T(8,128)} %get-tuple-element.38), channel_id=1, source_target_pairs={{0,8},{8,16},{16,24},{1,9},{9,17},{17,25},{2,10},{10,18},{18,26},{... | collective-permute-start | bytes 786440 | tf_op jit(solution)/shard_map/ppermute | solution.py:24
  42.2 3.3 %collective-permute-start.23 = (f32[32,192]{1,0:T(8,128)S(1)}, f32[32,192]{1,0:T(8,128)S(1)}, u32[]{:S(2)}, u32[]{:S(2)}) collective-permute-start(f32[32,192]{1,0:T(8,128)S(1)} %add_add_fusion), channel_id=1, source_target_pairs={{0,7},{1,0},{2,1},{3,2},{4,3},{5,4},{6,5},{7,6},{8,15},{9,8},{10,9... | collective-permute-start | bytes 73736 | tf_op jit(solution)/shard_map/ppermute | solution.py:24
  47.2 2.7 %collective-permute-start.20 = (f32[32,192]{1,0:T(8,128)S(1)}, f32[32,192]{1,0:T(8,128)S(1)}, u32[]{:S(2)}, u32[]{:S(2)}) collective-permute-start(f32[32,192]{1,0:T(8,128)S(1)} %add_add_fusion), channel_id=1, source_target_pairs={{0,4},{1,5},{2,6},{3,7},{4,0},{5,1},{6,2},{7,3},{8,12},{9,13},{10,... | collective-permute-start | bytes 73736 | tf_op jit(solution)/shard_map/ppermute | solution.py:24
  54.3 3.4 %collective-permute-done.18 = f32[32,192]{1,0:T(8,128)S(1)} collective-permute-done((f32[32,192]{1,0:T(8,128)S(1)}, f32[32,192]{1,0:T(8,128)S(1)}, u32[]{:S(2)}, u32[]{:S(2)}) %collective-permute-start.18) | collective-permute-done | bytes 24608 | tf_op jit(solution)/shard_map/ppermute | solution.py:24
  62.6 2.2 %copy-done = bf16[2,1024,1024]{2,1,0:T(8,128)(2,1)S(1)} copy-done((bf16[2,1024,1024]{2,1,0:T(8,128)(2,1)S(1)}, bf16[2,1024,1024]{2,1,0:T(8,128)(2,1)}, u32[]{:S(2)}) %copy-start) | copy-done | bytes 4194328
  64.8 2.2 %copy-done.2 = bf16[2,1024,1024]{2,1,0:T(8,128)(2,1)S(1)} copy-done((bf16[2,1024,1024]{2,1,0:T(8,128)(2,1)S(1)}, bf16[2,1024,1024]{2,1,0:T(8,128)(2,1)}, u32[]{:S(2)}) %copy-start.2) | copy-done | bytes 4194328
  67.0 4.9 %first.1 = (f32[2,256,128]{2,1,0:T(8,128)S(1)}, f32[2,256,128]{2,1,0:T(8,128)S(1)}, f32[2,2,256,128]{3,2,1,0:T(8,128)S(1)}, f32[256,128]{1,0:T(8,128)S(1)}, f32[...) custom-call(f32[2,2,256,128]{3,2,1,0:T(8,128)S(1)} %copy-done.3, ...), custom_call_target="tpu_custom_call" | custom-call | flops 1610612736 | bytes 8388608 | tf_op jit(solution)/shard_map/first/pallas_call | solution.py:402
  72.0 1.7 %collective-permute-start.5 = (f32[48,128]{1,0:T(8,128)S(1)}, f32[48,128]{1,0:T(8,128)S(1)}, u32[]{:S(2)}, u32[]{:S(2)}) collective-permute-start(f32[48,128]{1,0:T(8,128)S(1)} %get-tuple-element.43), channel_id=1, source_target_pairs={{0,16},{8,24},{16,0},{24,8},{1,17},{9,25},{17,1},{25,9},{2,18},{10... | collective-permute-start | bytes 73736 | tf_op jit(solution)/shard_map/ppermute | solution.py:24
  75.9 2.6 %collective-permute-done.4 = f32[48,128]{1,0:T(8,128)S(1)} collective-permute-done((f32[48,128]{1,0:T(8,128)S(1)}, f32[48,128]{1,0:T(8,128)S(1)}, u32[]{:S(2)}, u32[]{:S(2)}) %collective-permute-start.4) | collective-permute-done | bytes 24608 | tf_op jit(solution)/shard_map/ppermute | solution.py:24
  82.2 4.6 %collective-permute-start.26 = (f32[2,256,128]{2,1,0:T(8,128)S(1)}, f32[2,256,128]{2,1,0:T(8,128)S(1)}, u32[]{:S(2)}, u32[]{:S(2)}) collective-permute-start(f32[2,256,128]{2,1,0:T(8,128)S(1)} %get-tuple-element.45.refs_15_), channel_id=1, source_target_pairs={{0,8},{8,16},{16,24},{1,9},{9,17},{17,25},{2,10},{10,18},{18,26},{... | collective-permute-start | bytes 786440 | tf_op jit(solution)/shard_map/ppermute | solution.py:24
  86.8 2.8 %collective-permute-start.10 = (f32[48,128]{1,0:T(8,128)S(1)}, f32[48,128]{1,0:T(8,128)S(1)}, u32[]{:S(2)}, u32[]{:S(2)}) collective-permute-start(f32[48,128]{1,0:T(8,128)S(1)} %add_add_fusion.3.refs_1_), channel_id=1, source_target_pairs={{0,4},{1,5},{2,6},{3,7},{4,0},{5,1},{6,2},{7,3},{8,12},{9,13},{10,... | collective-permute-start | bytes 73736 | tf_op jit(solution)/shard_map/ppermute | solution.py:24
  92.0 2.0 %collective-permute-done.9.refs_4_ = f32[48,128]{1,0:T(8,128)S(1)} collective-permute-done((f32[48,128]{1,0:T(8,128)S(1)}, f32[48,128]{1,0:T(8,128)S(1)}, u32[]{:S(2)}, u32[]{:S(2)}) %collective-permute-start.9) | collective-permute-done | bytes 24608 | tf_op jit(solution)/shard_map/ppermute | solution.py:24
  95.6 4.9 %collective-permute-done.7.refs_2_ = f32[48,128]{1,0:T(8,128)S(1)} collective-permute-done((f32[48,128]{1,0:T(8,128)S(1)}, f32[48,128]{1,0:T(8,128)S(1)}, u32[]{:S(2)}, u32[]{:S(2)}) %collective-permute-start.7) | collective-permute-done | bytes 24608 | tf_op jit(solution)/shard_map/ppermute | solution.py:24
  100.5 6.2 %step0.1 = (f32[2,256,128]{2,1,0:T(8,128)S(1)}, f32[2,256,128]{2,1,0:T(8,128)S(1)}, f32[2,2,256,128]{3,2,1,0:T(8,128)S(1)}, f32[256,128]{1,0:T(8,128)S(1)}, f32[...) custom-call(s32[2,4]{1,0:T(2,128)S(1)} %pad_add_fusion.refs_0_, ...), custom_call_target="tpu_custom_call" | custom-call | flops 1610612736 | bytes 8388608 | tf_op jit(solution)/shard_map/step0/pallas_call | solution.py:435
  110.4 4.6 %collective-permute-start.40 = (f32[2,256,128]{2,1,0:T(8,128)S(1)}, f32[2,256,128]{2,1,0:T(8,128)S(1)}, u32[]{:S(2)}, u32[]{:S(2)}) collective-permute-start(f32[2,256,128]{2,1,0:T(8,128)S(1)} %get-tuple-element.52.refs_15_), channel_id=1, source_target_pairs={{0,8},{8,16},{16,24},{1,9},{9,17},{17,25},{2,10},{10,18},{18,26},{... | collective-permute-start | bytes 786440 | tf_op jit(solution)/shard_map/ppermute | solution.py:24
  116.6 3.7 %collective-permute-start.43 = (f32[256,128]{1,0:T(8,128)S(1)}, f32[256,128]{1,0:T(8,128)S(1)}, u32[]{:S(2)}, u32[]{:S(2)}) collective-permute-start(f32[256,128]{1,0:T(8,128)S(1)} %get-tuple-element.55), channel_id=1, source_target_pairs={{0,7},{1,0},{2,1},{3,2},{4,3},{5,4},{6,5},{7,6},{8,15},{9,8},{10,9... | collective-permute-start | bytes 393224 | tf_op jit(solution)/shard_map/ppermute | solution.py:24
  120.3 3.5 %collective-permute-done.37.refs_6_ = f32[48,128]{1,0:T(8,128)S(1)} collective-permute-done((f32[48,128]{1,0:T(8,128)S(1)}, f32[48,128]{1,0:T(8,128)S(1)}, u32[]{:S(2)}, u32[]{:S(2)}) %collective-permute-start.37) | collective-permute-done | bytes 24608 | tf_op jit(solution)/shard_map/ppermute | solution.py:24
  123.8 4.7 %collective-permute-done.36.refs_5_ = f32[48,128]{1,0:T(8,128)S(1)} collective-permute-done((f32[48,128]{1,0:T(8,128)S(1)}, f32[48,128]{1,0:T(8,128)S(1)}, u32[]{:S(2)}, u32[]{:S(2)}) %collective-permute-start.36) | collective-permute-done | bytes 24608 | tf_op jit(solution)/shard_map/ppermute | solution.py:24
  128.5 4.1 %collective-permute-done.35.refs_4_ = f32[48,128]{1,0:T(8,128)S(1)} collective-permute-done((f32[48,128]{1,0:T(8,128)S(1)}, f32[48,128]{1,0:T(8,128)S(1)}, u32[]{:S(2)}, u32[]{:S(2)}) %collective-permute-start.35) | collective-permute-done | bytes 24608 | tf_op jit(solution)/shard_map/ppermute | solution.py:24
  133.0 5.3 %collective-permute-done.34.refs_3_ = f32[48,128]{1,0:T(8,128)S(1)} collective-permute-done((f32[48,128]{1,0:T(8,128)S(1)}, f32[48,128]{1,0:T(8,128)S(1)}, u32[]{:S(2)}, u32[]{:S(2)}) %collective-permute-start.34) | collective-permute-done | bytes 24608 | tf_op jit(solution)/shard_map/ppermute | solution.py:24
  138.3 5.0 %collective-permute-done.33.refs_2_ = f32[48,128]{1,0:T(8,128)S(1)} collective-permute-done((f32[48,128]{1,0:T(8,128)S(1)}, f32[48,128]{1,0:T(8,128)S(1)}, u32[]{:S(2)}, u32[]{:S(2)}) %collective-permute-start.33) | collective-permute-done | bytes 24608 | tf_op jit(solution)/shard_map/ppermute | solution.py:24
  143.4 7.1 %step1.1 = (f32[2,256,128]{2,1,0:T(8,128)S(1)}, f32[2,256,128]{2,1,0:T(8,128)S(1)}, f32[2,2,256,128]{3,2,1,0:T(8,128)S(1)}, f32[256,128]{1,0:T(8,128)S(1)}, f32[...) custom-call(s32[2,4]{1,0:T(2,128)S(1)} %pad_add_fusion.refs_0_, ...), custom_call_target="tpu_custom_call" | custom-call | flops 1610612736 | bytes 8388608 | tf_op jit(solution)/shard_map/step1/pallas_call | solution.py:435
  150.9 3.1 %collective-permute-start.45 = (f32[48,128]{1,0:T(8,128)S(1)}, f32[48,128]{1,0:T(8,128)S(1)}, u32[]{:S(2)}, u32[]{:S(2)}) collective-permute-start(f32[48,128]{1,0:T(8,128)S(1)} %get-tuple-element.59), channel_id=1, source_target_pairs={{0,16},{8,24},{16,0},{24,8},{1,17},{9,25},{17,1},{25,9},{2,18},{10... | collective-permute-start | bytes 73736 | tf_op jit(solution)/shard_map/ppermute | solution.py:24
  155.8 2.9 %collective-permute-done.44 = f32[48,128]{1,0:T(8,128)S(1)} collective-permute-done((f32[48,128]{1,0:T(8,128)S(1)}, f32[48,128]{1,0:T(8,128)S(1)}, u32[]{:S(2)}, u32[]{:S(2)}) %collective-permute-start.44) | collective-permute-done | bytes 24608 | tf_op jit(solution)/shard_map/ppermute | solution.py:24
  162.7 2.0 %collective-permute-start.49 = (f32[48,128]{1,0:T(8,128)S(1)}, f32[48,128]{1,0:T(8,128)S(1)}, u32[]{:S(2)}, u32[]{:S(2)}) collective-permute-start(f32[48,128]{1,0:T(8,128)S(1)} %add_add_fusion.1.refs_1_), channel_id=1, source_target_pairs={{0,3},{1,4},{2,5},{3,6},{4,7},{5,0},{6,1},{7,2},{8,11},{9,12},{10,... | collective-permute-start | bytes 73736 | tf_op jit(solution)/shard_map/ppermute | solution.py:24
  166.9 3.7 %collective-permute-done.48.refs_3_ = f32[48,128]{1,0:T(8,128)S(1)} collective-permute-done((f32[48,128]{1,0:T(8,128)S(1)}, f32[48,128]{1,0:T(8,128)S(1)}, u32[]{:S(2)}, u32[]{:S(2)}) %collective-permute-start.48) | collective-permute-done | bytes 24608 | tf_op jit(solution)/shard_map/ppermute | solution.py:24
  170.6 2.1 %step2.1 = (f32[2,2,256,128]{3,2,1,0:T(8,128)}, f32[2,2,256,128]{3,2,1,0:T(8,128)}) custom-call(s32[2,4]{1,0:T(2,128)S(1)} %pad_add_fusion.refs_0_, f32[48,128]{1,0:T(8,128)S(1)} %add_add_fusion.1.refs_1_, f32[48,128]{1,0:T(8,128)S(1)} %collective-permute-done.47.refs_2_, f32[48,128]{1,0:T(8,128)S(1)} %collective-permute-done.48.refs_3_, ...), custom_call_target="tpu_custom_call" | custom-call | tf_op jit(solution)/shard_map/step2/pallas_call | solution.py:435
  (195 shorter events, 48.5 us)
Async XLA Ops:
  2.4 34.9 %collective-permute-start.15 = (f32[32,192]{1,0:T(8,128)S(1)}, f32[32,192]{1,0:T(8,128)S(1)}, u32[]{:S(2)}, u32[]{:S(2)}) collective-permute-start(f32[32,192]{1,0:T(8,128)S(1)} %bitcast.86), channel_id=1, source_target_pairs={{0,16},{8,24},{16,0},{24,8},{1,17},{9,25},{17,1},{25,9},{2,18},{10... | collective-permute-start | bytes 73736 | tf_op jit(solution)/shard_map/ppermute | solution.py:24
  5.5 31.8 %collective-permute-start.16 = (f32[32,192]{1,0:T(8,128)S(1)}, f32[32,192]{1,0:T(8,128)S(1)}, u32[]{:S(2)}, u32[]{:S(2)}) collective-permute-start(f32[32,192]{1,0:T(8,128)S(1)} %bitcast.87), channel_id=1, source_target_pairs={{0,24},{8,0},{16,8},{24,16},{1,25},{9,1},{17,9},{25,17},{2,26},{10... | collective-permute-start | bytes 73736 | tf_op jit(solution)/shard_map/ppermute | solution.py:24
  7.0 35.2 %collective-permute-start.14 = (f32[32,192]{1,0:T(8,128)S(1)}, f32[32,192]{1,0:T(8,128)S(1)}, u32[]{:S(2)}, u32[]{:S(2)}) collective-permute-start(f32[32,192]{1,0:T(8,128)S(1)} %bitcast.88), channel_id=1, source_target_pairs={{0,8},{8,16},{16,24},{24,0},{1,9},{9,17},{17,25},{25,1},{2,10},{10... | collective-permute-start | bytes 73736 | tf_op jit(solution)/shard_map/ppermute | solution.py:24
  8.3 20.0 %collective-permute-start.25 = (f32[1,12,256]{2,0,1:T(1,128)S(1)}, f32[1,12,256]{2,0,1:T(1,128)S(1)}, u32[]{:S(2)}, u32[]{:S(2)}) collective-permute-start(f32[1,12,256]{2,0,1:T(1,128)S(1)} %get-tuple-element.84), channel_id=1, source_target_pairs={{0,7},{1,0},{2,1},{3,2},{4,3},{5,4},{6,5},{7,6},{8,15},{9,8},{10,9... | collective-permute-start | bytes 36872 | tf_op jit(solution)/shard_map/ppermute | solution.py:24
  12.7 17.0 %collective-permute-start.1 = (f32[1,16,256]{2,0,1:T(1,128)S(1)}, f32[1,16,256]{2,0,1:T(1,128)S(1)}, u32[]{:S(2)}, u32[]{:S(2)}) collective-permute-start(f32[1,16,256]{2,0,1:T(1,128)S(1)} %concatenate.44), channel_id=1, source_target_pairs={{0,1},{1,2},{2,3},{3,4},{4,5},{5,6},{6,7},{7,0},{8,9},{9,10},{10,1... | collective-permute-start | bytes 49160 | tf_op jit(solution)/shard_map/ppermute | solution.py:24
  28.3 17.2 %collective-permute-start.24 = (f32[2,12,256]{2,0,1:T(2,128)S(1)}, f32[2,12,256]{2,0,1:T(2,128)S(1)}, u32[]{:S(2)}, u32[]{:S(2)}) collective-permute-start(f32[2,12,256]{2,0,1:T(2,128)S(1)} %get-tuple-element.86), channel_id=1, source_target_pairs={{8,0},{16,8},{24,16},{9,1},{17,9},{25,17},{10,2},{18,10},{26,18},{... | collective-permute-start | bytes 73736 | tf_op jit(solution)/shard_map/ppermute | solution.py:24
  29.7 16.3 %collective-permute-start = (f32[2,16,256]{2,0,1:T(2,128)S(1)}, f32[2,16,256]{2,0,1:T(2,128)S(1)}, u32[]{:S(2)}, u32[]{:S(2)}) collective-permute-start(f32[2,16,256]{2,0,1:T(2,128)S(1)} %pad_maximum_fusion.3), channel_id=1, source_target_pairs={{0,8},{8,16},{16,24},{1,9},{9,17},{17,25},{2,10},{10,18},{18,26},{... | collective-permute-start | bytes 98312 | tf_op jit(solution)/shard_map/ppermute | solution.py:24
  37.3 25.2 %collective-permute-start.3 = (f32[256,128]{1,0:T(8,128)}, f32[256,128]{1,0:T(8,128)S(1)}, u32[]{:S(2)}, u32[]{:S(2)}) collective-permute-start(f32[256,128]{1,0:T(8,128)} %get-tuple-element.39), channel_id=1, source_target_pairs={{0,1},{1,2},{2,3},{3,4},{4,5},{5,6},{6,7},{7,0},{8,9},{9,10},{10,1... | collective-permute-start | bytes 393224 | tf_op jit(solution)/shard_map/ppermute | solution.py:24
  37.3 25.2 %collective-permute-start.2 = (f32[2,256,128]{2,1,0:T(8,128)}, f32[2,256,128]{2,1,0:T(8,128)S(1)}, u32[]{:S(2)}, u32[]{:S(2)}) collective-permute-start(f32[2,256,128]{2,1,0:T(8,128)} %get-tuple-element.38), channel_id=1, source_target_pairs={{0,8},{8,16},{16,24},{1,9},{9,17},{17,25},{2,10},{10,18},{18,26},{... | collective-permute-start | bytes 786440 | tf_op jit(solution)/shard_map/ppermute | solution.py:24
  46.0 5.7 %collective-permute-start.21 = (f32[32,192]{1,0:T(8,128)S(1)}, f32[32,192]{1,0:T(8,128)}, u32[]{:S(2)}, u32[]{:S(2)}) collective-permute-start(f32[32,192]{1,0:T(8,128)S(1)} %add_add_fusion), channel_id=1, source_target_pairs={{0,5},{1,6},{2,7},{3,0},{4,1},{5,2},{6,3},{7,4},{8,13},{9,14},{10,... | collective-permute-start | bytes 73736 | tf_op jit(solution)/shard_map/ppermute | solution.py:24
  51.7 5.9 %collective-permute-start.18 = (f32[32,192]{1,0:T(8,128)S(1)}, f32[32,192]{1,0:T(8,128)S(1)}, u32[]{:S(2)}, u32[]{:S(2)}) collective-permute-start(f32[32,192]{1,0:T(8,128)S(1)} %add_add_fusion), channel_id=1, source_target_pairs={{0,2},{1,3},{2,4},{3,5},{4,6},{5,7},{6,0},{7,1},{8,10},{9,11},{10,... | collective-permute-start | bytes 73736 | tf_op jit(solution)/shard_map/ppermute | solution.py:24
  52.5 5.8 %collective-permute-start.17 = (f32[32,192]{1,0:T(8,128)S(1)}, f32[32,192]{1,0:T(8,128)S(1)}, u32[]{:S(2)}, u32[]{:S(2)}) collective-permute-start(f32[32,192]{1,0:T(8,128)S(1)} %add_add_fusion), channel_id=1, source_target_pairs={{0,1},{1,2},{2,3},{3,4},{4,5},{5,6},{6,7},{7,0},{8,9},{9,10},{10,1... | collective-permute-start | bytes 73736 | tf_op jit(solution)/shard_map/ppermute | solution.py:24
  78.4 8.3 %collective-permute-start.13 = (f32[48,128]{1,0:T(8,128)S(1)}, f32[48,128]{1,0:T(8,128)S(1)}, u32[]{:S(2)}, u32[]{:S(2)}) collective-permute-start(f32[48,128]{1,0:T(8,128)S(1)} %add_add_fusion.3.refs_1_), channel_id=1, source_target_pairs={{0,7},{1,0},{2,1},{3,2},{4,3},{5,4},{6,5},{7,6},{8,15},{9,8},{10,9... | collective-permute-start | bytes 73736 | tf_op jit(solution)/shard_map/ppermute | solution.py:24
  78.5 11.0 %collective-permute-start.12 = (f32[48,128]{1,0:T(8,128)S(1)}, f32[48,128]{1,0:T(8,128)S(1)}, u32[]{:S(2)}, u32[]{:S(2)}) collective-permute-start(f32[48,128]{1,0:T(8,128)S(1)} %add_add_fusion.3.refs_1_), channel_id=1, source_target_pairs={{0,6},{1,7},{2,0},{3,1},{4,2},{5,3},{6,4},{7,5},{8,14},{9,15},{10,... | collective-permute-start | bytes 73736 | tf_op jit(solution)/shard_map/ppermute | solution.py:24
  79.9 9.6 %collective-permute-start.11 = (f32[48,128]{1,0:T(8,128)S(1)}, f32[48,128]{1,0:T(8,128)S(1)}, u32[]{:S(2)}, u32[]{:S(2)}) collective-permute-start(f32[48,128]{1,0:T(8,128)S(1)} %add_add_fusion.3.refs_1_), channel_id=1, source_target_pairs={{0,5},{1,6},{2,7},{3,0},{4,1},{5,2},{6,3},{7,4},{8,13},{9,14},{10,... | collective-permute-start | bytes 73736 | tf_op jit(solution)/shard_map/ppermute | solution.py:24
  80.9 19.5 %collective-permute-start.27 = (f32[2,256,128]{2,1,0:T(8,128)S(1)}, f32[2,256,128]{2,1,0:T(8,128)S(1)}, u32[]{:S(2)}, u32[]{:S(2)}) collective-permute-start(f32[2,256,128]{2,1,0:T(8,128)S(1)} %get-tuple-element.44.refs_14_), channel_id=1, source_target_pairs={{8,0},{16,8},{24,16},{9,1},{17,9},{25,17},{10,2},{18,10},{26,18},{... | collective-permute-start | bytes 786440 | tf_op jit(solution)/shard_map/ppermute | solution.py:24
  82.2 18.3 %collective-permute-start.26 = (f32[2,256,128]{2,1,0:T(8,128)S(1)}, f32[2,256,128]{2,1,0:T(8,128)S(1)}, u32[]{:S(2)}, u32[]{:S(2)}) collective-permute-start(f32[2,256,128]{2,1,0:T(8,128)S(1)} %get-tuple-element.45.refs_15_), channel_id=1, source_target_pairs={{0,8},{8,16},{16,24},{1,9},{9,17},{17,25},{2,10},{10,18},{18,26},{... | collective-permute-start | bytes 786440 | tf_op jit(solution)/shard_map/ppermute | solution.py:24
  89.5 5.8 %collective-permute-start.8 = (f32[48,128]{1,0:T(8,128)S(1)}, f32[48,128]{1,0:T(8,128)S(1)}, u32[]{:S(2)}, u32[]{:S(2)}) collective-permute-start(f32[48,128]{1,0:T(8,128)S(1)} %add_add_fusion.3.refs_1_), channel_id=1, source_target_pairs={{0,2},{1,3},{2,4},{3,5},{4,6},{5,7},{6,0},{7,1},{8,10},{9,11},{10,... | collective-permute-start | bytes 73736 | tf_op jit(solution)/shard_map/ppermute | solution.py:24
  91.8 8.6 %collective-permute-start.28 = (f32[256,128]{1,0:T(8,128)S(1)}, f32[256,128]{1,0:T(8,128)S(1)}, u32[]{:S(2)}, u32[]{:S(2)}) collective-permute-start(f32[256,128]{1,0:T(8,128)S(1)} %get-tuple-element.47), channel_id=1, source_target_pairs={{0,1},{1,2},{2,3},{3,4},{4,5},{5,6},{6,7},{7,0},{8,9},{9,10},{10,1... | collective-permute-start | bytes 393224 | tf_op jit(solution)/shard_map/ppermute | solution.py:24
  94.0 6.5 %collective-permute-start.29 = (f32[256,128]{1,0:T(8,128)S(1)}, f32[256,128]{1,0:T(8,128)S(1)}, u32[]{:S(2)}, u32[]{:S(2)}) collective-permute-start(f32[256,128]{1,0:T(8,128)S(1)} %get-tuple-element.48), channel_id=1, source_target_pairs={{0,7},{1,0},{2,1},{3,2},{4,3},{5,4},{6,5},{7,6},{8,15},{9,8},{10,9... | collective-permute-start | bytes 393224 | tf_op jit(solution)/shard_map/ppermute | solution.py:24
  106.7 8.3 %collective-permute-start.32 = (f32[48,128]{1,0:T(8,128)S(1)}, f32[48,128]{1,0:T(8,128)S(1)}, u32[]{:S(2)}, u32[]{:S(2)}) collective-permute-start(f32[48,128]{1,0:T(8,128)S(1)} %get-tuple-element.50), channel_id=1, source_target_pairs={{0,24},{8,0},{16,8},{24,16},{1,25},{9,1},{17,9},{25,17},{2,26},{10... | collective-permute-start | bytes 73736 | tf_op jit(solution)/shard_map/ppermute | solution.py:24
  106.7 8.3 %collective-permute-start.31 = (f32[48,128]{1,0:T(8,128)S(1)}, f32[48,128]{1,0:T(8,128)S(1)}, u32[]{:S(2)}, u32[]{:S(2)}) collective-permute-start(f32[48,128]{1,0:T(8,128)S(1)} %get-tuple-element.50), channel_id=1, source_target_pairs={{0,16},{8,24},{16,0},{24,8},{1,17},{9,25},{17,1},{25,9},{2,18},{10... | collective-permute-start | bytes 73736 | tf_op jit(solution)/shard_map/ppermute | solution.py:24
  108.5 6.5 %collective-permute-start.30 = (f32[48,128]{1,0:T(8,128)S(1)}, f32[48,128]{1,0:T(8,128)S(1)}, u32[]{:S(2)}, u32[]{:S(2)}) collective-permute-start(f32[48,128]{1,0:T(8,128)S(1)} %get-tuple-element.50), channel_id=1, source_target_pairs={{0,8},{8,16},{16,24},{24,0},{1,9},{9,17},{17,25},{25,1},{2,10},{10... | collective-permute-start | bytes 73736 | tf_op jit(solution)/shard_map/ppermute | solution.py:24
  109.1 34.3 %collective-permute-start.41 = (f32[2,256,128]{2,1,0:T(8,128)S(1)}, f32[2,256,128]{2,1,0:T(8,128)S(1)}, u32[]{:S(2)}, u32[]{:S(2)}) collective-permute-start(f32[2,256,128]{2,1,0:T(8,128)S(1)} %get-tuple-element.51.refs_14_), channel_id=1, source_target_pairs={{8,0},{16,8},{24,16},{9,1},{17,9},{25,17},{10,2},{18,10},{26,18},{... | collective-permute-start | bytes 786440 | tf_op jit(solution)/shard_map/ppermute | solution.py:24
  110.4 33.0 %collective-permute-start.40 = (f32[2,256,128]{2,1,0:T(8,128)S(1)}, f32[2,256,128]{2,1,0:T(8,128)S(1)}, u32[]{:S(2)}, u32[]{:S(2)}) collective-permute-start(f32[2,256,128]{2,1,0:T(8,128)S(1)} %get-tuple-element.52.refs_15_), channel_id=1, source_target_pairs={{0,8},{8,16},{16,24},{1,9},{9,17},{17,25},{2,10},{10,18},{18,26},{... | collective-permute-start | bytes 786440 | tf_op jit(solution)/shard_map/ppermute | solution.py:24
  115.2 28.2 %collective-permute-start.42 = (f32[256,128]{1,0:T(8,128)S(1)}, f32[256,128]{1,0:T(8,128)S(1)}, u32[]{:S(2)}, u32[]{:S(2)}) collective-permute-start(f32[256,128]{1,0:T(8,128)S(1)} %get-tuple-element.54), channel_id=1, source_target_pairs={{0,1},{1,2},{2,3},{3,4},{4,5},{5,6},{6,7},{7,0},{8,9},{9,10},{10,1... | collective-permute-start | bytes 393224 | tf_op jit(solution)/shard_map/ppermute | solution.py:24
  116.6 26.8 %collective-permute-start.43 = (f32[256,128]{1,0:T(8,128)S(1)}, f32[256,128]{1,0:T(8,128)S(1)}, u32[]{:S(2)}, u32[]{:S(2)}) collective-permute-start(f32[256,128]{1,0:T(8,128)S(1)} %get-tuple-element.55), channel_id=1, source_target_pairs={{0,7},{1,0},{2,1},{3,2},{4,3},{5,4},{6,5},{7,6},{8,15},{9,8},{10,9... | collective-permute-start | bytes 393224 | tf_op jit(solution)/shard_map/ppermute | solution.py:24
  132.7 5.6 %collective-permute-start.34 = (f32[48,128]{1,0:T(8,128)S(1)}, f32[48,128]{1,0:T(8,128)S(1)}, u32[]{:S(2)}, u32[]{:S(2)}) collective-permute-start(f32[48,128]{1,0:T(8,128)S(1)} %add_add_fusion.2.refs_1_), channel_id=1, source_target_pairs={{0,2},{1,3},{2,4},{3,5},{4,6},{5,7},{6,0},{7,1},{8,10},{9,11},{10,... | collective-permute-start | bytes 73736 | tf_op jit(solution)/shard_map/ppermute | solution.py:24
  154.2 16.4 %collective-permute-start.55 = (f32[256,128]{1,0:T(8,128)S(1)}, f32[256,128]{1,0:T(8,128)S(1)}, u32[]{:S(2)}, u32[]{:S(2)}) collective-permute-start(f32[256,128]{1,0:T(8,128)S(1)} %get-tuple-element.64), channel_id=1, source_target_pairs={{0,7},{1,0},{2,1},{3,2},{4,3},{5,4},{6,5},{7,6},{8,15},{9,8},{10,9... | collective-permute-start | bytes 393224 | tf_op jit(solution)/shard_map/ppermute | solution.py:24
  154.2 16.4 %collective-permute-start.54 = (f32[2,256,128]{2,1,0:T(8,128)S(1)}, f32[2,256,128]{2,1,0:T(8,128)S(1)}, u32[]{:S(2)}, u32[]{:S(2)}) collective-permute-start(f32[2,256,128]{2,1,0:T(8,128)S(1)} %get-tuple-element.60.refs_14_), channel_id=1, source_target_pairs={{8,0},{16,8},{24,16},{9,1},{17,9},{25,17},{10,2},{18,10},{26,18},{... | collective-permute-start | bytes 786440 | tf_op jit(solution)/shard_map/ppermute | solution.py:24
  158.9 5.8 %collective-permute-start.51 = (f32[48,128]{1,0:T(8,128)S(1)}, f32[48,128]{1,0:T(8,128)S(1)}, u32[]{:S(2)}, u32[]{:S(2)}) collective-permute-start(f32[48,128]{1,0:T(8,128)S(1)} %add_add_fusion.1.refs_1_), channel_id=1, source_target_pairs={{0,5},{1,6},{2,7},{3,0},{4,1},{5,2},{6,3},{7,4},{8,13},{9,14},{10,... | collective-permute-start | bytes 73736 | tf_op jit(solution)/shard_map/ppermute | solution.py:24
  164.7 5.8 %collective-permute-start.48 = (f32[48,128]{1,0:T(8,128)S(1)}, f32[48,128]{1,0:T(8,128)S(1)}, u32[]{:S(2)}, u32[]{:S(2)}) collective-permute-start(f32[48,128]{1,0:T(8,128)S(1)} %add_add_fusion.1.refs_1_), channel_id=1, source_target_pairs={{0,2},{1,3},{2,4},{3,5},{4,6},{5,7},{6,0},{7,1},{8,10},{9,11},{10,... | collective-permute-start | bytes 73736 | tf_op jit(solution)/shard_map/ppermute | solution.py:24
  (29 other events, 174.9 us)

commit v2 on v1

v2 whole, which is shorter than its diff:
```python
import functools

import jax
import jax.numpy as jnp
import numpy as np
from jax import lax
from jax.experimental import pallas as pl
from jax.experimental.pallas import tpu as pltpu
from jax.sharding import PartitionSpec as P

ITERS = 3
NEAR, FAR, LEFT, RIGHT = range(4)
VMEM = pl.BlockSpec(memory_space=pltpu.VMEM)
SMEM = pl.BlockSpec(memory_space=pltpu.SMEM)
ANY = pl.BlockSpec(memory_space=pl.ANY)
F32, BF16 = jnp.float32, jnp.bfloat16


def shifted(value, axis, steps, wrap):
    count = lax.axis_size(axis)
    if wrap:
        pairs = [(source, (source + steps) % count) for source in range(count)]
    else:
        pairs = [(source, source + steps) for source in range(count) if 0 <= source + steps < count]
    return lax.ppermute(value, axis, pairs)


def summed(value, axis):
    others = [shifted(value, axis, k, True) for k in range(1, lax.axis_size(axis))]
    return functools.reduce(jnp.add, others, value)


def chip_parts(value, axis):
    count, stride = lax.axis_size(axis) // 2, 1
    parts = [value]
    while stride < count:
        radix = next((r for r in range(8, 1, -1) if (count // stride) % r == 0), count // stride)
        value = parts[0] if len(parts) == 1 else jnp.concatenate(parts, axis=0)
        parts = [value] + [shifted(value, axis, 2 * k * stride, True) for k in range(1, radix)]
        stride *= radix
    return parts


def swapped(value, axis):
    return lax.ppermute(value, axis, [(source, source ^ 1) for source in range(lax.axis_size(axis))])


def halves(value):
    high = value.astype(BF16)
    return high, (value - high.astype(F32)).astype(BF16)


def kept_halves(value):
    high = lax.reduce_precision(value, 8, 7)
    return high.astype(BF16), (value - high).astype(BF16)


def dot(first, second):
    return lax.dot_general(first, second, (((1,), (0,)), ((), ())), preferred_element_type=F32)


def rotated(buffer, value, start):
    size = value.shape[0]
    buffer[0:size] = value
    buffer[size:] = value
    return buffer[pl.ds(start, size)]


def corner_kernel(cuts, height, at, corner_map, corner_rows, slots):
    count, _, dofs = corner_rows.shape
    lane = lax.broadcasted_iota(jnp.int32, (1, dofs), 1)
    slots[...] = jnp.zeros_like(slots)
    for s in range(count):
        for a in range(cuts):
            keep = (at[0] == a).astype(F32)
            slots[s * height + 3 * a:s * height + 3 * a + 3] = corner_rows[s, 6:9] * keep
        number = (corner_map[s, 2] + 1).astype(F32)
        slots[s * height + 3 * cuts:s * height + 3 * cuts + 1] = jnp.where(lane == at[0], number, 0.0)


def put_coupling(ref, size, face, amount):
    for i in range(size // 128):
        rows = size + 16 * i
        ref[rows:rows + 12] = face[:, i * 128:(i + 1) * 128]
        ref[rows + 12:rows + 16] = jnp.full((4, 128), amount, F32)


def got_coupling(ref, size):
    return jnp.concatenate([ref[size + 16 * i:size + 16 * i + 12] for i in range(size // 128)], axis=1)


def prepare_kernel(at, offsets, gap, coupling, rows_table, residual, to_far, to_right, inner, c_rows, buffer):
    count, _, size, _ = gap.shape
    for s in range(count):
        for face in range(2):
            shift = offsets[s, face]
            value = gap[s, face] * (shift >= 0).astype(F32)
            residual[s, face] = value
            turned = -rotated(buffer.at[s, face], value, jnp.maximum(shift, 0))
            amount = (shift + 1).astype(F32)
            if face == 0:
                to_far[s, 0:size] = turned
                put_coupling(to_far.at[s], size, coupling[s, :, FAR * size:(FAR + 1) * size], amount)
            elif s == count - 1:
                to_right[0:size] = turned
                put_coupling(to_right, size, coupling[s, :, RIGHT * size:(RIGHT + 1) * size], amount)
            else:
                inner[s] = turned
        c_rows[s] = dot(rows_table[at[0]], paired(coupling[s])).astype(BF16)
    inner[count - 1] = jnp.zeros(inner.shape[1:], F32)


def paired(face):
    high, low = halves(face)
    rest = jnp.zeros((4, face.shape[1]), F32)
    both = jnp.concatenate([high.astype(F32), rest, low.astype(F32), rest], axis=0)
    return both.astype(BF16)


def spread_kernel(at, coupling, from_near, from_far, from_left, from_right, table, ct_own, ct_left, ct_right):
    count, size = coupling.shape[0], coupling.shape[2] // 4

    def turned(face, cycle):
        product = lax.dot_general(
            paired(face), table[cycle + 1], (((0,), (0,)), ((), ())), preferred_element_type=F32
        )
        return product.astype(BF16)

    for s in range(count):
        ct_own[s, 0:4 * size] = turned(coupling[s], at[0])
        ct_own[s, 4 * size:5 * size] = turned(got_coupling(from_far.at[s], size), at[0] + 1)
        ct_own[s, 5 * size:6 * size] = turned(got_coupling(from_near.at[s], size), at[0] - 1)
    ct_left[...] = turned(got_coupling(from_left, size), at[0])
    ct_right[...] = turned(got_coupling(from_right, size), at[0])


def split_kernel(block, high, low):
    for s in range(block.shape[0]):
        for i in range(0, block.shape[1], 256):
            high[s, i:i + 256], low[s, i:i + 256] = halves(block[s, i:i + 256])


def sum_kernel(parts, *refs):
    refs[parts + (len(refs) - parts - 1) // 2][...] = functools.reduce(jnp.add, [r[...] for r in refs[:parts]])


def stack_kernel(parts, *refs):
    out = refs[parts + (len(refs) - parts - 1) // 2]
    size = refs[0].shape[0]
    for i in range(parts):
        out[i * size:(i + 1) * size] = refs[i][...]


def relay(kernel, parts, shape, through, name):
    specs = [VMEM] * len(parts) + [ANY] * len(through)
    return pl.pallas_call(
        functools.partial(kernel, len(parts)),
        out_shape=(shape, *[jax.ShapeDtypeStruct(x.shape, x.dtype) for x in through]),
        in_specs=specs,
        out_specs=(VMEM, *[ANY] * len(through)),
        input_output_aliases={len(parts) + i: 1 + i for i in range(len(through))},
        name=name,
    )(*parts, *through)


def apply_flexibility(loads, a_high, a_low, coupling, height, outs, scratch, rr_rows):
    near, far, sides, to_left, to_right, terms = outs
    split = scratch["split"]
    count, size = len(loads), loads[0][0].shape[0]
    for s in range(count):
        for face in range(4):
            high, low = halves(loads[s][face])
            split[s, face * size:(face + 1) * size, 0:128] = high
            split[s, face * size:(face + 1) * size, 128:256] = low
    terms[...] = jnp.zeros_like(terms)
    total = jnp.zeros((1, 128), F32)
    width = coupling.shape[1] // 2
    for s in range(count):
        both = dot(coupling[s], split[s])
        mine = both[0:width, 0:128] + both[0:width, 128:256] + both[width:, 0:128]
        terms[s * height:s * height + width] += mine
    for s in range(count):
        whole = dot(a_high[s], split[s])
        whole = whole[:, 0:128] + whole[:, 128:256] + dot(a_low[s], split[s, :, 0:128])
        for face in range(4):
            product = whole[face * size:(face + 1) * size]
            total = total + jnp.sum(product * loads[s][face], axis=0, keepdims=True)
            if face == NEAR:
                near[s, 0:size] = product
            elif face == FAR:
                far[s] = product
            else:
                sides[s, face - 2] = product
                if face == LEFT and s == 0:
                    to_left[0:size] = product
                if face == RIGHT and s == count - 1:
                    to_right[...] = product
    squares = jnp.zeros((1, 128), F32)
    for s in range(count):
        for face in (FAR, RIGHT):
            squares = squares + jnp.sum(loads[s][face] * loads[s][face], axis=0, keepdims=True)
    terms[rr_rows:rr_rows + 1] = squares
    terms[rr_rows + 1:rr_rows + 2] = total


def finish_operator(offsets, terms, matrix, spread, product, received, height, rr_rows, scratch, faces):
    k_high, k_low = matrix
    ct_own, ct_left, ct_right = spread
    near, far, sides = product
    from_near, from_far, from_left, from_right = received
    count, size = far.shape[0], far.shape[1]
    side, mine, theirs = terms
    odd = side[0] == 1
    stacked, table = scratch["stack"], scratch["values"]
    span = count * height
    chips = mine.shape[0] // (span + height)
    terms = []
    for k in range(chips):
        first, second = (x[k * (span + height):(k + 1) * (span + height)] for x in (mine, theirs))
        terms += [jnp.where(odd, second, first), jnp.where(odd, first, second)]
    norm = functools.reduce(jnp.add, [t[rr_rows:rr_rows + 1] for t in terms])
    energy = functools.reduce(jnp.add, [t[rr_rows + 1:rr_rows + 2] for t in terms])
    for k in range(2 * chips):
        behind = k - 1 if k % 2 else (k + 3) % (2 * chips)
        stacked[k * span:(k + 1) * span] = terms[k][0:span]
        stacked[k * span:k * span + height] = terms[k][0:height] + terms[behind][span:span + height]
    coarse = stacked[...]
    high, low = halves(coarse)
    both = dot(k_high[...], jnp.concatenate([high, low], axis=1))
    values = both[:, 0:128] + both[:, 128:256] + dot(k_low[...], high)
    energy = energy + jnp.sum(coarse * values, axis=0, keepdims=True)

    table[...] = values

    def column(q):
        along = side[0] + q // count
        block = (2 * (-(along // 2)) + along % 2) % (2 * chips)
        at = block * span + (q % count) * height
        return table[pl.ds(pl.multiple_of(at, 8), height)]

    def tripled(q):
        high, low = halves(jnp.concatenate([column(q), column(q + 1)], axis=0))
        return jnp.concatenate([high, high, low], axis=0)

    own = [[None] * 4 for _ in range(count)]
    other = [[None] * 4 for _ in range(count)]
    for s in range(count):
        added = dot(ct_own[s], tripled(s))
        parts = [added[i * size:(i + 1) * size] for i in range(6)]
        raw = [near[s, 0:size], far[s], sides[s, 0], sides[s, 1]]
        own[s] = [raw[i] + parts[i] for i in range(4)]
        other[s][FAR] = from_far[s, 0:size] + parts[4]
        if NEAR in faces:
            other[s][NEAR] = from_near[s] + parts[5]
    other[count - 1][RIGHT] = from_right[0:size] + dot(ct_right[...], tripled(count))
    if LEFT in faces:
        other[0][LEFT] = from_left[...] + dot(ct_left[...], tripled(-1))
    for s in range(count):
        if s + 1 < count:
            other[s][RIGHT] = own[s + 1][LEFT]
        if s > 0:
            other[s][LEFT] = own[s - 1][RIGHT]
    result = [[None] * 4 for _ in range(count)]
    for s in range(count):
        for face in faces:
            shift = offsets[s, face]
            safe = jnp.maximum(shift, 0)
            start = safe if face in (NEAR, LEFT) else size - safe
            turned = rotated(scratch["turn"].at[s, face], other[s][face], start)
            result[s][face] = (own[s][face] - turned) * (shift >= 0).astype(F32)
    return result, norm, energy


def first_kernel(height, rr_rows, residual, from_near, from_left, inner, coupling, a_high, a_low, c_rows, *rest):
    outs, loads_out, split = rest[0:6], rest[6], rest[7]
    near, to_left = outs[0], outs[3]
    count, size = residual.shape[0], residual.shape[2]
    loads = []
    for s in range(count):
        left = from_left[0:size] if s == 0 else inner[s - 1]
        loads.append([from_near[s, 0:size], residual[s, 0], left, residual[s, 1]])
        for face in range(4):
            loads_out[s, face] = loads[s][face]
        put_coupling(near.at[s], size, coupling[s, :, NEAR * size:(NEAR + 1) * size], 0.0)
    put_coupling(to_left, size, coupling[0, :, LEFT * size:(LEFT + 1) * size], 0.0)
    apply_flexibility(loads, a_high, a_low, c_rows, height, outs, dict(split=split), rr_rows)


def step_kernel(which, height, rr_rows, *refs):
    refs = list(refs)
    take = lambda number: [refs.pop(0) for _ in range(number)]
    last = which == ITERS - 1
    (offsets,) = take(1)
    terms = take(3)
    matrix, spread, product, received = take(2), take(3), take(3), take(4)
    (loads,) = take(1)
    map_before, ways, found, scalars = (take(4) if which > 0 else [None] * 4)
    if not last:
        a_high, a_low, coupling = take(3)
        outs = take(6)
        loads_out, map_out = take(2)
        ways_out, found_out = take(2) if which > 0 else (None, None)
        (scalars_out,) = take(1)
        stack, values, turn, split = take(4)
        faces = (NEAR, FAR, LEFT, RIGHT)
    else:
        found_out, residual_out = take(2)
        stack, values, turn = take(3)
        faces = (FAR, RIGHT)
    count, size = loads.shape[0], loads.shape[2]
    scratch = dict(stack=stack, values=values, turn=turn)
    if not last:
        scratch["split"] = split
    mapped, norm, energy = finish_operator(
        offsets, terms, matrix, spread, product, received, height, rr_rows, scratch, faces
    )
    if which > 0:
        ratio = norm / scalars[0:1]
        energy = energy - ratio * norm / scalars[1:2]
    step = norm / energy
    fresh = [[None] * 4 for _ in range(count)]
    for s in range(count):
        for face in faces:
            here = mapped[s][face]
            now = loads[s, face]
            if which > 0:
                here = here + ratio * map_before[s, face]
            fresh[s][face] = now - step * here
            if not last:
                map_out[s, face] = here
                loads_out[s, face] = fresh[s][face]
            if face in (FAR, RIGHT):
                i = 0 if face == FAR else 1
                if which == 0:
                    continue
                if which == 1:
                    before = ways[s, face]
                    start = scalars[1:2] * before
                else:
                    before = ways[s, i]
                    start = found[s, i]
                way = now + ratio * before
                found_out[s, i] = start + step * way
                if last:
                    residual_out[s, i] = fresh[s][face]
                else:
                    ways_out[s, i] = way
    if not last:
        scalars_out[...] = jnp.concatenate([norm, step, jnp.zeros((6, 128), F32)], axis=0)
        apply_flexibility(fresh, a_high, a_low, coupling, height, outs, scratch, rr_rows)


def corner_tables(cuts, height):
    places = np.zeros((cuts + 2, 12, 2 * height), np.float32)
    for at in range(-1, cuts + 1):
        for k in range(4):
            cycle = at - 1 + k // 2
            if 0 <= cycle < cuts:
                for j in range(3):
                    places[at + 1, 3 * k + j, (k % 2) * height + 3 * cycle + j] = 1
    wide = 2 * height
    table = np.zeros((cuts + 2, 32, 3 * wide), np.float32)
    rows = np.zeros((cuts, 2 * wide, 32), np.float32)
    table[:, 0:12, 0:wide] = table[:, 16:28, wide:2 * wide] = table[:, 0:12, 2 * wide:] = places
    rows[:, 0:wide, 0:12] = rows[:, wide:, 16:28] = np.swapaxes(places[1:-1], 1, 2)
    return jnp.asarray(table, BF16), jnp.asarray(rows, BF16)


def corner_matrix(slots, numbers_at, cuts, height, odd):
    dofs = slots.shape[1]
    parts = chip_parts(summed(slots, "cuts"), "blk")
    mine = jnp.concatenate(parts, axis=0)
    theirs = swapped(mine, "blk")
    mine, theirs = (x.reshape(-1, slots.shape[0], dofs) for x in (mine, theirs))
    rows = jnp.stack([jnp.where(odd, theirs, mine), jnp.where(odd, mine, theirs)], axis=1)
    rows = rows.reshape(-1, height, dofs)
    numbers = rows[:, numbers_at, :cuts].astype(jnp.int32) - 1
    chosen = 3 * numbers[..., None] + jnp.arange(3, dtype=jnp.int32)
    chosen = jnp.pad(chosen.reshape(-1, 3 * cuts), ((0, 0), (0, height - 3 * cuts)), constant_values=-1).reshape(-1)
    pick = (jnp.arange(dofs, dtype=jnp.int32)[:, None] == chosen[None, :]).astype(BF16)
    used = (jnp.arange(height) < numbers_at)[:, None]
    high, low = kept_halves(jnp.where(used, rows, 0.0).reshape(-1, dofs))
    return [jnp.dot(part, pick, preferred_element_type=F32).astype(BF16) for part in (high, low)]


def per_device(gap_load, offsets, corner_map, flexibility, coupling, corner_rows):
    _, count, _, size, loads_n = gap_load.shape
    dofs = corner_rows.shape[-1]
    cuts, blocks = lax.axis_size("cuts"), lax.axis_size("blk")
    at = lax.axis_index("cuts").reshape(1)
    side = (lax.axis_index("blk") % 2).reshape(1)
    rr_rows = 3 * cuts
    height = -(-(rr_rows + 2) // 8) * 8
    gap, offsets, corner_map, flexibility, coupling, corner_rows = (
        x[0] for x in (gap_load, offsets, corner_map, flexibility, coupling, corner_rows)
    )
    total = flexibility.shape[1]
    below = 16 * (size // 128)
    shape = lambda *dims, kind=F32: jax.ShapeDtypeStruct(dims, kind)
    face = shape(size, loads_n)
    faces = shape(count, size, loads_n)
    pair = shape(count, 2, size, loads_n)
    four = shape(count, 4, size, loads_n)
    long_face = shape(size + below, loads_n)
    long_faces = shape(count, size + below, loads_n)
    params = pltpu.CompilerParams(vmem_limit_bytes=40 * 1024 * 1024)
    table, rows_table = corner_tables(cuts, height)

    slots = pl.pallas_call(
        functools.partial(corner_kernel, cuts, height),
        out_shape=shape(count * height, dofs),
        in_specs=[SMEM, SMEM, VMEM],
        out_specs=VMEM,
        name="corner",
    )(at, corner_map, corner_rows)
    residual, to_far, to_right, inner, c_rows = pl.pallas_call(
        prepare_kernel,
        out_shape=(pair, long_faces, long_face, faces, shape(count, 4 * height, total, kind=BF16)),
        in_specs=[SMEM, SMEM] + [VMEM] * 3,
        out_specs=(VMEM,) * 5,
        scratch_shapes=[pltpu.VMEM((count, 2, 2 * size, loads_n), F32)],
        name="prepare",
    )(at, offsets, gap, coupling, rows_table)
    from_near = shifted(to_far, "cuts", 1, False)
    from_left = shifted(to_right, "blk", 1, True)
    k_high, k_low = corner_matrix(slots, rr_rows, cuts, height, side[0] == 1)
    a_high, a_low = pl.pallas_call(
        split_kernel,
        out_shape=(jax.ShapeDtypeStruct(flexibility.shape, BF16),) * 2,
        in_specs=[VMEM],
        out_specs=(VMEM, VMEM),
        compiler_params=params,
        cost_estimate=pl.CostEstimate(flops=0, bytes_accessed=8 * flexibility.size, transcendentals=0),
        name="split",
    )(flexibility)
    near_offsets = from_near[:, size + 12, 0]
    left_offsets = jnp.concatenate([from_left[size + 12:size + 13, 0], (offsets[:-1, 1] + 1).astype(F32)])
    all_offsets = jnp.stack([
        near_offsets.astype(jnp.int32) - 1, offsets[:, 0], left_offsets.astype(jnp.int32) - 1, offsets[:, 1]
    ], axis=1)

    flops = 2 * count * total * total * loads_n * 3
    cost = pl.CostEstimate(flops=flops, bytes_accessed=4 * flexibility.size, transcendentals=0)
    terms_shape = shape((count + 1) * height, loads_n)
    sends = (faces, faces, pair, face, face, terms_shape)
    first_sends = (long_faces, faces, pair, long_face, face, terms_shape)
    a_buffers = [pltpu.VMEM((count, total, 2 * loads_n), BF16)]
    f_buffers = [
        pltpu.VMEM((blocks * count * height, loads_n), F32),
        pltpu.VMEM((blocks * count * height, loads_n), F32),
        pltpu.VMEM((count, 4, 2 * size, loads_n), F32),
    ]
    *out, loads = pl.pallas_call(
        functools.partial(first_kernel, height, rr_rows),
        out_shape=first_sends + (four,),
        in_specs=[VMEM] * 8,
        out_specs=(VMEM,) * 7,
        scratch_shapes=a_buffers,
        compiler_params=params,
        cost_estimate=cost,
        name="first",
    )(residual, from_near, from_left, inner, coupling, a_high, a_low, c_rows)

    state = []
    for which in range(ITERS):
        last = which == ITERS - 1
        near, far, sides, to_left, to_right, terms = out
        pieces = [terms] + [shifted(terms, "cuts", k, True) for k in range(1, cuts)]
        terms, near = relay(sum_kernel, pieces, terms_shape, [near], f"sum{which}")
        r_far = shifted(near, "cuts", -1, False)
        pieces = chip_parts(terms, "blk")
        mine, far, to_left, to_right = relay(
            stack_kernel, pieces, shape(blocks // 2 * terms_shape.shape[0], loads_n), [far, to_left, to_right],
            f"stack{which}",
        )
        theirs = swapped(mine, "blk")
        r_right = shifted(to_left, "blk", -1, True)
        if last:
            r_near, r_left = far, to_right
        else:
            r_near = shifted(far, "cuts", 1, False)
            r_left = shifted(to_right, "blk", 1, True)
        if which == 0:
            ct_own, ct_left, ct_right = pl.pallas_call(
                spread_kernel,
                out_shape=(
                    shape(count, 6 * size, 6 * height, kind=BF16),
                    shape(size, 6 * height, kind=BF16),
                    shape(size, 6 * height, kind=BF16),
                ),
                in_specs=[SMEM] + [VMEM] * 6,
                out_specs=(VMEM,) * 3,
                name="spread",
            )(at, coupling, from_near, r_far, from_left, r_right, table)
        args = [all_offsets, side, mine, theirs, k_high, k_low, ct_own, ct_left, ct_right, near, far, sides,
                r_near, r_far, r_left, r_right, loads, *state]
        specs = [SMEM, SMEM] + [VMEM] * (len(args) - 2)
        if last:
            outs, scratch = (pair, pair), f_buffers
        else:
            args += [a_high, a_low, c_rows]
            specs += [VMEM] * 3
            outs = sends + (four, four) + ((pair, pair) if which > 0 else ()) + (shape(8, loads_n),)
            scratch = f_buffers + a_buffers
        result = pl.pallas_call(
            functools.partial(step_kernel, which, height, rr_rows),
            out_shape=outs,
            in_specs=specs,
            out_specs=(VMEM,) * len(outs),
            scratch_shapes=scratch,
            compiler_params=params,
            cost_estimate=None if last else cost,
            name=f"step{which}",
        )(*args)
        if last:
            multipliers, residual = result
            break
        out = result[0:6]
        before, loads = loads, result[6]
        if which == 0:
            state = [result[7], before, before, result[8]]
        else:
            state = [result[7], result[8], result[9], result[10]]
    return multipliers[None], residual[None]


def solution(mesh):
    spec5, spec4, spec3 = (P("cuts", "blk", *[None] * k) for k in (3, 2, 1))
    return jax.shard_map(
        per_device,
        mesh=mesh,
        in_specs=(spec5, spec3, spec3, spec4, spec4, spec4),
        out_specs=(spec5, spec5),
        check_vma=False,
    )
```

time: 174 us -> 187 us (1.075); the launches traced: 173 us -> 184 us
  local copies, waits for them, and re-layouts: 13.2 us -> 63.2 us
  waiting for transfers between devices: 50.6 us -> 31.4 us
  starting transfers between devices: 63.3 us -> 47.6 us
  Pallas kernels: 31.5 us -> 37.8 us
  matrix products: 6.1 us -> 0.38 us
  other arithmetic: 5.32 us -> 1.67 us
    unnamed x12 -> x176, local copies, waits for them, and re-layouts: 5.21 us -> 60.3 us
    ppermute x56 -> x36, waiting for transfers between devices: 50.6 us -> 28.7 us  [shifted(): return lax.ppermute(value, axis, pairs)]
    ppermute x56 -> x36, starting transfers between devices: 63.3 us -> 47 us  [shifted(): return lax.ppermute(value, axis, pairs)]
    pallas_call x5 -> x13, Pallas kernels: 26.6 us -> 35.2 us  [the longest x3 15.7 us: per_device(): pl.pallas_call(functools.partial(step_kernel, which, height, rr_rows), ou...]
    dot_general x16 -> x2, matrix products: 6.1 us -> 0.38 us  [corner_matrix(): jnp.dot(part, pick, preferred_element_type=F32).astype(BF16)]
    ppermute x0 -> x4, waiting for transfers between devices: none -> 2.7 us  [swapped(): lax.ppermute(value, axis, [(source, source ^ 1) for source in range(lax.a...]
    pallas_call x1, Pallas kernels: 4.94 us -> 2.56 us  [per_device(): pl.pallas_call(functools.partial(first_kernel, height, rr_rows), out_shap...]
    slice x8 -> x4, local copies, waits for them, and re-layouts: 4.4 us -> 2.63 us  [the longest x1 1.28 us: per_device(): offsets[:-1, 1] + 1]
  transfers between devices with their start and end apart: 56 -> 40, of which waited for: 22 -> 23; matrix products, arithmetic and copies ran while one was open for 11% -> 4% of each run, Pallas kernels for 6% -> 8%
where the time goes in v2:
time: 187 us; the launch traced here: 184 us
  local copies, waits for them, and re-layouts  63.2 us (34%)
  starting transfers between devices  47.6 us (25%)
  Pallas kernels  37.8 us (20%)
  waiting for transfers between devices  31.4 us (17%)
    unnamed x176, local copies, waits for them, and re-layouts  60.3 us
    ppermute x36, starting transfers between devices, shifted(): return lax.ppermute(value, axis, pairs)  47 us
    ppermute x36, waiting for transfers between devices, shifted(): return lax.ppermute(value, axis, pairs)  28.7 us
    pallas_call x3, Pallas kernels, per_device(): pl.pallas_call(functools.partial(step_kernel, which, height, rr_rows), ou...  15.7 us
    pallas_call x6, Pallas kernels, relay(): pl.pallas_call(functools.partial(kernel, len(parts)), out_shape=(shape, *...  8.49 us
    pallas_call x1, Pallas kernels, per_device(): pl.pallas_call(split_kernel, out_shape=(jax.ShapeDtypeStruct(flexibility....  4.6 us
  transfers between devices with their start and end apart: 40, of which 23 were waited for; matrix products, arithmetic and copies ran while one was open for 4% of the time, Pallas kernels for 8%

profile of v2, /device:TPU:0, one launch (start us, length us, event | category | flops | bytes accessed | tf_op | source)
XLA Modules:
  0.0 183.8 jit_solution(15051136721103686810)
XLA Ops:
  3.4 3.9 %collective-permute-start.11 = (f32[32,192]{1,0:T(8,128)}, f32[32,192]{1,0:T(8,128)S(1)}, u32[]{:S(2)}, u32[]{:S(2)}) collective-permute-start(f32[32,192]{1,0:T(8,128)} %corner.1), channel_id=1, source_target_pairs={{0,24},{8,0},{16,8},{24,16},{1,25},{9,1},{17,9},{25,17},{2,26},{10... | collective-permute-start | bytes 73736 | tf_op jit(solution)/shard_map/ppermute | solution.py:25
  8.4 1.6 copy.50
  9.9 2.4 %prepare.1 = (f32[2,2,256,128]{3,2,1,0:T(8,128)}, f32[2,288,128]{2,1,0:T(8,128)}, f32[288,128]{1,0:T(8,128)}, f32[2,256,128]{2,1,0:T(8,128)}, bf16[2,64,1024]{2,1,0:T(8,128)(2,1)}) custom-call(s32[1]{0:T(128)} %bitcast.at, s32[2,2]{1,0:T(2,128)} %bitcast.43, f32[2,2,256,128]{3,2,1,0:T(8,128)} %bitcast.39, f32[2,12,1024]{2,1,0:T(8,128)} %bitcast.34, ...), custom_call_target="tpu_custom_call" | custom-call | tf_op jit(solution)/shard_map/prepare/pallas_call | solution.py:416
  12.4 4.3 %collective-permute-start = (f32[2,288,128]{2,1,0:T(8,128)}, f32[2,288,128]{2,1,0:T(8,128)S(1)}, u32[]{:S(2)}, u32[]{:S(2)}) collective-permute-start(f32[2,288,128]{2,1,0:T(8,128)} %get-tuple-element.59), channel_id=1, source_target_pairs={{0,8},{8,16},{16,24},{1,9},{9,17},{17,25},{2,10},{10,18},{18,26},{... | collective-permute-start | bytes 884744 | tf_op jit(solution)/shard_map/ppermute | solution.py:25
  17.5 3.7 %collective-permute-start.14 = (f32[32,192]{1,0:T(8,128)S(1)}, f32[32,192]{1,0:T(8,128)S(1)}, u32[]{:S(2)}, u32[]{:S(2)}) collective-permute-start(f32[32,192]{1,0:T(8,128)S(1)} %add_add_fusion), channel_id=1, source_target_pairs={{0,6},{1,7},{2,0},{3,1},{4,2},{5,3},{6,4},{7,5},{8,14},{9,15},{10,... | collective-permute-start | bytes 73736 | tf_op jit(solution)/shard_map/ppermute | solution.py:25
  27.2 4.6 %split.1 = (bf16[2,1024,1024]{2,1,0:T(8,128)(2,1)S(1)}, bf16[2,1024,1024]{2,1,0:T(8,128)(2,1)S(1)}) custom-call(f32[2,1024,1024]{2,1,0:T(8,128)} %bitcast.37), custom_call_target="tpu_custom_call" | custom-call | bytes 16777216 | tf_op jit(solution)/shard_map/split/pallas_call | solution.py:427
  31.8 2.0 %copy-done = bf16[2,1024,1024]{2,1,0:T(8,128)(2,1)} copy-done((bf16[2,1024,1024]{2,1,0:T(8,128)(2,1)}, bf16[2,1024,1024]{2,1,0:T(8,128)(2,1)S(1)}, u32[]{:S(2)}) %copy-start) | copy-done | bytes 4194328
  33.8 2.0 %copy-done.3 = bf16[2,1024,1024]{2,1,0:T(8,128)(2,1)} copy-done((bf16[2,1024,1024]{2,1,0:T(8,128)(2,1)}, bf16[2,1024,1024]{2,1,0:T(8,128)(2,1)S(1)}, u32[]{:S(2)}) %copy-start.3) | copy-done | bytes 4194328
  36.6 2.3 %copy-done.1 = bf16[2,1024,1024]{2,1,0:T(8,128)(2,1)S(1)} copy-done((bf16[2,1024,1024]{2,1,0:T(8,128)(2,1)S(1)}, bf16[2,1024,1024]{2,1,0:T(8,128)(2,1)}, u32[]{:S(2)}) %copy-start.1) | copy-done | bytes 4194328
  38.9 2.2 %copy-done.4 = bf16[2,1024,1024]{2,1,0:T(8,128)(2,1)S(1)} copy-done((bf16[2,1024,1024]{2,1,0:T(8,128)(2,1)S(1)}, bf16[2,1024,1024]{2,1,0:T(8,128)(2,1)}, u32[]{:S(2)}) %copy-start.4) | copy-done | bytes 4194328
  42.1 2.6 %first.1 = (f32[2,288,128]{2,1,0:T(8,128)S(1)}, f32[2,256,128]{2,1,0:T(8,128)S(1)}, f32[2,2,256,128]{3,2,1,0:T(8,128)S(1)}, f32[288,128]{1,0:T(8,128)S(1)}, f32[...) custom-call(f32[2,2,256,128]{3,2,1,0:T(8,128)S(1)} %copy-done.37, ...), custom_call_target="tpu_custom_call" | custom-call | flops 1610612736 | bytes 8388608 | tf_op jit(solution)/shard_map/first/pallas_call | solution.py:453
  50.6 2.4 %collective-permute-done.2.refs_1_ = f32[48,128]{1,0:T(8,128)S(1)} collective-permute-done((f32[48,128]{1,0:T(8,128)S(1)}, f32[48,128]{1,0:T(8,128)S(1)}, u32[]{:S(2)}, u32[]{:S(2)}) %collective-permute-start.2) | collective-permute-done | bytes 24608 | tf_op jit(solution)/shard_map/ppermute | solution.py:25
  61.0 1.8 collective-permute-done.5.refs_1_
  64.8 3.5 %collective-permute-start.17 = (f32[288,128]{1,0:T(8,128)}, f32[288,128]{1,0:T(8,128)S(1)}, u32[]{:S(2)}, u32[]{:S(2)}) collective-permute-start(f32[288,128]{1,0:T(8,128)} %get-tuple-element.74), channel_id=1, source_target_pairs={{0,7},{1,0},{2,1},{3,2},{4,3},{5,4},{6,5},{7,6},{8,15},{9,8},{10,9... | collective-permute-start | bytes 442376 | tf_op jit(solution)/shard_map/ppermute | solution.py:25
  68.4 2.1 %collective-permute-start.18 = (f32[2,256,128]{2,1,0:T(8,128)}, f32[2,256,128]{2,1,0:T(8,128)S(1)}, u32[]{:S(2)}, u32[]{:S(2)}) collective-permute-start(f32[2,256,128]{2,1,0:T(8,128)} %get-tuple-element.78.refs_10_), channel_id=1, source_target_pairs={{0,8},{8,16},{16,24},{1,9},{9,17},{17,25},{2,10},{10,18},{18,26},{... | collective-permute-start | bytes 786440 | tf_op jit(solution)/shard_map/ppermute | solution.py:25
  72.8 2.6 %spread.1 = (bf16[2,1536,96]{2,1,0:T(8,128)(2,1)}, bf16[256,96]{1,0:T(8,128)(2,1)}, bf16[256,96]{1,0:T(8,128)(2,1)}) custom-call(s32[1]{0:T(128)} %bitcast.at, f32[2,12,1024]{2,1,0:T(8,128)} %bitcast.35, f32[2,288,128]{2,1,0:T(8,128)} %copy-done.11, f32[2,288,128]{2,1,0:T(8,128)} %copy-done.14, f32[288,128]{1,0:T(8,128)} %copy-done.34, ...), custom_call_target="tpu_custom_call" | custom-call | tf_op jit(solution)/shard_map/spread/pallas_call | solution.py:484
  77.3 2.2 %copy-done.2 = bf16[2,1024,1024]{2,1,0:T(8,128)(2,1)S(1)} copy-done((bf16[2,1024,1024]{2,1,0:T(8,128)(2,1)S(1)}, bf16[2,1024,1024]{2,1,0:T(8,128)(2,1)}, u32[]{:S(2)}) %copy-start.2) | copy-done | bytes 4194328
  89.8 6.1 %step0.1 = (f32[2,256,128]{2,1,0:T(8,128)S(1)}, f32[2,256,128]{2,1,0:T(8,128)S(1)}, f32[2,2,256,128]{3,2,1,0:T(8,128)S(1)}, f32[256,128]{1,0:T(8,128)S(1)}, f32[...) custom-call(s32[2,4]{1,0:T(2,128)S(1)} %pad_add_fusion.refs_0_, ...), custom_call_target="tpu_custom_call" | custom-call | flops 1610612736 | bytes 8388608 | tf_op jit(solution)/shard_map/step0/pallas_call | solution.py:505
  105.2 2.2 %collective-permute-done.20.refs_1_ = f32[48,128]{1,0:T(8,128)S(1)} collective-permute-done((f32[48,128]{1,0:T(8,128)S(1)}, f32[48,128]{1,0:T(8,128)S(1)}, u32[]{:S(2)}, u32[]{:S(2)}) %collective-permute-start.20) | collective-permute-done | bytes 24608 | tf_op jit(solution)/shard_map/ppermute | solution.py:25
  109.4 1.7 collective-permute-start.25
  113.4 2.9 %collective-permute-done.24.refs_2_ = f32[48,128]{1,0:T(8,128)S(1)} collective-permute-done((f32[48,128]{1,0:T(8,128)}, f32[48,128]{1,0:T(8,128)S(1)}, u32[]{:S(2)}, u32[]{:S(2)}) %collective-permute-start.24) | collective-permute-done | bytes 24608 | tf_op jit(solution)/shard_map/ppermute | solution.py:25
  119.0 2.6 %collective-permute-start.27 = (f32[2,256,128]{2,1,0:T(8,128)}, f32[2,256,128]{2,1,0:T(8,128)S(1)}, u32[]{:S(2)}, u32[]{:S(2)}) collective-permute-start(f32[2,256,128]{2,1,0:T(8,128)} %get-tuple-element.90.refs_10_), channel_id=1, source_target_pairs={{0,8},{8,16},{16,24},{1,9},{9,17},{17,25},{2,10},{10,18},{18,26},{... | collective-permute-start | bytes 786440 | tf_op jit(solution)/shard_map/ppermute | solution.py:25
  121.7 3.5 %collective-permute-start.30 = (f32[256,128]{1,0:T(8,128)}, f32[256,128]{1,0:T(8,128)S(1)}, u32[]{:S(2)}, u32[]{:S(2)}) collective-permute-start(f32[256,128]{1,0:T(8,128)} %get-tuple-element.93), channel_id=1, source_target_pairs={{0,7},{1,0},{2,1},{3,2},{4,3},{5,4},{6,5},{7,6},{8,15},{9,8},{10,9... | collective-permute-start | bytes 393224 | tf_op jit(solution)/shard_map/ppermute | solution.py:25
  125.2 1.5 collective-permute-done.26.refs_3_
  126.7 2.5 %collective-permute-done.29.refs_14_ = f32[256,128]{1,0:T(8,128)S(1)} collective-permute-done((f32[256,128]{1,0:T(8,128)}, f32[256,128]{1,0:T(8,128)S(1)}, u32[]{:S(2)}, u32[]{:S(2)}) %collective-permute-start.29) | collective-permute-done | bytes 131104 | tf_op jit(solution)/shard_map/ppermute | solution.py:25
  137.2 7.4 %step1.1 = (f32[2,256,128]{2,1,0:T(8,128)S(1)}, f32[2,256,128]{2,1,0:T(8,128)S(1)}, f32[2,2,256,128]{3,2,1,0:T(8,128)S(1)}, f32[256,128]{1,0:T(8,128)S(1)}, f32[...) custom-call(s32[2,4]{1,0:T(2,128)S(1)} %pad_add_fusion.refs_0_, ...), custom_call_target="tpu_custom_call" | custom-call | flops 1610612736 | bytes 8388608 | tf_op jit(solution)/shard_map/step1/pallas_call | solution.py:505
  150.7 3.1 %collective-permute-start.32 = (f32[48,128]{1,0:T(8,128)S(1)}, f32[48,128]{1,0:T(8,128)S(1)}, u32[]{:S(2)}, u32[]{:S(2)}) collective-permute-start(f32[48,128]{1,0:T(8,128)S(1)} %get-tuple-element.97.refs_0_), channel_id=1, source_target_pairs={{0,16},{8,24},{16,0},{24,8},{1,17},{9,25},{17,1},{25,9},{2,18},{10... | collective-permute-start | bytes 73736 | tf_op jit(solution)/shard_map/ppermute | solution.py:25
  155.8 2.8 %collective-permute-done.31.refs_1_ = f32[48,128]{1,0:T(8,128)S(1)} collective-permute-done((f32[48,128]{1,0:T(8,128)S(1)}, f32[48,128]{1,0:T(8,128)S(1)}, u32[]{:S(2)}, u32[]{:S(2)}) %collective-permute-start.31) | collective-permute-done | bytes 24608 | tf_op jit(solution)/shard_map/ppermute | solution.py:25
  162.1 1.9 %collective-permute-start.34 = (f32[48,128]{1,0:T(8,128)}, f32[48,128]{1,0:T(8,128)S(1)}, u32[]{:S(2)}, u32[]{:S(2)}) collective-permute-start(f32[48,128]{1,0:T(8,128)} %get-tuple-element.99.refs_0_), channel_id=1, source_target_pairs={{0,2},{1,3},{2,4},{3,5},{4,6},{5,7},{6,0},{7,1},{8,10},{9,11},{10,... | collective-permute-start | bytes 73736 | tf_op jit(solution)/shard_map/ppermute | solution.py:25
  164.0 1.9 %collective-permute-done.36.refs_3_ = f32[48,128]{1,0:T(8,128)S(1)} collective-permute-done((f32[48,128]{1,0:T(8,128)}, f32[48,128]{1,0:T(8,128)S(1)}, u32[]{:S(2)}, u32[]{:S(2)}) %collective-permute-start.36) | collective-permute-done | bytes 24608 | tf_op jit(solution)/shard_map/ppermute | solution.py:25
  166.9 1.7 collective-permute-done.34.refs_1_
  181.6 2.2 %step2.1 = (f32[2,2,256,128]{3,2,1,0:T(8,128)}, f32[2,2,256,128]{3,2,1,0:T(8,128)}) custom-call(s32[2,4]{1,0:T(2,128)S(1)} %pad_add_fusion.refs_0_, s32[1]{0:T(128)} %bitcast.5.refs_1_, f32[192,128]{1,0:T(8,128)S(1)} %copy-done.64, f32[192,128]{1,0:T(8,128)S(1)} %collective-permute-done.37.refs_3_, bf16[256,256]{1,0:T(8,128)(2,1)S(1)} %convolution_convert_fusion.1.refs_4_, ...), custom_call_target="tpu_custom_call" | custom-call | tf_op jit(solution)/shard_map/step2/pallas_call | solution.py:505
  (263 shorter events, 91.9 us)
Async XLA Ops:
  3.4 13.3 %collective-permute-start.11 = (f32[32,192]{1,0:T(8,128)}, f32[32,192]{1,0:T(8,128)S(1)}, u32[]{:S(2)}, u32[]{:S(2)}) collective-permute-start(f32[32,192]{1,0:T(8,128)} %corner.1), channel_id=1, source_target_pairs={{0,24},{8,0},{16,8},{24,16},{1,25},{9,1},{17,9},{25,17},{2,26},{10... | collective-permute-start | bytes 73736 | tf_op jit(solution)/shard_map/ppermute | solution.py:25
  7.3 9.4 %collective-permute-start.10 = (f32[32,192]{1,0:T(8,128)}, f32[32,192]{1,0:T(8,128)S(1)}, u32[]{:S(2)}, u32[]{:S(2)}) collective-permute-start(f32[32,192]{1,0:T(8,128)} %corner.1), channel_id=1, source_target_pairs={{0,16},{8,24},{16,0},{24,8},{1,17},{9,25},{17,1},{25,9},{2,18},{10... | collective-permute-start | bytes 73736 | tf_op jit(solution)/shard_map/ppermute | solution.py:25
  7.8 8.9 %collective-permute-start.9 = (f32[32,192]{1,0:T(8,128)}, f32[32,192]{1,0:T(8,128)S(1)}, u32[]{:S(2)}, u32[]{:S(2)}) collective-permute-start(f32[32,192]{1,0:T(8,128)} %corner.1), channel_id=1, source_target_pairs={{0,8},{8,16},{16,24},{24,0},{1,9},{9,17},{17,25},{25,1},{2,10},{10... | collective-permute-start | bytes 73736 | tf_op jit(solution)/shard_map/ppermute | solution.py:25
  12.4 24.2 %collective-permute-start.1 = (f32[288,128]{1,0:T(8,128)}, f32[288,128]{1,0:T(8,128)S(1)}, u32[]{:S(2)}, u32[]{:S(2)}) collective-permute-start(f32[288,128]{1,0:T(8,128)} %get-tuple-element.60), channel_id=1, source_target_pairs={{0,1},{1,2},{2,3},{3,4},{4,5},{5,6},{6,7},{7,0},{8,9},{9,10},{10,1... | collective-permute-start | bytes 442376 | tf_op jit(solution)/shard_map/ppermute | solution.py:25
  12.4 24.2 %collective-permute-start = (f32[2,288,128]{2,1,0:T(8,128)}, f32[2,288,128]{2,1,0:T(8,128)S(1)}, u32[]{:S(2)}, u32[]{:S(2)}) collective-permute-start(f32[2,288,128]{2,1,0:T(8,128)} %get-tuple-element.59), channel_id=1, source_target_pairs={{0,8},{8,16},{16,24},{1,9},{9,17},{17,25},{2,10},{10,18},{18,26},{... | collective-permute-start | bytes 884744 | tf_op jit(solution)/shard_map/ppermute | solution.py:25
  17.5 7.4 %collective-permute-start.14 = (f32[32,192]{1,0:T(8,128)S(1)}, f32[32,192]{1,0:T(8,128)S(1)}, u32[]{:S(2)}, u32[]{:S(2)}) collective-permute-start(f32[32,192]{1,0:T(8,128)S(1)} %add_add_fusion), channel_id=1, source_target_pairs={{0,6},{1,7},{2,0},{3,1},{4,2},{5,3},{6,4},{7,5},{8,14},{9,15},{10,... | collective-permute-start | bytes 73736 | tf_op jit(solution)/shard_map/ppermute | solution.py:25
  21.1 5.2 %collective-permute-start.13 = (f32[32,192]{1,0:T(8,128)S(1)}, f32[32,192]{1,0:T(8,128)S(1)}, u32[]{:S(2)}, u32[]{:S(2)}) collective-permute-start(f32[32,192]{1,0:T(8,128)S(1)} %add_add_fusion), channel_id=1, source_target_pairs={{0,4},{1,5},{2,6},{3,7},{4,0},{5,1},{6,2},{7,3},{8,12},{9,13},{10,... | collective-permute-start | bytes 73736 | tf_op jit(solution)/shard_map/ppermute | solution.py:25
  21.2 5.7 %collective-permute-start.12 = (f32[32,192]{1,0:T(8,128)S(1)}, f32[32,192]{1,0:T(8,128)S(1)}, u32[]{:S(2)}, u32[]{:S(2)}) collective-permute-start(f32[32,192]{1,0:T(8,128)S(1)} %add_add_fusion), channel_id=1, source_target_pairs={{0,2},{1,3},{2,4},{3,5},{4,6},{5,7},{6,0},{7,1},{8,10},{9,11},{10,... | collective-permute-start | bytes 73736 | tf_op jit(solution)/shard_map/ppermute | solution.py:25
  26.9 8.9 %collective-permute-start.15 = (f32[128,192]{1,0:T(8,128)S(1)}, f32[128,192]{1,0:T(8,128)S(1)}, u32[]{:S(2)}, u32[]{:S(2)}) collective-permute-start(f32[128,192]{1,0:T(8,128)S(1)} %pad_maximum_fusion.1), channel_id=1, source_target_pairs={{0,1},{1,0},{2,3},{3,2},{4,5},{5,4},{6,7},{7,6},{8,9},{9,8},{10,11... | collective-permute-start | bytes 294920 | tf_op jit(solution)/shard_map/ppermute | solution.py:45
  48.2 4.7 %collective-permute-start.2 = (f32[48,128]{1,0:T(8,128)S(1)}, f32[48,128]{1,0:T(8,128)S(1)}, u32[]{:S(2)}, u32[]{:S(2)}) collective-permute-start(f32[48,128]{1,0:T(8,128)S(1)} %get-tuple-element.66.refs_0_), channel_id=1, source_target_pairs={{0,8},{8,16},{16,24},{24,0},{1,9},{9,17},{17,25},{25,1},{2,10},{10... | collective-permute-start | bytes 73736 | tf_op jit(solution)/shard_map/ppermute | solution.py:25
  54.9 5.0 %collective-permute-start.7 = (f32[48,128]{1,0:T(8,128)}, f32[48,128]{1,0:T(8,128)S(1)}, u32[]{:S(2)}, u32[]{:S(2)}) collective-permute-start(f32[48,128]{1,0:T(8,128)} %get-tuple-element.68.refs_0_), channel_id=1, source_target_pairs={{0,6},{1,7},{2,0},{3,1},{4,2},{5,3},{6,4},{7,5},{8,14},{9,15},{10,... | collective-permute-start | bytes 73736 | tf_op jit(solution)/shard_map/ppermute | solution.py:25
  56.1 4.9 %collective-permute-start.6 = (f32[48,128]{1,0:T(8,128)}, f32[48,128]{1,0:T(8,128)S(1)}, u32[]{:S(2)}, u32[]{:S(2)}) collective-permute-start(f32[48,128]{1,0:T(8,128)} %get-tuple-element.68.refs_0_), channel_id=1, source_target_pairs={{0,4},{1,5},{2,6},{3,7},{4,0},{5,1},{6,2},{7,3},{8,12},{9,13},{10,... | collective-permute-start | bytes 73736 | tf_op jit(solution)/shard_map/ppermute | solution.py:25
  57.0 5.8 %collective-permute-start.5 = (f32[48,128]{1,0:T(8,128)}, f32[48,128]{1,0:T(8,128)S(1)}, u32[]{:S(2)}, u32[]{:S(2)}) collective-permute-start(f32[48,128]{1,0:T(8,128)} %get-tuple-element.68.refs_0_), channel_id=1, source_target_pairs={{0,2},{1,3},{2,4},{3,5},{4,6},{5,7},{6,0},{7,1},{8,10},{9,11},{10,... | collective-permute-start | bytes 73736 | tf_op jit(solution)/shard_map/ppermute | solution.py:25
  58.7 12.7 %collective-permute-start.16 = (f32[2,288,128]{2,1,0:T(8,128)}, f32[2,288,128]{2,1,0:T(8,128)S(1)}, u32[]{:S(2)}, u32[]{:S(2)}) collective-permute-start(f32[2,288,128]{2,1,0:T(8,128)} %get-tuple-element.73.refs_9_), channel_id=1, source_target_pairs={{8,0},{16,8},{24,16},{9,1},{17,9},{25,17},{10,2},{18,10},{26,18},{... | collective-permute-start | bytes 884744 | tf_op jit(solution)/shard_map/ppermute | solution.py:25
  64.8 11.1 %collective-permute-start.19 = (f32[256,128]{1,0:T(8,128)}, f32[256,128]{1,0:T(8,128)S(1)}, u32[]{:S(2)}, u32[]{:S(2)}) collective-permute-start(f32[256,128]{1,0:T(8,128)} %get-tuple-element.80), channel_id=1, source_target_pairs={{0,1},{1,2},{2,3},{3,4},{4,5},{5,6},{6,7},{7,0},{8,9},{9,10},{10,1... | collective-permute-start | bytes 393224 | tf_op jit(solution)/shard_map/ppermute | solution.py:25
  64.8 6.5 %collective-permute-start.17 = (f32[288,128]{1,0:T(8,128)}, f32[288,128]{1,0:T(8,128)S(1)}, u32[]{:S(2)}, u32[]{:S(2)}) collective-permute-start(f32[288,128]{1,0:T(8,128)} %get-tuple-element.74), channel_id=1, source_target_pairs={{0,7},{1,0},{2,1},{3,2},{4,3},{5,4},{6,5},{7,6},{8,15},{9,8},{10,9... | collective-permute-start | bytes 442376 | tf_op jit(solution)/shard_map/ppermute | solution.py:25
  68.4 8.2 %collective-permute-start.18 = (f32[2,256,128]{2,1,0:T(8,128)}, f32[2,256,128]{2,1,0:T(8,128)S(1)}, u32[]{:S(2)}, u32[]{:S(2)}) collective-permute-start(f32[2,256,128]{2,1,0:T(8,128)} %get-tuple-element.78.refs_10_), channel_id=1, source_target_pairs={{0,8},{8,16},{16,24},{1,9},{9,17},{17,25},{2,10},{10,18},{18,26},{... | collective-permute-start | bytes 786440 | tf_op jit(solution)/shard_map/ppermute | solution.py:25
  70.5 4.9 %collective-permute-start.8 = (f32[192,128]{1,0:T(8,128)}, f32[192,128]{1,0:T(8,128)S(1)}, u32[]{:S(2)}, u32[]{:S(2)}) collective-permute-start(f32[192,128]{1,0:T(8,128)} %get-tuple-element.72.refs_2_), channel_id=1, source_target_pairs={{0,1},{1,0},{2,3},{3,2},{4,5},{5,4},{6,7},{7,6},{8,9},{9,8},{10,11... | collective-permute-start | bytes 294920 | tf_op jit(solution)/shard_map/ppermute | solution.py:45
  102.7 4.7 %collective-permute-start.20 = (f32[48,128]{1,0:T(8,128)S(1)}, f32[48,128]{1,0:T(8,128)S(1)}, u32[]{:S(2)}, u32[]{:S(2)}) collective-permute-start(f32[48,128]{1,0:T(8,128)S(1)} %get-tuple-element.82.refs_0_), channel_id=1, source_target_pairs={{0,8},{8,16},{16,24},{24,0},{1,9},{9,17},{17,25},{25,1},{2,10},{10... | collective-permute-start | bytes 73736 | tf_op jit(solution)/shard_map/ppermute | solution.py:25
  109.4 4.0 %collective-permute-start.25 = (f32[48,128]{1,0:T(8,128)}, f32[48,128]{1,0:T(8,128)S(1)}, u32[]{:S(2)}, u32[]{:S(2)}) collective-permute-start(f32[48,128]{1,0:T(8,128)} %get-tuple-element.84.refs_0_), channel_id=1, source_target_pairs={{0,6},{1,7},{2,0},{3,1},{4,2},{5,3},{6,4},{7,5},{8,14},{9,15},{10,... | collective-permute-start | bytes 73736 | tf_op jit(solution)/shard_map/ppermute | solution.py:25
  111.1 5.2 %collective-permute-start.24 = (f32[48,128]{1,0:T(8,128)}, f32[48,128]{1,0:T(8,128)S(1)}, u32[]{:S(2)}, u32[]{:S(2)}) collective-permute-start(f32[48,128]{1,0:T(8,128)} %get-tuple-element.84.refs_0_), channel_id=1, source_target_pairs={{0,4},{1,5},{2,6},{3,7},{4,0},{5,1},{6,2},{7,3},{8,12},{9,13},{10,... | collective-permute-start | bytes 73736 | tf_op jit(solution)/shard_map/ppermute | solution.py:25
  111.1 5.8 %collective-permute-start.23 = (f32[48,128]{1,0:T(8,128)}, f32[48,128]{1,0:T(8,128)S(1)}, u32[]{:S(2)}, u32[]{:S(2)}) collective-permute-start(f32[48,128]{1,0:T(8,128)} %get-tuple-element.84.refs_0_), channel_id=1, source_target_pairs={{0,2},{1,3},{2,4},{3,5},{4,6},{5,7},{6,0},{7,1},{8,10},{9,11},{10,... | collective-permute-start | bytes 73736 | tf_op jit(solution)/shard_map/ppermute | solution.py:25
  112.0 17.2 %collective-permute-start.28 = (f32[2,256,128]{2,1,0:T(8,128)}, f32[2,256,128]{2,1,0:T(8,128)S(1)}, u32[]{:S(2)}, u32[]{:S(2)}) collective-permute-start(f32[2,256,128]{2,1,0:T(8,128)} %get-tuple-element.89.refs_9_), channel_id=1, source_target_pairs={{8,0},{16,8},{24,16},{9,1},{17,9},{25,17},{10,2},{18,10},{26,18},{... | collective-permute-start | bytes 786440 | tf_op jit(solution)/shard_map/ppermute | solution.py:25
  119.0 11.0 %collective-permute-start.27 = (f32[2,256,128]{2,1,0:T(8,128)}, f32[2,256,128]{2,1,0:T(8,128)S(1)}, u32[]{:S(2)}, u32[]{:S(2)}) collective-permute-start(f32[2,256,128]{2,1,0:T(8,128)} %get-tuple-element.90.refs_10_), channel_id=1, source_target_pairs={{0,8},{8,16},{16,24},{1,9},{9,17},{17,25},{2,10},{10,18},{18,26},{... | collective-permute-start | bytes 786440 | tf_op jit(solution)/shard_map/ppermute | solution.py:25
  121.6 7.6 %collective-permute-start.29 = (f32[256,128]{1,0:T(8,128)}, f32[256,128]{1,0:T(8,128)S(1)}, u32[]{:S(2)}, u32[]{:S(2)}) collective-permute-start(f32[256,128]{1,0:T(8,128)} %get-tuple-element.92), channel_id=1, source_target_pairs={{0,1},{1,2},{2,3},{3,4},{4,5},{5,6},{6,7},{7,0},{8,9},{9,10},{10,1... | collective-permute-start | bytes 393224 | tf_op jit(solution)/shard_map/ppermute | solution.py:25
  121.7 7.6 %collective-permute-start.30 = (f32[256,128]{1,0:T(8,128)}, f32[256,128]{1,0:T(8,128)S(1)}, u32[]{:S(2)}, u32[]{:S(2)}) collective-permute-start(f32[256,128]{1,0:T(8,128)} %get-tuple-element.93), channel_id=1, source_target_pairs={{0,7},{1,0},{2,1},{3,2},{4,3},{5,4},{6,5},{7,6},{8,15},{9,8},{10,9... | collective-permute-start | bytes 393224 | tf_op jit(solution)/shard_map/ppermute | solution.py:25
  150.7 5.1 %collective-permute-start.32 = (f32[48,128]{1,0:T(8,128)S(1)}, f32[48,128]{1,0:T(8,128)S(1)}, u32[]{:S(2)}, u32[]{:S(2)}) collective-permute-start(f32[48,128]{1,0:T(8,128)S(1)} %get-tuple-element.97.refs_0_), channel_id=1, source_target_pairs={{0,16},{8,24},{16,0},{24,8},{1,17},{9,25},{17,1},{25,9},{2,18},{10... | collective-permute-start | bytes 73736 | tf_op jit(solution)/shard_map/ppermute | solution.py:25
  153.8 4.7 %collective-permute-start.31 = (f32[48,128]{1,0:T(8,128)S(1)}, f32[48,128]{1,0:T(8,128)S(1)}, u32[]{:S(2)}, u32[]{:S(2)}) collective-permute-start(f32[48,128]{1,0:T(8,128)S(1)} %get-tuple-element.97.refs_0_), channel_id=1, source_target_pairs={{0,8},{8,16},{16,24},{24,0},{1,9},{9,17},{17,25},{25,1},{2,10},{10... | collective-permute-start | bytes 73736 | tf_op jit(solution)/shard_map/ppermute | solution.py:25
  160.5 13.0 %collective-permute-start.38 = (f32[2,256,128]{2,1,0:T(8,128)}, f32[2,256,128]{2,1,0:T(8,128)S(1)}, u32[]{:S(2)}, u32[]{:S(2)}) collective-permute-start(f32[2,256,128]{2,1,0:T(8,128)} %get-tuple-element.104.refs_9_), channel_id=1, source_target_pairs={{8,0},{16,8},{24,16},{9,1},{17,9},{25,17},{10,2},{18,10},{26,18},{... | collective-permute-start | bytes 786440 | tf_op jit(solution)/shard_map/ppermute | solution.py:25
  161.8 4.1 %collective-permute-start.36 = (f32[48,128]{1,0:T(8,128)}, f32[48,128]{1,0:T(8,128)S(1)}, u32[]{:S(2)}, u32[]{:S(2)}) collective-permute-start(f32[48,128]{1,0:T(8,128)} %get-tuple-element.99.refs_0_), channel_id=1, source_target_pairs={{0,6},{1,7},{2,0},{3,1},{4,2},{5,3},{6,4},{7,5},{8,14},{9,15},{10,... | collective-permute-start | bytes 73736 | tf_op jit(solution)/shard_map/ppermute | solution.py:25
  161.9 5.0 %collective-permute-start.35 = (f32[48,128]{1,0:T(8,128)}, f32[48,128]{1,0:T(8,128)S(1)}, u32[]{:S(2)}, u32[]{:S(2)}) collective-permute-start(f32[48,128]{1,0:T(8,128)} %get-tuple-element.99.refs_0_), channel_id=1, source_target_pairs={{0,4},{1,5},{2,6},{3,7},{4,0},{5,1},{6,2},{7,3},{8,12},{9,13},{10,... | collective-permute-start | bytes 73736 | tf_op jit(solution)/shard_map/ppermute | solution.py:25
  162.1 6.6 %collective-permute-start.34 = (f32[48,128]{1,0:T(8,128)}, f32[48,128]{1,0:T(8,128)S(1)}, u32[]{:S(2)}, u32[]{:S(2)}) collective-permute-start(f32[48,128]{1,0:T(8,128)} %get-tuple-element.99.refs_0_), channel_id=1, source_target_pairs={{0,2},{1,3},{2,4},{3,5},{4,6},{5,7},{6,0},{7,1},{8,10},{9,11},{10,... | collective-permute-start | bytes 73736 | tf_op jit(solution)/shard_map/ppermute | solution.py:25
  (94 other events, 365.2 us)

commit v3 on v2

--- a/solution.py
+++ b/solution.py
@@ -151,6 +151,14 @@
         out[i * size:(i + 1) * size] = refs[i][...]
 
 
+def room(*shapes):
+    total = 0
+    for x in shapes:
+        dims = (1, 1, *x.shape)
+        total += int(np.prod(dims[:-2])) * -(-dims[-2] // 16) * 16 * -(-dims[-1] // 128) * 128 * np.dtype(x.dtype).itemsize
+    return pltpu.CompilerParams(vmem_limit_bytes=total + 2 * 1024 * 1024)
+
+
 def relay(kernel, parts, shape, through, name):
     specs = [VMEM] * len(parts) + [ANY] * len(through)
     return pl.pallas_call(
@@ -158,6 +166,7 @@
         out_shape=(shape, *[jax.ShapeDtypeStruct(x.shape, x.dtype) for x in through]),
         in_specs=specs,
         out_specs=(VMEM, *[ANY] * len(through)),
+        compiler_params=room(*parts, shape),
         input_output_aliases={len(parts) + i: 1 + i for i in range(len(through))},
         name=name,
     )(*parts, *through)
@@ -403,7 +412,6 @@
     four = shape(count, 4, size, loads_n)
     long_face = shape(size + below, loads_n)
     long_faces = shape(count, size + below, loads_n)
-    params = pltpu.CompilerParams(vmem_limit_bytes=40 * 1024 * 1024)
     table, rows_table = corner_tables(cuts, height)
 
     slots = pl.pallas_call(
@@ -411,6 +419,7 @@
         out_shape=shape(count * height, dofs),
         in_specs=[SMEM, SMEM, VMEM],
         out_specs=VMEM,
+        compiler_params=room(corner_rows, shape(count * height, dofs)),
         name="corner",
     )(at, corner_map, corner_rows)
     residual, to_far, to_right, inner, c_rows = pl.pallas_call(
@@ -419,6 +428,7 @@
         in_specs=[SMEM, SMEM] + [VMEM] * 3,
         out_specs=(VMEM,) * 5,
         scratch_shapes=[pltpu.VMEM((count, 2, 2 * size, loads_n), F32)],
+        compiler_params=room(gap, coupling, rows_table, pair, pair, pair, long_faces, long_faces, faces, coupling),
         name="prepare",
     )(at, offsets, gap, coupling, rows_table)
     from_near = shifted(to_far, "cuts", 1, False)
@@ -429,7 +439,7 @@
         out_shape=(jax.ShapeDtypeStruct(flexibility.shape, BF16),) * 2,
         in_specs=[VMEM],
         out_specs=(VMEM, VMEM),
-        compiler_params=params,
+        compiler_params=room(flexibility, flexibility),
         cost_estimate=pl.CostEstimate(flops=0, bytes_accessed=8 * flexibility.size, transcendentals=0),
         name="split",
     )(flexibility)
@@ -450,16 +460,17 @@
         pltpu.VMEM((blocks * count * height, loads_n), F32),
         pltpu.VMEM((count, 4, 2 * size, loads_n), F32),
     ]
+    first_args = (residual, from_near, from_left, inner, coupling, a_high, a_low, c_rows)
     *out, loads = pl.pallas_call(
         functools.partial(first_kernel, height, rr_rows),
         out_shape=first_sends + (four,),
         in_specs=[VMEM] * 8,
         out_specs=(VMEM,) * 7,
         scratch_shapes=a_buffers,
-        compiler_params=params,
+        compiler_params=room(*first_args, *first_sends, four, *a_buffers),
         cost_estimate=cost,
         name="first",
-    )(residual, from_near, from_left, inner, coupling, a_high, a_low, c_rows)
+    )(*first_args)
 
     state = []
     for which in range(ITERS):
@@ -490,6 +501,7 @@
                 ),
                 in_specs=[SMEM] + [VMEM] * 6,
                 out_specs=(VMEM,) * 3,
+                compiler_params=room(coupling, from_near, r_far, from_left, r_right, table, *[faces] * 6),
                 name="spread",
             )(at, coupling, from_near, r_far, from_left, r_right, table)
         args = [all_offsets, side, mine, theirs, k_high, k_low, ct_own, ct_left, ct_right, near, far, sides,
@@ -508,7 +520,7 @@
             in_specs=specs,
             out_specs=(VMEM,) * len(outs),
             scratch_shapes=scratch,
-            compiler_params=params,
+            compiler_params=room(*args[2:], *outs, *scratch),
             cost_estimate=None if last else cost,
             name=f"step{which}",
         )(*args)

time: 187 us -> 124 us (0.66); the launches traced: 184 us -> 123 us
  local copies, waits for them, and re-layouts: 63.2 us -> 19.7 us
  Pallas kernels: 37.8 us -> 17 us
  starting transfers between devices: 47.6 us -> 51.8 us
    unnamed x176 -> x28, local copies, waits for them, and re-layouts: 60.3 us -> 16.8 us
    pallas_call x6, Pallas kernels: 8.49 us -> 0.05 us  [relay(): pl.pallas_call(functools.partial(kernel, len(parts)), out_shape=(shape, *...]
    pallas_call x3, Pallas kernels: 15.7 us -> 11.3 us  [per_device(): pl.pallas_call(functools.partial(step_kernel, which, height, rr_rows), ou...]
    ppermute x36, starting transfers between devices: 47 us -> 51.2 us  [shifted(): return lax.ppermute(value, axis, pairs)]
    pallas_call x1, Pallas kernels: 4.6 us -> 1.13 us  [per_device(): pl.pallas_call(split_kernel, out_shape=(jax.ShapeDtypeStruct(flexibility....]
    pallas_call x1, Pallas kernels: 2.58 us -> 0.44 us  [per_device(): pl.pallas_call(spread_kernel, out_shape=(shape(count, 6 * size, 6 * heigh...]
  transfers between devices with their start and end apart: 40 -> 40, of which waited for: 23 -> 24; matrix products, arithmetic and copies ran while one was open for 4% -> 4% of each run, Pallas kernels for 8% -> 2%
where the time goes in v3:
time: 124 us; the launch traced here: 123 us
  starting transfers between devices  51.8 us (42%)
  waiting for transfers between devices  31.3 us (25%)
  local copies, waits for them, and re-layouts  19.7 us (16%)
  Pallas kernels  17 us (14%)
  between operations  1.66 us (1%)
    ppermute x36, starting transfers between devices, shifted(): return lax.ppermute(value, axis, pairs)  51.2 us
    ppermute x36, waiting for transfers between devices, shifted(): return lax.ppermute(value, axis, pairs)  28.7 us
    unnamed x28, local copies, waits for them, and re-layouts  16.8 us
    pallas_call x3, Pallas kernels, per_device(): pl.pallas_call(functools.partial(step_kernel, which, height, rr_rows), ou...  11.3 us
    pallas_call x1, Pallas kernels, per_device(): pl.pallas_call(functools.partial(first_kernel, height, rr_rows), out_shap...  2.65 us
    ppermute x4, waiting for transfers between devices, swapped(): lax.ppermute(value, axis, [(source, source ^ 1) for source in range(lax.a...  2.61 us
  transfers between devices with their start and end apart: 40, of which 24 were waited for; matrix products, arithmetic and copies ran while one was open for 4% of the time, Pallas kernels for 2%

profile of v3, /device:TPU:0, one launch (start us, length us, event | category | flops | bytes accessed | tf_op | source)
XLA Modules:
  0.0 122.9 jit_solution(16076888376878991355)
XLA Ops:
  2.6 3.9 %collective-permute-start.11 = (f32[32,192]{1,0:T(8,128)S(1)}, f32[32,192]{1,0:T(8,128)S(1)}, u32[]{:S(2)}, u32[]{:S(2)}) collective-permute-start(f32[32,192]{1,0:T(8,128)S(1)} %corner.1), channel_id=1, source_target_pairs={{0,24},{8,0},{16,8},{24,16},{1,25},{9,1},{17,9},{25,17},{2,26},{10... | collective-permute-start | bytes 73736 | tf_op jit(solution)/shard_map/ppermute | solution.py:25
  12.1 4.3 %collective-permute-start = (f32[2,288,128]{2,1,0:T(8,128)S(1)}, f32[2,288,128]{2,1,0:T(8,128)S(1)}, u32[]{:S(2)}, u32[]{:S(2)}) collective-permute-start(f32[2,288,128]{2,1,0:T(8,128)S(1)} %get-tuple-element.59), channel_id=1, source_target_pairs={{0,8},{8,16},{16,24},{1,9},{9,17},{17,25},{2,10},{10,18},{18,26},{... | collective-permute-start | bytes 884744 | tf_op jit(solution)/shard_map/ppermute | solution.py:25
  16.5 3.7 %collective-permute-start.14 = (f32[32,192]{1,0:T(8,128)S(1)}, f32[32,192]{1,0:T(8,128)S(1)}, u32[]{:S(2)}, u32[]{:S(2)}) collective-permute-start(f32[32,192]{1,0:T(8,128)S(1)} %add_add_fusion), channel_id=1, source_target_pairs={{0,6},{1,7},{2,0},{3,1},{4,2},{5,3},{6,4},{7,5},{8,14},{9,15},{10,... | collective-permute-start | bytes 73736 | tf_op jit(solution)/shard_map/ppermute | solution.py:25
  23.9 1.4 %collective-permute-done.13 = f32[32,192]{1,0:T(8,128)S(1)} collective-permute-done((f32[32,192]{1,0:T(8,128)S(1)}, f32[32,192]{1,0:T(8,128)S(1)}, u32[]{:S(2)}, u32[]{:S(2)}) %collective-permute-start.13) | collective-permute-done | bytes 24608 | tf_op jit(solution)/shard_map/ppermute | solution.py:25
  26.2 3.4 %copy-done.6 = f32[1,2,1024,1024]{3,2,1,0:T(8,128)S(1)} copy-done((f32[1,2,1024,1024]{3,2,1,0:T(8,128)S(1)}, f32[1,2,1024,1024]{3,2,1,0:T(8,128)}, u32[]{:S(2)}) %copy-start.6) | copy-done | bytes 8388632
  30.7 2.0 %copy-done = bf16[2,1024,1024]{2,1,0:T(8,128)(2,1)} copy-done((bf16[2,1024,1024]{2,1,0:T(8,128)(2,1)}, bf16[2,1024,1024]{2,1,0:T(8,128)(2,1)S(1)}, u32[]{:S(2)}) %copy-start) | copy-done | bytes 4194328
  32.7 2.0 %copy-done.3 = bf16[2,1024,1024]{2,1,0:T(8,128)(2,1)} copy-done((bf16[2,1024,1024]{2,1,0:T(8,128)(2,1)}, bf16[2,1024,1024]{2,1,0:T(8,128)(2,1)S(1)}, u32[]{:S(2)}) %copy-start.3) | copy-done | bytes 4194328
  35.5 2.2 %copy-done.1 = bf16[2,1024,1024]{2,1,0:T(8,128)(2,1)S(1)} copy-done((bf16[2,1024,1024]{2,1,0:T(8,128)(2,1)S(1)}, bf16[2,1024,1024]{2,1,0:T(8,128)(2,1)}, u32[]{:S(2)}) %copy-start.1) | copy-done | bytes 4194328
  37.6 2.2 %copy-done.4 = bf16[2,1024,1024]{2,1,0:T(8,128)(2,1)S(1)} copy-done((bf16[2,1024,1024]{2,1,0:T(8,128)(2,1)S(1)}, bf16[2,1024,1024]{2,1,0:T(8,128)(2,1)}, u32[]{:S(2)}) %copy-start.4) | copy-done | bytes 4194328
  39.8 2.6 %first.1 = (f32[2,288,128]{2,1,0:T(8,128)S(1)}, f32[2,256,128]{2,1,0:T(8,128)S(1)}, f32[2,2,256,128]{3,2,1,0:T(8,128)S(1)}, f32[288,128]{1,0:T(8,128)S(1)}, f32[...) custom-call(f32[2,2,256,128]{3,2,1,0:T(8,128)S(1)} %get-tuple-element.61.residual, ...), custom_call_target="tpu_custom_call" | custom-call | flops 1610612736 | bytes 8388608 | tf_op jit(solution)/shard_map/first/pallas_call | solution.py:464
  42.5 1.4 %collective-permute-start.3 = (f32[48,128]{1,0:T(8,128)S(1)}, f32[48,128]{1,0:T(8,128)S(1)}, u32[]{:S(2)}, u32[]{:S(2)}) collective-permute-start(f32[48,128]{1,0:T(8,128)S(1)} %get-tuple-element.66.refs_0_), channel_id=1, source_target_pairs={{0,16},{8,24},{16,0},{24,8},{1,17},{9,25},{17,1},{25,9},{2,18},{10... | collective-permute-start | bytes 73736 | tf_op jit(solution)/shard_map/ppermute | solution.py:25
  46.4 2.3 %collective-permute-done.2.refs_1_ = f32[48,128]{1,0:T(8,128)S(1)} collective-permute-done((f32[48,128]{1,0:T(8,128)S(1)}, f32[48,128]{1,0:T(8,128)S(1)}, u32[]{:S(2)}, u32[]{:S(2)}) %collective-permute-start.2) | collective-permute-done | bytes 24608 | tf_op jit(solution)/shard_map/ppermute | solution.py:25
  54.6 1.8 %collective-permute-done.5.refs_1_ = f32[48,128]{1,0:T(8,128)S(1)} collective-permute-done((f32[48,128]{1,0:T(8,128)S(1)}, f32[48,128]{1,0:T(8,128)S(1)}, u32[]{:S(2)}, u32[]{:S(2)}) %collective-permute-start.5) | collective-permute-done | bytes 24608 | tf_op jit(solution)/shard_map/ppermute | solution.py:25
  56.5 3.5 %collective-permute-start.17 = (f32[288,128]{1,0:T(8,128)S(1)}, f32[288,128]{1,0:T(8,128)S(1)}, u32[]{:S(2)}, u32[]{:S(2)}) collective-permute-start(f32[288,128]{1,0:T(8,128)S(1)} %get-tuple-element.74), channel_id=1, source_target_pairs={{0,7},{1,0},{2,1},{3,2},{4,3},{5,4},{6,5},{7,6},{8,15},{9,8},{10,9... | collective-permute-start | bytes 442376 | tf_op jit(solution)/shard_map/ppermute | solution.py:25
  60.0 2.1 %collective-permute-start.18 = (f32[2,256,128]{2,1,0:T(8,128)S(1)}, f32[2,256,128]{2,1,0:T(8,128)S(1)}, u32[]{:S(2)}, u32[]{:S(2)}) collective-permute-start(f32[2,256,128]{2,1,0:T(8,128)S(1)} %get-tuple-element.78.refs_10_), channel_id=1, source_target_pairs={{0,8},{8,16},{16,24},{1,9},{9,17},{17,25},{2,10},{10,18},{18,26},{... | collective-permute-start | bytes 786440 | tf_op jit(solution)/shard_map/ppermute | solution.py:25
  63.5 2.5 %collective-permute-done.18.refs_12_ = f32[2,256,128]{2,1,0:T(8,128)S(1)} collective-permute-done((f32[2,256,128]{2,1,0:T(8,128)S(1)}, f32[2,256,128]{2,1,0:T(8,128)S(1)}, u32[]{:S(2)}, u32[]{:S(2)}) %collective-permute-start.18) | collective-permute-done | bytes 262176 | tf_op jit(solution)/shard_map/ppermute | solution.py:25
  66.0 4.5 %step0.1 = (f32[2,256,128]{2,1,0:T(8,128)S(1)}, f32[2,256,128]{2,1,0:T(8,128)S(1)}, f32[2,2,256,128]{3,2,1,0:T(8,128)S(1)}, f32[256,128]{1,0:T(8,128)S(1)}, f32[...) custom-call(s32[2,4]{1,0:T(2,128)S(1)} %pad_add_fusion.refs_0_, ...), custom_call_target="tpu_custom_call" | custom-call | flops 1610612736 | bytes 8388608 | tf_op jit(solution)/shard_map/step0/pallas_call | solution.py:517
  70.4 3.5 %collective-permute-start.22 = (f32[48,128]{1,0:T(8,128)S(1)}, f32[48,128]{1,0:T(8,128)S(1)}, u32[]{:S(2)}, u32[]{:S(2)}) collective-permute-start(f32[48,128]{1,0:T(8,128)S(1)} %get-tuple-element.82.refs_0_), channel_id=1, source_target_pairs={{0,24},{8,0},{16,8},{24,16},{1,25},{9,1},{17,9},{25,17},{2,26},{10... | collective-permute-start | bytes 73736 | tf_op jit(solution)/shard_map/ppermute | solution.py:25
  74.4 1.9 %collective-permute-start.20 = (f32[48,128]{1,0:T(8,128)S(1)}, f32[48,128]{1,0:T(8,128)S(1)}, u32[]{:S(2)}, u32[]{:S(2)}) collective-permute-start(f32[48,128]{1,0:T(8,128)S(1)} %get-tuple-element.82.refs_0_), channel_id=1, source_target_pairs={{0,8},{8,16},{16,24},{24,0},{1,9},{9,17},{17,25},{25,1},{2,10},{10... | collective-permute-start | bytes 73736 | tf_op jit(solution)/shard_map/ppermute | solution.py:25
  77.8 1.4 %collective-permute-done.20.refs_1_ = f32[48,128]{1,0:T(8,128)S(1)} collective-permute-done((f32[48,128]{1,0:T(8,128)S(1)}, f32[48,128]{1,0:T(8,128)S(1)}, u32[]{:S(2)}, u32[]{:S(2)}) %collective-permute-start.20) | collective-permute-done | bytes 24608 | tf_op jit(solution)/shard_map/ppermute | solution.py:25
  79.2 2.3 %collective-permute-start.25 = (f32[48,128]{1,0:T(8,128)S(1)}, f32[48,128]{1,0:T(8,128)S(1)}, u32[]{:S(2)}, u32[]{:S(2)}) collective-permute-start(f32[48,128]{1,0:T(8,128)S(1)} %get-tuple-element.84.refs_0_), channel_id=1, source_target_pairs={{0,6},{1,7},{2,0},{3,1},{4,2},{5,3},{6,4},{7,5},{8,14},{9,15},{10,... | collective-permute-start | bytes 73736 | tf_op jit(solution)/shard_map/ppermute | solution.py:25
  81.5 1.4 %collective-permute-start.23 = (f32[48,128]{1,0:T(8,128)S(1)}, f32[48,128]{1,0:T(8,128)S(1)}, u32[]{:S(2)}, u32[]{:S(2)}) collective-permute-start(f32[48,128]{1,0:T(8,128)S(1)} %get-tuple-element.84.refs_0_), channel_id=1, source_target_pairs={{0,2},{1,3},{2,4},{3,5},{4,6},{5,7},{6,0},{7,1},{8,10},{9,11},{10,... | collective-permute-start | bytes 73736 | tf_op jit(solution)/shard_map/ppermute | solution.py:25
  84.2 2.0 %collective-permute-done.24.refs_2_ = f32[48,128]{1,0:T(8,128)S(1)} collective-permute-done((f32[48,128]{1,0:T(8,128)S(1)}, f32[48,128]{1,0:T(8,128)S(1)}, u32[]{:S(2)}, u32[]{:S(2)}) %collective-permute-start.24) | collective-permute-done | bytes 24608 | tf_op jit(solution)/shard_map/ppermute | solution.py:25
  87.1 3.0 %collective-permute-start.27 = (f32[2,256,128]{2,1,0:T(8,128)S(1)}, f32[2,256,128]{2,1,0:T(8,128)S(1)}, u32[]{:S(2)}, u32[]{:S(2)}) collective-permute-start(f32[2,256,128]{2,1,0:T(8,128)S(1)} %get-tuple-element.90.refs_10_), channel_id=1, source_target_pairs={{0,8},{8,16},{16,24},{1,9},{9,17},{17,25},{2,10},{10,18},{18,26},{... | collective-permute-start | bytes 786440 | tf_op jit(solution)/shard_map/ppermute | solution.py:25
  90.2 3.5 %collective-permute-start.30 = (f32[256,128]{1,0:T(8,128)S(1)}, f32[256,128]{1,0:T(8,128)S(1)}, u32[]{:S(2)}, u32[]{:S(2)}) collective-permute-start(f32[256,128]{1,0:T(8,128)S(1)} %get-tuple-element.93), channel_id=1, source_target_pairs={{0,7},{1,0},{2,1},{3,2},{4,3},{5,4},{6,5},{7,6},{8,15},{9,8},{10,9... | collective-permute-start | bytes 393224 | tf_op jit(solution)/shard_map/ppermute | solution.py:25
  95.0 2.4 %collective-permute-done.29.refs_14_ = f32[256,128]{1,0:T(8,128)S(1)} collective-permute-done((f32[256,128]{1,0:T(8,128)S(1)}, f32[256,128]{1,0:T(8,128)S(1)}, u32[]{:S(2)}, u32[]{:S(2)}) %collective-permute-start.29) | collective-permute-done | bytes 131104 | tf_op jit(solution)/shard_map/ppermute | solution.py:25
  97.4 4.6 %step1.1 = (f32[2,256,128]{2,1,0:T(8,128)S(1)}, f32[2,256,128]{2,1,0:T(8,128)S(1)}, f32[2,2,256,128]{3,2,1,0:T(8,128)S(1)}, f32[256,128]{1,0:T(8,128)S(1)}, f32[...) custom-call(s32[2,4]{1,0:T(2,128)S(1)} %pad_add_fusion.refs_0_, ...), custom_call_target="tpu_custom_call" | custom-call | flops 1610612736 | bytes 8388608 | tf_op jit(solution)/shard_map/step1/pallas_call | solution.py:517
  102.3 3.1 %collective-permute-start.32 = (f32[48,128]{1,0:T(8,128)S(1)}, f32[48,128]{1,0:T(8,128)S(1)}, u32[]{:S(2)}, u32[]{:S(2)}) collective-permute-start(f32[48,128]{1,0:T(8,128)S(1)} %get-tuple-element.97.refs_0_), channel_id=1, source_target_pairs={{0,16},{8,24},{16,0},{24,8},{1,17},{9,25},{17,1},{25,9},{2,18},{10... | collective-permute-start | bytes 73736 | tf_op jit(solution)/shard_map/ppermute | solution.py:25
  107.3 2.9 %collective-permute-done.31.refs_1_ = f32[48,128]{1,0:T(8,128)S(1)} collective-permute-done((f32[48,128]{1,0:T(8,128)S(1)}, f32[48,128]{1,0:T(8,128)S(1)}, u32[]{:S(2)}, u32[]{:S(2)}) %collective-permute-start.31) | collective-permute-done | bytes 24608 | tf_op jit(solution)/shard_map/ppermute | solution.py:25
  113.6 1.8 %collective-permute-done.36.refs_3_ = f32[48,128]{1,0:T(8,128)S(1)} collective-permute-done((f32[48,128]{1,0:T(8,128)S(1)}, f32[48,128]{1,0:T(8,128)S(1)}, u32[]{:S(2)}, u32[]{:S(2)}) %collective-permute-start.36) | collective-permute-done | bytes 24608 | tf_op jit(solution)/shard_map/ppermute | solution.py:25
  116.4 1.7 %collective-permute-done.34.refs_1_ = f32[48,128]{1,0:T(8,128)S(1)} collective-permute-done((f32[48,128]{1,0:T(8,128)S(1)}, f32[48,128]{1,0:T(8,128)S(1)}, u32[]{:S(2)}, u32[]{:S(2)}) %collective-permute-start.34) | collective-permute-done | bytes 24608 | tf_op jit(solution)/shard_map/ppermute | solution.py:25
  120.7 2.2 %step2.1 = (f32[2,2,256,128]{3,2,1,0:T(8,128)}, f32[2,2,256,128]{3,2,1,0:T(8,128)}) custom-call(s32[2,4]{1,0:T(2,128)S(1)} %pad_add_fusion.refs_0_, s32[1]{0:T(128)} %bitcast.5.refs_1_, f32[192,128]{1,0:T(8,128)S(1)} %get-tuple-element.103.refs_2_, f32[192,128]{1,0:T(8,128)S(1)} %collective-permute-done.37.refs_3_, ...), custom_call_target="tpu_custom_call" | custom-call | tf_op jit(solution)/shard_map/step2/pallas_call | solution.py:517
  (115 shorter events, 37.7 us)
Async XLA Ops:
  2.6 13.8 %collective-permute-start.11 = (f32[32,192]{1,0:T(8,128)S(1)}, f32[32,192]{1,0:T(8,128)S(1)}, u32[]{:S(2)}, u32[]{:S(2)}) collective-permute-start(f32[32,192]{1,0:T(8,128)S(1)} %corner.1), channel_id=1, source_target_pairs={{0,24},{8,0},{16,8},{24,16},{1,25},{9,1},{17,9},{25,17},{2,26},{10... | collective-permute-start | bytes 73736 | tf_op jit(solution)/shard_map/ppermute | solution.py:25
  6.6 9.9 %collective-permute-start.10 = (f32[32,192]{1,0:T(8,128)S(1)}, f32[32,192]{1,0:T(8,128)S(1)}, u32[]{:S(2)}, u32[]{:S(2)}) collective-permute-start(f32[32,192]{1,0:T(8,128)S(1)} %corner.1), channel_id=1, source_target_pairs={{0,16},{8,24},{16,0},{24,8},{1,17},{9,25},{17,1},{25,9},{2,18},{10... | collective-permute-start | bytes 73736 | tf_op jit(solution)/shard_map/ppermute | solution.py:25
  7.1 9.4 %collective-permute-start.9 = (f32[32,192]{1,0:T(8,128)S(1)}, f32[32,192]{1,0:T(8,128)S(1)}, u32[]{:S(2)}, u32[]{:S(2)}) collective-permute-start(f32[32,192]{1,0:T(8,128)S(1)} %corner.1), channel_id=1, source_target_pairs={{0,8},{8,16},{16,24},{24,0},{1,9},{9,17},{17,25},{25,1},{2,10},{10... | collective-permute-start | bytes 73736 | tf_op jit(solution)/shard_map/ppermute | solution.py:25
  12.1 23.4 %collective-permute-start.1 = (f32[288,128]{1,0:T(8,128)S(1)}, f32[288,128]{1,0:T(8,128)S(1)}, u32[]{:S(2)}, u32[]{:S(2)}) collective-permute-start(f32[288,128]{1,0:T(8,128)S(1)} %get-tuple-element.60), channel_id=1, source_target_pairs={{0,1},{1,2},{2,3},{3,4},{4,5},{5,6},{6,7},{7,0},{8,9},{9,10},{10,1... | collective-permute-start | bytes 442376 | tf_op jit(solution)/shard_map/ppermute | solution.py:25
  12.1 23.3 %collective-permute-start = (f32[2,288,128]{2,1,0:T(8,128)S(1)}, f32[2,288,128]{2,1,0:T(8,128)S(1)}, u32[]{:S(2)}, u32[]{:S(2)}) collective-permute-start(f32[2,288,128]{2,1,0:T(8,128)S(1)} %get-tuple-element.59), channel_id=1, source_target_pairs={{0,8},{8,16},{16,24},{1,9},{9,17},{17,25},{2,10},{10,18},{18,26},{... | collective-permute-start | bytes 884744 | tf_op jit(solution)/shard_map/ppermute | solution.py:25
  16.5 7.4 %collective-permute-start.14 = (f32[32,192]{1,0:T(8,128)S(1)}, f32[32,192]{1,0:T(8,128)S(1)}, u32[]{:S(2)}, u32[]{:S(2)}) collective-permute-start(f32[32,192]{1,0:T(8,128)S(1)} %add_add_fusion), channel_id=1, source_target_pairs={{0,6},{1,7},{2,0},{3,1},{4,2},{5,3},{6,4},{7,5},{8,14},{9,15},{10,... | collective-permute-start | bytes 73736 | tf_op jit(solution)/shard_map/ppermute | solution.py:25
  20.1 5.2 %collective-permute-start.13 = (f32[32,192]{1,0:T(8,128)S(1)}, f32[32,192]{1,0:T(8,128)S(1)}, u32[]{:S(2)}, u32[]{:S(2)}) collective-permute-start(f32[32,192]{1,0:T(8,128)S(1)} %add_add_fusion), channel_id=1, source_target_pairs={{0,4},{1,5},{2,6},{3,7},{4,0},{5,1},{6,2},{7,3},{8,12},{9,13},{10,... | collective-permute-start | bytes 73736 | tf_op jit(solution)/shard_map/ppermute | solution.py:25
  20.1 5.7 %collective-permute-start.12 = (f32[32,192]{1,0:T(8,128)S(1)}, f32[32,192]{1,0:T(8,128)S(1)}, u32[]{:S(2)}, u32[]{:S(2)}) collective-permute-start(f32[32,192]{1,0:T(8,128)S(1)} %add_add_fusion), channel_id=1, source_target_pairs={{0,2},{1,3},{2,4},{3,5},{4,6},{5,7},{6,0},{7,1},{8,10},{9,11},{10,... | collective-permute-start | bytes 73736 | tf_op jit(solution)/shard_map/ppermute | solution.py:25
  25.9 8.8 %collective-permute-start.15 = (f32[128,192]{1,0:T(8,128)S(1)}, f32[128,192]{1,0:T(8,128)S(1)}, u32[]{:S(2)}, u32[]{:S(2)}) collective-permute-start(f32[128,192]{1,0:T(8,128)S(1)} %pad_maximum_fusion.1), channel_id=1, source_target_pairs={{0,1},{1,0},{2,3},{3,2},{4,5},{5,4},{6,7},{7,6},{8,9},{9,8},{10,11... | collective-permute-start | bytes 294920 | tf_op jit(solution)/shard_map/ppermute | solution.py:45
  42.5 3.9 %collective-permute-start.3 = (f32[48,128]{1,0:T(8,128)S(1)}, f32[48,128]{1,0:T(8,128)S(1)}, u32[]{:S(2)}, u32[]{:S(2)}) collective-permute-start(f32[48,128]{1,0:T(8,128)S(1)} %get-tuple-element.66.refs_0_), channel_id=1, source_target_pairs={{0,16},{8,24},{16,0},{24,8},{1,17},{9,25},{17,1},{25,9},{2,18},{10... | collective-permute-start | bytes 73736 | tf_op jit(solution)/shard_map/ppermute | solution.py:25
  44.0 4.7 %collective-permute-start.2 = (f32[48,128]{1,0:T(8,128)S(1)}, f32[48,128]{1,0:T(8,128)S(1)}, u32[]{:S(2)}, u32[]{:S(2)}) collective-permute-start(f32[48,128]{1,0:T(8,128)S(1)} %get-tuple-element.66.refs_0_), channel_id=1, source_target_pairs={{0,8},{8,16},{16,24},{24,0},{1,9},{9,17},{17,25},{25,1},{2,10},{10... | collective-permute-start | bytes 73736 | tf_op jit(solution)/shard_map/ppermute | solution.py:25
  48.7 5.2 %collective-permute-start.7 = (f32[48,128]{1,0:T(8,128)S(1)}, f32[48,128]{1,0:T(8,128)S(1)}, u32[]{:S(2)}, u32[]{:S(2)}) collective-permute-start(f32[48,128]{1,0:T(8,128)S(1)} %get-tuple-element.68.refs_0_), channel_id=1, source_target_pairs={{0,6},{1,7},{2,0},{3,1},{4,2},{5,3},{6,4},{7,5},{8,14},{9,15},{10,... | collective-permute-start | bytes 73736 | tf_op jit(solution)/shard_map/ppermute | solution.py:25
  49.9 4.7 %collective-permute-start.6 = (f32[48,128]{1,0:T(8,128)S(1)}, f32[48,128]{1,0:T(8,128)S(1)}, u32[]{:S(2)}, u32[]{:S(2)}) collective-permute-start(f32[48,128]{1,0:T(8,128)S(1)} %get-tuple-element.68.refs_0_), channel_id=1, source_target_pairs={{0,4},{1,5},{2,6},{3,7},{4,0},{5,1},{6,2},{7,3},{8,12},{9,13},{10,... | collective-permute-start | bytes 73736 | tf_op jit(solution)/shard_map/ppermute | solution.py:25
  50.8 5.6 %collective-permute-start.5 = (f32[48,128]{1,0:T(8,128)S(1)}, f32[48,128]{1,0:T(8,128)S(1)}, u32[]{:S(2)}, u32[]{:S(2)}) collective-permute-start(f32[48,128]{1,0:T(8,128)S(1)} %get-tuple-element.68.refs_0_), channel_id=1, source_target_pairs={{0,2},{1,3},{2,4},{3,5},{4,6},{5,7},{6,0},{7,1},{8,10},{9,11},{10,... | collective-permute-start | bytes 73736 | tf_op jit(solution)/shard_map/ppermute | solution.py:25
  52.6 10.1 %collective-permute-start.16 = (f32[2,288,128]{2,1,0:T(8,128)S(1)}, f32[2,288,128]{2,1,0:T(8,128)S(1)}, u32[]{:S(2)}, u32[]{:S(2)}) collective-permute-start(f32[2,288,128]{2,1,0:T(8,128)S(1)} %get-tuple-element.73.refs_9_), channel_id=1, source_target_pairs={{8,0},{16,8},{24,16},{9,1},{17,9},{25,17},{10,2},{18,10},{26,18},{... | collective-permute-start | bytes 884744 | tf_op jit(solution)/shard_map/ppermute | solution.py:25
  56.4 7.1 %collective-permute-start.19 = (f32[256,128]{1,0:T(8,128)S(1)}, f32[256,128]{1,0:T(8,128)S(1)}, u32[]{:S(2)}, u32[]{:S(2)}) collective-permute-start(f32[256,128]{1,0:T(8,128)S(1)} %get-tuple-element.80), channel_id=1, source_target_pairs={{0,1},{1,2},{2,3},{3,4},{4,5},{5,6},{6,7},{7,0},{8,9},{9,10},{10,1... | collective-permute-start | bytes 393224 | tf_op jit(solution)/shard_map/ppermute | solution.py:25
  56.5 6.2 %collective-permute-start.17 = (f32[288,128]{1,0:T(8,128)S(1)}, f32[288,128]{1,0:T(8,128)S(1)}, u32[]{:S(2)}, u32[]{:S(2)}) collective-permute-start(f32[288,128]{1,0:T(8,128)S(1)} %get-tuple-element.74), channel_id=1, source_target_pairs={{0,7},{1,0},{2,1},{3,2},{4,3},{5,4},{6,5},{7,6},{8,15},{9,8},{10,9... | collective-permute-start | bytes 442376 | tf_op jit(solution)/shard_map/ppermute | solution.py:25
  60.0 5.9 %collective-permute-start.18 = (f32[2,256,128]{2,1,0:T(8,128)S(1)}, f32[2,256,128]{2,1,0:T(8,128)S(1)}, u32[]{:S(2)}, u32[]{:S(2)}) collective-permute-start(f32[2,256,128]{2,1,0:T(8,128)S(1)} %get-tuple-element.78.refs_10_), channel_id=1, source_target_pairs={{0,8},{8,16},{16,24},{1,9},{9,17},{17,25},{2,10},{10,18},{18,26},{... | collective-permute-start | bytes 786440 | tf_op jit(solution)/shard_map/ppermute | solution.py:25
  70.4 6.0 %collective-permute-start.22 = (f32[48,128]{1,0:T(8,128)S(1)}, f32[48,128]{1,0:T(8,128)S(1)}, u32[]{:S(2)}, u32[]{:S(2)}) collective-permute-start(f32[48,128]{1,0:T(8,128)S(1)} %get-tuple-element.82.refs_0_), channel_id=1, source_target_pairs={{0,24},{8,0},{16,8},{24,16},{1,25},{9,1},{17,9},{25,17},{2,26},{10... | collective-permute-start | bytes 73736 | tf_op jit(solution)/shard_map/ppermute | solution.py:25
  74.4 4.7 %collective-permute-start.20 = (f32[48,128]{1,0:T(8,128)S(1)}, f32[48,128]{1,0:T(8,128)S(1)}, u32[]{:S(2)}, u32[]{:S(2)}) collective-permute-start(f32[48,128]{1,0:T(8,128)S(1)} %get-tuple-element.82.refs_0_), channel_id=1, source_target_pairs={{0,8},{8,16},{16,24},{24,0},{1,9},{9,17},{17,25},{25,1},{2,10},{10... | collective-permute-start | bytes 73736 | tf_op jit(solution)/shard_map/ppermute | solution.py:25
  79.2 5.0 %collective-permute-start.25 = (f32[48,128]{1,0:T(8,128)S(1)}, f32[48,128]{1,0:T(8,128)S(1)}, u32[]{:S(2)}, u32[]{:S(2)}) collective-permute-start(f32[48,128]{1,0:T(8,128)S(1)} %get-tuple-element.84.refs_0_), channel_id=1, source_target_pairs={{0,6},{1,7},{2,0},{3,1},{4,2},{5,3},{6,4},{7,5},{8,14},{9,15},{10,... | collective-permute-start | bytes 73736 | tf_op jit(solution)/shard_map/ppermute | solution.py:25
  81.5 4.7 %collective-permute-start.24 = (f32[48,128]{1,0:T(8,128)S(1)}, f32[48,128]{1,0:T(8,128)S(1)}, u32[]{:S(2)}, u32[]{:S(2)}) collective-permute-start(f32[48,128]{1,0:T(8,128)S(1)} %get-tuple-element.84.refs_0_), channel_id=1, source_target_pairs={{0,4},{1,5},{2,6},{3,7},{4,0},{5,1},{6,2},{7,3},{8,12},{9,13},{10,... | collective-permute-start | bytes 73736 | tf_op jit(solution)/shard_map/ppermute | solution.py:25
  81.5 5.6 %collective-permute-start.23 = (f32[48,128]{1,0:T(8,128)S(1)}, f32[48,128]{1,0:T(8,128)S(1)}, u32[]{:S(2)}, u32[]{:S(2)}) collective-permute-start(f32[48,128]{1,0:T(8,128)S(1)} %get-tuple-element.84.refs_0_), channel_id=1, source_target_pairs={{0,2},{1,3},{2,4},{3,5},{4,6},{5,7},{6,0},{7,1},{8,10},{9,11},{10,... | collective-permute-start | bytes 73736 | tf_op jit(solution)/shard_map/ppermute | solution.py:25
  82.9 14.5 %collective-permute-start.28 = (f32[2,256,128]{2,1,0:T(8,128)S(1)}, f32[2,256,128]{2,1,0:T(8,128)S(1)}, u32[]{:S(2)}, u32[]{:S(2)}) collective-permute-start(f32[2,256,128]{2,1,0:T(8,128)S(1)} %get-tuple-element.89.refs_9_), channel_id=1, source_target_pairs={{8,0},{16,8},{24,16},{9,1},{17,9},{25,17},{10,2},{18,10},{26,18},{... | collective-permute-start | bytes 786440 | tf_op jit(solution)/shard_map/ppermute | solution.py:25
  87.1 10.3 %collective-permute-start.27 = (f32[2,256,128]{2,1,0:T(8,128)S(1)}, f32[2,256,128]{2,1,0:T(8,128)S(1)}, u32[]{:S(2)}, u32[]{:S(2)}) collective-permute-start(f32[2,256,128]{2,1,0:T(8,128)S(1)} %get-tuple-element.90.refs_10_), channel_id=1, source_target_pairs={{0,8},{8,16},{16,24},{1,9},{9,17},{17,25},{2,10},{10,18},{18,26},{... | collective-permute-start | bytes 786440 | tf_op jit(solution)/shard_map/ppermute | solution.py:25
  90.1 7.3 %collective-permute-start.29 = (f32[256,128]{1,0:T(8,128)S(1)}, f32[256,128]{1,0:T(8,128)S(1)}, u32[]{:S(2)}, u32[]{:S(2)}) collective-permute-start(f32[256,128]{1,0:T(8,128)S(1)} %get-tuple-element.92), channel_id=1, source_target_pairs={{0,1},{1,2},{2,3},{3,4},{4,5},{5,6},{6,7},{7,0},{8,9},{9,10},{10,1... | collective-permute-start | bytes 393224 | tf_op jit(solution)/shard_map/ppermute | solution.py:25
  90.2 7.2 %collective-permute-start.30 = (f32[256,128]{1,0:T(8,128)S(1)}, f32[256,128]{1,0:T(8,128)S(1)}, u32[]{:S(2)}, u32[]{:S(2)}) collective-permute-start(f32[256,128]{1,0:T(8,128)S(1)} %get-tuple-element.93), channel_id=1, source_target_pairs={{0,7},{1,0},{2,1},{3,2},{4,3},{5,4},{6,5},{7,6},{8,15},{9,8},{10,9... | collective-permute-start | bytes 393224 | tf_op jit(solution)/shard_map/ppermute | solution.py:25
  102.3 4.9 %collective-permute-start.32 = (f32[48,128]{1,0:T(8,128)S(1)}, f32[48,128]{1,0:T(8,128)S(1)}, u32[]{:S(2)}, u32[]{:S(2)}) collective-permute-start(f32[48,128]{1,0:T(8,128)S(1)} %get-tuple-element.97.refs_0_), channel_id=1, source_target_pairs={{0,16},{8,24},{16,0},{24,8},{1,17},{9,25},{17,1},{25,9},{2,18},{10... | collective-permute-start | bytes 73736 | tf_op jit(solution)/shard_map/ppermute | solution.py:25
  105.5 4.7 %collective-permute-start.31 = (f32[48,128]{1,0:T(8,128)S(1)}, f32[48,128]{1,0:T(8,128)S(1)}, u32[]{:S(2)}, u32[]{:S(2)}) collective-permute-start(f32[48,128]{1,0:T(8,128)S(1)} %get-tuple-element.97.refs_0_), channel_id=1, source_target_pairs={{0,8},{8,16},{16,24},{24,0},{1,9},{9,17},{17,25},{25,1},{2,10},{10... | collective-permute-start | bytes 73736 | tf_op jit(solution)/shard_map/ppermute | solution.py:25
  110.2 10.5 %collective-permute-start.38 = (f32[2,256,128]{2,1,0:T(8,128)S(1)}, f32[2,256,128]{2,1,0:T(8,128)S(1)}, u32[]{:S(2)}, u32[]{:S(2)}) collective-permute-start(f32[2,256,128]{2,1,0:T(8,128)S(1)} %get-tuple-element.104.refs_9_), channel_id=1, source_target_pairs={{8,0},{16,8},{24,16},{9,1},{17,9},{25,17},{10,2},{18,10},{26,18},{... | collective-permute-start | bytes 786440 | tf_op jit(solution)/shard_map/ppermute | solution.py:25
  111.6 4.9 %collective-permute-start.35 = (f32[48,128]{1,0:T(8,128)S(1)}, f32[48,128]{1,0:T(8,128)S(1)}, u32[]{:S(2)}, u32[]{:S(2)}) collective-permute-start(f32[48,128]{1,0:T(8,128)S(1)} %get-tuple-element.99.refs_0_), channel_id=1, source_target_pairs={{0,4},{1,5},{2,6},{3,7},{4,0},{5,1},{6,2},{7,3},{8,12},{9,13},{10,... | collective-permute-start | bytes 73736 | tf_op jit(solution)/shard_map/ppermute | solution.py:25
  112.5 5.6 %collective-permute-start.34 = (f32[48,128]{1,0:T(8,128)S(1)}, f32[48,128]{1,0:T(8,128)S(1)}, u32[]{:S(2)}, u32[]{:S(2)}) collective-permute-start(f32[48,128]{1,0:T(8,128)S(1)} %get-tuple-element.99.refs_0_), channel_id=1, source_target_pairs={{0,2},{1,3},{2,4},{3,5},{4,6},{5,7},{6,0},{7,1},{8,10},{9,11},{10,... | collective-permute-start | bytes 73736 | tf_op jit(solution)/shard_map/ppermute | solution.py:25
  (20 other events, 112.3 us)

commit v4 on v3

--- a/solution.py
+++ b/solution.py
@@ -66,18 +66,6 @@
     return buffer[pl.ds(start, size)]
 
 
-def corner_kernel(cuts, height, at, corner_map, corner_rows, slots):
-    count, _, dofs = corner_rows.shape
-    lane = lax.broadcasted_iota(jnp.int32, (1, dofs), 1)
-    slots[...] = jnp.zeros_like(slots)
-    for s in range(count):
-        for a in range(cuts):
-            keep = (at[0] == a).astype(F32)
-            slots[s * height + 3 * a:s * height + 3 * a + 3] = corner_rows[s, 6:9] * keep
-        number = (corner_map[s, 2] + 1).astype(F32)
-        slots[s * height + 3 * cuts:s * height + 3 * cuts + 1] = jnp.where(lane == at[0], number, 0.0)
-
-
 def put_coupling(ref, size, face, amount):
     for i in range(size // 128):
         rows = size + 16 * i
@@ -89,8 +77,20 @@
     return jnp.concatenate([ref[size + 16 * i:size + 16 * i + 12] for i in range(size // 128)], axis=1)
 
 
-def prepare_kernel(at, offsets, gap, coupling, rows_table, residual, to_far, to_right, inner, c_rows, buffer):
+def prepare_kernel(cuts, at, *refs):
+    sources, outs, buffer = refs[0:6], refs[6:13], refs[13]
+    held, sems = refs[14:20], refs[20]
+    residual, to_far, to_right, inner, c_rows, c_keep, corner = outs
+    offsets, corner_map, gap, coupling, corner_rows, rows_table = held
+    copies = [pltpu.make_async_copy(source, to, sems.at[i]) for i, (source, to) in enumerate(zip(sources, held))]
+    for copy in copies:
+        copy.start()
+    for copy in copies:
+        copy.wait()
     count, _, size, _ = gap.shape
+    for s in range(count):
+        for f in range(4):
+            c_keep[s, :, f * size:(f + 1) * size] = coupling[:, s, f * size:(f + 1) * size]
     for s in range(count):
         for face in range(2):
             shift = offsets[s, face]
@@ -100,14 +100,28 @@
             amount = (shift + 1).astype(F32)
             if face == 0:
                 to_far[s, 0:size] = turned
-                put_coupling(to_far.at[s], size, coupling[s, :, FAR * size:(FAR + 1) * size], amount)
+                put_coupling(to_far.at[s], size, c_keep[s, :, FAR * size:(FAR + 1) * size], amount)
             elif s == count - 1:
                 to_right[0:size] = turned
-                put_coupling(to_right, size, coupling[s, :, RIGHT * size:(RIGHT + 1) * size], amount)
+                put_coupling(to_right, size, c_keep[s, :, RIGHT * size:(RIGHT + 1) * size], amount)
             else:
                 inner[s] = turned
-        c_rows[s] = dot(rows_table[at[0]], paired(coupling[s])).astype(BF16)
+        c_rows[s] = dot(rows_table[at[0]], paired(c_keep[s])).astype(BF16)
     inner[count - 1] = jnp.zeros(inner.shape[1:], F32)
+    corner[...] = jnp.zeros_like(corner)
+    dofs, rows = corner_rows.shape[2], 3 * cuts
+    lanes = -(-dofs // 128)
+    lane = lax.broadcasted_iota(jnp.int32, (1, 128), 1)
+    number = jnp.zeros((1, 128), F32)
+    for s in range(count):
+        number = number + jnp.where(lane == at[0] * count + s, (corner_map[s, 2] + 1).astype(F32), 0.0)
+        for i in range(lanes):
+            wide = min(128, dofs - 128 * i)
+            for a in range(cuts):
+                keep = (at[0] == a).astype(F32)
+                first = (s * lanes + i) * rows + 3 * a
+                corner[first:first + 3, 0:wide] = corner_rows[6:9, s, 128 * i:128 * i + wide] * keep
+    corner[corner.shape[0] - 8:corner.shape[0] - 7] = number
 
 
 def paired(face):
@@ -132,12 +146,6 @@
         ct_own[s, 5 * size:6 * size] = turned(got_coupling(from_near.at[s], size), at[0] - 1)
     ct_left[...] = turned(got_coupling(from_left, size), at[0])
     ct_right[...] = turned(got_coupling(from_right, size), at[0])
-
-
-def split_kernel(block, high, low):
-    for s in range(block.shape[0]):
-        for i in range(0, block.shape[1], 256):
-            high[s, i:i + 256], low[s, i:i + 256] = halves(block[s, i:i + 256])
 
 
 def sum_kernel(parts, *refs):
@@ -163,7 +171,7 @@
     specs = [VMEM] * len(parts) + [ANY] * len(through)
     return pl.pallas_call(
         functools.partial(kernel, len(parts)),
-        out_shape=(shape, *[jax.ShapeDtypeStruct(x.shape, x.dtype) for x in through]),
+        out_shape=(jax.ShapeDtypeStruct(shape.shape, shape.dtype), *[jax.ShapeDtypeStruct(x.shape, x.dtype) for x in through]),
         in_specs=specs,
         out_specs=(VMEM, *[ANY] * len(through)),
         compiler_params=room(*parts, shape),
@@ -172,9 +180,9 @@
     )(*parts, *through)
 
 
-def apply_flexibility(loads, a_high, a_low, coupling, height, outs, scratch, rr_rows):
+def apply_flexibility(loads, flexibility, coupling, height, outs, scratch, rr_rows):
     near, far, sides, to_left, to_right, terms = outs
-    split = scratch["split"]
+    split, a_high, a_low = scratch["split"]
     count, size = len(loads), loads[0][0].shape[0]
     for s in range(count):
         for face in range(4):
@@ -189,6 +197,8 @@
         mine = both[0:width, 0:128] + both[0:width, 128:256] + both[width:, 0:128]
         terms[s * height:s * height + width] += mine
     for s in range(count):
+        for i in range(0, a_high.shape[1], size):
+            a_high[s, i:i + size], a_low[s, i:i + size] = halves(flexibility[s, i:i + size])
         whole = dot(a_high[s], split[s])
         whole = whole[:, 0:128] + whole[:, 128:256] + dot(a_low[s], split[s, :, 0:128])
         for face in range(4):
@@ -222,17 +232,21 @@
     odd = side[0] == 1
     stacked, table = scratch["stack"], scratch["values"]
     span = count * height
-    chips = mine.shape[0] // (span + height)
-    terms = []
-    for k in range(chips):
-        first, second = (x[k * (span + height):(k + 1) * (span + height)] for x in (mine, theirs))
-        terms += [jnp.where(odd, second, first), jnp.where(odd, first, second)]
+    chips = scratch["chips"]
+    stride = mine.shape[0] // chips
+    terms = [x[k * stride:k * stride + span + height] for x in (mine, theirs) for k in range(chips)]
     norm = functools.reduce(jnp.add, [t[rr_rows:rr_rows + 1] for t in terms])
     energy = functools.reduce(jnp.add, [t[rr_rows + 1:rr_rows + 2] for t in terms])
     for k in range(2 * chips):
-        behind = k - 1 if k % 2 else (k + 3) % (2 * chips)
+        chip, swap = k % chips, k // chips
+        near_by = terms[chip + (1 - swap) * chips][span:span + height]
+        farther = terms[(chip + 1) % chips + (1 - swap) * chips][span:span + height]
         stacked[k * span:(k + 1) * span] = terms[k][0:span]
-        stacked[k * span:k * span + height] = terms[k][0:height] + terms[behind][span:span + height]
+        if swap == 0:
+            extra = jnp.where(odd, near_by, farther)
+        else:
+            extra = jnp.where(odd, farther, near_by)
+        stacked[k * span:k * span + height] = terms[k][0:height] + extra
     coarse = stacked[...]
     high, low = halves(coarse)
     both = dot(k_high[...], jnp.concatenate([high, low], axis=1))
@@ -243,7 +257,7 @@
 
     def column(q):
         along = side[0] + q // count
-        block = (2 * (-(along // 2)) + along % 2) % (2 * chips)
+        block = (-(along // 2)) % chips + jnp.where(along % 2 == side[0], 0, chips)
         at = block * span + (q % count) * height
         return table[pl.ds(pl.multiple_of(at, 8), height)]
 
@@ -280,9 +294,9 @@
     return result, norm, energy
 
 
-def first_kernel(height, rr_rows, residual, from_near, from_left, inner, coupling, a_high, a_low, c_rows, *rest):
-    outs, loads_out, split = rest[0:6], rest[6], rest[7]
-    near, to_left = outs[0], outs[3]
+def first_kernel(height, rr_rows, residual, from_near, from_left, inner, coupling, corner, flexibility, c_rows, *rest):
+    outs, loads_out, split = rest[0:6], rest[6], rest[7:10]
+    near, to_left, terms = outs[0], outs[3], outs[5]
     count, size = residual.shape[0], residual.shape[2]
     loads = []
     for s in range(count):
@@ -292,10 +306,13 @@
             loads_out[s, face] = loads[s][face]
         put_coupling(near.at[s], size, coupling[s, :, NEAR * size:(NEAR + 1) * size], 0.0)
     put_coupling(to_left, size, coupling[0, :, LEFT * size:(LEFT + 1) * size], 0.0)
-    apply_flexibility(loads, a_high, a_low, c_rows, height, outs, dict(split=split), rr_rows)
-
-
-def step_kernel(which, height, rr_rows, *refs):
+    apply_flexibility(loads, flexibility, c_rows, height, outs, dict(split=split), rr_rows)
+    rows = corner.shape[0] - 8
+    terms[(count + 1) * height:] = corner[0:rows]
+    terms[rr_rows + 2:rr_rows + 3] = corner[rows:rows + 1]
+
+
+def step_kernel(which, chips, height, rr_rows, *refs):
     refs = list(refs)
     take = lambda number: [refs.pop(0) for _ in range(number)]
     last = which == ITERS - 1
@@ -305,19 +322,19 @@
     (loads,) = take(1)
     map_before, ways, found, scalars = (take(4) if which > 0 else [None] * 4)
     if not last:
-        a_high, a_low, coupling = take(3)
+        flexibility, coupling = take(2)
         outs = take(6)
         loads_out, map_out = take(2)
         ways_out, found_out = take(2) if which > 0 else (None, None)
         (scalars_out,) = take(1)
-        stack, values, turn, split = take(4)
+        stack, values, turn, *split = take(6)
         faces = (NEAR, FAR, LEFT, RIGHT)
     else:
         found_out, residual_out = take(2)
         stack, values, turn = take(3)
         faces = (FAR, RIGHT)
     count, size = loads.shape[0], loads.shape[2]
-    scratch = dict(stack=stack, values=values, turn=turn)
+    scratch = dict(stack=stack, values=values, turn=turn, chips=chips)
     if not last:
         scratch["split"] = split
     mapped, norm, energy = finish_operator(
@@ -356,7 +373,7 @@
                     ways_out[s, i] = way
     if not last:
         scalars_out[...] = jnp.concatenate([norm, step, jnp.zeros((6, 128), F32)], axis=0)
-        apply_flexibility(fresh, a_high, a_low, coupling, height, outs, scratch, rr_rows)
+        apply_flexibility(fresh, flexibility, coupling, height, outs, scratch, rr_rows)
 
 
 def corner_tables(cuts, height):
@@ -375,21 +392,22 @@
     return jnp.asarray(table, BF16), jnp.asarray(rows, BF16)
 
 
-def corner_matrix(slots, numbers_at, cuts, height, odd):
-    dofs = slots.shape[1]
-    parts = chip_parts(summed(slots, "cuts"), "blk")
-    mine = jnp.concatenate(parts, axis=0)
-    theirs = swapped(mine, "blk")
-    mine, theirs = (x.reshape(-1, slots.shape[0], dofs) for x in (mine, theirs))
-    rows = jnp.stack([jnp.where(odd, theirs, mine), jnp.where(odd, mine, theirs)], axis=1)
-    rows = rows.reshape(-1, height, dofs)
-    numbers = rows[:, numbers_at, :cuts].astype(jnp.int32) - 1
-    chosen = 3 * numbers[..., None] + jnp.arange(3, dtype=jnp.int32)
-    chosen = jnp.pad(chosen.reshape(-1, 3 * cuts), ((0, 0), (0, height - 3 * cuts)), constant_values=-1).reshape(-1)
-    pick = (jnp.arange(dofs, dtype=jnp.int32)[:, None] == chosen[None, :]).astype(BF16)
-    used = (jnp.arange(height) < numbers_at)[:, None]
-    high, low = kept_halves(jnp.where(used, rows, 0.0).reshape(-1, dofs))
-    return [jnp.dot(part, pick, preferred_element_type=F32).astype(BF16) for part in (high, low)]
+def corner_matrix(sources, count, dofs, cuts, height):
+    rows, lanes = 3 * cuts, -(-dofs // 128)
+    first = (count + 1) * height
+    numbers = jnp.concatenate([x[:, rows + 2, :cuts * count] for x in sources], axis=0).astype(jnp.int32) - 1
+    numbers = jnp.swapaxes(numbers.reshape(-1, cuts, count), 1, 2)
+    chosen = (3 * numbers[..., None] + jnp.arange(3, dtype=jnp.int32)).reshape(-1, rows)
+    chosen = jnp.pad(chosen, ((0, 0), (0, height - rows)), constant_values=-1).reshape(-1)
+    pick = (jnp.arange(128 * lanes, dtype=jnp.int32)[:, None] == chosen[None, :]).astype(BF16)
+    pick = pick.reshape(lanes, 128, -1)
+    found = [[], []]
+    for x in sources:
+        matrix = x[:, first:first + count * lanes * rows].reshape(-1, lanes, rows, 128)
+        for half, into in zip(kept_halves(matrix), found):
+            product = jnp.einsum("nlrd,ldc->nrc", half, pick, preferred_element_type=F32).astype(BF16)
+            into.append(jnp.pad(product, ((0, 0), (0, height - rows), (0, 0))).reshape(-1, product.shape[-1]))
+    return [jnp.concatenate(into, axis=0) for into in found]
 
 
 def per_device(gap_load, offsets, corner_map, flexibility, coupling, corner_rows):
@@ -399,7 +417,7 @@
     at = lax.axis_index("cuts").reshape(1)
     side = (lax.axis_index("blk") % 2).reshape(1)
     rr_rows = 3 * cuts
-    height = -(-(rr_rows + 2) // 8) * 8
+    height = -(-(rr_rows + 3) // 8) * 8
     gap, offsets, corner_map, flexibility, coupling, corner_rows = (
         x[0] for x in (gap_load, offsets, corner_map, flexibility, coupling, corner_rows)
     )
@@ -414,35 +432,30 @@
     long_faces = shape(count, size + below, loads_n)
     table, rows_table = corner_tables(cuts, height)
 
-    slots = pl.pallas_call(
-        functools.partial(corner_kernel, cuts, height),
-        out_shape=shape(count * height, dofs),
-        in_specs=[SMEM, SMEM, VMEM],
-        out_specs=VMEM,
-        compiler_params=room(corner_rows, shape(count * height, dofs)),
-        name="corner",
-    )(at, corner_map, corner_rows)
-    residual, to_far, to_right, inner, c_rows = pl.pallas_call(
-        prepare_kernel,
-        out_shape=(pair, long_faces, long_face, faces, shape(count, 4 * height, total, kind=BF16)),
-        in_specs=[SMEM, SMEM] + [VMEM] * 3,
-        out_specs=(VMEM,) * 5,
-        scratch_shapes=[pltpu.VMEM((count, 2, 2 * size, loads_n), F32)],
-        compiler_params=room(gap, coupling, rows_table, pair, pair, pair, long_faces, long_faces, faces, coupling),
+    corner_size = -(-(count * -(-dofs // 128) * rr_rows) // 8) * 8
+    corner_shape = shape(corner_size + 8, loads_n)
+    wide = shape(count, rr_rows, total)
+    held = [
+        pltpu.SMEM(offsets.shape, jnp.int32),
+        pltpu.SMEM(corner_map.shape, jnp.int32),
+        pltpu.VMEM(gap.shape, F32),
+        pltpu.VMEM((12, count, total), F32),
+        pltpu.VMEM((12, count, dofs), F32),
+        pltpu.VMEM(rows_table.shape, BF16),
+    ]
+    prepared = (pair, long_faces, long_face, faces, shape(count, 4 * height, total, kind=BF16), shape(count, 12, total),
+                corner_shape)
+    residual, to_far, to_right, inner, c_rows, c_keep, corner = pl.pallas_call(
+        functools.partial(prepare_kernel, cuts),
+        out_shape=prepared,
+        in_specs=[SMEM] + [ANY] * 6,
+        out_specs=(VMEM,) * 7,
+        scratch_shapes=[pltpu.VMEM((count, 2, 2 * size, loads_n), F32), *held, pltpu.SemaphoreType.DMA((6,))],
+        compiler_params=room(*prepared, pair, pair, *held[2:]),
         name="prepare",
-    )(at, offsets, gap, coupling, rows_table)
+    )(at, offsets, corner_map, gap, jnp.swapaxes(coupling, 0, 1), jnp.swapaxes(corner_rows, 0, 1), rows_table)
     from_near = shifted(to_far, "cuts", 1, False)
     from_left = shifted(to_right, "blk", 1, True)
-    k_high, k_low = corner_matrix(slots, rr_rows, cuts, height, side[0] == 1)
-    a_high, a_low = pl.pallas_call(
-        split_kernel,
-        out_shape=(jax.ShapeDtypeStruct(flexibility.shape, BF16),) * 2,
-        in_specs=[VMEM],
-        out_specs=(VMEM, VMEM),
-        compiler_params=room(flexibility, flexibility),
-        cost_estimate=pl.CostEstimate(flops=0, bytes_accessed=8 * flexibility.size, transcendentals=0),
-        name="split",
-    )(flexibility)
     near_offsets = from_near[:, size + 12, 0]
     left_offsets = jnp.concatenate([from_left[size + 12:size + 13, 0], (offsets[:-1, 1] + 1).astype(F32)])
     all_offsets = jnp.stack([
@@ -453,14 +466,15 @@
     cost = pl.CostEstimate(flops=flops, bytes_accessed=4 * flexibility.size, transcendentals=0)
     terms_shape = shape((count + 1) * height, loads_n)
     sends = (faces, faces, pair, face, face, terms_shape)
-    first_sends = (long_faces, faces, pair, long_face, face, terms_shape)
-    a_buffers = [pltpu.VMEM((count, total, 2 * loads_n), BF16)]
+    first_terms = shape((count + 1) * height + corner_size, loads_n)
+    first_sends = (long_faces, faces, pair, long_face, face, first_terms)
+    a_buffers = [pltpu.VMEM((count, total, 2 * loads_n), BF16)] + [pltpu.VMEM(flexibility.shape, BF16)] * 2
     f_buffers = [
         pltpu.VMEM((blocks * count * height, loads_n), F32),
         pltpu.VMEM((blocks * count * height, loads_n), F32),
         pltpu.VMEM((count, 4, 2 * size, loads_n), F32),
     ]
-    first_args = (residual, from_near, from_left, inner, coupling, a_high, a_low, c_rows)
+    first_args = (residual, from_near, from_left, inner, c_keep, corner, flexibility, c_rows)
     *out, loads = pl.pallas_call(
         functools.partial(first_kernel, height, rr_rows),
         out_shape=first_sends + (four,),
@@ -477,20 +491,24 @@
         last = which == ITERS - 1
         near, far, sides, to_left, to_right, terms = out
         pieces = [terms] + [shifted(terms, "cuts", k, True) for k in range(1, cuts)]
-        terms, near = relay(sum_kernel, pieces, terms_shape, [near], f"sum{which}")
+        r_right = shifted(to_left, "blk", -1, True)
+        through = [near, r_right]
+        if not last:
+            through.append(shifted(to_right, "blk", 1, True))
+        terms, near, r_right, *r_left = relay(sum_kernel, pieces, terms, through, f"sum{which}")
+        r_left = to_right if last else r_left[0]
         r_far = shifted(near, "cuts", -1, False)
         pieces = chip_parts(terms, "blk")
-        mine, far, to_left, to_right = relay(
-            stack_kernel, pieces, shape(blocks // 2 * terms_shape.shape[0], loads_n), [far, to_left, to_right],
-            f"stack{which}",
+        mine, far = relay(
+            stack_kernel, pieces, shape(blocks // 2 * terms.shape[0], loads_n), [far], f"stack{which}"
         )
+        r_near = far if last else shifted(far, "cuts", 1, False)
         theirs = swapped(mine, "blk")
-        r_right = shifted(to_left, "blk", -1, True)
-        if last:
-            r_near, r_left = far, to_right
-        else:
-            r_near = shifted(far, "cuts", 1, False)
-            r_left = shifted(to_right, "blk", 1, True)
+        if which == 0:
+            stride = terms.shape[0]
+            k_high, k_low = corner_matrix(
+                [x.reshape(-1, stride, loads_n) for x in (mine, theirs)], count, dofs, cuts, height
+            )
         if which == 0:
             ct_own, ct_left, ct_right = pl.pallas_call(
                 spread_kernel,
@@ -501,21 +519,21 @@
                 ),
                 in_specs=[SMEM] + [VMEM] * 6,
                 out_specs=(VMEM,) * 3,
-                compiler_params=room(coupling, from_near, r_far, from_left, r_right, table, *[faces] * 6),
+                compiler_params=room(c_keep, from_near, r_far, from_left, r_right, table, *[faces] * 6),
                 name="spread",
-            )(at, coupling, from_near, r_far, from_left, r_right, table)
+            )(at, c_keep, from_near, r_far, from_left, r_right, table)
         args = [all_offsets, side, mine, theirs, k_high, k_low, ct_own, ct_left, ct_right, near, far, sides,
                 r_near, r_far, r_left, r_right, loads, *state]
         specs = [SMEM, SMEM] + [VMEM] * (len(args) - 2)
         if last:
             outs, scratch = (pair, pair), f_buffers
         else:
-            args += [a_high, a_low, c_rows]
-            specs += [VMEM] * 3
+            args += [flexibility, c_rows]
+            specs += [VMEM] * 2
             outs = sends + (four, four) + ((pair, pair) if which > 0 else ()) + (shape(8, loads_n),)
             scratch = f_buffers + a_buffers
         result = pl.pallas_call(
-            functools.partial(step_kernel, which, height, rr_rows),
+            functools.partial(step_kernel, which, blocks // 2, height, rr_rows),
             out_shape=outs,
             in_specs=specs,
             out_specs=(VMEM,) * len(outs),

time: 124 us -> 133 us (1.073)
  starting transfers between devices: 51.8 us -> 46.2 us
  local copies, waits for them, and re-layouts: 19.7 us -> 25 us
  matrix products: 0.38 us -> 4.57 us
  other arithmetic: 1 us -> 2.91 us
  Pallas kernels: 17 us -> 18.6 us
    ppermute x36 -> x30, starting transfers between devices: 51.2 us -> 46 us  [shifted(): return lax.ppermute(value, axis, pairs)]
    slice x1 -> x4, local copies, waits for them, and re-layouts: 0.01 us -> 4.54 us  [the longest x2 3.09 us: corner_matrix(): x[:, first:first + count * lanes * rows].reshape(-1, lanes, rows, 128)]
    unnamed x28 -> x24, local copies, waits for them, and re-layouts: 16.8 us -> 12.6 us
    dot_general x2 -> x4, matrix products: 0.38 us -> 4.57 us  [corner_matrix(): jnp.einsum('nlrd,ldc->nrc', half, pick, preferred_element_type=F32)]
    reshape x0 -> x2, local copies, waits for them, and re-layouts: none -> 3.11 us  [corner_matrix(): x[:, first:first + count * lanes * rows].reshape(-1, lanes, rows, 128)]
    add x4, local copies, waits for them, and re-layouts: 0.11 us -> 2.15 us  [corner_matrix(): 3 * numbers[..., None] + jnp.arange(3, dtype=jnp.int32)]
    ppermute x36 -> x30, waiting for transfers between devices: 28.7 us -> 30 us  [shifted(): return lax.ppermute(value, axis, pairs)]
    pallas_call x12 -> x10, Pallas kernels: 14 us -> 14.9 us  [the longest x3 12.4 us: per_device(): pl.pallas_call(functools.partial(step_kernel, which, blocks // 2, height,...]
  transfers between devices with their start and end apart: 40 -> 33, of which waited for: 24 -> 18; matrix products, arithmetic and copies ran while one was open for 4% -> 15% of each run, Pallas kernels for 2% -> 0%
where the time goes in v4:
time: 133 us; the launch traced here: 131 us
  starting transfers between devices  46.2 us (35%)
  waiting for transfers between devices  32.6 us (25%)
  local copies, waits for them, and re-layouts  25 us (19%)
  Pallas kernels  18.6 us (14%)
  matrix products  4.57 us (3%)
  other arithmetic  2.91 us (2%)
  between operations  1.46 us (1%)
    ppermute x30, starting transfers between devices, shifted(): return lax.ppermute(value, axis, pairs)  46 us
    ppermute x30, waiting for transfers between devices, shifted(): return lax.ppermute(value, axis, pairs)  30 us
    unnamed x24, local copies, waits for them, and re-layouts  12.6 us
    pallas_call x3, Pallas kernels, per_device(): pl.pallas_call(functools.partial(step_kernel, which, blocks // 2, height,...  12.4 us
    dot_general x4, matrix products, corner_matrix(): jnp.einsum('nlrd,ldc->nrc', half, pick, preferred_element_type=F32)  4.57 us
    pallas_call x1, Pallas kernels, per_device(): pl.pallas_call(functools.partial(first_kernel, height, rr_rows), out_shap...  3.26 us
    reshape x2, local copies, waits for them, and re-layouts, corner_matrix(): x[:, first:first + count * lanes * rows].reshape(-1, lanes, rows, 128)  3.11 us
    slice x2, local copies, waits for them, and re-layouts, corner_matrix(): x[:, first:first + count * lanes * rows].reshape(-1, lanes, rows, 128)  3.09 us
  transfers between devices with their start and end apart: 33, of which 18 were waited for; matrix products, arithmetic and copies ran while one was open for 15% of the time, Pallas kernels for 0%

profile of v4, /device:TPU:0, one launch (start us, length us, event | category | flops | bytes accessed | tf_op | source)
XLA Modules:
  0.0 131.4 jit_solution(9643634096479928636)
XLA Ops:
  6.5 4.9 %collective-permute-start = (f32[2,288,128]{2,1,0:T(8,128)S(1)}, f32[2,288,128]{2,1,0:T(8,128)S(1)}, u32[]{:S(2)}, u32[]{:S(2)}) collective-permute-start(f32[2,288,128]{2,1,0:T(8,128)S(1)} %get-tuple-element.58), channel_id=1, source_target_pairs={{0,8},{8,16},{16,24},{1,9},{9,17},{17,25},{2,10},{10,18},{18,26},{... | collective-permute-start | bytes 884744 | tf_op jit(solution)/shard_map/ppermute | solution.py:25
  11.5 6.4 %collective-permute-done.1.from_left = f32[288,128]{1,0:T(8,128)S(1)} collective-permute-done((f32[288,128]{1,0:T(8,128)S(1)}, f32[288,128]{1,0:T(8,128)S(1)}, u32[]{:S(2)}, u32[]{:S(2)}) %collective-permute-start.1) | collective-permute-done | bytes 147488 | tf_op jit(solution)/shard_map/ppermute | solution.py:25
  17.8 3.4 %copy-done = f32[1,2,1024,1024]{3,2,1,0:T(8,128)S(1)} copy-done((f32[1,2,1024,1024]{3,2,1,0:T(8,128)S(1)}, f32[1,2,1024,1024]{3,2,1,0:T(8,128)}, u32[]{:S(2)}) %copy-start) | copy-done | bytes 8388632
  21.2 3.3 %first.1 = (f32[2,288,128]{2,1,0:T(8,128)S(1)}, f32[2,256,128]{2,1,0:T(8,128)S(1)}, f32[2,2,256,128]{3,2,1,0:T(8,128)S(1)}, f32[288,128]{1,0:T(8,128)}, f32[256,...) custom-call(f32[2,2,256,128]{3,2,1,0:T(8,128)S(1)} %get-tuple-element.60.residual, ...), custom_call_target="tpu_custom_call" | custom-call | flops 1610612736 | bytes 8388608 | tf_op jit(solution)/shard_map/first/pallas_call | solution.py:478
  24.5 3.5 %collective-permute-start.5 = (f32[288,128]{1,0:T(8,128)}, f32[288,128]{1,0:T(8,128)S(1)}, u32[]{:S(2)}, u32[]{:S(2)}) collective-permute-start(f32[288,128]{1,0:T(8,128)} %get-tuple-element.67), channel_id=1, source_target_pairs={{0,7},{1,0},{2,1},{3,2},{4,3},{5,4},{6,5},{7,6},{8,15},{9,8},{10,9... | collective-permute-start | bytes 442376 | tf_op jit(solution)/shard_map/ppermute | solution.py:25
  28.1 3.2 %collective-permute-start.4 = (f32[96,128]{1,0:T(8,128)}, f32[96,128]{1,0:T(8,128)S(1)}, u32[]{:S(2)}, u32[]{:S(2)}) collective-permute-start(f32[96,128]{1,0:T(8,128)} %get-tuple-element.65.refs_0_), channel_id=1, source_target_pairs={{0,24},{8,0},{16,8},{24,16},{1,25},{9,1},{17,9},{25,17},{2,26},{10... | collective-permute-start | bytes 147464 | tf_op jit(solution)/shard_map/ppermute | solution.py:25
  31.8 1.5 %collective-permute-start.2 = (f32[96,128]{1,0:T(8,128)}, f32[96,128]{1,0:T(8,128)S(1)}, u32[]{:S(2)}, u32[]{:S(2)}) collective-permute-start(f32[96,128]{1,0:T(8,128)} %get-tuple-element.65.refs_0_), channel_id=1, source_target_pairs={{0,8},{8,16},{16,24},{24,0},{1,9},{9,17},{17,25},{25,1},{2,10},{10... | collective-permute-start | bytes 147464 | tf_op jit(solution)/shard_map/ppermute | solution.py:25
  37.9 1.9 %collective-permute-start.9 = (f32[96,128]{1,0:T(8,128)S(1)}, f32[96,128]{1,0:T(8,128)S(1)}, u32[]{:S(2)}, u32[]{:S(2)}) collective-permute-start(f32[96,128]{1,0:T(8,128)S(1)} %get-tuple-element.69.refs_0_), channel_id=1, source_target_pairs={{0,6},{1,7},{2,0},{3,1},{4,2},{5,3},{6,4},{7,5},{8,14},{9,15},{10,... | collective-permute-start | bytes 147464 | tf_op jit(solution)/shard_map/ppermute | solution.py:25
  42.5 2.4 %collective-permute-done.8.refs_2_ = f32[96,128]{1,0:T(8,128)S(1)} collective-permute-done((f32[96,128]{1,0:T(8,128)S(1)}, f32[96,128]{1,0:T(8,128)S(1)}, u32[]{:S(2)}, u32[]{:S(2)}) %collective-permute-start.8) | collective-permute-done | bytes 49184 | tf_op jit(solution)/shard_map/ppermute | solution.py:25
  48.4 1.6 %slice.38 = f32[4,48,128]{2,1,0:T(8,128)} slice(f32[4,96,128]{2,1,0:T(8,128)} %bitcast.11), slice={[0:4], [48:96], [0:128]} | slice | bytes 196608 | tf_op jit(solution)/shard_map/slice | solution.py:406
  50.0 1.6 %reshape.113 = f32[8,2,12,128]{3,2,1,0:T(8,128)} reshape(f32[4,48,128]{2,1,0:T(8,128)} %slice.38) | data formatting | bytes 196608 | tf_op jit(solution)/shard_map/reshape | solution.py:406
  51.6 5.2 %collective-permute-start.12 = (f32[2,256,128]{2,1,0:T(8,128)S(1)}, f32[2,256,128]{2,1,0:T(8,128)}, u32[]{:S(2)}, u32[]{:S(2)}) collective-permute-start(f32[2,256,128]{2,1,0:T(8,128)S(1)} %get-tuple-element.77.refs_10_), channel_id=1, source_target_pairs={{0,8},{8,16},{16,24},{1,9},{9,17},{17,25},{2,10},{10,18},{18,26},{... | collective-permute-start | bytes 786440 | tf_op jit(solution)/shard_map/ppermute | solution.py:25
  62.4 1.5 %slice.41 = f32[4,48,128]{2,1,0:T(8,128)} slice(f32[4,96,128]{2,1,0:T(8,128)} %bitcast.13), slice={[0:4], [48:96], [0:128]} | slice | bytes 196608 | tf_op jit(solution)/shard_map/slice | solution.py:406
  65.2 1.6 %reshape.116 = f32[8,2,12,128]{3,2,1,0:T(8,128)} reshape(f32[4,48,128]{2,1,0:T(8,128)} %slice.41) | data formatting | bytes 196608 | tf_op jit(solution)/shard_map/reshape | solution.py:406
  71.2 3.4 %copy-done.1 = f32[1,2,1024,1024]{3,2,1,0:T(8,128)S(1)} copy-done((f32[1,2,1024,1024]{3,2,1,0:T(8,128)S(1)}, f32[1,2,1024,1024]{3,2,1,0:T(8,128)}, u32[]{:S(2)}) %copy-start.1) | copy-done | bytes 8388632
  74.6 5.4 %step0.1 = (f32[2,256,128]{2,1,0:T(8,128)S(1)}, f32[2,256,128]{2,1,0:T(8,128)S(1)}, f32[2,2,256,128]{3,2,1,0:T(8,128)S(1)}, f32[256,128]{1,0:T(8,128)S(1)}, f32[...) custom-call(s32[2,4]{1,0:T(2,128)S(1)} %pad_add_fusion.refs_0_, ...), custom_call_target="tpu_custom_call" | custom-call | flops 1610612736 | bytes 8388608 | tf_op jit(solution)/shard_map/step0/pallas_call | solution.py:535
  80.5 2.4 %collective-permute-start.14 = (f32[48,128]{1,0:T(8,128)S(1)}, f32[48,128]{1,0:T(8,128)S(1)}, u32[]{:S(2)}, u32[]{:S(2)}) collective-permute-start(f32[48,128]{1,0:T(8,128)S(1)} %get-tuple-element.81.refs_0_), channel_id=1, source_target_pairs={{0,16},{8,24},{16,0},{24,8},{1,17},{9,25},{17,1},{25,9},{2,18},{10... | collective-permute-start | bytes 73736 | tf_op jit(solution)/shard_map/ppermute | solution.py:25
  84.8 2.9 %collective-permute-done.13.refs_1_ = f32[48,128]{1,0:T(8,128)S(1)} collective-permute-done((f32[48,128]{1,0:T(8,128)S(1)}, f32[48,128]{1,0:T(8,128)S(1)}, u32[]{:S(2)}, u32[]{:S(2)}) %collective-permute-start.13) | collective-permute-done | bytes 24608 | tf_op jit(solution)/shard_map/ppermute | solution.py:25
  87.7 1.7 %collective-permute-start.20 = (f32[48,128]{1,0:T(8,128)S(1)}, f32[48,128]{1,0:T(8,128)S(1)}, u32[]{:S(2)}, u32[]{:S(2)}) collective-permute-start(f32[48,128]{1,0:T(8,128)S(1)} %get-tuple-element.85.refs_0_), channel_id=1, source_target_pairs={{0,6},{1,7},{2,0},{3,1},{4,2},{5,3},{6,4},{7,5},{8,14},{9,15},{10,... | collective-permute-start | bytes 73736 | tf_op jit(solution)/shard_map/ppermute | solution.py:25
  92.2 2.3 %collective-permute-done.19.refs_2_ = f32[48,128]{1,0:T(8,128)S(1)} collective-permute-done((f32[48,128]{1,0:T(8,128)S(1)}, f32[48,128]{1,0:T(8,128)S(1)}, u32[]{:S(2)}, u32[]{:S(2)}) %collective-permute-start.19) | collective-permute-done | bytes 24608 | tf_op jit(solution)/shard_map/ppermute | solution.py:25
  94.4 1.4 %collective-permute-done.18.refs_1_ = f32[48,128]{1,0:T(8,128)S(1)} collective-permute-done((f32[48,128]{1,0:T(8,128)S(1)}, f32[48,128]{1,0:T(8,128)S(1)}, u32[]{:S(2)}, u32[]{:S(2)}) %collective-permute-start.18) | collective-permute-done | bytes 24608 | tf_op jit(solution)/shard_map/ppermute | solution.py:25
  95.9 1.7 %collective-permute-start.22 = (f32[2,256,128]{2,1,0:T(8,128)S(1)}, f32[2,256,128]{2,1,0:T(8,128)S(1)}, u32[]{:S(2)}, u32[]{:S(2)}) collective-permute-start(f32[2,256,128]{2,1,0:T(8,128)S(1)} %get-tuple-element.89.refs_10_), channel_id=1, source_target_pairs={{0,8},{8,16},{16,24},{1,9},{9,17},{17,25},{2,10},{10,18},{18,26},{... | collective-permute-start | bytes 786440 | tf_op jit(solution)/shard_map/ppermute | solution.py:25
  98.9 2.7 %collective-permute-done.23.refs_13_ = f32[2,256,128]{2,1,0:T(8,128)S(1)} collective-permute-done((f32[2,256,128]{2,1,0:T(8,128)S(1)}, f32[2,256,128]{2,1,0:T(8,128)S(1)}, u32[]{:S(2)}, u32[]{:S(2)}) %collective-permute-start.23) | collective-permute-done | bytes 262176 | tf_op jit(solution)/shard_map/ppermute | solution.py:25
  101.6 4.8 %step1.1 = (f32[2,256,128]{2,1,0:T(8,128)S(1)}, f32[2,256,128]{2,1,0:T(8,128)S(1)}, f32[2,2,256,128]{3,2,1,0:T(8,128)S(1)}, f32[256,128]{1,0:T(8,128)S(1)}, f32[...) custom-call(s32[2,4]{1,0:T(2,128)S(1)} %pad_add_fusion.refs_0_, ...), custom_call_target="tpu_custom_call" | custom-call | flops 1610612736 | bytes 8388608 | tf_op jit(solution)/shard_map/step1/pallas_call | solution.py:535
  106.6 5.1 %collective-permute-start.26 = (f32[48,128]{1,0:T(8,128)S(1)}, f32[48,128]{1,0:T(8,128)S(1)}, u32[]{:S(2)}, u32[]{:S(2)}) collective-permute-start(f32[48,128]{1,0:T(8,128)S(1)} %get-tuple-element.96.refs_0_), channel_id=1, source_target_pairs={{0,24},{8,0},{16,8},{24,16},{1,25},{9,1},{17,9},{25,17},{2,26},{10... | collective-permute-start | bytes 73736 | tf_op jit(solution)/shard_map/ppermute | solution.py:25
  112.7 2.0 %collective-permute-start.24 = (f32[48,128]{1,0:T(8,128)S(1)}, f32[48,128]{1,0:T(8,128)S(1)}, u32[]{:S(2)}, u32[]{:S(2)}) collective-permute-start(f32[48,128]{1,0:T(8,128)S(1)} %get-tuple-element.96.refs_0_), channel_id=1, source_target_pairs={{0,8},{8,16},{16,24},{24,0},{1,9},{9,17},{17,25},{25,1},{2,10},{10... | collective-permute-start | bytes 73736 | tf_op jit(solution)/shard_map/ppermute | solution.py:25
  115.6 1.9 %collective-permute-done.24.refs_1_ = f32[48,128]{1,0:T(8,128)S(1)} collective-permute-done((f32[48,128]{1,0:T(8,128)S(1)}, f32[48,128]{1,0:T(8,128)S(1)}, u32[]{:S(2)}, u32[]{:S(2)}) %collective-permute-start.24) | collective-permute-done | bytes 24608 | tf_op jit(solution)/shard_map/ppermute | solution.py:25
  117.5 1.3 collective-permute-start.32
  118.8 2.5 %collective-permute-start.30 = (f32[48,128]{1,0:T(8,128)S(1)}, f32[48,128]{1,0:T(8,128)S(1)}, u32[]{:S(2)}, u32[]{:S(2)}) collective-permute-start(f32[48,128]{1,0:T(8,128)S(1)} %get-tuple-element.99.refs_0_), channel_id=1, source_target_pairs={{0,6},{1,7},{2,0},{3,1},{4,2},{5,3},{6,4},{7,5},{8,14},{9,15},{10,... | collective-permute-start | bytes 73736 | tf_op jit(solution)/shard_map/ppermute | solution.py:25
  122.8 3.2 %collective-permute-done.29.refs_2_ = f32[48,128]{1,0:T(8,128)S(1)} collective-permute-done((f32[48,128]{1,0:T(8,128)S(1)}, f32[48,128]{1,0:T(8,128)S(1)}, u32[]{:S(2)}, u32[]{:S(2)}) %collective-permute-start.29) | collective-permute-done | bytes 24608 | tf_op jit(solution)/shard_map/ppermute | solution.py:25
  126.0 1.7 %collective-permute-done.28.refs_1_ = f32[48,128]{1,0:T(8,128)S(1)} collective-permute-done((f32[48,128]{1,0:T(8,128)S(1)}, f32[48,128]{1,0:T(8,128)S(1)}, u32[]{:S(2)}, u32[]{:S(2)}) %collective-permute-start.28) | collective-permute-done | bytes 24608 | tf_op jit(solution)/shard_map/ppermute | solution.py:25
  129.1 2.2 %step2.1 = (f32[2,2,256,128]{3,2,1,0:T(8,128)}, f32[2,2,256,128]{3,2,1,0:T(8,128)}) custom-call(s32[2,4]{1,0:T(2,128)S(1)} %pad_add_fusion.refs_0_, s32[1]{0:T(128)} %bitcast.9.refs_1_, f32[192,128]{1,0:T(8,128)S(1)} %get-tuple-element.101.refs_2_, f32[192,128]{1,0:T(8,128)S(1)} %collective-permute-done.31.refs_3_, ...), custom_call_target="tpu_custom_call" | custom-call | tf_op jit(solution)/shard_map/step2/pallas_call | solution.py:535
  (101 shorter events, 39.5 us)
Async XLA Ops:
  6.5 11.3 %collective-permute-start = (f32[2,288,128]{2,1,0:T(8,128)S(1)}, f32[2,288,128]{2,1,0:T(8,128)S(1)}, u32[]{:S(2)}, u32[]{:S(2)}) collective-permute-start(f32[2,288,128]{2,1,0:T(8,128)S(1)} %get-tuple-element.58), channel_id=1, source_target_pairs={{0,8},{8,16},{16,24},{1,9},{9,17},{17,25},{2,10},{10,18},{18,26},{... | collective-permute-start | bytes 884744 | tf_op jit(solution)/shard_map/ppermute | solution.py:25
  11.4 6.4 %collective-permute-start.1 = (f32[288,128]{1,0:T(8,128)S(1)}, f32[288,128]{1,0:T(8,128)S(1)}, u32[]{:S(2)}, u32[]{:S(2)}) collective-permute-start(f32[288,128]{1,0:T(8,128)S(1)} %get-tuple-element.59), channel_id=1, source_target_pairs={{0,1},{1,2},{2,3},{3,4},{4,5},{5,6},{6,7},{7,0},{8,9},{9,10},{10,1... | collective-permute-start | bytes 442376 | tf_op jit(solution)/shard_map/ppermute | solution.py:25
  24.5 12.6 %collective-permute-start.6 = (f32[256,128]{1,0:T(8,128)}, f32[256,128]{1,0:T(8,128)S(1)}, u32[]{:S(2)}, u32[]{:S(2)}) collective-permute-start(f32[256,128]{1,0:T(8,128)} %get-tuple-element.68), channel_id=1, source_target_pairs={{0,1},{1,2},{2,3},{3,4},{4,5},{5,6},{6,7},{7,0},{8,9},{9,10},{10,1... | collective-permute-start | bytes 393224 | tf_op jit(solution)/shard_map/ppermute | solution.py:25
  24.5 12.6 %collective-permute-start.5 = (f32[288,128]{1,0:T(8,128)}, f32[288,128]{1,0:T(8,128)S(1)}, u32[]{:S(2)}, u32[]{:S(2)}) collective-permute-start(f32[288,128]{1,0:T(8,128)} %get-tuple-element.67), channel_id=1, source_target_pairs={{0,7},{1,0},{2,1},{3,2},{4,3},{5,4},{6,5},{7,6},{8,15},{9,8},{10,9... | collective-permute-start | bytes 442376 | tf_op jit(solution)/shard_map/ppermute | solution.py:25
  28.1 8.2 %collective-permute-start.4 = (f32[96,128]{1,0:T(8,128)}, f32[96,128]{1,0:T(8,128)S(1)}, u32[]{:S(2)}, u32[]{:S(2)}) collective-permute-start(f32[96,128]{1,0:T(8,128)} %get-tuple-element.65.refs_0_), channel_id=1, source_target_pairs={{0,24},{8,0},{16,8},{24,16},{1,25},{9,1},{17,9},{25,17},{2,26},{10... | collective-permute-start | bytes 147464 | tf_op jit(solution)/shard_map/ppermute | solution.py:25
  31.3 4.9 %collective-permute-start.3 = (f32[96,128]{1,0:T(8,128)}, f32[96,128]{1,0:T(8,128)S(1)}, u32[]{:S(2)}, u32[]{:S(2)}) collective-permute-start(f32[96,128]{1,0:T(8,128)} %get-tuple-element.65.refs_0_), channel_id=1, source_target_pairs={{0,16},{8,24},{16,0},{24,8},{1,17},{9,25},{17,1},{25,9},{2,18},{10... | collective-permute-start | bytes 147464 | tf_op jit(solution)/shard_map/ppermute | solution.py:25
  31.8 5.2 %collective-permute-start.2 = (f32[96,128]{1,0:T(8,128)}, f32[96,128]{1,0:T(8,128)S(1)}, u32[]{:S(2)}, u32[]{:S(2)}) collective-permute-start(f32[96,128]{1,0:T(8,128)} %get-tuple-element.65.refs_0_), channel_id=1, source_target_pairs={{0,8},{8,16},{16,24},{24,0},{1,9},{9,17},{17,25},{25,1},{2,10},{10... | collective-permute-start | bytes 147464 | tf_op jit(solution)/shard_map/ppermute | solution.py:25
  37.9 4.6 %collective-permute-start.9 = (f32[96,128]{1,0:T(8,128)S(1)}, f32[96,128]{1,0:T(8,128)S(1)}, u32[]{:S(2)}, u32[]{:S(2)}) collective-permute-start(f32[96,128]{1,0:T(8,128)S(1)} %get-tuple-element.69.refs_0_), channel_id=1, source_target_pairs={{0,6},{1,7},{2,0},{3,1},{4,2},{5,3},{6,4},{7,5},{8,14},{9,15},{10,... | collective-permute-start | bytes 147464 | tf_op jit(solution)/shard_map/ppermute | solution.py:25
  39.7 5.2 %collective-permute-start.8 = (f32[96,128]{1,0:T(8,128)S(1)}, f32[96,128]{1,0:T(8,128)S(1)}, u32[]{:S(2)}, u32[]{:S(2)}) collective-permute-start(f32[96,128]{1,0:T(8,128)S(1)} %get-tuple-element.69.refs_0_), channel_id=1, source_target_pairs={{0,4},{1,5},{2,6},{3,7},{4,0},{5,1},{6,2},{7,3},{8,12},{9,13},{10,... | collective-permute-start | bytes 147464 | tf_op jit(solution)/shard_map/ppermute | solution.py:25
  39.7 5.9 %collective-permute-start.7 = (f32[96,128]{1,0:T(8,128)S(1)}, f32[96,128]{1,0:T(8,128)S(1)}, u32[]{:S(2)}, u32[]{:S(2)}) collective-permute-start(f32[96,128]{1,0:T(8,128)S(1)} %get-tuple-element.69.refs_0_), channel_id=1, source_target_pairs={{0,2},{1,3},{2,4},{3,5},{4,6},{5,7},{6,0},{7,1},{8,10},{9,11},{10,... | collective-permute-start | bytes 147464 | tf_op jit(solution)/shard_map/ppermute | solution.py:25
  46.3 10.5 %collective-permute-start.10 = (f32[384,128]{1,0:T(8,128)}, f32[384,128]{1,0:T(8,128)}, u32[]{:S(2)}, u32[]{:S(2)}) collective-permute-start(f32[384,128]{1,0:T(8,128)} %get-tuple-element.71.refs_2_), channel_id=1, source_target_pairs={{0,1},{1,0},{2,3},{3,2},{4,5},{5,4},{6,7},{7,6},{8,9},{9,8},{10,11... | collective-permute-start | bytes 589832 | tf_op jit(solution)/shard_map/ppermute | solution.py:45
  46.4 23.6 %collective-permute-start.11 = (f32[2,288,128]{2,1,0:T(8,128)S(1)}, f32[2,288,128]{2,1,0:T(8,128)S(1)}, u32[]{:S(2)}, u32[]{:S(2)}) collective-permute-start(f32[2,288,128]{2,1,0:T(8,128)S(1)} %get-tuple-element.72.refs_9_), channel_id=1, source_target_pairs={{8,0},{16,8},{24,16},{9,1},{17,9},{25,17},{10,2},{18,10},{26,18},{... | collective-permute-start | bytes 884744 | tf_op jit(solution)/shard_map/ppermute | solution.py:25
  51.6 19.6 %collective-permute-start.12 = (f32[2,256,128]{2,1,0:T(8,128)S(1)}, f32[2,256,128]{2,1,0:T(8,128)}, u32[]{:S(2)}, u32[]{:S(2)}) collective-permute-start(f32[2,256,128]{2,1,0:T(8,128)S(1)} %get-tuple-element.77.refs_10_), channel_id=1, source_target_pairs={{0,8},{8,16},{16,24},{1,9},{9,17},{17,25},{2,10},{10,18},{18,26},{... | collective-permute-start | bytes 786440 | tf_op jit(solution)/shard_map/ppermute | solution.py:25
  80.0 7.7 %collective-permute-start.16 = (f32[256,128]{1,0:T(8,128)S(1)}, f32[256,128]{1,0:T(8,128)S(1)}, u32[]{:S(2)}, u32[]{:S(2)}) collective-permute-start(f32[256,128]{1,0:T(8,128)S(1)} %get-tuple-element.83), channel_id=1, source_target_pairs={{0,7},{1,0},{2,1},{3,2},{4,3},{5,4},{6,5},{7,6},{8,15},{9,8},{10,9... | collective-permute-start | bytes 393224 | tf_op jit(solution)/shard_map/ppermute | solution.py:25
  80.3 7.3 %collective-permute-start.17 = (f32[256,128]{1,0:T(8,128)S(1)}, f32[256,128]{1,0:T(8,128)S(1)}, u32[]{:S(2)}, u32[]{:S(2)}) collective-permute-start(f32[256,128]{1,0:T(8,128)S(1)} %get-tuple-element.84), channel_id=1, source_target_pairs={{0,1},{1,2},{2,3},{3,4},{4,5},{5,6},{6,7},{7,0},{8,9},{9,10},{10,1... | collective-permute-start | bytes 393224 | tf_op jit(solution)/shard_map/ppermute | solution.py:25
  80.5 3.9 %collective-permute-start.15 = (f32[48,128]{1,0:T(8,128)S(1)}, f32[48,128]{1,0:T(8,128)S(1)}, u32[]{:S(2)}, u32[]{:S(2)}) collective-permute-start(f32[48,128]{1,0:T(8,128)S(1)} %get-tuple-element.81.refs_0_), channel_id=1, source_target_pairs={{0,24},{8,0},{16,8},{24,16},{1,25},{9,1},{17,9},{25,17},{2,26},{10... | collective-permute-start | bytes 73736 | tf_op jit(solution)/shard_map/ppermute | solution.py:25
  80.5 4.2 %collective-permute-start.14 = (f32[48,128]{1,0:T(8,128)S(1)}, f32[48,128]{1,0:T(8,128)S(1)}, u32[]{:S(2)}, u32[]{:S(2)}) collective-permute-start(f32[48,128]{1,0:T(8,128)S(1)} %get-tuple-element.81.refs_0_), channel_id=1, source_target_pairs={{0,16},{8,24},{16,0},{24,8},{1,17},{9,25},{17,1},{25,9},{2,18},{10... | collective-permute-start | bytes 73736 | tf_op jit(solution)/shard_map/ppermute | solution.py:25
  82.9 4.7 %collective-permute-start.13 = (f32[48,128]{1,0:T(8,128)S(1)}, f32[48,128]{1,0:T(8,128)S(1)}, u32[]{:S(2)}, u32[]{:S(2)}) collective-permute-start(f32[48,128]{1,0:T(8,128)S(1)} %get-tuple-element.81.refs_0_), channel_id=1, source_target_pairs={{0,8},{8,16},{16,24},{24,0},{1,9},{9,17},{17,25},{25,1},{2,10},{10... | collective-permute-start | bytes 73736 | tf_op jit(solution)/shard_map/ppermute | solution.py:25
  87.7 4.5 %collective-permute-start.20 = (f32[48,128]{1,0:T(8,128)S(1)}, f32[48,128]{1,0:T(8,128)S(1)}, u32[]{:S(2)}, u32[]{:S(2)}) collective-permute-start(f32[48,128]{1,0:T(8,128)S(1)} %get-tuple-element.85.refs_0_), channel_id=1, source_target_pairs={{0,6},{1,7},{2,0},{3,1},{4,2},{5,3},{6,4},{7,5},{8,14},{9,15},{10,... | collective-permute-start | bytes 73736 | tf_op jit(solution)/shard_map/ppermute | solution.py:25
  89.3 5.1 %collective-permute-start.19 = (f32[48,128]{1,0:T(8,128)S(1)}, f32[48,128]{1,0:T(8,128)S(1)}, u32[]{:S(2)}, u32[]{:S(2)}) collective-permute-start(f32[48,128]{1,0:T(8,128)S(1)} %get-tuple-element.85.refs_0_), channel_id=1, source_target_pairs={{0,4},{1,5},{2,6},{3,7},{4,0},{5,1},{6,2},{7,3},{8,12},{9,13},{10,... | collective-permute-start | bytes 73736 | tf_op jit(solution)/shard_map/ppermute | solution.py:25
  90.2 5.6 %collective-permute-start.18 = (f32[48,128]{1,0:T(8,128)S(1)}, f32[48,128]{1,0:T(8,128)S(1)}, u32[]{:S(2)}, u32[]{:S(2)}) collective-permute-start(f32[48,128]{1,0:T(8,128)S(1)} %get-tuple-element.85.refs_0_), channel_id=1, source_target_pairs={{0,2},{1,3},{2,4},{3,5},{4,6},{5,7},{6,0},{7,1},{8,10},{9,11},{10,... | collective-permute-start | bytes 73736 | tf_op jit(solution)/shard_map/ppermute | solution.py:25
  90.9 10.7 %collective-permute-start.23 = (f32[2,256,128]{2,1,0:T(8,128)S(1)}, f32[2,256,128]{2,1,0:T(8,128)S(1)}, u32[]{:S(2)}, u32[]{:S(2)}) collective-permute-start(f32[2,256,128]{2,1,0:T(8,128)S(1)} %get-tuple-element.88.refs_9_), channel_id=1, source_target_pairs={{8,0},{16,8},{24,16},{9,1},{17,9},{25,17},{10,2},{18,10},{26,18},{... | collective-permute-start | bytes 786440 | tf_op jit(solution)/shard_map/ppermute | solution.py:25
  95.9 5.7 %collective-permute-start.22 = (f32[2,256,128]{2,1,0:T(8,128)S(1)}, f32[2,256,128]{2,1,0:T(8,128)S(1)}, u32[]{:S(2)}, u32[]{:S(2)}) collective-permute-start(f32[2,256,128]{2,1,0:T(8,128)S(1)} %get-tuple-element.89.refs_10_), channel_id=1, source_target_pairs={{0,8},{8,16},{16,24},{1,9},{9,17},{17,25},{2,10},{10,18},{18,26},{... | collective-permute-start | bytes 786440 | tf_op jit(solution)/shard_map/ppermute | solution.py:25
  97.6 1.4 %collective-permute-start.21 = (f32[192,128]{1,0:T(8,128)S(1)}, f32[192,128]{1,0:T(8,128)S(1)}, u32[]{:S(2)}, u32[]{:S(2)}) collective-permute-start(f32[192,128]{1,0:T(8,128)S(1)} %get-tuple-element.87.refs_2_), channel_id=1, source_target_pairs={{0,1},{1,0},{2,3},{3,2},{4,5},{5,4},{6,7},{7,6},{8,9},{9,8},{10,11... | collective-permute-start | bytes 294920 | tf_op jit(solution)/shard_map/ppermute | solution.py:45
  106.4 11.1 %collective-permute-start.27 = (f32[256,128]{1,0:T(8,128)S(1)}, f32[256,128]{1,0:T(8,128)S(1)}, u32[]{:S(2)}, u32[]{:S(2)}) collective-permute-start(f32[256,128]{1,0:T(8,128)S(1)} %get-tuple-element.98), channel_id=1, source_target_pairs={{0,7},{1,0},{2,1},{3,2},{4,3},{5,4},{6,5},{7,6},{8,15},{9,8},{10,9... | collective-permute-start | bytes 393224 | tf_op jit(solution)/shard_map/ppermute | solution.py:25
  106.6 8.2 %collective-permute-start.26 = (f32[48,128]{1,0:T(8,128)S(1)}, f32[48,128]{1,0:T(8,128)S(1)}, u32[]{:S(2)}, u32[]{:S(2)}) collective-permute-start(f32[48,128]{1,0:T(8,128)S(1)} %get-tuple-element.96.refs_0_), channel_id=1, source_target_pairs={{0,24},{8,0},{16,8},{24,16},{1,25},{9,1},{17,9},{25,17},{2,26},{10... | collective-permute-start | bytes 73736 | tf_op jit(solution)/shard_map/ppermute | solution.py:25
  111.7 3.8 %collective-permute-start.25 = (f32[48,128]{1,0:T(8,128)S(1)}, f32[48,128]{1,0:T(8,128)S(1)}, u32[]{:S(2)}, u32[]{:S(2)}) collective-permute-start(f32[48,128]{1,0:T(8,128)S(1)} %get-tuple-element.96.refs_0_), channel_id=1, source_target_pairs={{0,16},{8,24},{16,0},{24,8},{1,17},{9,25},{17,1},{25,9},{2,18},{10... | collective-permute-start | bytes 73736 | tf_op jit(solution)/shard_map/ppermute | solution.py:25
  112.7 4.7 %collective-permute-start.24 = (f32[48,128]{1,0:T(8,128)S(1)}, f32[48,128]{1,0:T(8,128)S(1)}, u32[]{:S(2)}, u32[]{:S(2)}) collective-permute-start(f32[48,128]{1,0:T(8,128)S(1)} %get-tuple-element.96.refs_0_), channel_id=1, source_target_pairs={{0,8},{8,16},{16,24},{24,0},{1,9},{9,17},{17,25},{25,1},{2,10},{10... | collective-permute-start | bytes 73736 | tf_op jit(solution)/shard_map/ppermute | solution.py:25
  117.5 11.7 %collective-permute-start.32 = (f32[2,256,128]{2,1,0:T(8,128)S(1)}, f32[2,256,128]{2,1,0:T(8,128)S(1)}, u32[]{:S(2)}, u32[]{:S(2)}) collective-permute-start(f32[2,256,128]{2,1,0:T(8,128)S(1)} %get-tuple-element.102.refs_9_), channel_id=1, source_target_pairs={{8,0},{16,8},{24,16},{9,1},{17,9},{25,17},{10,2},{18,10},{26,18},{... | collective-permute-start | bytes 786440 | tf_op jit(solution)/shard_map/ppermute | solution.py:25
  118.8 4.1 %collective-permute-start.30 = (f32[48,128]{1,0:T(8,128)S(1)}, f32[48,128]{1,0:T(8,128)S(1)}, u32[]{:S(2)}, u32[]{:S(2)}) collective-permute-start(f32[48,128]{1,0:T(8,128)S(1)} %get-tuple-element.99.refs_0_), channel_id=1, source_target_pairs={{0,6},{1,7},{2,0},{3,1},{4,2},{5,3},{6,4},{7,5},{8,14},{9,15},{10,... | collective-permute-start | bytes 73736 | tf_op jit(solution)/shard_map/ppermute | solution.py:25
  121.3 4.7 %collective-permute-start.29 = (f32[48,128]{1,0:T(8,128)S(1)}, f32[48,128]{1,0:T(8,128)S(1)}, u32[]{:S(2)}, u32[]{:S(2)}) collective-permute-start(f32[48,128]{1,0:T(8,128)S(1)} %get-tuple-element.99.refs_0_), channel_id=1, source_target_pairs={{0,4},{1,5},{2,6},{3,7},{4,0},{5,1},{6,2},{7,3},{8,12},{9,13},{10,... | collective-permute-start | bytes 73736 | tf_op jit(solution)/shard_map/ppermute | solution.py:25
  122.1 5.6 %collective-permute-start.28 = (f32[48,128]{1,0:T(8,128)S(1)}, f32[48,128]{1,0:T(8,128)S(1)}, u32[]{:S(2)}, u32[]{:S(2)}) collective-permute-start(f32[48,128]{1,0:T(8,128)S(1)} %get-tuple-element.99.refs_0_), channel_id=1, source_target_pairs={{0,2},{1,3},{2,4},{3,5},{4,6},{5,7},{6,0},{7,1},{8,10},{9,11},{10,... | collective-permute-start | bytes 73736 | tf_op jit(solution)/shard_map/ppermute | solution.py:25
  (12 other events, 68.2 us)

commit v5 on v4

--- a/solution.py
+++ b/solution.py
@@ -13,6 +13,7 @@
 VMEM = pl.BlockSpec(memory_space=pltpu.VMEM)
 SMEM = pl.BlockSpec(memory_space=pltpu.SMEM)
 ANY = pl.BlockSpec(memory_space=pl.ANY)
+HBM = pl.BlockSpec(memory_space=pltpu.HBM)
 F32, BF16 = jnp.float32, jnp.bfloat16
 
 
@@ -50,11 +51,6 @@
     return high, (value - high.astype(F32)).astype(BF16)
 
 
-def kept_halves(value):
-    high = lax.reduce_precision(value, 8, 7)
-    return high.astype(BF16), (value - high).astype(BF16)
-
-
 def dot(first, second):
     return lax.dot_general(first, second, (((1,), (0,)), ((), ())), preferred_element_type=F32)
 
@@ -78,9 +74,9 @@
 
 
 def prepare_kernel(cuts, at, *refs):
-    sources, outs, buffer = refs[0:6], refs[6:13], refs[13]
-    held, sems = refs[14:20], refs[20]
-    residual, to_far, to_right, inner, c_rows, c_keep, corner = outs
+    sources, outs, buffer = refs[0:6], refs[6:14], refs[14]
+    held, sems = refs[15:21], refs[21]
+    residual, to_far, to_right, inner, c_rows, c_keep, corner, own_offsets = outs
     offsets, corner_map, gap, coupling, corner_rows, rows_table = held
     copies = [pltpu.make_async_copy(source, to, sems.at[i]) for i, (source, to) in enumerate(zip(sources, held))]
     for copy in copies:
@@ -110,18 +106,47 @@
     inner[count - 1] = jnp.zeros(inner.shape[1:], F32)
     corner[...] = jnp.zeros_like(corner)
     dofs, rows = corner_rows.shape[2], 3 * cuts
-    lanes = -(-dofs // 128)
-    lane = lax.broadcasted_iota(jnp.int32, (1, 128), 1)
-    number = jnp.zeros((1, 128), F32)
-    for s in range(count):
-        number = number + jnp.where(lane == at[0] * count + s, (corner_map[s, 2] + 1).astype(F32), 0.0)
+    lanes = dofs // 128 + 1
+    lane = lax.broadcasted_iota(jnp.int32, (3, 128), 1)
+    row = lax.broadcasted_iota(jnp.int32, (3, 128), 0)
+    for s in range(count):
+        number = (3 * corner_map[s, 2] + 1 + row).astype(F32)
         for i in range(lanes):
             wide = min(128, dofs - 128 * i)
             for a in range(cuts):
                 keep = (at[0] == a).astype(F32)
                 first = (s * lanes + i) * rows + 3 * a
-                corner[first:first + 3, 0:wide] = corner_rows[6:9, s, 128 * i:128 * i + wide] * keep
-    corner[corner.shape[0] - 8:corner.shape[0] - 7] = number
+                if wide > 0:
+                    corner[first:first + 3, 0:wide] = corner_rows[6:9, s, 128 * i:128 * i + wide] * keep
+                if i == lanes - 1:
+                    before = corner[first:first + 3]
+                    corner[first:first + 3] = jnp.where(lane == dofs % 128, number * keep, before)
+    for s in range(count):
+        for face in range(2):
+            own_offsets[s, face] = offsets[s, face]
+
+
+def matrix_kernel(cuts, dofs, height, count, chips, mine, theirs, k_high, k_low, rows, pick):
+    used, lanes, stride = 3 * cuts, dofs // 128 + 1, mine.shape[0] // chips
+    rows[...] = jnp.zeros_like(rows)
+    for i, source in enumerate((mine, theirs)):
+        for k in range(chips):
+            for s in range(count):
+                to = ((i * chips + k) * count + s) * height
+                for l in range(lanes):
+                    first = k * stride + (count + 1) * height + (s * lanes + l) * used
+                    rows[to:to + used, 128 * l:128 * (l + 1)] = source[first:first + used]
+    lane = lax.broadcasted_iota(jnp.int32, pick.shape, 1)
+    number = rows[:, dofs:dofs + 1].astype(jnp.int32)
+    pick[...] = jnp.where(lane + 1 == number, 1.0, 0.0).astype(BF16)
+    tile = 256 if rows.shape[0] % 256 == 0 else rows.shape[0]
+
+    @pl.loop(0, rows.shape[0] // tile)
+    def _(t):
+        at = pl.ds(pl.multiple_of(t * tile, tile), tile)
+        for half, out in zip(halves(rows[at]), (k_high, k_low)):
+            product = lax.dot_general(half, pick[...], (((1,), (1,)), ((), ())), preferred_element_type=F32)
+            out[at] = product.astype(BF16)
 
 
 def paired(face):
@@ -131,7 +156,7 @@
     return both.astype(BF16)
 
 
-def spread_kernel(at, coupling, from_near, from_far, from_left, from_right, table, ct_own, ct_left, ct_right):
+def spread_kernel(at, own_offsets, coupling, from_near, from_far, from_left, from_right, table, ct_own, ct_left, ct_right, offsets):
     count, size = coupling.shape[0], coupling.shape[2] // 4
 
     def turned(face, cycle):
@@ -146,6 +171,12 @@
         ct_own[s, 5 * size:6 * size] = turned(got_coupling(from_near.at[s], size), at[0] - 1)
     ct_left[...] = turned(got_coupling(from_left, size), at[0])
     ct_right[...] = turned(got_coupling(from_right, size), at[0])
+    noted = lambda ref: jnp.max(ref[size + 12:size + 16]).astype(jnp.int32) - 1
+    for s in range(count):
+        offsets[s, NEAR] = noted(from_near.at[s])
+        offsets[s, FAR] = own_offsets[s, 0]
+        offsets[s, LEFT] = noted(from_left) if s == 0 else own_offsets[s - 1, 1]
+        offsets[s, RIGHT] = own_offsets[s, 1]
 
 
 def sum_kernel(parts, *refs):
@@ -180,16 +211,16 @@
     )(*parts, *through)
 
 
-def apply_flexibility(loads, flexibility, coupling, height, outs, scratch, rr_rows):
+def apply_flexibility(loads, fetched, coupling, height, outs, scratch, rr_rows):
     near, far, sides, to_left, to_right, terms = outs
-    split, a_high, a_low = scratch["split"]
+    split, a_high, a_low, flexibility = scratch["split"][0:4]
     count, size = len(loads), loads[0][0].shape[0]
     for s in range(count):
         for face in range(4):
             high, low = halves(loads[s][face])
             split[s, face * size:(face + 1) * size, 0:128] = high
             split[s, face * size:(face + 1) * size, 128:256] = low
-    terms[...] = jnp.zeros_like(terms)
+    terms[0:(count + 1) * height] = jnp.zeros(((count + 1) * height, 128), F32)
     total = jnp.zeros((1, 128), F32)
     width = coupling.shape[1] // 2
     for s in range(count):
@@ -198,6 +229,7 @@
         terms[s * height:s * height + width] += mine
     for s in range(count):
         for i in range(0, a_high.shape[1], size):
+            fetched(s, i // size)
             a_high[s, i:i + size], a_low[s, i:i + size] = halves(flexibility[s, i:i + size])
         whole = dot(a_high[s], split[s])
         whole = whole[:, 0:128] + whole[:, 128:256] + dot(a_low[s], split[s, :, 0:128])
@@ -294,10 +326,21 @@
     return result, norm, energy
 
 
+def fetch(source, to, sems, size):
+    copies = {}
+    for s in range(source.shape[0]):
+        for i in range(source.shape[1] // size):
+            rows = pl.ds(i * size, size)
+            copies[s, i] = pltpu.make_async_copy(source.at[s, rows], to.at[s, rows], sems.at[s, i])
+            copies[s, i].start()
+    return lambda s, i: copies[s, i].wait()
+
+
 def first_kernel(height, rr_rows, residual, from_near, from_left, inner, coupling, corner, flexibility, c_rows, *rest):
-    outs, loads_out, split = rest[0:6], rest[6], rest[7:10]
+    outs, loads_out, split = rest[0:6], rest[6], rest[7:12]
     near, to_left, terms = outs[0], outs[3], outs[5]
     count, size = residual.shape[0], residual.shape[2]
+    fetched = fetch(flexibility, split[3], split[4], size)
     loads = []
     for s in range(count):
         left = from_left[0:size] if s == 0 else inner[s - 1]
@@ -306,10 +349,8 @@
             loads_out[s, face] = loads[s][face]
         put_coupling(near.at[s], size, coupling[s, :, NEAR * size:(NEAR + 1) * size], 0.0)
     put_coupling(to_left, size, coupling[0, :, LEFT * size:(LEFT + 1) * size], 0.0)
-    apply_flexibility(loads, flexibility, c_rows, height, outs, dict(split=split), rr_rows)
-    rows = corner.shape[0] - 8
-    terms[(count + 1) * height:] = corner[0:rows]
-    terms[rr_rows + 2:rr_rows + 3] = corner[rows:rows + 1]
+    apply_flexibility(loads, fetched, c_rows, height, outs, dict(split=split), rr_rows)
+    terms[(count + 1) * height:] = corner[...]
 
 
 def step_kernel(which, chips, height, rr_rows, *refs):
@@ -322,12 +363,12 @@
     (loads,) = take(1)
     map_before, ways, found, scalars = (take(4) if which > 0 else [None] * 4)
     if not last:
-        flexibility, coupling = take(2)
+        coupling, flexibility = take(2)
         outs = take(6)
         loads_out, map_out = take(2)
         ways_out, found_out = take(2) if which > 0 else (None, None)
         (scalars_out,) = take(1)
-        stack, values, turn, *split = take(6)
+        stack, values, turn, *split = take(8)
         faces = (NEAR, FAR, LEFT, RIGHT)
     else:
         found_out, residual_out = take(2)
@@ -337,6 +378,7 @@
     scratch = dict(stack=stack, values=values, turn=turn, chips=chips)
     if not last:
         scratch["split"] = split
+        fetched = fetch(flexibility, split[3], split[4], size)
     mapped, norm, energy = finish_operator(
         offsets, terms, matrix, spread, product, received, height, rr_rows, scratch, faces
     )
@@ -373,7 +415,7 @@
                     ways_out[s, i] = way
     if not last:
         scalars_out[...] = jnp.concatenate([norm, step, jnp.zeros((6, 128), F32)], axis=0)
-        apply_flexibility(fresh, flexibility, coupling, height, outs, scratch, rr_rows)
+        apply_flexibility(fresh, fetched, coupling, height, outs, scratch, rr_rows)
 
 
 def corner_tables(cuts, height):
@@ -392,24 +434,6 @@
     return jnp.asarray(table, BF16), jnp.asarray(rows, BF16)
 
 
-def corner_matrix(sources, count, dofs, cuts, height):
-    rows, lanes = 3 * cuts, -(-dofs // 128)
-    first = (count + 1) * height
-    numbers = jnp.concatenate([x[:, rows + 2, :cuts * count] for x in sources], axis=0).astype(jnp.int32) - 1
-    numbers = jnp.swapaxes(numbers.reshape(-1, cuts, count), 1, 2)
-    chosen = (3 * numbers[..., None] + jnp.arange(3, dtype=jnp.int32)).reshape(-1, rows)
-    chosen = jnp.pad(chosen, ((0, 0), (0, height - rows)), constant_values=-1).reshape(-1)
-    pick = (jnp.arange(128 * lanes, dtype=jnp.int32)[:, None] == chosen[None, :]).astype(BF16)
-    pick = pick.reshape(lanes, 128, -1)
-    found = [[], []]
-    for x in sources:
-        matrix = x[:, first:first + count * lanes * rows].reshape(-1, lanes, rows, 128)
-        for half, into in zip(kept_halves(matrix), found):
-            product = jnp.einsum("nlrd,ldc->nrc", half, pick, preferred_element_type=F32).astype(BF16)
-            into.append(jnp.pad(product, ((0, 0), (0, height - rows), (0, 0))).reshape(-1, product.shape[-1]))
-    return [jnp.concatenate(into, axis=0) for into in found]
-
-
 def per_device(gap_load, offsets, corner_map, flexibility, coupling, corner_rows):
     _, count, _, size, loads_n = gap_load.shape
     dofs = corner_rows.shape[-1]
@@ -417,7 +441,7 @@
     at = lax.axis_index("cuts").reshape(1)
     side = (lax.axis_index("blk") % 2).reshape(1)
     rr_rows = 3 * cuts
-    height = -(-(rr_rows + 3) // 8) * 8
+    height = -(-(rr_rows + 2) // 8) * 8
     gap, offsets, corner_map, flexibility, coupling, corner_rows = (
         x[0] for x in (gap_load, offsets, corner_map, flexibility, coupling, corner_rows)
     )
@@ -432,8 +456,8 @@
     long_faces = shape(count, size + below, loads_n)
     table, rows_table = corner_tables(cuts, height)
 
-    corner_size = -(-(count * -(-dofs // 128) * rr_rows) // 8) * 8
-    corner_shape = shape(corner_size + 8, loads_n)
+    corner_size = -(-(count * (dofs // 128 + 1) * rr_rows) // 8) * 8
+    corner_shape = shape(corner_size, loads_n)
     wide = shape(count, rr_rows, total)
     held = [
         pltpu.SMEM(offsets.shape, jnp.int32),
@@ -445,30 +469,26 @@
     ]
     prepared = (pair, long_faces, long_face, faces, shape(count, 4 * height, total, kind=BF16), shape(count, 12, total),
                 corner_shape)
-    residual, to_far, to_right, inner, c_rows, c_keep, corner = pl.pallas_call(
+    residual, to_far, to_right, inner, c_rows, c_keep, corner, own_offsets = pl.pallas_call(
         functools.partial(prepare_kernel, cuts),
-        out_shape=prepared,
-        in_specs=[SMEM] + [ANY] * 6,
-        out_specs=(VMEM,) * 7,
+        out_shape=prepared + (shape(count, 2, kind=jnp.int32),),
+        in_specs=[SMEM] + [HBM] * 6,
+        out_specs=(VMEM,) * 7 + (SMEM,),
         scratch_shapes=[pltpu.VMEM((count, 2, 2 * size, loads_n), F32), *held, pltpu.SemaphoreType.DMA((6,))],
         compiler_params=room(*prepared, pair, pair, *held[2:]),
         name="prepare",
     )(at, offsets, corner_map, gap, jnp.swapaxes(coupling, 0, 1), jnp.swapaxes(corner_rows, 0, 1), rows_table)
     from_near = shifted(to_far, "cuts", 1, False)
     from_left = shifted(to_right, "blk", 1, True)
-    near_offsets = from_near[:, size + 12, 0]
-    left_offsets = jnp.concatenate([from_left[size + 12:size + 13, 0], (offsets[:-1, 1] + 1).astype(F32)])
-    all_offsets = jnp.stack([
-        near_offsets.astype(jnp.int32) - 1, offsets[:, 0], left_offsets.astype(jnp.int32) - 1, offsets[:, 1]
-    ], axis=1)
-
     flops = 2 * count * total * total * loads_n * 3
     cost = pl.CostEstimate(flops=flops, bytes_accessed=4 * flexibility.size, transcendentals=0)
     terms_shape = shape((count + 1) * height, loads_n)
     sends = (faces, faces, pair, face, face, terms_shape)
     first_terms = shape((count + 1) * height + corner_size, loads_n)
     first_sends = (long_faces, faces, pair, long_face, face, first_terms)
-    a_buffers = [pltpu.VMEM((count, total, 2 * loads_n), BF16)] + [pltpu.VMEM(flexibility.shape, BF16)] * 2
+    a_buffers = [pltpu.VMEM((count, total, 2 * loads_n), BF16)] + [pltpu.VMEM(flexibility.shape, BF16)] * 2 + [
+        pltpu.VMEM(flexibility.shape, F32), pltpu.SemaphoreType.DMA((count, total // size))
+    ]
     f_buffers = [
         pltpu.VMEM((blocks * count * height, loads_n), F32),
         pltpu.VMEM((blocks * count * height, loads_n), F32),
@@ -478,10 +498,10 @@
     *out, loads = pl.pallas_call(
         functools.partial(first_kernel, height, rr_rows),
         out_shape=first_sends + (four,),
-        in_specs=[VMEM] * 8,
+        in_specs=[VMEM] * 6 + [HBM, VMEM],
         out_specs=(VMEM,) * 7,
         scratch_shapes=a_buffers,
-        compiler_params=room(*first_args, *first_sends, four, *a_buffers),
+        compiler_params=room(*first_args[:6], c_rows, *first_sends, four, *a_buffers[:-1]),
         cost_estimate=cost,
         name="first",
     )(*first_args)
@@ -505,31 +525,38 @@
         r_near = far if last else shifted(far, "cuts", 1, False)
         theirs = swapped(mine, "blk")
         if which == 0:
-            stride = terms.shape[0]
-            k_high, k_low = corner_matrix(
-                [x.reshape(-1, stride, loads_n) for x in (mine, theirs)], count, dofs, cuts, height
-            )
-        if which == 0:
-            ct_own, ct_left, ct_right = pl.pallas_call(
+            k_shape = shape(blocks * count * height, blocks * count * height, kind=BF16)
+            held = [pltpu.VMEM((k_shape.shape[0], 128 * (dofs // 128 + 1)), kind) for kind in (F32, BF16)]
+            k_high, k_low = pl.pallas_call(
+                functools.partial(matrix_kernel, cuts, dofs, height, count, blocks // 2),
+                out_shape=(k_shape, k_shape),
+                in_specs=[VMEM] * 2,
+                out_specs=(VMEM,) * 2,
+                scratch_shapes=held,
+                compiler_params=room(mine, theirs, k_shape, k_shape, *held),
+                name="matrix",
+            )(mine, theirs)
+            ct_own, ct_left, ct_right, all_offsets = pl.pallas_call(
                 spread_kernel,
                 out_shape=(
                     shape(count, 6 * size, 6 * height, kind=BF16),
                     shape(size, 6 * height, kind=BF16),
                     shape(size, 6 * height, kind=BF16),
+                    shape(count, 4, kind=jnp.int32),
                 ),
-                in_specs=[SMEM] + [VMEM] * 6,
-                out_specs=(VMEM,) * 3,
+                in_specs=[SMEM] * 2 + [VMEM] * 6,
+                out_specs=(VMEM,) * 3 + (SMEM,),
                 compiler_params=room(c_keep, from_near, r_far, from_left, r_right, table, *[faces] * 6),
                 name="spread",
-            )(at, c_keep, from_near, r_far, from_left, r_right, table)
+            )(at, own_offsets, c_keep, from_near, r_far, from_left, r_right, table)
         args = [all_offsets, side, mine, theirs, k_high, k_low, ct_own, ct_left, ct_right, near, far, sides,
                 r_near, r_far, r_left, r_right, loads, *state]
         specs = [SMEM, SMEM] + [VMEM] * (len(args) - 2)
         if last:
             outs, scratch = (pair, pair), f_buffers
         else:
-            args += [flexibility, c_rows]
-            specs += [VMEM] * 2
+            args += [c_rows, flexibility]
+            specs += [VMEM, HBM]
             outs = sends + (four, four) + ((pair, pair) if which > 0 else ()) + (shape(8, loads_n),)
             scratch = f_buffers + a_buffers
         result = pl.pallas_call(
@@ -538,7 +565,7 @@
             in_specs=specs,
             out_specs=(VMEM,) * len(outs),
             scratch_shapes=scratch,
-            compiler_params=room(*args[2:], *outs, *scratch),
+            compiler_params=room(*args[2:] if last else args[2:-1], *outs, *(scratch if last else scratch[:-1])),
             cost_estimate=None if last else cost,
             name=f"step{which}",
         )(*args)

time: 133 us -> 126 us (0.947)
  local copies, waits for them, and re-layouts: 25 us -> 16.1 us
  Pallas kernels: 18.6 us -> 23.3 us
  matrix products: 4.57 us -> 0 us
  waiting for transfers between devices: 32.6 us -> 35.7 us
  other arithmetic: 2.91 us -> 0 us
  starting transfers between devices: 46.2 us -> 48.6 us
    slice x7 -> x0, local copies, waits for them, and re-layouts: 5.74 us -> none  [the longest x2 3.09 us: corner_matrix(): x[:, first:first + count * lanes * rows].reshape(-1, lanes, rows, 128)]
    dot_general x4 -> x0, matrix products: 4.57 us -> none  [corner_matrix(): jnp.einsum('nlrd,ldc->nrc', half, pick, preferred_element_type=F32)]
    unnamed x24, local copies, waits for them, and re-layouts: 12.6 us -> 16.1 us
    reshape x2 -> x0, local copies, waits for them, and re-layouts: 3.11 us -> none  [corner_matrix(): x[:, first:first + count * lanes * rows].reshape(-1, lanes, rows, 128)]
    pallas_call x3, Pallas kernels: 12.4 us -> 15.2 us  [per_device(): pl.pallas_call(functools.partial(step_kernel, which, blocks // 2, height,...]
    ppermute x30, starting transfers between devices: 46 us -> 48.5 us  [shifted(): return lax.ppermute(value, axis, pairs)]
    add x4 -> x0, local copies, waits for them, and re-layouts: 2.15 us -> none  [corner_matrix(): 3 * numbers[..., None] + jnp.arange(3, dtype=jnp.int32)]
    ppermute x30, waiting for transfers between devices: 30 us -> 31.7 us  [shifted(): return lax.ppermute(value, axis, pairs)]
  transfers between devices with their start and end apart: 33 -> 33, of which waited for: 18 -> 19; matrix products, arithmetic and copies ran while one was open for 15% -> 0% of each run, Pallas kernels for 0% -> 2%
where the time goes in v5:
time: 126 us; the launch traced here: 125 us
  starting transfers between devices  48.6 us (39%)
  waiting for transfers between devices  35.7 us (28%)
  Pallas kernels  23.3 us (18%)
  local copies, waits for them, and re-layouts  16.1 us (13%)
    ppermute x30, starting transfers between devices, shifted(): return lax.ppermute(value, axis, pairs)  48.5 us
    ppermute x30, waiting for transfers between devices, shifted(): return lax.ppermute(value, axis, pairs)  31.7 us
    unnamed x24, local copies, waits for them, and re-layouts  16.1 us
    pallas_call x3, Pallas kernels, per_device(): pl.pallas_call(functools.partial(step_kernel, which, blocks // 2, height,...  15.2 us
    pallas_call x1, Pallas kernels, per_device(): pl.pallas_call(functools.partial(first_kernel, height, rr_rows), out_shap...  4.73 us
    ppermute x3, waiting for transfers between devices, swapped(): lax.ppermute(value, axis, [(source, source ^ 1) for source in range(lax.a...  4.01 us
  transfers between devices with their start and end apart: 33, of which 19 were waited for; matrix products, arithmetic and copies ran while one was open for 0% of the time, Pallas kernels for 2%

profile of v5, /device:TPU:0, one launch (start us, length us, event | category | flops | bytes accessed | tf_op | source)
XLA Modules:
  0.0 124.5 jit_solution(6071438907348118489)
XLA Ops:
  5.5 1.5 %prepare.1 = (f32[2,2,256,128]{3,2,1,0:T(8,128)S(1)}, f32[2,288,128]{2,1,0:T(8,128)S(1)}, f32[288,128]{1,0:T(8,128)S(1)}, f32[2,256,128]{2,1,0:T(8,128)S(1)}, bf...) custom-call(s32[1]{0:T(128)} %bitcast.at, ...), custom_call_target="tpu_custom_call" | custom-call | tf_op jit(solution)/shard_map/prepare/pallas_call | solution.py:472
  7.0 4.9 %collective-permute-start = (f32[2,288,128]{2,1,0:T(8,128)S(1)}, f32[2,288,128]{2,1,0:T(8,128)S(1)}, u32[]{:S(2)}, u32[]{:S(2)}) collective-permute-start(f32[2,288,128]{2,1,0:T(8,128)S(1)} %get-tuple-element.64), channel_id=1, source_target_pairs={{0,8},{8,16},{16,24},{1,9},{9,17},{17,25},{2,10},{10,18},{18,26},{... | collective-permute-start | bytes 884744 | tf_op jit(solution)/shard_map/ppermute | solution.py:26
  11.9 6.4 %collective-permute-done.1.from_left = f32[288,128]{1,0:T(8,128)S(1)} collective-permute-done((f32[288,128]{1,0:T(8,128)S(1)}, f32[288,128]{1,0:T(8,128)S(1)}, u32[]{:S(2)}, u32[]{:S(2)}) %collective-permute-start.1) | collective-permute-done | bytes 147488 | tf_op jit(solution)/shard_map/ppermute | solution.py:26
  18.3 3.4 %copy-done = f32[1,2,1024,1024]{3,2,1,0:T(8,128)S(1)} copy-done((f32[1,2,1024,1024]{3,2,1,0:T(8,128)S(1)}, f32[1,2,1024,1024]{3,2,1,0:T(8,128)}, u32[]{:S(2)}) %copy-start) | copy-done | bytes 8388632
  21.7 4.7 %first.1 = (f32[2,288,128]{2,1,0:T(8,128)S(1)}, f32[2,256,128]{2,1,0:T(8,128)S(1)}, f32[2,2,256,128]{3,2,1,0:T(8,128)S(1)}, f32[288,128]{1,0:T(8,128)S(1)}, f32[...) custom-call(f32[2,2,256,128]{3,2,1,0:T(8,128)S(1)} %get-tuple-element.65.residual, ...), custom_call_target="tpu_custom_call" | custom-call | flops 1610612736 | bytes 8388608 | tf_op jit(solution)/shard_map/first/pallas_call | solution.py:498
  26.4 2.0 %collective-permute-start.5 = (f32[288,128]{1,0:T(8,128)S(1)}, f32[288,128]{1,0:T(8,128)S(1)}, u32[]{:S(2)}, u32[]{:S(2)}) collective-permute-start(f32[288,128]{1,0:T(8,128)S(1)} %get-tuple-element.72), channel_id=1, source_target_pairs={{0,7},{1,0},{2,1},{3,2},{4,3},{5,4},{6,5},{7,6},{8,15},{9,8},{10,9... | collective-permute-start | bytes 442376 | tf_op jit(solution)/shard_map/ppermute | solution.py:26
  28.4 3.4 %collective-permute-start.4 = (f32[96,128]{1,0:T(8,128)S(1)}, f32[96,128]{1,0:T(8,128)S(1)}, u32[]{:S(2)}, u32[]{:S(2)}) collective-permute-start(f32[96,128]{1,0:T(8,128)S(1)} %get-tuple-element.70.refs_0_), channel_id=1, source_target_pairs={{0,24},{8,0},{16,8},{24,16},{1,25},{9,1},{17,9},{25,17},{2,26},{10... | collective-permute-start | bytes 147464 | tf_op jit(solution)/shard_map/ppermute | solution.py:26
  32.4 1.5 %collective-permute-start.2 = (f32[96,128]{1,0:T(8,128)S(1)}, f32[96,128]{1,0:T(8,128)S(1)}, u32[]{:S(2)}, u32[]{:S(2)}) collective-permute-start(f32[96,128]{1,0:T(8,128)S(1)} %get-tuple-element.70.refs_0_), channel_id=1, source_target_pairs={{0,8},{8,16},{16,24},{24,0},{1,9},{9,17},{17,25},{25,1},{2,10},{10... | collective-permute-start | bytes 147464 | tf_op jit(solution)/shard_map/ppermute | solution.py:26
  34.0 2.3 %collective-permute-done.3.refs_2_ = f32[96,128]{1,0:T(8,128)S(1)} collective-permute-done((f32[96,128]{1,0:T(8,128)S(1)}, f32[96,128]{1,0:T(8,128)S(1)}, u32[]{:S(2)}, u32[]{:S(2)}) %collective-permute-start.3) | collective-permute-done | bytes 49184 | tf_op jit(solution)/shard_map/ppermute | solution.py:26
  37.4 2.1 %collective-permute-start.10 = (f32[96,128]{1,0:T(8,128)S(1)}, f32[96,128]{1,0:T(8,128)S(1)}, u32[]{:S(2)}, u32[]{:S(2)}) collective-permute-start(f32[96,128]{1,0:T(8,128)S(1)} %get-tuple-element.77.refs_0_), channel_id=1, source_target_pairs={{0,6},{1,7},{2,0},{3,1},{4,2},{5,3},{6,4},{7,5},{8,14},{9,15},{10,... | collective-permute-start | bytes 147464 | tf_op jit(solution)/shard_map/ppermute | solution.py:26
  42.0 3.6 %collective-permute-done.9.refs_2_ = f32[96,128]{1,0:T(8,128)S(1)} collective-permute-done((f32[96,128]{1,0:T(8,128)S(1)}, f32[96,128]{1,0:T(8,128)S(1)}, u32[]{:S(2)}, u32[]{:S(2)}) %collective-permute-start.9) | collective-permute-done | bytes 49184 | tf_op jit(solution)/shard_map/ppermute | solution.py:26
  45.6 3.2 %collective-permute-start.12 = (f32[2,256,128]{2,1,0:T(8,128)S(1)}, f32[2,256,128]{2,1,0:T(8,128)}, u32[]{:S(2)}, u32[]{:S(2)}) collective-permute-start(f32[2,256,128]{2,1,0:T(8,128)S(1)} %get-tuple-element.85.refs_10_), channel_id=1, source_target_pairs={{0,8},{8,16},{16,24},{1,9},{9,17},{17,25},{2,10},{10,18},{18,26},{... | collective-permute-start | bytes 786440 | tf_op jit(solution)/shard_map/ppermute | solution.py:26
  51.4 1.5 %spread.1 = (bf16[2,1536,96]{2,1,0:T(8,128)(2,1)S(1)}, bf16[256,96]{1,0:T(8,128)(2,1)S(1)}, bf16[256,96]{1,0:T(8,128)(2,1)S(1)}, s32[2,4]{1,0:T(2,128)S(1)}) custom-call(s32[1]{0:T(128)} %bitcast.at, s32[2,2]{1,0:T(2,128)S(1)} %get-tuple-element.62.own_offsets, f32[2,12,1024]{2,1,0:T(8,128)S(1)} %get-tuple-element.63.coupling, ...), custom_call_target="tpu_custom_call" | custom-call | tf_op jit(solution)/shard_map/spread/pallas_call | solution.py:539
  52.9 3.4 %copy-done.1 = f32[1,2,1024,1024]{3,2,1,0:T(8,128)S(1)} copy-done((f32[1,2,1024,1024]{3,2,1,0:T(8,128)S(1)}, f32[1,2,1024,1024]{3,2,1,0:T(8,128)}, u32[]{:S(2)}) %copy-start.1) | copy-done | bytes 8388632
  57.3 6.6 %step0.1 = (f32[2,256,128]{2,1,0:T(8,128)S(1)}, f32[2,256,128]{2,1,0:T(8,128)S(1)}, f32[2,2,256,128]{3,2,1,0:T(8,128)S(1)}, f32[256,128]{1,0:T(8,128)S(1)}, f32[...) custom-call(s32[2,4]{1,0:T(2,128)S(1)} %get-tuple-element.76.refs_0_, ...), custom_call_target="tpu_custom_call" | custom-call | flops 1610612736 | bytes 8388608 | tf_op jit(solution)/shard_map/step0/pallas_call | solution.py:562
  64.8 5.7 %collective-permute-start.15 = (f32[48,128]{1,0:T(8,128)S(1)}, f32[48,128]{1,0:T(8,128)S(1)}, u32[]{:S(2)}, u32[]{:S(2)}) collective-permute-start(f32[48,128]{1,0:T(8,128)S(1)} %get-tuple-element.89.refs_0_), channel_id=1, source_target_pairs={{0,24},{8,0},{16,8},{24,16},{1,25},{9,1},{17,9},{25,17},{2,26},{10... | collective-permute-start | bytes 73736 | tf_op jit(solution)/shard_map/ppermute | solution.py:26
  70.5 2.0 %collective-permute-start.13 = (f32[48,128]{1,0:T(8,128)S(1)}, f32[48,128]{1,0:T(8,128)S(1)}, u32[]{:S(2)}, u32[]{:S(2)}) collective-permute-start(f32[48,128]{1,0:T(8,128)S(1)} %get-tuple-element.89.refs_0_), channel_id=1, source_target_pairs={{0,8},{8,16},{16,24},{24,0},{1,9},{9,17},{17,25},{25,1},{2,10},{10... | collective-permute-start | bytes 73736 | tf_op jit(solution)/shard_map/ppermute | solution.py:26
  72.5 2.0 %collective-permute-done.14.refs_2_ = f32[48,128]{1,0:T(8,128)S(1)} collective-permute-done((f32[48,128]{1,0:T(8,128)S(1)}, f32[48,128]{1,0:T(8,128)S(1)}, u32[]{:S(2)}, u32[]{:S(2)}) %collective-permute-start.14) | collective-permute-done | bytes 24608 | tf_op jit(solution)/shard_map/ppermute | solution.py:26
  75.4 2.0 %collective-permute-start.20 = (f32[48,128]{1,0:T(8,128)S(1)}, f32[48,128]{1,0:T(8,128)S(1)}, u32[]{:S(2)}, u32[]{:S(2)}) collective-permute-start(f32[48,128]{1,0:T(8,128)S(1)} %get-tuple-element.93.refs_0_), channel_id=1, source_target_pairs={{0,6},{1,7},{2,0},{3,1},{4,2},{5,3},{6,4},{7,5},{8,14},{9,15},{10,... | collective-permute-start | bytes 73736 | tf_op jit(solution)/shard_map/ppermute | solution.py:26
  80.0 2.4 %collective-permute-done.19.refs_2_ = f32[48,128]{1,0:T(8,128)S(1)} collective-permute-done((f32[48,128]{1,0:T(8,128)S(1)}, f32[48,128]{1,0:T(8,128)S(1)}, u32[]{:S(2)}, u32[]{:S(2)}) %collective-permute-start.19) | collective-permute-done | bytes 24608 | tf_op jit(solution)/shard_map/ppermute | solution.py:26
  82.4 1.5 %collective-permute-done.18.refs_1_ = f32[48,128]{1,0:T(8,128)S(1)} collective-permute-done((f32[48,128]{1,0:T(8,128)S(1)}, f32[48,128]{1,0:T(8,128)S(1)}, u32[]{:S(2)}, u32[]{:S(2)}) %collective-permute-start.18) | collective-permute-done | bytes 24608 | tf_op jit(solution)/shard_map/ppermute | solution.py:26
  83.9 3.0 %collective-permute-start.22 = (f32[2,256,128]{2,1,0:T(8,128)S(1)}, f32[2,256,128]{2,1,0:T(8,128)S(1)}, u32[]{:S(2)}, u32[]{:S(2)}) collective-permute-start(f32[2,256,128]{2,1,0:T(8,128)S(1)} %get-tuple-element.97.refs_10_), channel_id=1, source_target_pairs={{0,8},{8,16},{16,24},{1,9},{9,17},{17,25},{2,10},{10,18},{18,26},{... | collective-permute-start | bytes 786440 | tf_op jit(solution)/shard_map/ppermute | solution.py:26
  88.3 2.5 %collective-permute-done.22.refs_12_ = f32[2,256,128]{2,1,0:T(8,128)S(1)} collective-permute-done((f32[2,256,128]{2,1,0:T(8,128)S(1)}, f32[2,256,128]{2,1,0:T(8,128)S(1)}, u32[]{:S(2)}, u32[]{:S(2)}) %collective-permute-start.22) | collective-permute-done | bytes 262176 | tf_op jit(solution)/shard_map/ppermute | solution.py:26
  90.8 3.4 %copy-done.2 = f32[1,2,1024,1024]{3,2,1,0:T(8,128)S(1)} copy-done((f32[1,2,1024,1024]{3,2,1,0:T(8,128)S(1)}, f32[1,2,1024,1024]{3,2,1,0:T(8,128)}, u32[]{:S(2)}) %copy-start.2) | copy-done | bytes 8388632
  94.2 6.3 %step1.1 = (f32[2,256,128]{2,1,0:T(8,128)S(1)}, f32[2,256,128]{2,1,0:T(8,128)S(1)}, f32[2,2,256,128]{3,2,1,0:T(8,128)S(1)}, f32[256,128]{1,0:T(8,128)S(1)}, f32[...) custom-call(s32[2,4]{1,0:T(2,128)S(1)} %get-tuple-element.76.refs_0_, ...), custom_call_target="tpu_custom_call" | custom-call | flops 1610612736 | bytes 8388608 | tf_op jit(solution)/shard_map/step1/pallas_call | solution.py:562
  100.6 5.1 %collective-permute-start.26 = (f32[48,128]{1,0:T(8,128)S(1)}, f32[48,128]{1,0:T(8,128)S(1)}, u32[]{:S(2)}, u32[]{:S(2)}) collective-permute-start(f32[48,128]{1,0:T(8,128)S(1)} %get-tuple-element.104.refs_0_), channel_id=1, source_target_pairs={{0,24},{8,0},{16,8},{24,16},{1,25},{9,1},{17,9},{25,17},{2,26},{10... | collective-permute-start | bytes 73736 | tf_op jit(solution)/shard_map/ppermute | solution.py:26
  105.7 1.9 %collective-permute-start.24 = (f32[48,128]{1,0:T(8,128)S(1)}, f32[48,128]{1,0:T(8,128)S(1)}, u32[]{:S(2)}, u32[]{:S(2)}) collective-permute-start(f32[48,128]{1,0:T(8,128)S(1)} %get-tuple-element.104.refs_0_), channel_id=1, source_target_pairs={{0,8},{8,16},{16,24},{24,0},{1,9},{9,17},{17,25},{25,1},{2,10},{10... | collective-permute-start | bytes 73736 | tf_op jit(solution)/shard_map/ppermute | solution.py:26
  107.6 1.9 %collective-permute-done.25.refs_2_ = f32[48,128]{1,0:T(8,128)S(1)} collective-permute-done((f32[48,128]{1,0:T(8,128)S(1)}, f32[48,128]{1,0:T(8,128)S(1)}, u32[]{:S(2)}, u32[]{:S(2)}) %collective-permute-start.25) | collective-permute-done | bytes 24608 | tf_op jit(solution)/shard_map/ppermute | solution.py:26
  111.7 2.7 %collective-permute-start.30 = (f32[48,128]{1,0:T(8,128)S(1)}, f32[48,128]{1,0:T(8,128)S(1)}, u32[]{:S(2)}, u32[]{:S(2)}) collective-permute-start(f32[48,128]{1,0:T(8,128)S(1)} %get-tuple-element.107.refs_0_), channel_id=1, source_target_pairs={{0,6},{1,7},{2,0},{3,1},{4,2},{5,3},{6,4},{7,5},{8,14},{9,15},{10,... | collective-permute-start | bytes 73736 | tf_op jit(solution)/shard_map/ppermute | solution.py:26
  116.0 3.2 %collective-permute-done.29.refs_2_ = f32[48,128]{1,0:T(8,128)S(1)} collective-permute-done((f32[48,128]{1,0:T(8,128)S(1)}, f32[48,128]{1,0:T(8,128)S(1)}, u32[]{:S(2)}, u32[]{:S(2)}) %collective-permute-start.29) | collective-permute-done | bytes 24608 | tf_op jit(solution)/shard_map/ppermute | solution.py:26
  119.2 1.7 %collective-permute-done.28.refs_1_ = f32[48,128]{1,0:T(8,128)S(1)} collective-permute-done((f32[48,128]{1,0:T(8,128)S(1)}, f32[48,128]{1,0:T(8,128)S(1)}, u32[]{:S(2)}, u32[]{:S(2)}) %collective-permute-start.28) | collective-permute-done | bytes 24608 | tf_op jit(solution)/shard_map/ppermute | solution.py:26
  122.3 2.2 %step2.1 = (f32[2,2,256,128]{3,2,1,0:T(8,128)}, f32[2,2,256,128]{3,2,1,0:T(8,128)}) custom-call(s32[2,4]{1,0:T(2,128)S(1)} %get-tuple-element.76.refs_0_, s32[1]{0:T(128)} %bitcast.9.refs_1_, f32[192,128]{1,0:T(8,128)S(1)} %get-tuple-element.109.refs_2_, f32[192,128]{1,0:T(8,128)S(1)} %collective-permute-done.31.refs_3_, ...), custom_call_target="tpu_custom_call" | custom-call | tf_op jit(solution)/shard_map/step2/pallas_call | solution.py:562
  (71 shorter events, 23.5 us)
Async XLA Ops:
  7.0 11.3 %collective-permute-start = (f32[2,288,128]{2,1,0:T(8,128)S(1)}, f32[2,288,128]{2,1,0:T(8,128)S(1)}, u32[]{:S(2)}, u32[]{:S(2)}) collective-permute-start(f32[2,288,128]{2,1,0:T(8,128)S(1)} %get-tuple-element.64), channel_id=1, source_target_pairs={{0,8},{8,16},{16,24},{1,9},{9,17},{17,25},{2,10},{10,18},{18,26},{... | collective-permute-start | bytes 884744 | tf_op jit(solution)/shard_map/ppermute | solution.py:26
  11.8 6.4 %collective-permute-start.1 = (f32[288,128]{1,0:T(8,128)S(1)}, f32[288,128]{1,0:T(8,128)S(1)}, u32[]{:S(2)}, u32[]{:S(2)}) collective-permute-start(f32[288,128]{1,0:T(8,128)S(1)} %get-tuple-element.66), channel_id=1, source_target_pairs={{0,1},{1,2},{2,3},{3,4},{4,5},{5,6},{6,7},{7,0},{8,9},{9,10},{10,1... | collective-permute-start | bytes 442376 | tf_op jit(solution)/shard_map/ppermute | solution.py:26
  26.4 11.0 %collective-permute-start.5 = (f32[288,128]{1,0:T(8,128)S(1)}, f32[288,128]{1,0:T(8,128)S(1)}, u32[]{:S(2)}, u32[]{:S(2)}) collective-permute-start(f32[288,128]{1,0:T(8,128)S(1)} %get-tuple-element.72), channel_id=1, source_target_pairs={{0,7},{1,0},{2,1},{3,2},{4,3},{5,4},{6,5},{7,6},{8,15},{9,8},{10,9... | collective-permute-start | bytes 442376 | tf_op jit(solution)/shard_map/ppermute | solution.py:26
  28.4 8.9 %collective-permute-start.6 = (f32[256,128]{1,0:T(8,128)S(1)}, f32[256,128]{1,0:T(8,128)S(1)}, u32[]{:S(2)}, u32[]{:S(2)}) collective-permute-start(f32[256,128]{1,0:T(8,128)S(1)} %get-tuple-element.73), channel_id=1, source_target_pairs={{0,1},{1,2},{2,3},{3,4},{4,5},{5,6},{6,7},{7,0},{8,9},{9,10},{10,1... | collective-permute-start | bytes 393224 | tf_op jit(solution)/shard_map/ppermute | solution.py:26
  28.4 5.5 %collective-permute-start.4 = (f32[96,128]{1,0:T(8,128)S(1)}, f32[96,128]{1,0:T(8,128)S(1)}, u32[]{:S(2)}, u32[]{:S(2)}) collective-permute-start(f32[96,128]{1,0:T(8,128)S(1)} %get-tuple-element.70.refs_0_), channel_id=1, source_target_pairs={{0,24},{8,0},{16,8},{24,16},{1,25},{9,1},{17,9},{25,17},{2,26},{10... | collective-permute-start | bytes 147464 | tf_op jit(solution)/shard_map/ppermute | solution.py:26
  31.9 4.3 %collective-permute-start.3 = (f32[96,128]{1,0:T(8,128)S(1)}, f32[96,128]{1,0:T(8,128)S(1)}, u32[]{:S(2)}, u32[]{:S(2)}) collective-permute-start(f32[96,128]{1,0:T(8,128)S(1)} %get-tuple-element.70.refs_0_), channel_id=1, source_target_pairs={{0,16},{8,24},{16,0},{24,8},{1,17},{9,25},{17,1},{25,9},{2,18},{10... | collective-permute-start | bytes 147464 | tf_op jit(solution)/shard_map/ppermute | solution.py:26
  32.4 5.0 %collective-permute-start.2 = (f32[96,128]{1,0:T(8,128)S(1)}, f32[96,128]{1,0:T(8,128)S(1)}, u32[]{:S(2)}, u32[]{:S(2)}) collective-permute-start(f32[96,128]{1,0:T(8,128)S(1)} %get-tuple-element.70.refs_0_), channel_id=1, source_target_pairs={{0,8},{8,16},{16,24},{24,0},{1,9},{9,17},{17,25},{25,1},{2,10},{10... | collective-permute-start | bytes 147464 | tf_op jit(solution)/shard_map/ppermute | solution.py:26
  37.4 4.5 %collective-permute-start.10 = (f32[96,128]{1,0:T(8,128)S(1)}, f32[96,128]{1,0:T(8,128)S(1)}, u32[]{:S(2)}, u32[]{:S(2)}) collective-permute-start(f32[96,128]{1,0:T(8,128)S(1)} %get-tuple-element.77.refs_0_), channel_id=1, source_target_pairs={{0,6},{1,7},{2,0},{3,1},{4,2},{5,3},{6,4},{7,5},{8,14},{9,15},{10,... | collective-permute-start | bytes 147464 | tf_op jit(solution)/shard_map/ppermute | solution.py:26
  39.5 6.1 %collective-permute-start.9 = (f32[96,128]{1,0:T(8,128)S(1)}, f32[96,128]{1,0:T(8,128)S(1)}, u32[]{:S(2)}, u32[]{:S(2)}) collective-permute-start(f32[96,128]{1,0:T(8,128)S(1)} %get-tuple-element.77.refs_0_), channel_id=1, source_target_pairs={{0,4},{1,5},{2,6},{3,7},{4,0},{5,1},{6,2},{7,3},{8,12},{9,13},{10,... | collective-permute-start | bytes 147464 | tf_op jit(solution)/shard_map/ppermute | solution.py:26
  39.5 6.1 %collective-permute-start.8 = (f32[96,128]{1,0:T(8,128)S(1)}, f32[96,128]{1,0:T(8,128)S(1)}, u32[]{:S(2)}, u32[]{:S(2)}) collective-permute-start(f32[96,128]{1,0:T(8,128)S(1)} %get-tuple-element.77.refs_0_), channel_id=1, source_target_pairs={{0,2},{1,3},{2,4},{3,5},{4,6},{5,7},{6,0},{7,1},{8,10},{9,11},{10,... | collective-permute-start | bytes 147464 | tf_op jit(solution)/shard_map/ppermute | solution.py:26
  40.7 10.7 %collective-permute-start.7 = (f32[2,288,128]{2,1,0:T(8,128)S(1)}, f32[2,288,128]{2,1,0:T(8,128)S(1)}, u32[]{:S(2)}, u32[]{:S(2)}) collective-permute-start(f32[2,288,128]{2,1,0:T(8,128)S(1)} %get-tuple-element.74.refs_9_), channel_id=1, source_target_pairs={{8,0},{16,8},{24,16},{9,1},{17,9},{25,17},{10,2},{18,10},{26,18},{... | collective-permute-start | bytes 884744 | tf_op jit(solution)/shard_map/ppermute | solution.py:26
  45.6 7.3 %collective-permute-start.12 = (f32[2,256,128]{2,1,0:T(8,128)S(1)}, f32[2,256,128]{2,1,0:T(8,128)}, u32[]{:S(2)}, u32[]{:S(2)}) collective-permute-start(f32[2,256,128]{2,1,0:T(8,128)S(1)} %get-tuple-element.85.refs_10_), channel_id=1, source_target_pairs={{0,8},{8,16},{16,24},{1,9},{9,17},{17,25},{2,10},{10,18},{18,26},{... | collective-permute-start | bytes 786440 | tf_op jit(solution)/shard_map/ppermute | solution.py:26
  48.8 1.4 %collective-permute-start.11 = (f32[384,128]{1,0:T(8,128)S(1)}, f32[384,128]{1,0:T(8,128)S(1)}, u32[]{:S(2)}, u32[]{:S(2)}) collective-permute-start(f32[384,128]{1,0:T(8,128)S(1)} %get-tuple-element.79.mine.refs_2_), channel_id=1, source_target_pairs={{0,1},{1,0},{2,3},{3,2},{4,5},{5,4},{6,7},{7,6},{8,9},{9,8},{10,11... | collective-permute-start | bytes 589832 | tf_op jit(solution)/shard_map/ppermute | solution.py:46
  63.9 11.5 %collective-permute-start.16 = (f32[256,128]{1,0:T(8,128)S(1)}, f32[256,128]{1,0:T(8,128)S(1)}, u32[]{:S(2)}, u32[]{:S(2)}) collective-permute-start(f32[256,128]{1,0:T(8,128)S(1)} %get-tuple-element.91), channel_id=1, source_target_pairs={{0,7},{1,0},{2,1},{3,2},{4,3},{5,4},{6,5},{7,6},{8,15},{9,8},{10,9... | collective-permute-start | bytes 393224 | tf_op jit(solution)/shard_map/ppermute | solution.py:26
  64.8 10.6 %collective-permute-start.17 = (f32[256,128]{1,0:T(8,128)S(1)}, f32[256,128]{1,0:T(8,128)S(1)}, u32[]{:S(2)}, u32[]{:S(2)}) collective-permute-start(f32[256,128]{1,0:T(8,128)S(1)} %get-tuple-element.92), channel_id=1, source_target_pairs={{0,1},{1,2},{2,3},{3,4},{4,5},{5,6},{6,7},{7,0},{8,9},{9,10},{10,1... | collective-permute-start | bytes 393224 | tf_op jit(solution)/shard_map/ppermute | solution.py:26
  64.8 7.7 %collective-permute-start.15 = (f32[48,128]{1,0:T(8,128)S(1)}, f32[48,128]{1,0:T(8,128)S(1)}, u32[]{:S(2)}, u32[]{:S(2)}) collective-permute-start(f32[48,128]{1,0:T(8,128)S(1)} %get-tuple-element.89.refs_0_), channel_id=1, source_target_pairs={{0,24},{8,0},{16,8},{24,16},{1,25},{9,1},{17,9},{25,17},{2,26},{10... | collective-permute-start | bytes 73736 | tf_op jit(solution)/shard_map/ppermute | solution.py:26
  70.4 4.1 %collective-permute-start.14 = (f32[48,128]{1,0:T(8,128)S(1)}, f32[48,128]{1,0:T(8,128)S(1)}, u32[]{:S(2)}, u32[]{:S(2)}) collective-permute-start(f32[48,128]{1,0:T(8,128)S(1)} %get-tuple-element.89.refs_0_), channel_id=1, source_target_pairs={{0,16},{8,24},{16,0},{24,8},{1,17},{9,25},{17,1},{25,9},{2,18},{10... | collective-permute-start | bytes 73736 | tf_op jit(solution)/shard_map/ppermute | solution.py:26
  70.5 5.0 %collective-permute-start.13 = (f32[48,128]{1,0:T(8,128)S(1)}, f32[48,128]{1,0:T(8,128)S(1)}, u32[]{:S(2)}, u32[]{:S(2)}) collective-permute-start(f32[48,128]{1,0:T(8,128)S(1)} %get-tuple-element.89.refs_0_), channel_id=1, source_target_pairs={{0,8},{8,16},{16,24},{24,0},{1,9},{9,17},{17,25},{25,1},{2,10},{10... | collective-permute-start | bytes 73736 | tf_op jit(solution)/shard_map/ppermute | solution.py:26
  75.4 4.5 %collective-permute-start.20 = (f32[48,128]{1,0:T(8,128)S(1)}, f32[48,128]{1,0:T(8,128)S(1)}, u32[]{:S(2)}, u32[]{:S(2)}) collective-permute-start(f32[48,128]{1,0:T(8,128)S(1)} %get-tuple-element.93.refs_0_), channel_id=1, source_target_pairs={{0,6},{1,7},{2,0},{3,1},{4,2},{5,3},{6,4},{7,5},{8,14},{9,15},{10,... | collective-permute-start | bytes 73736 | tf_op jit(solution)/shard_map/ppermute | solution.py:26
  77.4 5.0 %collective-permute-start.19 = (f32[48,128]{1,0:T(8,128)S(1)}, f32[48,128]{1,0:T(8,128)S(1)}, u32[]{:S(2)}, u32[]{:S(2)}) collective-permute-start(f32[48,128]{1,0:T(8,128)S(1)} %get-tuple-element.93.refs_0_), channel_id=1, source_target_pairs={{0,4},{1,5},{2,6},{3,7},{4,0},{5,1},{6,2},{7,3},{8,12},{9,13},{10,... | collective-permute-start | bytes 73736 | tf_op jit(solution)/shard_map/ppermute | solution.py:26
  78.3 5.6 %collective-permute-start.18 = (f32[48,128]{1,0:T(8,128)S(1)}, f32[48,128]{1,0:T(8,128)S(1)}, u32[]{:S(2)}, u32[]{:S(2)}) collective-permute-start(f32[48,128]{1,0:T(8,128)S(1)} %get-tuple-element.93.refs_0_), channel_id=1, source_target_pairs={{0,2},{1,3},{2,4},{3,5},{4,6},{5,7},{6,0},{7,1},{8,10},{9,11},{10,... | collective-permute-start | bytes 73736 | tf_op jit(solution)/shard_map/ppermute | solution.py:26
  78.7 9.6 %collective-permute-start.23 = (f32[2,256,128]{2,1,0:T(8,128)S(1)}, f32[2,256,128]{2,1,0:T(8,128)S(1)}, u32[]{:S(2)}, u32[]{:S(2)}) collective-permute-start(f32[2,256,128]{2,1,0:T(8,128)S(1)} %get-tuple-element.96.refs_9_), channel_id=1, source_target_pairs={{8,0},{16,8},{24,16},{9,1},{17,9},{25,17},{10,2},{18,10},{26,18},{... | collective-permute-start | bytes 786440 | tf_op jit(solution)/shard_map/ppermute | solution.py:26
  83.9 6.9 %collective-permute-start.22 = (f32[2,256,128]{2,1,0:T(8,128)S(1)}, f32[2,256,128]{2,1,0:T(8,128)S(1)}, u32[]{:S(2)}, u32[]{:S(2)}) collective-permute-start(f32[2,256,128]{2,1,0:T(8,128)S(1)} %get-tuple-element.97.refs_10_), channel_id=1, source_target_pairs={{0,8},{8,16},{16,24},{1,9},{9,17},{17,25},{2,10},{10,18},{18,26},{... | collective-permute-start | bytes 786440 | tf_op jit(solution)/shard_map/ppermute | solution.py:26
  86.9 1.4 %collective-permute-start.21 = (f32[192,128]{1,0:T(8,128)S(1)}, f32[192,128]{1,0:T(8,128)S(1)}, u32[]{:S(2)}, u32[]{:S(2)}) collective-permute-start(f32[192,128]{1,0:T(8,128)S(1)} %get-tuple-element.95.refs_2_), channel_id=1, source_target_pairs={{0,1},{1,0},{2,3},{3,2},{4,5},{5,4},{6,7},{7,6},{8,9},{9,8},{10,11... | collective-permute-start | bytes 294920 | tf_op jit(solution)/shard_map/ppermute | solution.py:46
  100.5 9.9 %collective-permute-start.27 = (f32[256,128]{1,0:T(8,128)S(1)}, f32[256,128]{1,0:T(8,128)S(1)}, u32[]{:S(2)}, u32[]{:S(2)}) collective-permute-start(f32[256,128]{1,0:T(8,128)S(1)} %get-tuple-element.106), channel_id=1, source_target_pairs={{0,7},{1,0},{2,1},{3,2},{4,3},{5,4},{6,5},{7,6},{8,15},{9,8},{10,9... | collective-permute-start | bytes 393224 | tf_op jit(solution)/shard_map/ppermute | solution.py:26
  100.6 7.1 %collective-permute-start.26 = (f32[48,128]{1,0:T(8,128)S(1)}, f32[48,128]{1,0:T(8,128)S(1)}, u32[]{:S(2)}, u32[]{:S(2)}) collective-permute-start(f32[48,128]{1,0:T(8,128)S(1)} %get-tuple-element.104.refs_0_), channel_id=1, source_target_pairs={{0,24},{8,0},{16,8},{24,16},{1,25},{9,1},{17,9},{25,17},{2,26},{10... | collective-permute-start | bytes 73736 | tf_op jit(solution)/shard_map/ppermute | solution.py:26
  105.7 3.8 %collective-permute-start.25 = (f32[48,128]{1,0:T(8,128)S(1)}, f32[48,128]{1,0:T(8,128)S(1)}, u32[]{:S(2)}, u32[]{:S(2)}) collective-permute-start(f32[48,128]{1,0:T(8,128)S(1)} %get-tuple-element.104.refs_0_), channel_id=1, source_target_pairs={{0,16},{8,24},{16,0},{24,8},{1,17},{9,25},{17,1},{25,9},{2,18},{10... | collective-permute-start | bytes 73736 | tf_op jit(solution)/shard_map/ppermute | solution.py:26
  105.7 4.7 %collective-permute-start.24 = (f32[48,128]{1,0:T(8,128)S(1)}, f32[48,128]{1,0:T(8,128)S(1)}, u32[]{:S(2)}, u32[]{:S(2)}) collective-permute-start(f32[48,128]{1,0:T(8,128)S(1)} %get-tuple-element.104.refs_0_), channel_id=1, source_target_pairs={{0,8},{8,16},{16,24},{24,0},{1,9},{9,17},{17,25},{25,1},{2,10},{10... | collective-permute-start | bytes 73736 | tf_op jit(solution)/shard_map/ppermute | solution.py:26
  110.4 11.9 %collective-permute-start.32 = (f32[2,256,128]{2,1,0:T(8,128)S(1)}, f32[2,256,128]{2,1,0:T(8,128)S(1)}, u32[]{:S(2)}, u32[]{:S(2)}) collective-permute-start(f32[2,256,128]{2,1,0:T(8,128)S(1)} %get-tuple-element.110.refs_9_), channel_id=1, source_target_pairs={{8,0},{16,8},{24,16},{9,1},{17,9},{25,17},{10,2},{18,10},{26,18},{... | collective-permute-start | bytes 786440 | tf_op jit(solution)/shard_map/ppermute | solution.py:26
  111.7 4.2 %collective-permute-start.30 = (f32[48,128]{1,0:T(8,128)S(1)}, f32[48,128]{1,0:T(8,128)S(1)}, u32[]{:S(2)}, u32[]{:S(2)}) collective-permute-start(f32[48,128]{1,0:T(8,128)S(1)} %get-tuple-element.107.refs_0_), channel_id=1, source_target_pairs={{0,6},{1,7},{2,0},{3,1},{4,2},{5,3},{6,4},{7,5},{8,14},{9,15},{10,... | collective-permute-start | bytes 73736 | tf_op jit(solution)/shard_map/ppermute | solution.py:26
  114.5 4.7 %collective-permute-start.29 = (f32[48,128]{1,0:T(8,128)S(1)}, f32[48,128]{1,0:T(8,128)S(1)}, u32[]{:S(2)}, u32[]{:S(2)}) collective-permute-start(f32[48,128]{1,0:T(8,128)S(1)} %get-tuple-element.107.refs_0_), channel_id=1, source_target_pairs={{0,4},{1,5},{2,6},{3,7},{4,0},{5,1},{6,2},{7,3},{8,12},{9,13},{10,... | collective-permute-start | bytes 73736 | tf_op jit(solution)/shard_map/ppermute | solution.py:26
  115.3 5.6 %collective-permute-start.28 = (f32[48,128]{1,0:T(8,128)S(1)}, f32[48,128]{1,0:T(8,128)S(1)}, u32[]{:S(2)}, u32[]{:S(2)}) collective-permute-start(f32[48,128]{1,0:T(8,128)S(1)} %get-tuple-element.107.refs_0_), channel_id=1, source_target_pairs={{0,2},{1,3},{2,4},{3,5},{4,6},{5,7},{6,0},{7,1},{8,10},{9,11},{10,... | collective-permute-start | bytes 73736 | tf_op jit(solution)/shard_map/ppermute | solution.py:26
  (13 other events, 85.7 us)

commit v6 on v5

--- a/solution.py
+++ b/solution.py
@@ -40,6 +40,12 @@
         parts = [value] + [shifted(value, axis, 2 * k * stride, True) for k in range(1, radix)]
         stride *= radix
     return parts
+
+
+def chip_neighbour(value, axis):
+    count = lax.axis_size(axis)
+    pairs = [(source, (source + (1 if source % 2 else -1)) % count) for source in range(count)]
+    return lax.ppermute(value, axis, pairs)
 
 
 def swapped(value, axis):
@@ -126,8 +132,8 @@
             own_offsets[s, face] = offsets[s, face]
 
 
-def matrix_kernel(cuts, dofs, height, count, chips, mine, theirs, k_high, k_low, rows, pick):
-    used, lanes, stride = 3 * cuts, dofs // 128 + 1, mine.shape[0] // chips
+def matrix_kernel(cuts, dofs, height, count, chips, stride, mine, theirs, k_high, k_low, rows, pick):
+    used, lanes = 3 * cuts, dofs // 128 + 1
     rows[...] = jnp.zeros_like(rows)
     for i, source in enumerate((mine, theirs)):
         for k in range(chips):
@@ -156,7 +162,7 @@
     return both.astype(BF16)
 
 
-def spread_kernel(at, own_offsets, coupling, from_near, from_far, from_left, from_right, table, ct_own, ct_left, ct_right, offsets):
+def spread_kernel(stacked, at, side, own_offsets, coupling, from_near, from_far, from_left, across, theirs, table, ct_own, ct_left, ct_right, offsets):
     count, size = coupling.shape[0], coupling.shape[2] // 4
 
     def turned(face, cycle):
@@ -170,7 +176,8 @@
         ct_own[s, 4 * size:5 * size] = turned(got_coupling(from_far.at[s], size), at[0] + 1)
         ct_own[s, 5 * size:6 * size] = turned(got_coupling(from_near.at[s], size), at[0] - 1)
     ct_left[...] = turned(got_coupling(from_left, size), at[0])
-    ct_right[...] = turned(got_coupling(from_right, size), at[0])
+    inside = got_coupling(theirs.at[stacked:], size)
+    ct_right[...] = turned(jnp.where(side[0] == 1, got_coupling(across, size), inside), at[0])
     noted = lambda ref: jnp.max(ref[size + 12:size + 16]).astype(jnp.int32) - 1
     for s in range(count):
         offsets[s, NEAR] = noted(from_near.at[s])
@@ -179,15 +186,24 @@
         offsets[s, RIGHT] = own_offsets[s, 1]
 
 
+def split_kernel(block, *outs):
+    for s in range(block.shape[0]):
+        for i in range(0, block.shape[1], 256):
+            for half, pair in zip(halves(block[s, i:i + 256]), (outs[0::2], outs[1::2])):
+                for out in pair:
+                    out[s, i:i + 256] = half
+
+
 def sum_kernel(parts, *refs):
     refs[parts + (len(refs) - parts - 1) // 2][...] = functools.reduce(jnp.add, [r[...] for r in refs[:parts]])
 
 
 def stack_kernel(parts, *refs):
     out = refs[parts + (len(refs) - parts - 1) // 2]
-    size = refs[0].shape[0]
-    for i in range(parts):
-        out[i * size:(i + 1) * size] = refs[i][...]
+    at = 0
+    for ref in refs[:parts]:
+        out[at:at + ref.shape[0]] = ref[...]
+        at += ref.shape[0]
 
 
 def room(*shapes):
@@ -211,9 +227,9 @@
     )(*parts, *through)
 
 
-def apply_flexibility(loads, fetched, coupling, height, outs, scratch, rr_rows):
-    near, far, sides, to_left, to_right, terms = outs
-    split, a_high, a_low, flexibility = scratch["split"][0:4]
+def apply_flexibility(loads, side, a_high, a_low, coupling, height, outs, split, rr_rows):
+    near, far, sides, inside, across, terms = outs
+    odd = side[0] == 1
     count, size = len(loads), loads[0][0].shape[0]
     for s in range(count):
         for face in range(4):
@@ -228,9 +244,6 @@
         mine = both[0:width, 0:128] + both[0:width, 128:256] + both[width:, 0:128]
         terms[s * height:s * height + width] += mine
     for s in range(count):
-        for i in range(0, a_high.shape[1], size):
-            fetched(s, i // size)
-            a_high[s, i:i + size], a_low[s, i:i + size] = halves(flexibility[s, i:i + size])
         whole = dot(a_high[s], split[s])
         whole = whole[:, 0:128] + whole[:, 128:256] + dot(a_low[s], split[s, :, 0:128])
         for face in range(4):
@@ -242,10 +255,9 @@
                 far[s] = product
             else:
                 sides[s, face - 2] = product
-                if face == LEFT and s == 0:
-                    to_left[0:size] = product
-                if face == RIGHT and s == count - 1:
-                    to_right[...] = product
+    left, right = sides[0, 0], sides[count - 1, 1]
+    inside[0:size] = jnp.where(odd, left, right)
+    across[0:size] = jnp.where(odd, right, left)
     squares = jnp.zeros((1, 128), F32)
     for s in range(count):
         for face in (FAR, RIGHT):
@@ -258,14 +270,15 @@
     k_high, k_low = matrix
     ct_own, ct_left, ct_right = spread
     near, far, sides = product
-    from_near, from_far, from_left, from_right = received
+    from_near, from_far, across = received
     count, size = far.shape[0], far.shape[1]
     side, mine, theirs = terms
     odd = side[0] == 1
     stacked, table = scratch["stack"], scratch["values"]
     span = count * height
-    chips = scratch["chips"]
-    stride = mine.shape[0] // chips
+    chips, stride = scratch["chips"], scratch["stride"]
+    inside, across = theirs[chips * stride:chips * stride + size], across[0:size]
+    from_left, from_right = jnp.where(odd, inside, across), jnp.where(odd, across, inside)
     terms = [x[k * stride:k * stride + span + height] for x in (mine, theirs) for k in range(chips)]
     norm = functools.reduce(jnp.add, [t[rr_rows:rr_rows + 1] for t in terms])
     energy = functools.reduce(jnp.add, [t[rr_rows + 1:rr_rows + 2] for t in terms])
@@ -307,9 +320,9 @@
         other[s][FAR] = from_far[s, 0:size] + parts[4]
         if NEAR in faces:
             other[s][NEAR] = from_near[s] + parts[5]
-    other[count - 1][RIGHT] = from_right[0:size] + dot(ct_right[...], tripled(count))
+    other[count - 1][RIGHT] = from_right + dot(ct_right[...], tripled(count))
     if LEFT in faces:
-        other[0][LEFT] = from_left[...] + dot(ct_left[...], tripled(-1))
+        other[0][LEFT] = from_left + dot(ct_left[...], tripled(-1))
     for s in range(count):
         if s + 1 < count:
             other[s][RIGHT] = own[s + 1][LEFT]
@@ -326,21 +339,12 @@
     return result, norm, energy
 
 
-def fetch(source, to, sems, size):
-    copies = {}
-    for s in range(source.shape[0]):
-        for i in range(source.shape[1] // size):
-            rows = pl.ds(i * size, size)
-            copies[s, i] = pltpu.make_async_copy(source.at[s, rows], to.at[s, rows], sems.at[s, i])
-            copies[s, i].start()
-    return lambda s, i: copies[s, i].wait()
-
-
-def first_kernel(height, rr_rows, residual, from_near, from_left, inner, coupling, corner, flexibility, c_rows, *rest):
-    outs, loads_out, split = rest[0:6], rest[6], rest[7:12]
-    near, to_left, terms = outs[0], outs[3], outs[5]
+def first_kernel(
+    height, rr_rows, side, residual, from_near, from_left, inner, coupling, corner, a_high, a_low, c_rows, *rest
+):
+    outs, loads_out, split = rest[0:6], rest[6], rest[7]
+    near, inside, across, terms = outs[0], outs[3], outs[4], outs[5]
     count, size = residual.shape[0], residual.shape[2]
-    fetched = fetch(flexibility, split[3], split[4], size)
     loads = []
     for s in range(count):
         left = from_left[0:size] if s == 0 else inner[s - 1]
@@ -348,37 +352,35 @@
         for face in range(4):
             loads_out[s, face] = loads[s][face]
         put_coupling(near.at[s], size, coupling[s, :, NEAR * size:(NEAR + 1) * size], 0.0)
-    put_coupling(to_left, size, coupling[0, :, LEFT * size:(LEFT + 1) * size], 0.0)
-    apply_flexibility(loads, fetched, c_rows, height, outs, dict(split=split), rr_rows)
+    for ref in (inside, across):
+        put_coupling(ref, size, coupling[0, :, LEFT * size:(LEFT + 1) * size], 0.0)
+    apply_flexibility(loads, side, a_high, a_low, c_rows, height, outs, split, rr_rows)
     terms[(count + 1) * height:] = corner[...]
 
 
-def step_kernel(which, chips, height, rr_rows, *refs):
+def step_kernel(which, chips, stride, height, rr_rows, *refs):
     refs = list(refs)
     take = lambda number: [refs.pop(0) for _ in range(number)]
     last = which == ITERS - 1
     (offsets,) = take(1)
     terms = take(3)
-    matrix, spread, product, received = take(2), take(3), take(3), take(4)
+    matrix, spread, product, received = take(2), take(3), take(3), take(3)
     (loads,) = take(1)
     map_before, ways, found, scalars = (take(4) if which > 0 else [None] * 4)
     if not last:
-        coupling, flexibility = take(2)
+        a_high, a_low, coupling = take(3)
         outs = take(6)
         loads_out, map_out = take(2)
         ways_out, found_out = take(2) if which > 0 else (None, None)
         (scalars_out,) = take(1)
-        stack, values, turn, *split = take(8)
+        stack, values, turn, split = take(4)
         faces = (NEAR, FAR, LEFT, RIGHT)
     else:
         found_out, residual_out = take(2)
         stack, values, turn = take(3)
         faces = (FAR, RIGHT)
     count, size = loads.shape[0], loads.shape[2]
-    scratch = dict(stack=stack, values=values, turn=turn, chips=chips)
-    if not last:
-        scratch["split"] = split
-        fetched = fetch(flexibility, split[3], split[4], size)
+    scratch = dict(stack=stack, values=values, turn=turn, chips=chips, stride=stride)
     mapped, norm, energy = finish_operator(
         offsets, terms, matrix, spread, product, received, height, rr_rows, scratch, faces
     )
@@ -415,7 +417,7 @@
                     ways_out[s, i] = way
     if not last:
         scalars_out[...] = jnp.concatenate([norm, step, jnp.zeros((6, 128), F32)], axis=0)
-        apply_flexibility(fresh, fetched, coupling, height, outs, scratch, rr_rows)
+        apply_flexibility(fresh, terms[0], a_high, a_low, coupling, height, outs, split, rr_rows)
 
 
 def corner_tables(cuts, height):
@@ -480,28 +482,37 @@
     )(at, offsets, corner_map, gap, jnp.swapaxes(coupling, 0, 1), jnp.swapaxes(corner_rows, 0, 1), rows_table)
     from_near = shifted(to_far, "cuts", 1, False)
     from_left = shifted(to_right, "blk", 1, True)
+    a_shape = jax.ShapeDtypeStruct(flexibility.shape, BF16)
+    first_high, first_low, a_high, a_low = pl.pallas_call(
+        split_kernel,
+        out_shape=(a_shape,) * 4,
+        in_specs=[VMEM],
+        out_specs=(VMEM,) * 4,
+        compiler_params=room(flexibility, *[a_shape] * 4),
+        cost_estimate=pl.CostEstimate(flops=0, bytes_accessed=12 * flexibility.size, transcendentals=0),
+        name="split",
+    )(flexibility)
+
     flops = 2 * count * total * total * loads_n * 3
     cost = pl.CostEstimate(flops=flops, bytes_accessed=4 * flexibility.size, transcendentals=0)
     terms_shape = shape((count + 1) * height, loads_n)
     sends = (faces, faces, pair, face, face, terms_shape)
     first_terms = shape((count + 1) * height + corner_size, loads_n)
-    first_sends = (long_faces, faces, pair, long_face, face, first_terms)
-    a_buffers = [pltpu.VMEM((count, total, 2 * loads_n), BF16)] + [pltpu.VMEM(flexibility.shape, BF16)] * 2 + [
-        pltpu.VMEM(flexibility.shape, F32), pltpu.SemaphoreType.DMA((count, total // size))
-    ]
+    first_sends = (long_faces, faces, pair, long_face, long_face, first_terms)
+    a_buffers = [pltpu.VMEM((count, total, 2 * loads_n), BF16)]
     f_buffers = [
         pltpu.VMEM((blocks * count * height, loads_n), F32),
         pltpu.VMEM((blocks * count * height, loads_n), F32),
         pltpu.VMEM((count, 4, 2 * size, loads_n), F32),
     ]
-    first_args = (residual, from_near, from_left, inner, c_keep, corner, flexibility, c_rows)
+    first_args = (side, residual, from_near, from_left, inner, c_keep, corner, first_high, first_low, c_rows)
     *out, loads = pl.pallas_call(
         functools.partial(first_kernel, height, rr_rows),
         out_shape=first_sends + (four,),
-        in_specs=[VMEM] * 6 + [HBM, VMEM],
+        in_specs=[SMEM] + [VMEM] * 9,
         out_specs=(VMEM,) * 7,
         scratch_shapes=a_buffers,
-        compiler_params=room(*first_args[:6], c_rows, *first_sends, four, *a_buffers[:-1]),
+        compiler_params=room(*first_args[1:], *first_sends, four, *a_buffers),
         cost_estimate=cost,
         name="first",
     )(*first_args)
@@ -509,18 +520,15 @@
     state = []
     for which in range(ITERS):
         last = which == ITERS - 1
-        near, far, sides, to_left, to_right, terms = out
+        near, far, sides, inside, across, terms = out
         pieces = [terms] + [shifted(terms, "cuts", k, True) for k in range(1, cuts)]
-        r_right = shifted(to_left, "blk", -1, True)
-        through = [near, r_right]
-        if not last:
-            through.append(shifted(to_right, "blk", 1, True))
-        terms, near, r_right, *r_left = relay(sum_kernel, pieces, terms, through, f"sum{which}")
-        r_left = to_right if last else r_left[0]
+        across = chip_neighbour(across, "blk")
+        terms, near, across = relay(sum_kernel, pieces, terms, [near, across], f"sum{which}")
         r_far = shifted(near, "cuts", -1, False)
         pieces = chip_parts(terms, "blk")
+        stacked = blocks // 2 * terms.shape[0]
         mine, far = relay(
-            stack_kernel, pieces, shape(blocks // 2 * terms.shape[0], loads_n), [far], f"stack{which}"
+            stack_kernel, [*pieces, inside], shape(stacked + inside.shape[0], loads_n), [far], f"stack{which}"
         )
         r_near = far if last else shifted(far, "cuts", 1, False)
         theirs = swapped(mine, "blk")
@@ -528,7 +536,7 @@
             k_shape = shape(blocks * count * height, blocks * count * height, kind=BF16)
             held = [pltpu.VMEM((k_shape.shape[0], 128 * (dofs // 128 + 1)), kind) for kind in (F32, BF16)]
             k_high, k_low = pl.pallas_call(
-                functools.partial(matrix_kernel, cuts, dofs, height, count, blocks // 2),
+                functools.partial(matrix_kernel, cuts, dofs, height, count, blocks // 2, terms.shape[0]),
                 out_shape=(k_shape, k_shape),
                 in_specs=[VMEM] * 2,
                 out_specs=(VMEM,) * 2,
@@ -537,35 +545,35 @@
                 name="matrix",
             )(mine, theirs)
             ct_own, ct_left, ct_right, all_offsets = pl.pallas_call(
-                spread_kernel,
+                functools.partial(spread_kernel, stacked),
                 out_shape=(
                     shape(count, 6 * size, 6 * height, kind=BF16),
                     shape(size, 6 * height, kind=BF16),
                     shape(size, 6 * height, kind=BF16),
                     shape(count, 4, kind=jnp.int32),
                 ),
-                in_specs=[SMEM] * 2 + [VMEM] * 6,
+                in_specs=[SMEM] * 3 + [VMEM] * 7,
                 out_specs=(VMEM,) * 3 + (SMEM,),
-                compiler_params=room(c_keep, from_near, r_far, from_left, r_right, table, *[faces] * 6),
+                compiler_params=room(c_keep, from_near, r_far, from_left, across, theirs, table, *[faces] * 6),
                 name="spread",
-            )(at, own_offsets, c_keep, from_near, r_far, from_left, r_right, table)
+            )(at, side, own_offsets, c_keep, from_near, r_far, from_left, across, theirs, table)
         args = [all_offsets, side, mine, theirs, k_high, k_low, ct_own, ct_left, ct_right, near, far, sides,
-                r_near, r_far, r_left, r_right, loads, *state]
+                r_near, r_far, across, loads, *state]
         specs = [SMEM, SMEM] + [VMEM] * (len(args) - 2)
         if last:
             outs, scratch = (pair, pair), f_buffers
         else:
-            args += [c_rows, flexibility]
-            specs += [VMEM, HBM]
+            args += [a_high, a_low, c_rows]
+            specs += [VMEM] * 3
             outs = sends + (four, four) + ((pair, pair) if which > 0 else ()) + (shape(8, loads_n),)
             scratch = f_buffers + a_buffers
         result = pl.pallas_call(
-            functools.partial(step_kernel, which, blocks // 2, height, rr_rows),
+            functools.partial(step_kernel, which, blocks // 2, terms.shape[0], height, rr_rows),
             out_shape=outs,
             in_specs=specs,
             out_specs=(VMEM,) * len(outs),
             scratch_shapes=scratch,
-            compiler_params=room(*args[2:] if last else args[2:-1], *outs, *(scratch if last else scratch[:-1])),
+            compiler_params=room(*args[2:], *outs, *scratch),
             cost_estimate=None if last else cost,
             name=f"step{which}",
         )(*args)

time: 126 us -> 124 us (0.984)
  Pallas kernels: 23.3 us -> 18.7 us
  local copies, waits for them, and re-layouts: 16.1 us -> 20.6 us
    unnamed x24 -> x32, local copies, waits for them, and re-layouts: 16.1 us -> 20.6 us
    ppermute x30 -> x25, starting transfers between devices: 48.5 us -> 44.5 us  [shifted(): return lax.ppermute(value, axis, pairs)]
    ppermute x0 -> x3, starting transfers between devices: none -> 3.73 us  [chip_neighbour(): return lax.ppermute(value, axis, pairs)]
    pallas_call x4 -> x5, Pallas kernels: 16.7 us -> 14.2 us  [the longest x3 11.3 us: per_device(): pl.pallas_call(functools.partial(step_kernel, which, blocks // 2, terms.s...]
    pallas_call x1, Pallas kernels: 4.73 us -> 2.6 us  [per_device(): pl.pallas_call(functools.partial(first_kernel, height, rr_rows), out_shap...]
    ppermute x30 -> x25, waiting for transfers between devices: 31.7 us -> 31.5 us  [shifted(): return lax.ppermute(value, axis, pairs)]
  transfers between devices with their start and end apart: 33 -> 31, of which waited for: 19 -> 20; matrix products, arithmetic and copies ran while one was open for 0% -> 0% of each run, Pallas kernels for 2% -> 3%
where the time goes in v6:
time: 124 us; the launch traced here: 123 us
  starting transfers between devices  48.4 us (39%)
  waiting for transfers between devices  34.5 us (28%)
  local copies, waits for them, and re-layouts  20.6 us (17%)
  Pallas kernels  18.7 us (15%)
    ppermute x25, starting transfers between devices, shifted(): return lax.ppermute(value, axis, pairs)  44.5 us
    ppermute x25, waiting for transfers between devices, shifted(): return lax.ppermute(value, axis, pairs)  31.5 us
    unnamed x32, local copies, waits for them, and re-layouts  20.6 us
    pallas_call x3, Pallas kernels, per_device(): pl.pallas_call(functools.partial(step_kernel, which, blocks // 2, terms.s...  11.3 us
    ppermute x3, starting transfers between devices, chip_neighbour(): return lax.ppermute(value, axis, pairs)  3.73 us
    ppermute x3, waiting for transfers between devices, swapped(): lax.ppermute(value, axis, [(source, source ^ 1) for source in range(lax.a...  2.95 us
    pallas_call x1, Pallas kernels, per_device(): pl.pallas_call(functools.partial(first_kernel, height, rr_rows), out_shap...  2.6 us
  transfers between devices with their start and end apart: 31, of which 20 were waited for; matrix products, arithmetic and copies ran while one was open for 0% of the time, Pallas kernels for 3%

profile of v6, /device:TPU:0, one launch (start us, length us, event | category | flops | bytes accessed | tf_op | source)
XLA Modules:
  0.0 123.1 jit_solution(482622497943062595)
XLA Ops:
  7.0 4.9 %collective-permute-start = (f32[2,288,128]{2,1,0:T(8,128)S(1)}, f32[2,288,128]{2,1,0:T(8,128)S(1)}, u32[]{:S(2)}, u32[]{:S(2)}) collective-permute-start(f32[2,288,128]{2,1,0:T(8,128)S(1)} %get-tuple-element.66), channel_id=1, source_target_pairs={{0,8},{8,16},{16,24},{1,9},{9,17},{17,25},{2,10},{10,18},{18,26},{... | collective-permute-start | bytes 884744 | tf_op jit(solution)/shard_map/ppermute | solution.py:26
  11.9 3.4 %copy-done.4 = f32[1,2,1024,1024]{3,2,1,0:T(8,128)S(1)} copy-done((f32[1,2,1024,1024]{3,2,1,0:T(8,128)S(1)}, f32[1,2,1024,1024]{3,2,1,0:T(8,128)}, u32[]{:S(2)}) %copy-start.4) | copy-done | bytes 8388632
  16.7 2.0 %copy-done = bf16[2,1024,1024]{2,1,0:T(8,128)(2,1)} copy-done((bf16[2,1024,1024]{2,1,0:T(8,128)(2,1)}, bf16[2,1024,1024]{2,1,0:T(8,128)(2,1)S(1)}, u32[]{:S(2)}) %copy-start) | copy-done | bytes 4194328
  18.7 2.0 %copy-done.2 = bf16[2,1024,1024]{2,1,0:T(8,128)(2,1)} copy-done((bf16[2,1024,1024]{2,1,0:T(8,128)(2,1)}, bf16[2,1024,1024]{2,1,0:T(8,128)(2,1)S(1)}, u32[]{:S(2)}) %copy-start.2) | copy-done | bytes 4194328
  20.7 2.1 %copy-done.5 = bf16[2,1024,1024]{2,1,0:T(8,128)(2,1)} copy-done((bf16[2,1024,1024]{2,1,0:T(8,128)(2,1)}, bf16[2,1024,1024]{2,1,0:T(8,128)(2,1)S(1)}, u32[]{:S(2)}) %copy-start.5) | copy-done | bytes 4194328
  22.8 1.9 %copy-done.7 = bf16[2,1024,1024]{2,1,0:T(8,128)(2,1)} copy-done((bf16[2,1024,1024]{2,1,0:T(8,128)(2,1)}, bf16[2,1024,1024]{2,1,0:T(8,128)(2,1)S(1)}, u32[]{:S(2)}) %copy-start.7) | copy-done | bytes 4194328
  24.7 2.2 %copy-done.6 = bf16[2,1024,1024]{2,1,0:T(8,128)(2,1)S(1)} copy-done((bf16[2,1024,1024]{2,1,0:T(8,128)(2,1)S(1)}, bf16[2,1024,1024]{2,1,0:T(8,128)(2,1)}, u32[]{:S(2)}) %copy-start.6) | copy-done | bytes 4194328
  26.9 2.2 %copy-done.8 = bf16[2,1024,1024]{2,1,0:T(8,128)(2,1)S(1)} copy-done((bf16[2,1024,1024]{2,1,0:T(8,128)(2,1)S(1)}, bf16[2,1024,1024]{2,1,0:T(8,128)(2,1)}, u32[]{:S(2)}) %copy-start.8) | copy-done | bytes 4194328
  29.1 2.6 %first.1 = (f32[2,288,128]{2,1,0:T(8,128)S(1)}, f32[2,256,128]{2,1,0:T(8,128)S(1)}, f32[2,2,256,128]{3,2,1,0:T(8,128)S(1)}, f32[288,128]{1,0:T(8,128)S(1)}, f32[...) custom-call(s32[1]{0:T(128)} %bitcast.1.side.refs_1_, ...), custom_call_target="tpu_custom_call" | custom-call | flops 1610612736 | bytes 8388608 | tf_op jit(solution)/shard_map/first/pallas_call | solution.py:509
  31.7 3.6 %collective-permute-start.5 = (f32[288,128]{1,0:T(8,128)S(1)}, f32[288,128]{1,0:T(8,128)S(1)}, u32[]{:S(2)}, u32[]{:S(2)}) collective-permute-start(f32[288,128]{1,0:T(8,128)S(1)} %get-tuple-element.76), channel_id=1, source_target_pairs={{0,7},{1,2},{2,1},{3,4},{4,3},{5,6},{6,5},{7,0},{8,15},{9,10},{10,... | collective-permute-start | bytes 442376 | tf_op jit(solution)/shard_map/ppermute | solution.py:48
  35.6 2.6 %collective-permute-start.3 = (f32[96,128]{1,0:T(8,128)S(1)}, f32[96,128]{1,0:T(8,128)S(1)}, u32[]{:S(2)}, u32[]{:S(2)}) collective-permute-start(f32[96,128]{1,0:T(8,128)S(1)} %get-tuple-element.74.refs_0_), channel_id=1, source_target_pairs={{0,16},{8,24},{16,0},{24,8},{1,17},{9,25},{17,1},{25,9},{2,18},{10... | collective-permute-start | bytes 147464 | tf_op jit(solution)/shard_map/ppermute | solution.py:26
  40.4 2.8 %collective-permute-done.2.refs_1_ = f32[96,128]{1,0:T(8,128)S(1)} collective-permute-done((f32[96,128]{1,0:T(8,128)S(1)}, f32[96,128]{1,0:T(8,128)S(1)}, u32[]{:S(2)}, u32[]{:S(2)}) %collective-permute-start.2) | collective-permute-done | bytes 49184 | tf_op jit(solution)/shard_map/ppermute | solution.py:26
  43.2 1.9 %collective-permute-start.9 = (f32[96,128]{1,0:T(8,128)S(1)}, f32[96,128]{1,0:T(8,128)S(1)}, u32[]{:S(2)}, u32[]{:S(2)}) collective-permute-start(f32[96,128]{1,0:T(8,128)S(1)} %get-tuple-element.79.refs_0_), channel_id=1, source_target_pairs={{0,6},{1,7},{2,0},{3,1},{4,2},{5,3},{6,4},{7,5},{8,14},{9,15},{10,... | collective-permute-start | bytes 147464 | tf_op jit(solution)/shard_map/ppermute | solution.py:26
  47.8 2.5 %collective-permute-done.8.refs_2_ = f32[96,128]{1,0:T(8,128)S(1)} collective-permute-done((f32[96,128]{1,0:T(8,128)S(1)}, f32[96,128]{1,0:T(8,128)S(1)}, u32[]{:S(2)}, u32[]{:S(2)}) %collective-permute-start.8) | collective-permute-done | bytes 49184 | tf_op jit(solution)/shard_map/ppermute | solution.py:26
  52.4 4.6 %collective-permute-start.11 = (f32[2,256,128]{2,1,0:T(8,128)S(1)}, f32[2,256,128]{2,1,0:T(8,128)S(1)}, u32[]{:S(2)}, u32[]{:S(2)}) collective-permute-start(f32[2,256,128]{2,1,0:T(8,128)S(1)} %get-tuple-element.89.refs_10_), channel_id=1, source_target_pairs={{0,8},{8,16},{16,24},{1,9},{9,17},{17,25},{2,10},{10,18},{18,26},{... | collective-permute-start | bytes 786440 | tf_op jit(solution)/shard_map/ppermute | solution.py:26
  57.3 5.5 %collective-permute-done.6.from_far.refs_13_ = f32[2,288,128]{2,1,0:T(8,128)S(1)} collective-permute-done((f32[2,288,128]{2,1,0:T(8,128)S(1)}, f32[2,288,128]{2,1,0:T(8,128)S(1)}, u32[]{:S(2)}, u32[]{:S(2)}) %collective-permute-start.6) | collective-permute-done | bytes 294944 | tf_op jit(solution)/shard_map/ppermute | solution.py:26
  64.3 4.5 %step0.1 = (f32[2,256,128]{2,1,0:T(8,128)S(1)}, f32[2,256,128]{2,1,0:T(8,128)S(1)}, f32[2,2,256,128]{3,2,1,0:T(8,128)S(1)}, f32[256,128]{1,0:T(8,128)S(1)}, f32[...) custom-call(s32[2,4]{1,0:T(2,128)S(1)} %get-tuple-element.83.refs_0_, ...), custom_call_target="tpu_custom_call" | custom-call | flops 1610612736 | bytes 8388608 | tf_op jit(solution)/shard_map/step0/pallas_call | solution.py:570
  68.9 4.5 %collective-permute-start.14 = (f32[48,128]{1,0:T(8,128)S(1)}, f32[48,128]{1,0:T(8,128)S(1)}, u32[]{:S(2)}, u32[]{:S(2)}) collective-permute-start(f32[48,128]{1,0:T(8,128)S(1)} %get-tuple-element.94.refs_0_), channel_id=1, source_target_pairs={{0,24},{8,0},{16,8},{24,16},{1,25},{9,1},{17,9},{25,17},{2,26},{10... | collective-permute-start | bytes 73736 | tf_op jit(solution)/shard_map/ppermute | solution.py:26
  74.1 2.0 %collective-permute-start.12 = (f32[48,128]{1,0:T(8,128)S(1)}, f32[48,128]{1,0:T(8,128)S(1)}, u32[]{:S(2)}, u32[]{:S(2)}) collective-permute-start(f32[48,128]{1,0:T(8,128)S(1)} %get-tuple-element.94.refs_0_), channel_id=1, source_target_pairs={{0,8},{8,16},{16,24},{24,0},{1,9},{9,17},{17,25},{25,1},{2,10},{10... | collective-permute-start | bytes 73736 | tf_op jit(solution)/shard_map/ppermute | solution.py:26
  78.8 1.8 %collective-permute-start.18 = (f32[48,128]{1,0:T(8,128)S(1)}, f32[48,128]{1,0:T(8,128)S(1)}, u32[]{:S(2)}, u32[]{:S(2)}) collective-permute-start(f32[48,128]{1,0:T(8,128)S(1)} %get-tuple-element.97.refs_0_), channel_id=1, source_target_pairs={{0,6},{1,7},{2,0},{3,1},{4,2},{5,3},{6,4},{7,5},{8,14},{9,15},{10,... | collective-permute-start | bytes 73736 | tf_op jit(solution)/shard_map/ppermute | solution.py:26
  83.4 2.0 %collective-permute-done.17.refs_2_ = f32[48,128]{1,0:T(8,128)S(1)} collective-permute-done((f32[48,128]{1,0:T(8,128)S(1)}, f32[48,128]{1,0:T(8,128)S(1)}, u32[]{:S(2)}, u32[]{:S(2)}) %collective-permute-start.17) | collective-permute-done | bytes 24608 | tf_op jit(solution)/shard_map/ppermute | solution.py:26
  85.4 1.8 %collective-permute-done.16.refs_1_ = f32[48,128]{1,0:T(8,128)S(1)} collective-permute-done((f32[48,128]{1,0:T(8,128)S(1)}, f32[48,128]{1,0:T(8,128)S(1)}, u32[]{:S(2)}, u32[]{:S(2)}) %collective-permute-start.16) | collective-permute-done | bytes 24608 | tf_op jit(solution)/shard_map/ppermute | solution.py:26
  87.2 3.2 %collective-permute-start.20 = (f32[2,256,128]{2,1,0:T(8,128)S(1)}, f32[2,256,128]{2,1,0:T(8,128)S(1)}, u32[]{:S(2)}, u32[]{:S(2)}) collective-permute-start(f32[2,256,128]{2,1,0:T(8,128)S(1)} %get-tuple-element.102.refs_10_), channel_id=1, source_target_pairs={{0,8},{8,16},{16,24},{1,9},{9,17},{17,25},{2,10},{10,18},{18,26},{... | collective-permute-start | bytes 786440 | tf_op jit(solution)/shard_map/ppermute | solution.py:26
  92.3 1.8 %collective-permute-done.20.refs_12_ = f32[2,256,128]{2,1,0:T(8,128)S(1)} collective-permute-done((f32[2,256,128]{2,1,0:T(8,128)S(1)}, f32[2,256,128]{2,1,0:T(8,128)S(1)}, u32[]{:S(2)}, u32[]{:S(2)}) %collective-permute-start.20) | collective-permute-done | bytes 262176 | tf_op jit(solution)/shard_map/ppermute | solution.py:26
  94.1 4.6 %step1.1 = (f32[2,256,128]{2,1,0:T(8,128)S(1)}, f32[2,256,128]{2,1,0:T(8,128)S(1)}, f32[2,2,256,128]{3,2,1,0:T(8,128)S(1)}, f32[256,128]{1,0:T(8,128)S(1)}, f32[...) custom-call(s32[2,4]{1,0:T(2,128)S(1)} %get-tuple-element.83.refs_0_, ...), custom_call_target="tpu_custom_call" | custom-call | flops 1610612736 | bytes 8388608 | tf_op jit(solution)/shard_map/step1/pallas_call | solution.py:570
  98.7 5.4 %collective-permute-start.24 = (f32[48,128]{1,0:T(8,128)S(1)}, f32[48,128]{1,0:T(8,128)S(1)}, u32[]{:S(2)}, u32[]{:S(2)}) collective-permute-start(f32[48,128]{1,0:T(8,128)S(1)} %get-tuple-element.108.refs_0_), channel_id=1, source_target_pairs={{0,24},{8,0},{16,8},{24,16},{1,25},{9,1},{17,9},{25,17},{2,26},{10... | collective-permute-start | bytes 73736 | tf_op jit(solution)/shard_map/ppermute | solution.py:26
  104.2 2.0 %collective-permute-start.22 = (f32[48,128]{1,0:T(8,128)S(1)}, f32[48,128]{1,0:T(8,128)S(1)}, u32[]{:S(2)}, u32[]{:S(2)}) collective-permute-start(f32[48,128]{1,0:T(8,128)S(1)} %get-tuple-element.108.refs_0_), channel_id=1, source_target_pairs={{0,8},{8,16},{16,24},{24,0},{1,9},{9,17},{17,25},{25,1},{2,10},{10... | collective-permute-start | bytes 73736 | tf_op jit(solution)/shard_map/ppermute | solution.py:26
  106.2 1.8 %collective-permute-done.23.refs_2_ = f32[48,128]{1,0:T(8,128)S(1)} collective-permute-done((f32[48,128]{1,0:T(8,128)S(1)}, f32[48,128]{1,0:T(8,128)S(1)}, u32[]{:S(2)}, u32[]{:S(2)}) %collective-permute-start.23) | collective-permute-done | bytes 24608 | tf_op jit(solution)/shard_map/ppermute | solution.py:26
  110.3 2.5 %collective-permute-start.28 = (f32[48,128]{1,0:T(8,128)S(1)}, f32[48,128]{1,0:T(8,128)S(1)}, u32[]{:S(2)}, u32[]{:S(2)}) collective-permute-start(f32[48,128]{1,0:T(8,128)S(1)} %get-tuple-element.111.refs_0_), channel_id=1, source_target_pairs={{0,6},{1,7},{2,0},{3,1},{4,2},{5,3},{6,4},{7,5},{8,14},{9,15},{10,... | collective-permute-start | bytes 73736 | tf_op jit(solution)/shard_map/ppermute | solution.py:26
  114.3 3.2 %collective-permute-done.27.refs_2_ = f32[48,128]{1,0:T(8,128)S(1)} collective-permute-done((f32[48,128]{1,0:T(8,128)S(1)}, f32[48,128]{1,0:T(8,128)S(1)}, u32[]{:S(2)}, u32[]{:S(2)}) %collective-permute-start.27) | collective-permute-done | bytes 24608 | tf_op jit(solution)/shard_map/ppermute | solution.py:26
  117.5 1.7 %collective-permute-done.26.refs_1_ = f32[48,128]{1,0:T(8,128)S(1)} collective-permute-done((f32[48,128]{1,0:T(8,128)S(1)}, f32[48,128]{1,0:T(8,128)S(1)}, u32[]{:S(2)}, u32[]{:S(2)}) %collective-permute-start.26) | collective-permute-done | bytes 24608 | tf_op jit(solution)/shard_map/ppermute | solution.py:26
  120.8 2.3 %step2.1 = (f32[2,2,256,128]{3,2,1,0:T(8,128)}, f32[2,2,256,128]{3,2,1,0:T(8,128)}) custom-call(s32[2,4]{1,0:T(2,128)S(1)} %get-tuple-element.83.refs_0_, s32[1]{0:T(128)} %bitcast.1.side.refs_1_, f32[448,128]{1,0:T(8,128)S(1)} %get-tuple-element.114.refs_2_, f32[448,128]{1,0:T(8,128)S(1)} %collective-permute-done.29.refs_3_, ...), custom_call_target="tpu_custom_call" | custom-call | tf_op jit(solution)/shard_map/step2/pallas_call | solution.py:570
  (76 shorter events, 30.5 us)
Async XLA Ops:
  7.0 17.7 %collective-permute-start = (f32[2,288,128]{2,1,0:T(8,128)S(1)}, f32[2,288,128]{2,1,0:T(8,128)S(1)}, u32[]{:S(2)}, u32[]{:S(2)}) collective-permute-start(f32[2,288,128]{2,1,0:T(8,128)S(1)} %get-tuple-element.66), channel_id=1, source_target_pairs={{0,8},{8,16},{16,24},{1,9},{9,17},{17,25},{2,10},{10,18},{18,26},{... | collective-permute-start | bytes 884744 | tf_op jit(solution)/shard_map/ppermute | solution.py:26
  11.8 12.8 %collective-permute-start.1 = (f32[288,128]{1,0:T(8,128)S(1)}, f32[288,128]{1,0:T(8,128)S(1)}, u32[]{:S(2)}, u32[]{:S(2)}) collective-permute-start(f32[288,128]{1,0:T(8,128)S(1)} %get-tuple-element.68), channel_id=1, source_target_pairs={{0,1},{1,2},{2,3},{3,4},{4,5},{5,6},{6,7},{7,0},{8,9},{9,10},{10,1... | collective-permute-start | bytes 442376 | tf_op jit(solution)/shard_map/ppermute | solution.py:26
  29.1 35.3 %copy-start.3 = (bf16[2,1024,1024]{2,1,0:T(8,128)(2,1)S(1)}, bf16[2,1024,1024]{2,1,0:T(8,128)(2,1)}, u32[]{:S(2)}) copy-start(bf16[2,1024,1024]{2,1,0:T(8,128)(2,1)} %copy-done.2) | copy-start | bytes 12582916
  31.7 11.5 %collective-permute-start.5 = (f32[288,128]{1,0:T(8,128)S(1)}, f32[288,128]{1,0:T(8,128)S(1)}, u32[]{:S(2)}, u32[]{:S(2)}) collective-permute-start(f32[288,128]{1,0:T(8,128)S(1)} %get-tuple-element.76), channel_id=1, source_target_pairs={{0,7},{1,2},{2,1},{3,4},{4,3},{5,6},{6,5},{7,0},{8,15},{9,10},{10,... | collective-permute-start | bytes 442376 | tf_op jit(solution)/shard_map/ppermute | solution.py:48
  35.3 4.1 %collective-permute-start.4 = (f32[96,128]{1,0:T(8,128)S(1)}, f32[96,128]{1,0:T(8,128)S(1)}, u32[]{:S(2)}, u32[]{:S(2)}) collective-permute-start(f32[96,128]{1,0:T(8,128)S(1)} %get-tuple-element.74.refs_0_), channel_id=1, source_target_pairs={{0,24},{8,0},{16,8},{24,16},{1,25},{9,1},{17,9},{25,17},{2,26},{10... | collective-permute-start | bytes 147464 | tf_op jit(solution)/shard_map/ppermute | solution.py:26
  35.6 4.8 %collective-permute-start.3 = (f32[96,128]{1,0:T(8,128)S(1)}, f32[96,128]{1,0:T(8,128)S(1)}, u32[]{:S(2)}, u32[]{:S(2)}) collective-permute-start(f32[96,128]{1,0:T(8,128)S(1)} %get-tuple-element.74.refs_0_), channel_id=1, source_target_pairs={{0,16},{8,24},{16,0},{24,8},{1,17},{9,25},{17,1},{25,9},{2,18},{10... | collective-permute-start | bytes 147464 | tf_op jit(solution)/shard_map/ppermute | solution.py:26
  38.2 5.0 %collective-permute-start.2 = (f32[96,128]{1,0:T(8,128)S(1)}, f32[96,128]{1,0:T(8,128)S(1)}, u32[]{:S(2)}, u32[]{:S(2)}) collective-permute-start(f32[96,128]{1,0:T(8,128)S(1)} %get-tuple-element.74.refs_0_), channel_id=1, source_target_pairs={{0,8},{8,16},{16,24},{24,0},{1,9},{9,17},{17,25},{25,1},{2,10},{10... | collective-permute-start | bytes 147464 | tf_op jit(solution)/shard_map/ppermute | solution.py:26
  43.2 4.6 %collective-permute-start.9 = (f32[96,128]{1,0:T(8,128)S(1)}, f32[96,128]{1,0:T(8,128)S(1)}, u32[]{:S(2)}, u32[]{:S(2)}) collective-permute-start(f32[96,128]{1,0:T(8,128)S(1)} %get-tuple-element.79.refs_0_), channel_id=1, source_target_pairs={{0,6},{1,7},{2,0},{3,1},{4,2},{5,3},{6,4},{7,5},{8,14},{9,15},{10,... | collective-permute-start | bytes 147464 | tf_op jit(solution)/shard_map/ppermute | solution.py:26
  45.1 5.2 %collective-permute-start.8 = (f32[96,128]{1,0:T(8,128)S(1)}, f32[96,128]{1,0:T(8,128)S(1)}, u32[]{:S(2)}, u32[]{:S(2)}) collective-permute-start(f32[96,128]{1,0:T(8,128)S(1)} %get-tuple-element.79.refs_0_), channel_id=1, source_target_pairs={{0,4},{1,5},{2,6},{3,7},{4,0},{5,1},{6,2},{7,3},{8,12},{9,13},{10,... | collective-permute-start | bytes 147464 | tf_op jit(solution)/shard_map/ppermute | solution.py:26
  45.1 5.9 %collective-permute-start.7 = (f32[96,128]{1,0:T(8,128)S(1)}, f32[96,128]{1,0:T(8,128)S(1)}, u32[]{:S(2)}, u32[]{:S(2)}) collective-permute-start(f32[96,128]{1,0:T(8,128)S(1)} %get-tuple-element.79.refs_0_), channel_id=1, source_target_pairs={{0,2},{1,3},{2,4},{3,5},{4,6},{5,7},{6,0},{7,1},{8,10},{9,11},{10,... | collective-permute-start | bytes 147464 | tf_op jit(solution)/shard_map/ppermute | solution.py:26
  51.0 6.0 %collective-permute-start.10 = (f32[672,128]{1,0:T(8,128)S(1)}, f32[672,128]{1,0:T(8,128)S(1)}, u32[]{:S(2)}, u32[]{:S(2)}) collective-permute-start(f32[672,128]{1,0:T(8,128)S(1)} %get-tuple-element.82.mine.refs_2_), channel_id=1, source_target_pairs={{0,1},{1,0},{2,3},{3,2},{4,5},{5,4},{6,7},{7,6},{8,9},{9,8},{10,11... | collective-permute-start | bytes 1032200 | tf_op jit(solution)/shard_map/ppermute | solution.py:52
  51.1 11.7 %collective-permute-start.6 = (f32[2,288,128]{2,1,0:T(8,128)S(1)}, f32[2,288,128]{2,1,0:T(8,128)S(1)}, u32[]{:S(2)}, u32[]{:S(2)}) collective-permute-start(f32[2,288,128]{2,1,0:T(8,128)S(1)} %get-tuple-element.77.refs_9_), channel_id=1, source_target_pairs={{8,0},{16,8},{24,16},{9,1},{17,9},{25,17},{10,2},{18,10},{26,18},{... | collective-permute-start | bytes 884744 | tf_op jit(solution)/shard_map/ppermute | solution.py:26
  52.4 11.9 %collective-permute-start.11 = (f32[2,256,128]{2,1,0:T(8,128)S(1)}, f32[2,256,128]{2,1,0:T(8,128)S(1)}, u32[]{:S(2)}, u32[]{:S(2)}) collective-permute-start(f32[2,256,128]{2,1,0:T(8,128)S(1)} %get-tuple-element.89.refs_10_), channel_id=1, source_target_pairs={{0,8},{8,16},{16,24},{1,9},{9,17},{17,25},{2,10},{10,18},{18,26},{... | collective-permute-start | bytes 786440 | tf_op jit(solution)/shard_map/ppermute | solution.py:26
  68.8 10.0 %collective-permute-start.15 = (f32[256,128]{1,0:T(8,128)S(1)}, f32[256,128]{1,0:T(8,128)S(1)}, u32[]{:S(2)}, u32[]{:S(2)}) collective-permute-start(f32[256,128]{1,0:T(8,128)S(1)} %get-tuple-element.96), channel_id=1, source_target_pairs={{0,7},{1,2},{2,1},{3,4},{4,3},{5,6},{6,5},{7,0},{8,15},{9,10},{10,... | collective-permute-start | bytes 393224 | tf_op jit(solution)/shard_map/ppermute | solution.py:48
  68.9 7.2 %collective-permute-start.14 = (f32[48,128]{1,0:T(8,128)S(1)}, f32[48,128]{1,0:T(8,128)S(1)}, u32[]{:S(2)}, u32[]{:S(2)}) collective-permute-start(f32[48,128]{1,0:T(8,128)S(1)} %get-tuple-element.94.refs_0_), channel_id=1, source_target_pairs={{0,24},{8,0},{16,8},{24,16},{1,25},{9,1},{17,9},{25,17},{2,26},{10... | collective-permute-start | bytes 73736 | tf_op jit(solution)/shard_map/ppermute | solution.py:26
  73.4 4.1 %collective-permute-start.13 = (f32[48,128]{1,0:T(8,128)S(1)}, f32[48,128]{1,0:T(8,128)S(1)}, u32[]{:S(2)}, u32[]{:S(2)}) collective-permute-start(f32[48,128]{1,0:T(8,128)S(1)} %get-tuple-element.94.refs_0_), channel_id=1, source_target_pairs={{0,16},{8,24},{16,0},{24,8},{1,17},{9,25},{17,1},{25,9},{2,18},{10... | collective-permute-start | bytes 73736 | tf_op jit(solution)/shard_map/ppermute | solution.py:26
  74.1 4.7 %collective-permute-start.12 = (f32[48,128]{1,0:T(8,128)S(1)}, f32[48,128]{1,0:T(8,128)S(1)}, u32[]{:S(2)}, u32[]{:S(2)}) collective-permute-start(f32[48,128]{1,0:T(8,128)S(1)} %get-tuple-element.94.refs_0_), channel_id=1, source_target_pairs={{0,8},{8,16},{16,24},{24,0},{1,9},{9,17},{17,25},{25,1},{2,10},{10... | collective-permute-start | bytes 73736 | tf_op jit(solution)/shard_map/ppermute | solution.py:26
  78.8 4.5 %collective-permute-start.18 = (f32[48,128]{1,0:T(8,128)S(1)}, f32[48,128]{1,0:T(8,128)S(1)}, u32[]{:S(2)}, u32[]{:S(2)}) collective-permute-start(f32[48,128]{1,0:T(8,128)S(1)} %get-tuple-element.97.refs_0_), channel_id=1, source_target_pairs={{0,6},{1,7},{2,0},{3,1},{4,2},{5,3},{6,4},{7,5},{8,14},{9,15},{10,... | collective-permute-start | bytes 73736 | tf_op jit(solution)/shard_map/ppermute | solution.py:26
  80.7 4.7 %collective-permute-start.17 = (f32[48,128]{1,0:T(8,128)S(1)}, f32[48,128]{1,0:T(8,128)S(1)}, u32[]{:S(2)}, u32[]{:S(2)}) collective-permute-start(f32[48,128]{1,0:T(8,128)S(1)} %get-tuple-element.97.refs_0_), channel_id=1, source_target_pairs={{0,4},{1,5},{2,6},{3,7},{4,0},{5,1},{6,2},{7,3},{8,12},{9,13},{10,... | collective-permute-start | bytes 73736 | tf_op jit(solution)/shard_map/ppermute | solution.py:26
  81.5 5.6 %collective-permute-start.16 = (f32[48,128]{1,0:T(8,128)S(1)}, f32[48,128]{1,0:T(8,128)S(1)}, u32[]{:S(2)}, u32[]{:S(2)}) collective-permute-start(f32[48,128]{1,0:T(8,128)S(1)} %get-tuple-element.97.refs_0_), channel_id=1, source_target_pairs={{0,2},{1,3},{2,4},{3,5},{4,6},{5,7},{6,0},{7,1},{8,10},{9,11},{10,... | collective-permute-start | bytes 73736 | tf_op jit(solution)/shard_map/ppermute | solution.py:26
  82.1 10.2 %collective-permute-start.21 = (f32[2,256,128]{2,1,0:T(8,128)S(1)}, f32[2,256,128]{2,1,0:T(8,128)S(1)}, u32[]{:S(2)}, u32[]{:S(2)}) collective-permute-start(f32[2,256,128]{2,1,0:T(8,128)S(1)} %get-tuple-element.101.refs_9_), channel_id=1, source_target_pairs={{8,0},{16,8},{24,16},{9,1},{17,9},{25,17},{10,2},{18,10},{26,18},{... | collective-permute-start | bytes 786440 | tf_op jit(solution)/shard_map/ppermute | solution.py:26
  87.2 6.9 %collective-permute-start.20 = (f32[2,256,128]{2,1,0:T(8,128)S(1)}, f32[2,256,128]{2,1,0:T(8,128)S(1)}, u32[]{:S(2)}, u32[]{:S(2)}) collective-permute-start(f32[2,256,128]{2,1,0:T(8,128)S(1)} %get-tuple-element.102.refs_10_), channel_id=1, source_target_pairs={{0,8},{8,16},{16,24},{1,9},{9,17},{17,25},{2,10},{10,18},{18,26},{... | collective-permute-start | bytes 786440 | tf_op jit(solution)/shard_map/ppermute | solution.py:26
  90.4 1.6 %collective-permute-start.19 = (f32[448,128]{1,0:T(8,128)S(1)}, f32[448,128]{1,0:T(8,128)S(1)}, u32[]{:S(2)}, u32[]{:S(2)}) collective-permute-start(f32[448,128]{1,0:T(8,128)S(1)} %get-tuple-element.100.refs_2_), channel_id=1, source_target_pairs={{0,1},{1,0},{2,3},{3,2},{4,5},{5,4},{6,7},{7,6},{8,9},{9,8},{10,11... | collective-permute-start | bytes 688136 | tf_op jit(solution)/shard_map/ppermute | solution.py:52
  98.7 10.3 %collective-permute-start.25 = (f32[256,128]{1,0:T(8,128)S(1)}, f32[256,128]{1,0:T(8,128)S(1)}, u32[]{:S(2)}, u32[]{:S(2)}) collective-permute-start(f32[256,128]{1,0:T(8,128)S(1)} %get-tuple-element.110), channel_id=1, source_target_pairs={{0,7},{1,2},{2,1},{3,4},{4,3},{5,6},{6,5},{7,0},{8,15},{9,10},{10,... | collective-permute-start | bytes 393224 | tf_op jit(solution)/shard_map/ppermute | solution.py:48
  98.7 7.5 %collective-permute-start.24 = (f32[48,128]{1,0:T(8,128)S(1)}, f32[48,128]{1,0:T(8,128)S(1)}, u32[]{:S(2)}, u32[]{:S(2)}) collective-permute-start(f32[48,128]{1,0:T(8,128)S(1)} %get-tuple-element.108.refs_0_), channel_id=1, source_target_pairs={{0,24},{8,0},{16,8},{24,16},{1,25},{9,1},{17,9},{25,17},{2,26},{10... | collective-permute-start | bytes 73736 | tf_op jit(solution)/shard_map/ppermute | solution.py:26
  104.2 3.8 %collective-permute-start.23 = (f32[48,128]{1,0:T(8,128)S(1)}, f32[48,128]{1,0:T(8,128)S(1)}, u32[]{:S(2)}, u32[]{:S(2)}) collective-permute-start(f32[48,128]{1,0:T(8,128)S(1)} %get-tuple-element.108.refs_0_), channel_id=1, source_target_pairs={{0,16},{8,24},{16,0},{24,8},{1,17},{9,25},{17,1},{25,9},{2,18},{10... | collective-permute-start | bytes 73736 | tf_op jit(solution)/shard_map/ppermute | solution.py:26
  104.2 4.8 %collective-permute-start.22 = (f32[48,128]{1,0:T(8,128)S(1)}, f32[48,128]{1,0:T(8,128)S(1)}, u32[]{:S(2)}, u32[]{:S(2)}) collective-permute-start(f32[48,128]{1,0:T(8,128)S(1)} %get-tuple-element.108.refs_0_), channel_id=1, source_target_pairs={{0,8},{8,16},{16,24},{24,0},{1,9},{9,17},{17,25},{25,1},{2,10},{10... | collective-permute-start | bytes 73736 | tf_op jit(solution)/shard_map/ppermute | solution.py:26
  109.0 11.9 %collective-permute-start.30 = (f32[2,256,128]{2,1,0:T(8,128)S(1)}, f32[2,256,128]{2,1,0:T(8,128)S(1)}, u32[]{:S(2)}, u32[]{:S(2)}) collective-permute-start(f32[2,256,128]{2,1,0:T(8,128)S(1)} %get-tuple-element.115.refs_9_), channel_id=1, source_target_pairs={{8,0},{16,8},{24,16},{9,1},{17,9},{25,17},{10,2},{18,10},{26,18},{... | collective-permute-start | bytes 786440 | tf_op jit(solution)/shard_map/ppermute | solution.py:26
  110.3 4.0 %collective-permute-start.28 = (f32[48,128]{1,0:T(8,128)S(1)}, f32[48,128]{1,0:T(8,128)S(1)}, u32[]{:S(2)}, u32[]{:S(2)}) collective-permute-start(f32[48,128]{1,0:T(8,128)S(1)} %get-tuple-element.111.refs_0_), channel_id=1, source_target_pairs={{0,6},{1,7},{2,0},{3,1},{4,2},{5,3},{6,4},{7,5},{8,14},{9,15},{10,... | collective-permute-start | bytes 73736 | tf_op jit(solution)/shard_map/ppermute | solution.py:26
  112.8 4.7 %collective-permute-start.27 = (f32[48,128]{1,0:T(8,128)S(1)}, f32[48,128]{1,0:T(8,128)S(1)}, u32[]{:S(2)}, u32[]{:S(2)}) collective-permute-start(f32[48,128]{1,0:T(8,128)S(1)} %get-tuple-element.111.refs_0_), channel_id=1, source_target_pairs={{0,4},{1,5},{2,6},{3,7},{4,0},{5,1},{6,2},{7,3},{8,12},{9,13},{10,... | collective-permute-start | bytes 73736 | tf_op jit(solution)/shard_map/ppermute | solution.py:26
  113.6 5.6 %collective-permute-start.26 = (f32[48,128]{1,0:T(8,128)S(1)}, f32[48,128]{1,0:T(8,128)S(1)}, u32[]{:S(2)}, u32[]{:S(2)}) collective-permute-start(f32[48,128]{1,0:T(8,128)S(1)} %get-tuple-element.111.refs_0_), channel_id=1, source_target_pairs={{0,2},{1,3},{2,4},{3,5},{4,6},{5,7},{6,0},{7,1},{8,10},{9,11},{10,... | collective-permute-start | bytes 73736 | tf_op jit(solution)/shard_map/ppermute | solution.py:26
  119.3 1.6 %collective-permute-start.29 = (f32[448,128]{1,0:T(8,128)S(1)}, f32[448,128]{1,0:T(8,128)S(1)}, u32[]{:S(2)}, u32[]{:S(2)}) collective-permute-start(f32[448,128]{1,0:T(8,128)S(1)} %get-tuple-element.114.refs_2_), channel_id=1, source_target_pairs={{0,1},{1,0},{2,3},{3,2},{4,5},{5,4},{6,7},{7,6},{8,9},{9,8},{10,11... | collective-permute-start | bytes 688136 | tf_op jit(solution)/shard_map/ppermute | solution.py:52
  (15 other events, 89.6 us)

commit v7 on v6

--- a/solution.py
+++ b/solution.py
@@ -80,10 +80,10 @@
 
 
 def prepare_kernel(cuts, at, *refs):
-    sources, outs, buffer = refs[0:6], refs[6:14], refs[14]
-    held, sems = refs[15:21], refs[21]
+    sources, outs, buffer = refs[0:5], refs[5:13], refs[13]
+    held, sems, wide = refs[14:19], refs[19], refs[20]
     residual, to_far, to_right, inner, c_rows, c_keep, corner, own_offsets = outs
-    offsets, corner_map, gap, coupling, corner_rows, rows_table = held
+    offsets, corner_map, gap, coupling, corner_rows = held
     copies = [pltpu.make_async_copy(source, to, sems.at[i]) for i, (source, to) in enumerate(zip(sources, held))]
     for copy in copies:
         copy.start()
@@ -108,7 +108,20 @@
                 put_coupling(to_right, size, c_keep[s, :, RIGHT * size:(RIGHT + 1) * size], amount)
             else:
                 inner[s] = turned
-        c_rows[s] = dot(rows_table[at[0]], paired(c_keep[s])).astype(BF16)
+    width = wide.shape[1] // 2
+    wide[...] = jnp.zeros_like(wide)
+    for a in range(cuts):
+
+        @pl.when(at[0] == a)
+        def _():
+            for s in range(count):
+                for k in range(4):
+                    to = (k % 2) * width + 3 * (a - 1 + k // 2)
+                    if a - 1 + k // 2 >= 0:
+                        wide[s, to:to + 3] = c_keep[s, 3 * k:3 * k + 3]
+
+    for s in range(count):
+        c_rows[s, 0:2 * width], c_rows[s, 2 * width:] = halves(wide[s])
     inner[count - 1] = jnp.zeros(inner.shape[1:], F32)
     corner[...] = jnp.zeros_like(corner)
     dofs, rows = corner_rows.shape[2], 3 * cuts
@@ -186,12 +199,24 @@
         offsets[s, RIGHT] = own_offsets[s, 1]
 
 
-def split_kernel(block, *outs):
-    for s in range(block.shape[0]):
-        for i in range(0, block.shape[1], 256):
-            for half, pair in zip(halves(block[s, i:i + 256]), (outs[0::2], outs[1::2])):
-                for out in pair:
-                    out[s, i:i + 256] = half
+def beside(value):
+    return jnp.concatenate(halves(value), axis=1)
+
+
+def three_passes(first, second):
+    high, low = halves(first)
+    both = dot(high, second)
+    return both[:, 0:128] + both[:, 128:256] + dot(low, second[:, 0:128])
+
+
+def own_kernel(residual, flexibility, product):
+    count, size = residual.shape[0], residual.shape[2]
+    for s in range(count):
+        total = None
+        for i, face in enumerate((FAR, RIGHT)):
+            part = three_passes(flexibility[s, :, face * size:(face + 1) * size], beside(residual[s, i]))
+            total = part if total is None else total + part
+        product[s] = total
 
 
 def sum_kernel(parts, *refs):
@@ -227,7 +252,7 @@
     )(*parts, *through)
 
 
-def apply_flexibility(loads, side, a_high, a_low, coupling, height, outs, split, rr_rows):
+def apply_flexibility(loads, side, flexibility, known, coupling, height, outs, split, rr_rows):
     near, far, sides, inside, across, terms = outs
     odd = side[0] == 1
     count, size = len(loads), loads[0][0].shape[0]
@@ -244,8 +269,13 @@
         mine = both[0:width, 0:128] + both[0:width, 128:256] + both[width:, 0:128]
         terms[s * height:s * height + width] += mine
     for s in range(count):
-        whole = dot(a_high[s], split[s])
-        whole = whole[:, 0:128] + whole[:, 128:256] + dot(a_low[s], split[s, :, 0:128])
+        if known is None:
+            whole = three_passes(flexibility[s], split[s])
+        else:
+            whole = known[s]
+            for face in (NEAR, LEFT):
+                part = slice(face * size, (face + 1) * size)
+                whole = whole + three_passes(flexibility[s, :, part], split[s, part])
         for face in range(4):
             product = whole[face * size:(face + 1) * size]
             total = total + jnp.sum(product * loads[s][face], axis=0, keepdims=True)
@@ -340,7 +370,7 @@
 
 
 def first_kernel(
-    height, rr_rows, side, residual, from_near, from_left, inner, coupling, corner, a_high, a_low, c_rows, *rest
+    height, rr_rows, side, residual, from_near, from_left, inner, coupling, corner, known, flexibility, c_rows, *rest
 ):
     outs, loads_out, split = rest[0:6], rest[6], rest[7]
     near, inside, across, terms = outs[0], outs[3], outs[4], outs[5]
@@ -354,7 +384,7 @@
         put_coupling(near.at[s], size, coupling[s, :, NEAR * size:(NEAR + 1) * size], 0.0)
     for ref in (inside, across):
         put_coupling(ref, size, coupling[0, :, LEFT * size:(LEFT + 1) * size], 0.0)
-    apply_flexibility(loads, side, a_high, a_low, c_rows, height, outs, split, rr_rows)
+    apply_flexibility(loads, side, flexibility, known, c_rows, height, outs, split, rr_rows)
     terms[(count + 1) * height:] = corner[...]
 
 
@@ -368,7 +398,7 @@
     (loads,) = take(1)
     map_before, ways, found, scalars = (take(4) if which > 0 else [None] * 4)
     if not last:
-        a_high, a_low, coupling = take(3)
+        flexibility, coupling = take(2)
         outs = take(6)
         loads_out, map_out = take(2)
         ways_out, found_out = take(2) if which > 0 else (None, None)
@@ -417,7 +447,7 @@
                     ways_out[s, i] = way
     if not last:
         scalars_out[...] = jnp.concatenate([norm, step, jnp.zeros((6, 128), F32)], axis=0)
-        apply_flexibility(fresh, terms[0], a_high, a_low, coupling, height, outs, split, rr_rows)
+        apply_flexibility(fresh, terms[0], flexibility, None, coupling, height, outs, split, rr_rows)
 
 
 def corner_tables(cuts, height):
@@ -430,10 +460,8 @@
                     places[at + 1, 3 * k + j, (k % 2) * height + 3 * cycle + j] = 1
     wide = 2 * height
     table = np.zeros((cuts + 2, 32, 3 * wide), np.float32)
-    rows = np.zeros((cuts, 2 * wide, 32), np.float32)
     table[:, 0:12, 0:wide] = table[:, 16:28, wide:2 * wide] = table[:, 0:12, 2 * wide:] = places
-    rows[:, 0:wide, 0:12] = rows[:, wide:, 16:28] = np.swapaxes(places[1:-1], 1, 2)
-    return jnp.asarray(table, BF16), jnp.asarray(rows, BF16)
+    return jnp.asarray(table, BF16)
 
 
 def per_device(gap_load, offsets, corner_map, flexibility, coupling, corner_rows):
@@ -456,7 +484,7 @@
     four = shape(count, 4, size, loads_n)
     long_face = shape(size + below, loads_n)
     long_faces = shape(count, size + below, loads_n)
-    table, rows_table = corner_tables(cuts, height)
+    table = corner_tables(cuts, height)
 
     corner_size = -(-(count * (dofs // 128 + 1) * rr_rows) // 8) * 8
     corner_shape = shape(corner_size, loads_n)
@@ -467,31 +495,33 @@
         pltpu.VMEM(gap.shape, F32),
         pltpu.VMEM((12, count, total), F32),
         pltpu.VMEM((12, count, dofs), F32),
-        pltpu.VMEM(rows_table.shape, BF16),
     ]
     prepared = (pair, long_faces, long_face, faces, shape(count, 4 * height, total, kind=BF16), shape(count, 12, total),
                 corner_shape)
     residual, to_far, to_right, inner, c_rows, c_keep, corner, own_offsets = pl.pallas_call(
         functools.partial(prepare_kernel, cuts),
         out_shape=prepared + (shape(count, 2, kind=jnp.int32),),
-        in_specs=[SMEM] + [HBM] * 6,
+        in_specs=[SMEM] + [HBM] * 5,
         out_specs=(VMEM,) * 7 + (SMEM,),
-        scratch_shapes=[pltpu.VMEM((count, 2, 2 * size, loads_n), F32), *held, pltpu.SemaphoreType.DMA((6,))],
-        compiler_params=room(*prepared, pair, pair, *held[2:]),
+        scratch_shapes=[pltpu.VMEM((count, 2, 2 * size, loads_n), F32), *held, pltpu.SemaphoreType.DMA((5,)),
+                        pltpu.VMEM((count, 2 * height, total), F32)],
+        compiler_params=room(*prepared, pair, pair, *held[2:], shape(count, 2 * height, total)),
         name="prepare",
-    )(at, offsets, corner_map, gap, jnp.swapaxes(coupling, 0, 1), jnp.swapaxes(corner_rows, 0, 1), rows_table)
+    )(at, offsets, corner_map, gap, jnp.swapaxes(coupling, 0, 1), jnp.swapaxes(corner_rows, 0, 1))
     from_near = shifted(to_far, "cuts", 1, False)
     from_left = shifted(to_right, "blk", 1, True)
-    a_shape = jax.ShapeDtypeStruct(flexibility.shape, BF16)
-    first_high, first_low, a_high, a_low = pl.pallas_call(
-        split_kernel,
-        out_shape=(a_shape,) * 4,
-        in_specs=[VMEM],
-        out_specs=(VMEM,) * 4,
-        compiler_params=room(flexibility, *[a_shape] * 4),
-        cost_estimate=pl.CostEstimate(flops=0, bytes_accessed=12 * flexibility.size, transcendentals=0),
-        name="split",
-    )(flexibility)
+    own_shape = shape(count, total, loads_n)
+    own_part = pl.pallas_call(
+        own_kernel,
+        out_shape=own_shape,
+        in_specs=[VMEM] * 2,
+        out_specs=VMEM,
+        compiler_params=room(residual, flexibility, flexibility, own_shape),
+        cost_estimate=pl.CostEstimate(
+            flops=3 * count * total * total * loads_n, bytes_accessed=4 * flexibility.size, transcendentals=0
+        ),
+        name="own",
+    )(residual, flexibility)
 
     flops = 2 * count * total * total * loads_n * 3
     cost = pl.CostEstimate(flops=flops, bytes_accessed=4 * flexibility.size, transcendentals=0)
@@ -505,14 +535,14 @@
         pltpu.VMEM((blocks * count * height, loads_n), F32),
         pltpu.VMEM((count, 4, 2 * size, loads_n), F32),
     ]
-    first_args = (side, residual, from_near, from_left, inner, c_keep, corner, first_high, first_low, c_rows)
+    first_args = (side, residual, from_near, from_left, inner, c_keep, corner, own_part, flexibility, c_rows)
     *out, loads = pl.pallas_call(
         functools.partial(first_kernel, height, rr_rows),
         out_shape=first_sends + (four,),
         in_specs=[SMEM] + [VMEM] * 9,
         out_specs=(VMEM,) * 7,
         scratch_shapes=a_buffers,
-        compiler_params=room(*first_args[1:], *first_sends, four, *a_buffers),
+        compiler_params=room(*first_args[1:], *first_sends, four, flexibility, *a_buffers),
         cost_estimate=cost,
         name="first",
     )(*first_args)
@@ -522,14 +552,14 @@
         last = which == ITERS - 1
         near, far, sides, inside, across, terms = out
         pieces = [terms] + [shifted(terms, "cuts", k, True) for k in range(1, cuts)]
-        across = chip_neighbour(across, "blk")
-        terms, near, across = relay(sum_kernel, pieces, terms, [near, across], f"sum{which}")
+        terms, near = relay(sum_kernel, pieces, terms, [near], f"sum{which}")
         r_far = shifted(near, "cuts", -1, False)
         pieces = chip_parts(terms, "blk")
         stacked = blocks // 2 * terms.shape[0]
-        mine, far = relay(
-            stack_kernel, [*pieces, inside], shape(stacked + inside.shape[0], loads_n), [far], f"stack{which}"
+        mine, far, across = relay(
+            stack_kernel, [*pieces, inside], shape(stacked + inside.shape[0], loads_n), [far, across], f"stack{which}"
         )
+        across = chip_neighbour(across, "blk")
         r_near = far if last else shifted(far, "cuts", 1, False)
         theirs = swapped(mine, "blk")
         if which == 0:
@@ -563,8 +593,8 @@
         if last:
             outs, scratch = (pair, pair), f_buffers
         else:
-            args += [a_high, a_low, c_rows]
-            specs += [VMEM] * 3
+            args += [flexibility, c_rows]
+            specs += [VMEM] * 2
             outs = sends + (four, four) + ((pair, pair) if which > 0 else ()) + (shape(8, loads_n),)
             scratch = f_buffers + a_buffers
         result = pl.pallas_call(
@@ -573,7 +603,7 @@
             in_specs=specs,
             out_specs=(VMEM,) * len(outs),
             scratch_shapes=scratch,
-            compiler_params=room(*args[2:], *outs, *scratch),
+            compiler_params=room(*args[2:], *outs, *scratch, *([] if last else [flexibility])),
             cost_estimate=None if last else cost,
             name=f"step{which}",
         )(*args)

time: 124 us -> 112 us (0.903)
  local copies, waits for them, and re-layouts: 20.6 us -> 7.83 us
  waiting for transfers between devices: 34.5 us -> 39.9 us
  starting transfers between devices: 48.4 us -> 45.5 us
    ppermute x3, waiting for transfers between devices: 0.01 us -> 16 us  [chip_neighbour(): return lax.ppermute(value, axis, pairs)]
    unnamed x32 -> x16, local copies, waits for them, and re-layouts: 20.6 us -> 7.83 us
    ppermute x25, waiting for transfers between devices: 31.5 us -> 23.9 us  [shifted(): return lax.ppermute(value, axis, pairs)]
    ppermute x25, starting transfers between devices: 44.5 us -> 41.4 us  [shifted(): return lax.ppermute(value, axis, pairs)]
    ppermute x3, waiting for transfers between devices: 2.95 us -> 0.01 us  [swapped(): lax.ppermute(value, axis, [(source, source ^ 1) for source in range(lax.a...]
  transfers between devices with their start and end apart: 31 -> 31, of which waited for: 20 -> 18; matrix products, arithmetic and copies ran while one was open for 0% -> 0% of each run, Pallas kernels for 3% -> 3%
where the time goes in v7:
time: 112 us
  starting transfers between devices  45.5 us (41%)
  waiting for transfers between devices  39.9 us (36%)
  Pallas kernels  17.7 us (16%)
  local copies, waits for them, and re-layouts  7.83 us (7%)
    ppermute x25, starting transfers between devices, shifted(): return lax.ppermute(value, axis, pairs)  41.4 us
    ppermute x25, waiting for transfers between devices, shifted(): return lax.ppermute(value, axis, pairs)  23.9 us
    ppermute x3, waiting for transfers between devices, chip_neighbour(): return lax.ppermute(value, axis, pairs)  16 us
    pallas_call x3, Pallas kernels, per_device(): pl.pallas_call(functools.partial(step_kernel, which, blocks // 2, terms.s...  11.4 us
    unnamed x16, local copies, waits for them, and re-layouts  7.83 us
    ppermute x3, starting transfers between devices, chip_neighbour(): return lax.ppermute(value, axis, pairs)  3.91 us
  transfers between devices with their start and end apart: 31, of which 18 were waited for; matrix products, arithmetic and copies ran while one was open for 0% of the time, Pallas kernels for 3%

profile of v7, /device:TPU:0, one launch (start us, length us, event | category | flops | bytes accessed | tf_op | source)
XLA Modules:
  0.0 111.8 jit_solution(9200329939756946495)
XLA Ops:
  4.7 1.4 %prepare.1 = (f32[2,2,256,128]{3,2,1,0:T(8,128)S(1)}, f32[2,288,128]{2,1,0:T(8,128)S(1)}, f32[288,128]{1,0:T(8,128)S(1)}, f32[2,256,128]{2,1,0:T(8,128)S(1)}, bf...) custom-call(s32[1]{0:T(128)} %bitcast.at, ...), custom_call_target="tpu_custom_call" | custom-call | tf_op jit(solution)/shard_map/prepare/pallas_call | solution.py:501
  6.1 4.9 %collective-permute-start = (f32[2,288,128]{2,1,0:T(8,128)S(1)}, f32[2,288,128]{2,1,0:T(8,128)S(1)}, u32[]{:S(2)}, u32[]{:S(2)}) collective-permute-start(f32[2,288,128]{2,1,0:T(8,128)S(1)} %get-tuple-element.62), channel_id=1, source_target_pairs={{0,8},{8,16},{16,24},{1,9},{9,17},{17,25},{2,10},{10,18},{18,26},{... | collective-permute-start | bytes 884744 | tf_op jit(solution)/shard_map/ppermute | solution.py:26
  11.1 3.4 %copy-done = f32[1,2,1024,1024]{3,2,1,0:T(8,128)S(1)} copy-done((f32[1,2,1024,1024]{3,2,1,0:T(8,128)S(1)}, f32[1,2,1024,1024]{3,2,1,0:T(8,128)}, u32[]{:S(2)}) %copy-start) | copy-done | bytes 8388632
  15.7 1.7 %collective-permute-done.1.from_left = f32[288,128]{1,0:T(8,128)S(1)} collective-permute-done((f32[288,128]{1,0:T(8,128)S(1)}, f32[288,128]{1,0:T(8,128)S(1)}, u32[]{:S(2)}, u32[]{:S(2)}) %collective-permute-start.1) | collective-permute-done | bytes 147488 | tf_op jit(solution)/shard_map/ppermute | solution.py:26
  17.8 1.6 %first.1 = (f32[2,288,128]{2,1,0:T(8,128)S(1)}, f32[2,256,128]{2,1,0:T(8,128)S(1)}, f32[2,2,256,128]{3,2,1,0:T(8,128)S(1)}, f32[288,128]{1,0:T(8,128)S(1)}, f32[...) custom-call(s32[1]{0:T(128)} %bitcast.1.side.refs_1_, ...), custom_call_target="tpu_custom_call" | custom-call | flops 1610612736 | bytes 8388608 | tf_op jit(solution)/shard_map/first/pallas_call | solution.py:539
  19.4 2.9 %collective-permute-start.4 = (f32[96,128]{1,0:T(8,128)S(1)}, f32[96,128]{1,0:T(8,128)S(1)}, u32[]{:S(2)}, u32[]{:S(2)}) collective-permute-start(f32[96,128]{1,0:T(8,128)S(1)} %get-tuple-element.68.refs_0_), channel_id=1, source_target_pairs={{0,24},{8,0},{16,8},{24,16},{1,25},{9,1},{17,9},{25,17},{2,26},{10... | collective-permute-start | bytes 147464 | tf_op jit(solution)/shard_map/ppermute | solution.py:26
  22.8 1.5 %collective-permute-start.2 = (f32[96,128]{1,0:T(8,128)S(1)}, f32[96,128]{1,0:T(8,128)S(1)}, u32[]{:S(2)}, u32[]{:S(2)}) collective-permute-start(f32[96,128]{1,0:T(8,128)S(1)} %get-tuple-element.68.refs_0_), channel_id=1, source_target_pairs={{0,8},{8,16},{16,24},{24,0},{1,9},{9,17},{17,25},{25,1},{2,10},{10... | collective-permute-start | bytes 147464 | tf_op jit(solution)/shard_map/ppermute | solution.py:26
  24.3 2.1 %collective-permute-done.3.refs_2_ = f32[96,128]{1,0:T(8,128)S(1)} collective-permute-done((f32[96,128]{1,0:T(8,128)S(1)}, f32[96,128]{1,0:T(8,128)S(1)}, u32[]{:S(2)}, u32[]{:S(2)}) %collective-permute-start.3) | collective-permute-done | bytes 49184 | tf_op jit(solution)/shard_map/ppermute | solution.py:26
  26.4 1.7 %collective-permute-done.2.refs_1_ = f32[96,128]{1,0:T(8,128)S(1)} collective-permute-done((f32[96,128]{1,0:T(8,128)S(1)}, f32[96,128]{1,0:T(8,128)S(1)}, u32[]{:S(2)}, u32[]{:S(2)}) %collective-permute-start.2) | collective-permute-done | bytes 49184 | tf_op jit(solution)/shard_map/ppermute | solution.py:26
  28.1 3.4 %collective-permute-start.8 = (f32[96,128]{1,0:T(8,128)S(1)}, f32[96,128]{1,0:T(8,128)S(1)}, u32[]{:S(2)}, u32[]{:S(2)}) collective-permute-start(f32[96,128]{1,0:T(8,128)S(1)} %get-tuple-element.71.refs_0_), channel_id=1, source_target_pairs={{0,6},{1,7},{2,0},{3,1},{4,2},{5,3},{6,4},{7,5},{8,14},{9,15},{10,... | collective-permute-start | bytes 147464 | tf_op jit(solution)/shard_map/ppermute | solution.py:26
  33.2 3.2 %collective-permute-done.7.refs_2_ = f32[96,128]{1,0:T(8,128)S(1)} collective-permute-done((f32[96,128]{1,0:T(8,128)S(1)}, f32[96,128]{1,0:T(8,128)S(1)}, u32[]{:S(2)}, u32[]{:S(2)}) %collective-permute-start.7) | collective-permute-done | bytes 49184 | tf_op jit(solution)/shard_map/ppermute | solution.py:26
  38.8 4.6 %collective-permute-start.11 = (f32[2,256,128]{2,1,0:T(8,128)S(1)}, f32[2,256,128]{2,1,0:T(8,128)S(1)}, u32[]{:S(2)}, u32[]{:S(2)}) collective-permute-start(f32[2,256,128]{2,1,0:T(8,128)S(1)} %get-tuple-element.83.refs_10_), channel_id=1, source_target_pairs={{0,8},{8,16},{16,24},{1,9},{9,17},{17,25},{2,10},{10,18},{18,26},{... | collective-permute-start | bytes 786440 | tf_op jit(solution)/shard_map/ppermute | solution.py:26
  44.2 6.0 %collective-permute-done.9.across.refs_14_ = f32[288,128]{1,0:T(8,128)S(1)} collective-permute-done((f32[288,128]{1,0:T(8,128)S(1)}, f32[288,128]{1,0:T(8,128)S(1)}, u32[]{:S(2)}, u32[]{:S(2)}) %collective-permute-start.9) | collective-permute-done | bytes 147488 | tf_op jit(solution)/shard_map/ppermute | solution.py:48
  50.2 1.5 %spread.1 = (bf16[2,1536,96]{2,1,0:T(8,128)(2,1)S(1)}, bf16[256,96]{1,0:T(8,128)(2,1)S(1)}, bf16[256,96]{1,0:T(8,128)(2,1)S(1)}, s32[2,4]{1,0:T(2,128)S(1)}) custom-call(s32[1]{0:T(128)} %bitcast.at, s32[1]{0:T(128)} %bitcast.1.side.refs_1_, s32[2,2]{1,0:T(2,128)S(1)} %get-tuple-element.60.own_offsets, f32[2,12,1024]{2,1,0:T(8,128)S(1)} %get-tuple-element.61.coupling, ...), custom_call_target="tpu_custom_call" | custom-call | tf_op jit(solution)/shard_map/spread/pallas_call | solution.py:577
  51.8 4.5 %step0.1 = (f32[2,256,128]{2,1,0:T(8,128)S(1)}, f32[2,256,128]{2,1,0:T(8,128)S(1)}, f32[2,2,256,128]{3,2,1,0:T(8,128)S(1)}, f32[256,128]{1,0:T(8,128)S(1)}, f32[...) custom-call(s32[2,4]{1,0:T(2,128)S(1)} %get-tuple-element.77.refs_0_, ...), custom_call_target="tpu_custom_call" | custom-call | flops 1610612736 | bytes 8388608 | tf_op jit(solution)/shard_map/step0/pallas_call | solution.py:600
  56.3 4.1 %collective-permute-start.14 = (f32[48,128]{1,0:T(8,128)S(1)}, f32[48,128]{1,0:T(8,128)S(1)}, u32[]{:S(2)}, u32[]{:S(2)}) collective-permute-start(f32[48,128]{1,0:T(8,128)S(1)} %get-tuple-element.86.refs_0_), channel_id=1, source_target_pairs={{0,24},{8,0},{16,8},{24,16},{1,25},{9,1},{17,9},{25,17},{2,26},{10... | collective-permute-start | bytes 73736 | tf_op jit(solution)/shard_map/ppermute | solution.py:26
  60.5 1.9 %collective-permute-start.12 = (f32[48,128]{1,0:T(8,128)S(1)}, f32[48,128]{1,0:T(8,128)S(1)}, u32[]{:S(2)}, u32[]{:S(2)}) collective-permute-start(f32[48,128]{1,0:T(8,128)S(1)} %get-tuple-element.86.refs_0_), channel_id=1, source_target_pairs={{0,8},{8,16},{16,24},{24,0},{1,9},{9,17},{17,25},{25,1},{2,10},{10... | collective-permute-start | bytes 73736 | tf_op jit(solution)/shard_map/ppermute | solution.py:26
  62.4 1.8 %collective-permute-done.13.refs_2_ = f32[48,128]{1,0:T(8,128)S(1)} collective-permute-done((f32[48,128]{1,0:T(8,128)S(1)}, f32[48,128]{1,0:T(8,128)S(1)}, u32[]{:S(2)}, u32[]{:S(2)}) %collective-permute-start.13) | collective-permute-done | bytes 24608 | tf_op jit(solution)/shard_map/ppermute | solution.py:26
  66.4 1.9 %collective-permute-start.15 = (f32[48,128]{1,0:T(8,128)S(1)}, f32[48,128]{1,0:T(8,128)S(1)}, u32[]{:S(2)}, u32[]{:S(2)}) collective-permute-start(f32[48,128]{1,0:T(8,128)S(1)} %get-tuple-element.88.refs_0_), channel_id=1, source_target_pairs={{0,2},{1,3},{2,4},{3,5},{4,6},{5,7},{6,0},{7,1},{8,10},{9,11},{10,... | collective-permute-start | bytes 73736 | tf_op jit(solution)/shard_map/ppermute | solution.py:26
  72.1 3.1 %collective-permute-start.19 = (f32[2,256,128]{2,1,0:T(8,128)S(1)}, f32[2,256,128]{2,1,0:T(8,128)S(1)}, u32[]{:S(2)}, u32[]{:S(2)}) collective-permute-start(f32[2,256,128]{2,1,0:T(8,128)S(1)} %get-tuple-element.94.refs_10_), channel_id=1, source_target_pairs={{0,8},{8,16},{16,24},{1,9},{9,17},{17,25},{2,10},{10,18},{18,26},{... | collective-permute-start | bytes 786440 | tf_op jit(solution)/shard_map/ppermute | solution.py:26
  75.3 1.5 %collective-permute-start.21 = (f32[256,128]{1,0:T(8,128)S(1)}, f32[256,128]{1,0:T(8,128)S(1)}, u32[]{:S(2)}, u32[]{:S(2)}) collective-permute-start(f32[256,128]{1,0:T(8,128)S(1)} %get-tuple-element.96), channel_id=1, source_target_pairs={{0,7},{1,2},{2,1},{3,4},{4,3},{5,6},{6,5},{7,0},{8,15},{9,10},{10,... | collective-permute-start | bytes 393224 | tf_op jit(solution)/shard_map/ppermute | solution.py:48
  76.8 5.5 %collective-permute-done.21.refs_14_ = f32[256,128]{1,0:T(8,128)S(1)} collective-permute-done((f32[256,128]{1,0:T(8,128)S(1)}, f32[256,128]{1,0:T(8,128)S(1)}, u32[]{:S(2)}, u32[]{:S(2)}) %collective-permute-start.21) | collective-permute-done | bytes 131104 | tf_op jit(solution)/shard_map/ppermute | solution.py:48
  82.3 4.7 %step1.1 = (f32[2,256,128]{2,1,0:T(8,128)S(1)}, f32[2,256,128]{2,1,0:T(8,128)S(1)}, f32[2,2,256,128]{3,2,1,0:T(8,128)S(1)}, f32[256,128]{1,0:T(8,128)S(1)}, f32[...) custom-call(s32[2,4]{1,0:T(2,128)S(1)} %get-tuple-element.77.refs_0_, ...), custom_call_target="tpu_custom_call" | custom-call | flops 1610612736 | bytes 8388608 | tf_op jit(solution)/shard_map/step1/pallas_call | solution.py:600
  87.0 1.3 %collective-permute-start.24 = (f32[48,128]{1,0:T(8,128)S(1)}, f32[48,128]{1,0:T(8,128)S(1)}, u32[]{:S(2)}, u32[]{:S(2)}) collective-permute-start(f32[48,128]{1,0:T(8,128)S(1)} %get-tuple-element.100.refs_0_), channel_id=1, source_target_pairs={{0,24},{8,0},{16,8},{24,16},{1,25},{9,1},{17,9},{25,17},{2,26},{10... | collective-permute-start | bytes 73736 | tf_op jit(solution)/shard_map/ppermute | solution.py:26
  88.3 2.1 %collective-permute-start.23 = (f32[48,128]{1,0:T(8,128)S(1)}, f32[48,128]{1,0:T(8,128)S(1)}, u32[]{:S(2)}, u32[]{:S(2)}) collective-permute-start(f32[48,128]{1,0:T(8,128)S(1)} %get-tuple-element.100.refs_0_), channel_id=1, source_target_pairs={{0,16},{8,24},{16,0},{24,8},{1,17},{9,25},{17,1},{25,9},{2,18},{10... | collective-permute-start | bytes 73736 | tf_op jit(solution)/shard_map/ppermute | solution.py:26
  90.9 1.3 %collective-permute-done.23.refs_2_ = f32[48,128]{1,0:T(8,128)S(1)} collective-permute-done((f32[48,128]{1,0:T(8,128)S(1)}, f32[48,128]{1,0:T(8,128)S(1)}, u32[]{:S(2)}, u32[]{:S(2)}) %collective-permute-start.23) | collective-permute-done | bytes 24608 | tf_op jit(solution)/shard_map/ppermute | solution.py:26
  92.3 2.9 %collective-permute-done.22.refs_1_ = f32[48,128]{1,0:T(8,128)S(1)} collective-permute-done((f32[48,128]{1,0:T(8,128)S(1)}, f32[48,128]{1,0:T(8,128)S(1)}, u32[]{:S(2)}, u32[]{:S(2)}) %collective-permute-start.22) | collective-permute-done | bytes 24608 | tf_op jit(solution)/shard_map/ppermute | solution.py:26
  98.6 2.1 %collective-permute-done.27.refs_3_ = f32[48,128]{1,0:T(8,128)S(1)} collective-permute-done((f32[48,128]{1,0:T(8,128)S(1)}, f32[48,128]{1,0:T(8,128)S(1)}, u32[]{:S(2)}, u32[]{:S(2)}) %collective-permute-start.27) | collective-permute-done | bytes 24608 | tf_op jit(solution)/shard_map/ppermute | solution.py:26
  101.5 1.5 %collective-permute-done.25.refs_1_ = f32[48,128]{1,0:T(8,128)S(1)} collective-permute-done((f32[48,128]{1,0:T(8,128)S(1)}, f32[48,128]{1,0:T(8,128)S(1)}, u32[]{:S(2)}, u32[]{:S(2)}) %collective-permute-start.25) | collective-permute-done | bytes 24608 | tf_op jit(solution)/shard_map/ppermute | solution.py:26
  103.1 1.9 %collective-permute-start.30 = (f32[256,128]{1,0:T(8,128)S(1)}, f32[256,128]{1,0:T(8,128)S(1)}, u32[]{:S(2)}, u32[]{:S(2)}) collective-permute-start(f32[256,128]{1,0:T(8,128)S(1)} %get-tuple-element.110), channel_id=1, source_target_pairs={{0,7},{1,2},{2,1},{3,4},{4,3},{5,6},{6,5},{7,0},{8,15},{9,10},{10,... | collective-permute-start | bytes 393224 | tf_op jit(solution)/shard_map/ppermute | solution.py:48
  104.9 4.6 %collective-permute-done.30.refs_14_ = f32[256,128]{1,0:T(8,128)S(1)} collective-permute-done((f32[256,128]{1,0:T(8,128)S(1)}, f32[256,128]{1,0:T(8,128)S(1)}, u32[]{:S(2)}, u32[]{:S(2)}) %collective-permute-start.30) | collective-permute-done | bytes 131104 | tf_op jit(solution)/shard_map/ppermute | solution.py:48
  109.6 2.3 %step2.1 = (f32[2,2,256,128]{3,2,1,0:T(8,128)}, f32[2,2,256,128]{3,2,1,0:T(8,128)}) custom-call(s32[2,4]{1,0:T(2,128)S(1)} %get-tuple-element.77.refs_0_, s32[1]{0:T(128)} %bitcast.1.side.refs_1_, f32[448,128]{1,0:T(8,128)S(1)} %get-tuple-element.106.refs_2_, f32[448,128]{1,0:T(8,128)S(1)} %collective-permute-done.28.refs_3_, ...), custom_call_target="tpu_custom_call" | custom-call | tf_op jit(solution)/shard_map/step2/pallas_call | solution.py:600
  (60 shorter events, 22.1 us)
Async XLA Ops:
  6.1 11.3 %collective-permute-start = (f32[2,288,128]{2,1,0:T(8,128)S(1)}, f32[2,288,128]{2,1,0:T(8,128)S(1)}, u32[]{:S(2)}, u32[]{:S(2)}) collective-permute-start(f32[2,288,128]{2,1,0:T(8,128)S(1)} %get-tuple-element.62), channel_id=1, source_target_pairs={{0,8},{8,16},{16,24},{1,9},{9,17},{17,25},{2,10},{10,18},{18,26},{... | collective-permute-start | bytes 884744 | tf_op jit(solution)/shard_map/ppermute | solution.py:26
  11.0 6.4 %collective-permute-start.1 = (f32[288,128]{1,0:T(8,128)S(1)}, f32[288,128]{1,0:T(8,128)S(1)}, u32[]{:S(2)}, u32[]{:S(2)}) collective-permute-start(f32[288,128]{1,0:T(8,128)S(1)} %get-tuple-element.64), channel_id=1, source_target_pairs={{0,1},{1,2},{2,3},{3,4},{4,5},{5,6},{6,7},{7,0},{8,9},{9,10},{10,1... | collective-permute-start | bytes 442376 | tf_op jit(solution)/shard_map/ppermute | solution.py:26
  15.7 34.5 %copy-start.4 = (bf16[6,32,96]{2,1,0:T(8,128)(2,1)S(1)}, bf16[6,32,96]{2,1,0:T(8,128)(2,1)}, u32[]{:S(2)}) copy-start(bf16[6,32,96]{2,1,0:T(8,128)(2,1)} %constant.23.clone.table) | copy-start | bytes 110596
  19.4 4.9 %collective-permute-start.4 = (f32[96,128]{1,0:T(8,128)S(1)}, f32[96,128]{1,0:T(8,128)S(1)}, u32[]{:S(2)}, u32[]{:S(2)}) collective-permute-start(f32[96,128]{1,0:T(8,128)S(1)} %get-tuple-element.68.refs_0_), channel_id=1, source_target_pairs={{0,24},{8,0},{16,8},{24,16},{1,25},{9,1},{17,9},{25,17},{2,26},{10... | collective-permute-start | bytes 147464 | tf_op jit(solution)/shard_map/ppermute | solution.py:26
  22.3 4.1 %collective-permute-start.3 = (f32[96,128]{1,0:T(8,128)S(1)}, f32[96,128]{1,0:T(8,128)S(1)}, u32[]{:S(2)}, u32[]{:S(2)}) collective-permute-start(f32[96,128]{1,0:T(8,128)S(1)} %get-tuple-element.68.refs_0_), channel_id=1, source_target_pairs={{0,16},{8,24},{16,0},{24,8},{1,17},{9,25},{17,1},{25,9},{2,18},{10... | collective-permute-start | bytes 147464 | tf_op jit(solution)/shard_map/ppermute | solution.py:26
  22.8 5.3 %collective-permute-start.2 = (f32[96,128]{1,0:T(8,128)S(1)}, f32[96,128]{1,0:T(8,128)S(1)}, u32[]{:S(2)}, u32[]{:S(2)}) collective-permute-start(f32[96,128]{1,0:T(8,128)S(1)} %get-tuple-element.68.refs_0_), channel_id=1, source_target_pairs={{0,8},{8,16},{16,24},{24,0},{1,9},{9,17},{17,25},{25,1},{2,10},{10... | collective-permute-start | bytes 147464 | tf_op jit(solution)/shard_map/ppermute | solution.py:26
  28.1 5.1 %collective-permute-start.8 = (f32[96,128]{1,0:T(8,128)S(1)}, f32[96,128]{1,0:T(8,128)S(1)}, u32[]{:S(2)}, u32[]{:S(2)}) collective-permute-start(f32[96,128]{1,0:T(8,128)S(1)} %get-tuple-element.71.refs_0_), channel_id=1, source_target_pairs={{0,6},{1,7},{2,0},{3,1},{4,2},{5,3},{6,4},{7,5},{8,14},{9,15},{10,... | collective-permute-start | bytes 147464 | tf_op jit(solution)/shard_map/ppermute | solution.py:26
  31.5 5.0 %collective-permute-start.7 = (f32[96,128]{1,0:T(8,128)S(1)}, f32[96,128]{1,0:T(8,128)S(1)}, u32[]{:S(2)}, u32[]{:S(2)}) collective-permute-start(f32[96,128]{1,0:T(8,128)S(1)} %get-tuple-element.71.refs_0_), channel_id=1, source_target_pairs={{0,4},{1,5},{2,6},{3,7},{4,0},{5,1},{6,2},{7,3},{8,12},{9,13},{10,... | collective-permute-start | bytes 147464 | tf_op jit(solution)/shard_map/ppermute | solution.py:26
  31.5 5.9 %collective-permute-start.6 = (f32[96,128]{1,0:T(8,128)S(1)}, f32[96,128]{1,0:T(8,128)S(1)}, u32[]{:S(2)}, u32[]{:S(2)}) collective-permute-start(f32[96,128]{1,0:T(8,128)S(1)} %get-tuple-element.71.refs_0_), channel_id=1, source_target_pairs={{0,2},{1,3},{2,4},{3,5},{4,6},{5,7},{6,0},{7,1},{8,10},{9,11},{10,... | collective-permute-start | bytes 147464 | tf_op jit(solution)/shard_map/ppermute | solution.py:26
  37.4 6.5 %collective-permute-start.10 = (f32[672,128]{1,0:T(8,128)S(1)}, f32[672,128]{1,0:T(8,128)S(1)}, u32[]{:S(2)}, u32[]{:S(2)}) collective-permute-start(f32[672,128]{1,0:T(8,128)S(1)} %get-tuple-element.76.mine.refs_2_), channel_id=1, source_target_pairs={{0,1},{1,0},{2,3},{3,2},{4,5},{5,4},{6,7},{7,6},{8,9},{9,8},{10,11... | collective-permute-start | bytes 1032200 | tf_op jit(solution)/shard_map/ppermute | solution.py:52
  37.5 12.8 %collective-permute-start.5 = (f32[2,288,128]{2,1,0:T(8,128)S(1)}, f32[2,288,128]{2,1,0:T(8,128)S(1)}, u32[]{:S(2)}, u32[]{:S(2)}) collective-permute-start(f32[2,288,128]{2,1,0:T(8,128)S(1)} %get-tuple-element.70.refs_9_), channel_id=1, source_target_pairs={{8,0},{16,8},{24,16},{9,1},{17,9},{25,17},{10,2},{18,10},{26,18},{... | collective-permute-start | bytes 884744 | tf_op jit(solution)/shard_map/ppermute | solution.py:26
  38.8 13.0 %collective-permute-start.11 = (f32[2,256,128]{2,1,0:T(8,128)S(1)}, f32[2,256,128]{2,1,0:T(8,128)S(1)}, u32[]{:S(2)}, u32[]{:S(2)}) collective-permute-start(f32[2,256,128]{2,1,0:T(8,128)S(1)} %get-tuple-element.83.refs_10_), channel_id=1, source_target_pairs={{0,8},{8,16},{16,24},{1,9},{9,17},{17,25},{2,10},{10,18},{18,26},{... | collective-permute-start | bytes 786440 | tf_op jit(solution)/shard_map/ppermute | solution.py:26
  43.3 6.9 %collective-permute-start.9 = (f32[288,128]{1,0:T(8,128)S(1)}, f32[288,128]{1,0:T(8,128)S(1)}, u32[]{:S(2)}, u32[]{:S(2)}) collective-permute-start(f32[288,128]{1,0:T(8,128)S(1)} %get-tuple-element.75), channel_id=1, source_target_pairs={{0,7},{1,2},{2,1},{3,4},{4,3},{5,6},{6,5},{7,0},{8,15},{9,10},{10,... | collective-permute-start | bytes 442376 | tf_op jit(solution)/shard_map/ppermute | solution.py:48
  56.3 6.1 %collective-permute-start.14 = (f32[48,128]{1,0:T(8,128)S(1)}, f32[48,128]{1,0:T(8,128)S(1)}, u32[]{:S(2)}, u32[]{:S(2)}) collective-permute-start(f32[48,128]{1,0:T(8,128)S(1)} %get-tuple-element.86.refs_0_), channel_id=1, source_target_pairs={{0,24},{8,0},{16,8},{24,16},{1,25},{9,1},{17,9},{25,17},{2,26},{10... | collective-permute-start | bytes 73736 | tf_op jit(solution)/shard_map/ppermute | solution.py:26
  60.4 3.8 %collective-permute-start.13 = (f32[48,128]{1,0:T(8,128)S(1)}, f32[48,128]{1,0:T(8,128)S(1)}, u32[]{:S(2)}, u32[]{:S(2)}) collective-permute-start(f32[48,128]{1,0:T(8,128)S(1)} %get-tuple-element.86.refs_0_), channel_id=1, source_target_pairs={{0,16},{8,24},{16,0},{24,8},{1,17},{9,25},{17,1},{25,9},{2,18},{10... | collective-permute-start | bytes 73736 | tf_op jit(solution)/shard_map/ppermute | solution.py:26
  60.5 4.7 %collective-permute-start.12 = (f32[48,128]{1,0:T(8,128)S(1)}, f32[48,128]{1,0:T(8,128)S(1)}, u32[]{:S(2)}, u32[]{:S(2)}) collective-permute-start(f32[48,128]{1,0:T(8,128)S(1)} %get-tuple-element.86.refs_0_), channel_id=1, source_target_pairs={{0,8},{8,16},{16,24},{24,0},{1,9},{9,17},{17,25},{25,1},{2,10},{10... | collective-permute-start | bytes 73736 | tf_op jit(solution)/shard_map/ppermute | solution.py:26
  65.2 4.5 %collective-permute-start.17 = (f32[48,128]{1,0:T(8,128)S(1)}, f32[48,128]{1,0:T(8,128)S(1)}, u32[]{:S(2)}, u32[]{:S(2)}) collective-permute-start(f32[48,128]{1,0:T(8,128)S(1)} %get-tuple-element.88.refs_0_), channel_id=1, source_target_pairs={{0,6},{1,7},{2,0},{3,1},{4,2},{5,3},{6,4},{7,5},{8,14},{9,15},{10,... | collective-permute-start | bytes 73736 | tf_op jit(solution)/shard_map/ppermute | solution.py:26
  66.2 4.7 %collective-permute-start.16 = (f32[48,128]{1,0:T(8,128)S(1)}, f32[48,128]{1,0:T(8,128)S(1)}, u32[]{:S(2)}, u32[]{:S(2)}) collective-permute-start(f32[48,128]{1,0:T(8,128)S(1)} %get-tuple-element.88.refs_0_), channel_id=1, source_target_pairs={{0,4},{1,5},{2,6},{3,7},{4,0},{5,1},{6,2},{7,3},{8,12},{9,13},{10,... | collective-permute-start | bytes 73736 | tf_op jit(solution)/shard_map/ppermute | solution.py:26
  66.4 5.6 %collective-permute-start.15 = (f32[48,128]{1,0:T(8,128)S(1)}, f32[48,128]{1,0:T(8,128)S(1)}, u32[]{:S(2)}, u32[]{:S(2)}) collective-permute-start(f32[48,128]{1,0:T(8,128)S(1)} %get-tuple-element.88.refs_0_), channel_id=1, source_target_pairs={{0,2},{1,3},{2,4},{3,5},{4,6},{5,7},{6,0},{7,1},{8,10},{9,11},{10,... | collective-permute-start | bytes 73736 | tf_op jit(solution)/shard_map/ppermute | solution.py:26
  68.4 13.9 %collective-permute-start.20 = (f32[2,256,128]{2,1,0:T(8,128)S(1)}, f32[2,256,128]{2,1,0:T(8,128)S(1)}, u32[]{:S(2)}, u32[]{:S(2)}) collective-permute-start(f32[2,256,128]{2,1,0:T(8,128)S(1)} %get-tuple-element.93.refs_9_), channel_id=1, source_target_pairs={{8,0},{16,8},{24,16},{9,1},{17,9},{25,17},{10,2},{18,10},{26,18},{... | collective-permute-start | bytes 786440 | tf_op jit(solution)/shard_map/ppermute | solution.py:26
  72.1 10.2 %collective-permute-start.19 = (f32[2,256,128]{2,1,0:T(8,128)S(1)}, f32[2,256,128]{2,1,0:T(8,128)S(1)}, u32[]{:S(2)}, u32[]{:S(2)}) collective-permute-start(f32[2,256,128]{2,1,0:T(8,128)S(1)} %get-tuple-element.94.refs_10_), channel_id=1, source_target_pairs={{0,8},{8,16},{16,24},{1,9},{9,17},{17,25},{2,10},{10,18},{18,26},{... | collective-permute-start | bytes 786440 | tf_op jit(solution)/shard_map/ppermute | solution.py:26
  75.2 7.0 %collective-permute-start.18 = (f32[448,128]{1,0:T(8,128)S(1)}, f32[448,128]{1,0:T(8,128)S(1)}, u32[]{:S(2)}, u32[]{:S(2)}) collective-permute-start(f32[448,128]{1,0:T(8,128)S(1)} %get-tuple-element.92.refs_2_), channel_id=1, source_target_pairs={{0,1},{1,0},{2,3},{3,2},{4,5},{5,4},{6,7},{7,6},{8,9},{9,8},{10,11... | collective-permute-start | bytes 688136 | tf_op jit(solution)/shard_map/ppermute | solution.py:52
  75.3 7.0 %collective-permute-start.21 = (f32[256,128]{1,0:T(8,128)S(1)}, f32[256,128]{1,0:T(8,128)S(1)}, u32[]{:S(2)}, u32[]{:S(2)}) collective-permute-start(f32[256,128]{1,0:T(8,128)S(1)} %get-tuple-element.96), channel_id=1, source_target_pairs={{0,7},{1,2},{2,1},{3,4},{4,3},{5,6},{6,5},{7,0},{8,15},{9,10},{10,... | collective-permute-start | bytes 393224 | tf_op jit(solution)/shard_map/ppermute | solution.py:48
  87.0 3.9 %collective-permute-start.24 = (f32[48,128]{1,0:T(8,128)S(1)}, f32[48,128]{1,0:T(8,128)S(1)}, u32[]{:S(2)}, u32[]{:S(2)}) collective-permute-start(f32[48,128]{1,0:T(8,128)S(1)} %get-tuple-element.100.refs_0_), channel_id=1, source_target_pairs={{0,24},{8,0},{16,8},{24,16},{1,25},{9,1},{17,9},{25,17},{2,26},{10... | collective-permute-start | bytes 73736 | tf_op jit(solution)/shard_map/ppermute | solution.py:26
  88.3 4.0 %collective-permute-start.23 = (f32[48,128]{1,0:T(8,128)S(1)}, f32[48,128]{1,0:T(8,128)S(1)}, u32[]{:S(2)}, u32[]{:S(2)}) collective-permute-start(f32[48,128]{1,0:T(8,128)S(1)} %get-tuple-element.100.refs_0_), channel_id=1, source_target_pairs={{0,16},{8,24},{16,0},{24,8},{1,17},{9,25},{17,1},{25,9},{2,18},{10... | collective-permute-start | bytes 73736 | tf_op jit(solution)/shard_map/ppermute | solution.py:26
  90.4 4.7 %collective-permute-start.22 = (f32[48,128]{1,0:T(8,128)S(1)}, f32[48,128]{1,0:T(8,128)S(1)}, u32[]{:S(2)}, u32[]{:S(2)}) collective-permute-start(f32[48,128]{1,0:T(8,128)S(1)} %get-tuple-element.100.refs_0_), channel_id=1, source_target_pairs={{0,8},{8,16},{16,24},{24,0},{1,9},{9,17},{17,25},{25,1},{2,10},{10... | collective-permute-start | bytes 73736 | tf_op jit(solution)/shard_map/ppermute | solution.py:26
  95.2 14.4 %collective-permute-start.29 = (f32[2,256,128]{2,1,0:T(8,128)S(1)}, f32[2,256,128]{2,1,0:T(8,128)S(1)}, u32[]{:S(2)}, u32[]{:S(2)}) collective-permute-start(f32[2,256,128]{2,1,0:T(8,128)S(1)} %get-tuple-element.107.refs_9_), channel_id=1, source_target_pairs={{8,0},{16,8},{24,16},{9,1},{17,9},{25,17},{10,2},{18,10},{26,18},{... | collective-permute-start | bytes 786440 | tf_op jit(solution)/shard_map/ppermute | solution.py:26
  96.5 4.1 %collective-permute-start.27 = (f32[48,128]{1,0:T(8,128)S(1)}, f32[48,128]{1,0:T(8,128)S(1)}, u32[]{:S(2)}, u32[]{:S(2)}) collective-permute-start(f32[48,128]{1,0:T(8,128)S(1)} %get-tuple-element.102.refs_0_), channel_id=1, source_target_pairs={{0,6},{1,7},{2,0},{3,1},{4,2},{5,3},{6,4},{7,5},{8,14},{9,15},{10,... | collective-permute-start | bytes 73736 | tf_op jit(solution)/shard_map/ppermute | solution.py:26
  96.8 4.8 %collective-permute-start.26 = (f32[48,128]{1,0:T(8,128)S(1)}, f32[48,128]{1,0:T(8,128)S(1)}, u32[]{:S(2)}, u32[]{:S(2)}) collective-permute-start(f32[48,128]{1,0:T(8,128)S(1)} %get-tuple-element.102.refs_0_), channel_id=1, source_target_pairs={{0,4},{1,5},{2,6},{3,7},{4,0},{5,1},{6,2},{7,3},{8,12},{9,13},{10,... | collective-permute-start | bytes 73736 | tf_op jit(solution)/shard_map/ppermute | solution.py:26
  97.3 5.7 %collective-permute-start.25 = (f32[48,128]{1,0:T(8,128)S(1)}, f32[48,128]{1,0:T(8,128)S(1)}, u32[]{:S(2)}, u32[]{:S(2)}) collective-permute-start(f32[48,128]{1,0:T(8,128)S(1)} %get-tuple-element.102.refs_0_), channel_id=1, source_target_pairs={{0,2},{1,3},{2,4},{3,5},{4,6},{5,7},{6,0},{7,1},{8,10},{9,11},{10,... | collective-permute-start | bytes 73736 | tf_op jit(solution)/shard_map/ppermute | solution.py:26
  103.0 6.6 %collective-permute-start.28 = (f32[448,128]{1,0:T(8,128)S(1)}, f32[448,128]{1,0:T(8,128)S(1)}, u32[]{:S(2)}, u32[]{:S(2)}) collective-permute-start(f32[448,128]{1,0:T(8,128)S(1)} %get-tuple-element.106.refs_2_), channel_id=1, source_target_pairs={{0,1},{1,0},{2,3},{3,2},{4,5},{5,4},{6,7},{7,6},{8,9},{9,8},{10,11... | collective-permute-start | bytes 688136 | tf_op jit(solution)/shard_map/ppermute | solution.py:52
  103.1 6.5 %collective-permute-start.30 = (f32[256,128]{1,0:T(8,128)S(1)}, f32[256,128]{1,0:T(8,128)S(1)}, u32[]{:S(2)}, u32[]{:S(2)}) collective-permute-start(f32[256,128]{1,0:T(8,128)S(1)} %get-tuple-element.110), channel_id=1, source_target_pairs={{0,7},{1,2},{2,1},{3,4},{4,3},{5,6},{6,5},{7,0},{8,15},{9,10},{10,... | collective-permute-start | bytes 393224 | tf_op jit(solution)/shard_map/ppermute | solution.py:48
  (7 other events, 10.8 us)

commit v8 on v7

--- a/solution.py
+++ b/solution.py
@@ -42,9 +42,10 @@
     return parts
 
 
-def chip_neighbour(value, axis):
+def chip_neighbour(value, axis, back_only):
     count = lax.axis_size(axis)
-    pairs = [(source, (source + (1 if source % 2 else -1)) % count) for source in range(count)]
+    sources = range(0, count, 2 if back_only else 1)
+    pairs = [(source, (source + (1 if source % 2 else -1)) % count) for source in sources]
     return lax.ppermute(value, axis, pairs)
 
 
@@ -175,28 +176,31 @@
     return both.astype(BF16)
 
 
-def spread_kernel(stacked, at, side, own_offsets, coupling, from_near, from_far, from_left, across, theirs, table, ct_own, ct_left, ct_right, offsets):
+def turned(face, table):
+    product = lax.dot_general(paired(face), table, (((0,), (0,)), ((), ())), preferred_element_type=F32)
+    return product.astype(BF16)
+
+
+def spread_kernel(at, own_offsets, coupling, from_near, from_left, table, ct_own, ct_left, offsets):
     count, size = coupling.shape[0], coupling.shape[2] // 4
-
-    def turned(face, cycle):
-        product = lax.dot_general(
-            paired(face), table[cycle + 1], (((0,), (0,)), ((), ())), preferred_element_type=F32
-        )
-        return product.astype(BF16)
-
-    for s in range(count):
-        ct_own[s, 0:4 * size] = turned(coupling[s], at[0])
-        ct_own[s, 4 * size:5 * size] = turned(got_coupling(from_far.at[s], size), at[0] + 1)
-        ct_own[s, 5 * size:6 * size] = turned(got_coupling(from_near.at[s], size), at[0] - 1)
-    ct_left[...] = turned(got_coupling(from_left, size), at[0])
-    inside = got_coupling(theirs.at[stacked:], size)
-    ct_right[...] = turned(jnp.where(side[0] == 1, got_coupling(across, size), inside), at[0])
+    for s in range(count):
+        ct_own[s, 0:4 * size] = turned(coupling[s], table[at[0] + 1])
+        ct_own[s, 4 * size:5 * size] = turned(got_coupling(from_near.at[s], size), table[at[0]])
+    ct_left[...] = turned(got_coupling(from_left, size), table[at[0] + 1])
     noted = lambda ref: jnp.max(ref[size + 12:size + 16]).astype(jnp.int32) - 1
     for s in range(count):
         offsets[s, NEAR] = noted(from_near.at[s])
         offsets[s, FAR] = own_offsets[s, 0]
         offsets[s, LEFT] = noted(from_left) if s == 0 else own_offsets[s - 1, 1]
         offsets[s, RIGHT] = own_offsets[s, 1]
+
+
+def spread_back_kernel(stacked, at, side, from_far, across, theirs, table, ct_far, ct_right):
+    count, size = ct_far.shape[0], ct_far.shape[1]
+    for s in range(count):
+        ct_far[s] = turned(got_coupling(from_far.at[s], size), table[at[0] + 2])
+    inside = got_coupling(theirs.at[stacked:], size)
+    ct_right[...] = turned(jnp.where(side[0] == 1, got_coupling(across, size), inside), table[at[0] + 1])
 
 
 def beside(value):
@@ -298,7 +302,7 @@
 
 def finish_operator(offsets, terms, matrix, spread, product, received, height, rr_rows, scratch, faces):
     k_high, k_low = matrix
-    ct_own, ct_left, ct_right = spread
+    ct_own, ct_far, ct_left, ct_right = spread
     near, far, sides = product
     from_near, from_far, across = received
     count, size = far.shape[0], far.shape[1]
@@ -343,13 +347,14 @@
     own = [[None] * 4 for _ in range(count)]
     other = [[None] * 4 for _ in range(count)]
     for s in range(count):
-        added = dot(ct_own[s], tripled(s))
-        parts = [added[i * size:(i + 1) * size] for i in range(6)]
+        columns = tripled(s)
+        added = dot(ct_own[s], columns)
+        parts = [added[i * size:(i + 1) * size] for i in range(5)]
         raw = [near[s, 0:size], far[s], sides[s, 0], sides[s, 1]]
         own[s] = [raw[i] + parts[i] for i in range(4)]
-        other[s][FAR] = from_far[s, 0:size] + parts[4]
+        other[s][FAR] = from_far[s, 0:size] + dot(ct_far[s], columns)
         if NEAR in faces:
-            other[s][NEAR] = from_near[s] + parts[5]
+            other[s][NEAR] = from_near[s] + parts[4]
     other[count - 1][RIGHT] = from_right + dot(ct_right[...], tripled(count))
     if LEFT in faces:
         other[0][LEFT] = from_left + dot(ct_left[...], tripled(-1))
@@ -394,7 +399,7 @@
     last = which == ITERS - 1
     (offsets,) = take(1)
     terms = take(3)
-    matrix, spread, product, received = take(2), take(3), take(3), take(3)
+    matrix, spread, product, received = take(2), take(4), take(3), take(3)
     (loads,) = take(1)
     map_before, ways, found, scalars = (take(4) if which > 0 else [None] * 4)
     if not last:
@@ -510,6 +515,18 @@
     )(at, offsets, corner_map, gap, jnp.swapaxes(coupling, 0, 1), jnp.swapaxes(corner_rows, 0, 1))
     from_near = shifted(to_far, "cuts", 1, False)
     from_left = shifted(to_right, "blk", 1, True)
+    ct_own, ct_left, all_offsets = pl.pallas_call(
+        spread_kernel,
+        out_shape=(
+            shape(count, 5 * size, 6 * height, kind=BF16),
+            shape(size, 6 * height, kind=BF16),
+            shape(count, 4, kind=jnp.int32),
+        ),
+        in_specs=[SMEM] * 2 + [VMEM] * 4,
+        out_specs=(VMEM, VMEM, SMEM),
+        compiler_params=room(c_keep, from_near, from_left, table, *[faces] * 4),
+        name="spread",
+    )(at, own_offsets, c_keep, from_near, from_left, table)
     own_shape = shape(count, total, loads_n)
     own_part = pl.pallas_call(
         own_kernel,
@@ -552,14 +569,15 @@
         last = which == ITERS - 1
         near, far, sides, inside, across, terms = out
         pieces = [terms] + [shifted(terms, "cuts", k, True) for k in range(1, cuts)]
-        terms, near = relay(sum_kernel, pieces, terms, [near], f"sum{which}")
+        terms, near, across = relay(sum_kernel, pieces, terms, [near, across], f"sum{which}")
+        across = chip_neighbour(across, "blk", last)
         r_far = shifted(near, "cuts", -1, False)
         pieces = chip_parts(terms, "blk")
         stacked = blocks // 2 * terms.shape[0]
-        mine, far, across = relay(
-            stack_kernel, [*pieces, inside], shape(stacked + inside.shape[0], loads_n), [far, across], f"stack{which}"
+        mine, far, across, r_far = relay(
+            stack_kernel, [*pieces, inside], shape(stacked + inside.shape[0], loads_n), [far, across, r_far],
+            f"stack{which}",
         )
-        across = chip_neighbour(across, "blk")
         r_near = far if last else shifted(far, "cuts", 1, False)
         theirs = swapped(mine, "blk")
         if which == 0:
@@ -574,20 +592,15 @@
                 compiler_params=room(mine, theirs, k_shape, k_shape, *held),
                 name="matrix",
             )(mine, theirs)
-            ct_own, ct_left, ct_right, all_offsets = pl.pallas_call(
-                functools.partial(spread_kernel, stacked),
-                out_shape=(
-                    shape(count, 6 * size, 6 * height, kind=BF16),
-                    shape(size, 6 * height, kind=BF16),
-                    shape(size, 6 * height, kind=BF16),
-                    shape(count, 4, kind=jnp.int32),
-                ),
-                in_specs=[SMEM] * 3 + [VMEM] * 7,
-                out_specs=(VMEM,) * 3 + (SMEM,),
-                compiler_params=room(c_keep, from_near, r_far, from_left, across, theirs, table, *[faces] * 6),
-                name="spread",
-            )(at, side, own_offsets, c_keep, from_near, r_far, from_left, across, theirs, table)
-        args = [all_offsets, side, mine, theirs, k_high, k_low, ct_own, ct_left, ct_right, near, far, sides,
+            ct_far, ct_right = pl.pallas_call(
+                functools.partial(spread_back_kernel, stacked),
+                out_shape=(shape(count, size, 6 * height, kind=BF16), shape(size, 6 * height, kind=BF16)),
+                in_specs=[SMEM] * 2 + [VMEM] * 4,
+                out_specs=(VMEM,) * 2,
+                compiler_params=room(r_far, across, theirs, table, *[faces] * 3),
+                name="spread_back",
+            )(at, side, r_far, across, theirs, table)
+        args = [all_offsets, side, mine, theirs, k_high, k_low, ct_own, ct_far, ct_left, ct_right, near, far, sides,
                 r_near, r_far, across, loads, *state]
         specs = [SMEM, SMEM] + [VMEM] * (len(args) - 2)
         if last:

time: 112 us -> 113 us (level)
  starting transfers between devices: 45.5 us -> 46.7 us
    ppermute x3, waiting for transfers between devices: 16 us -> 0.01 us  [chip_neighbour(): return lax.ppermute(value, axis, pairs)]
    ppermute x25, waiting for transfers between devices: 23.9 us -> 36.4 us  [shifted(): return lax.ppermute(value, axis, pairs)]
    ppermute x3, waiting for transfers between devices: 0.01 us -> 2.59 us  [swapped(): lax.ppermute(value, axis, [(source, source ^ 1) for source in range(lax.a...]
    ppermute x25, starting transfers between devices: 41.4 us -> 42.9 us  [shifted(): return lax.ppermute(value, axis, pairs)]
  transfers between devices with their start and end apart: 31 -> 31, of which waited for: 18 -> 19; matrix products, arithmetic and copies ran while one was open for 0% -> 0% of each run, Pallas kernels for 3% -> 3%
where the time goes in v8:
time: 113 us; the launch traced here: 112 us
  starting transfers between devices  46.7 us (41%)
  waiting for transfers between devices  39 us (35%)
  Pallas kernels  17.6 us (16%)
  local copies, waits for them, and re-layouts  7.83 us (7%)
    ppermute x25, starting transfers between devices, shifted(): return lax.ppermute(value, axis, pairs)  42.9 us
    ppermute x25, waiting for transfers between devices, shifted(): return lax.ppermute(value, axis, pairs)  36.4 us
    pallas_call x3, Pallas kernels, per_device(): pl.pallas_call(functools.partial(step_kernel, which, blocks // 2, terms.s...  11.1 us
    unnamed x16, local copies, waits for them, and re-layouts  7.83 us
    ppermute x3, starting transfers between devices, chip_neighbour(): return lax.ppermute(value, axis, pairs)  2.83 us
    ppermute x3, waiting for transfers between devices, swapped(): lax.ppermute(value, axis, [(source, source ^ 1) for source in range(lax.a...  2.59 us
  transfers between devices with their start and end apart: 31, of which 19 were waited for; matrix products, arithmetic and copies ran while one was open for 0% of the time, Pallas kernels for 3%

profile of v8, /device:TPU:0, one launch (start us, length us, event | category | flops | bytes accessed | tf_op | source)
XLA Modules:
  0.0 112.0 jit_solution(4109277484448792441)
XLA Ops:
  4.7 1.4 %prepare.1 = (f32[2,2,256,128]{3,2,1,0:T(8,128)S(1)}, f32[2,288,128]{2,1,0:T(8,128)S(1)}, f32[288,128]{1,0:T(8,128)S(1)}, f32[2,256,128]{2,1,0:T(8,128)S(1)}, bf...) custom-call(s32[1]{0:T(128)} %bitcast.at, ...), custom_call_target="tpu_custom_call" | custom-call | tf_op jit(solution)/shard_map/prepare/pallas_call | solution.py:506
  6.1 4.9 %collective-permute-start = (f32[2,288,128]{2,1,0:T(8,128)S(1)}, f32[2,288,128]{2,1,0:T(8,128)S(1)}, u32[]{:S(2)}, u32[]{:S(2)}) collective-permute-start(f32[2,288,128]{2,1,0:T(8,128)S(1)} %get-tuple-element.69), channel_id=1, source_target_pairs={{0,8},{8,16},{16,24},{1,9},{9,17},{17,25},{2,10},{10,18},{18,26},{... | collective-permute-start | bytes 884744 | tf_op jit(solution)/shard_map/ppermute | solution.py:26
  11.1 3.4 %copy-done = f32[1,2,1024,1024]{3,2,1,0:T(8,128)S(1)} copy-done((f32[1,2,1024,1024]{3,2,1,0:T(8,128)S(1)}, f32[1,2,1024,1024]{3,2,1,0:T(8,128)}, u32[]{:S(2)}) %copy-start) | copy-done | bytes 8388632
  15.7 1.7 %collective-permute-done.1.from_left = f32[288,128]{1,0:T(8,128)S(1)} collective-permute-done((f32[288,128]{1,0:T(8,128)S(1)}, f32[288,128]{1,0:T(8,128)S(1)}, u32[]{:S(2)}, u32[]{:S(2)}) %collective-permute-start.1) | collective-permute-done | bytes 147488 | tf_op jit(solution)/shard_map/ppermute | solution.py:26
  17.8 1.6 %first.1 = (f32[2,288,128]{2,1,0:T(8,128)S(1)}, f32[2,256,128]{2,1,0:T(8,128)S(1)}, f32[2,2,256,128]{3,2,1,0:T(8,128)S(1)}, f32[288,128]{1,0:T(8,128)S(1)}, f32[...) custom-call(s32[1]{0:T(128)} %bitcast.8.side.refs_1_, ...), custom_call_target="tpu_custom_call" | custom-call | flops 1610612736 | bytes 8388608 | tf_op jit(solution)/shard_map/first/pallas_call | solution.py:556
  19.4 2.9 %collective-permute-start.4 = (f32[96,128]{1,0:T(8,128)S(1)}, f32[96,128]{1,0:T(8,128)S(1)}, u32[]{:S(2)}, u32[]{:S(2)}) collective-permute-start(f32[96,128]{1,0:T(8,128)S(1)} %get-tuple-element.76.refs_0_), channel_id=1, source_target_pairs={{0,24},{8,0},{16,8},{24,16},{1,25},{9,1},{17,9},{25,17},{2,26},{10... | collective-permute-start | bytes 147464 | tf_op jit(solution)/shard_map/ppermute | solution.py:26
  22.8 1.5 %collective-permute-start.2 = (f32[96,128]{1,0:T(8,128)S(1)}, f32[96,128]{1,0:T(8,128)S(1)}, u32[]{:S(2)}, u32[]{:S(2)}) collective-permute-start(f32[96,128]{1,0:T(8,128)S(1)} %get-tuple-element.76.refs_0_), channel_id=1, source_target_pairs={{0,8},{8,16},{16,24},{24,0},{1,9},{9,17},{17,25},{25,1},{2,10},{10... | collective-permute-start | bytes 147464 | tf_op jit(solution)/shard_map/ppermute | solution.py:26
  24.3 2.1 %collective-permute-done.3.refs_2_ = f32[96,128]{1,0:T(8,128)S(1)} collective-permute-done((f32[96,128]{1,0:T(8,128)S(1)}, f32[96,128]{1,0:T(8,128)S(1)}, u32[]{:S(2)}, u32[]{:S(2)}) %collective-permute-start.3) | collective-permute-done | bytes 49184 | tf_op jit(solution)/shard_map/ppermute | solution.py:26
  26.4 1.7 %collective-permute-done.2.refs_1_ = f32[96,128]{1,0:T(8,128)S(1)} collective-permute-done((f32[96,128]{1,0:T(8,128)S(1)}, f32[96,128]{1,0:T(8,128)S(1)}, u32[]{:S(2)}, u32[]{:S(2)}) %collective-permute-start.2) | collective-permute-done | bytes 49184 | tf_op jit(solution)/shard_map/ppermute | solution.py:26
  29.4 1.5 %collective-permute-start.8 = (f32[288,128]{1,0:T(8,128)S(1)}, f32[288,128]{1,0:T(8,128)S(1)}, u32[]{:S(2)}, u32[]{:S(2)}) collective-permute-start(f32[288,128]{1,0:T(8,128)S(1)} %get-tuple-element.82), channel_id=1, source_target_pairs={{0,7},{1,2},{2,1},{3,4},{4,3},{5,6},{6,5},{7,0},{8,15},{9,10},{10,... | collective-permute-start | bytes 442376 | tf_op jit(solution)/shard_map/ppermute | solution.py:49
  30.8 2.1 %collective-permute-start.7 = (f32[96,128]{1,0:T(8,128)S(1)}, f32[96,128]{1,0:T(8,128)S(1)}, u32[]{:S(2)}, u32[]{:S(2)}) collective-permute-start(f32[96,128]{1,0:T(8,128)S(1)} %get-tuple-element.79.refs_0_), channel_id=1, source_target_pairs={{0,6},{1,7},{2,0},{3,1},{4,2},{5,3},{6,4},{7,5},{8,14},{9,15},{10,... | collective-permute-start | bytes 147464 | tf_op jit(solution)/shard_map/ppermute | solution.py:26
  34.1 2.3 %collective-permute-done.7.refs_3_ = f32[96,128]{1,0:T(8,128)S(1)} collective-permute-done((f32[96,128]{1,0:T(8,128)S(1)}, f32[96,128]{1,0:T(8,128)S(1)}, u32[]{:S(2)}, u32[]{:S(2)}) %collective-permute-start.7) | collective-permute-done | bytes 49184 | tf_op jit(solution)/shard_map/ppermute | solution.py:26
  36.4 4.5 %collective-permute-done.6.refs_2_ = f32[96,128]{1,0:T(8,128)S(1)} collective-permute-done((f32[96,128]{1,0:T(8,128)S(1)}, f32[96,128]{1,0:T(8,128)S(1)}, u32[]{:S(2)}, u32[]{:S(2)}) %collective-permute-start.6) | collective-permute-done | bytes 49184 | tf_op jit(solution)/shard_map/ppermute | solution.py:26
  41.1 4.6 %collective-permute-start.11 = (f32[2,256,128]{2,1,0:T(8,128)S(1)}, f32[2,256,128]{2,1,0:T(8,128)S(1)}, u32[]{:S(2)}, u32[]{:S(2)}) collective-permute-start(f32[2,256,128]{2,1,0:T(8,128)S(1)} %get-tuple-element.93.refs_11_), channel_id=1, source_target_pairs={{0,8},{8,16},{16,24},{1,9},{9,17},{17,25},{2,10},{10,18},{18,26},{... | collective-permute-start | bytes 786440 | tf_op jit(solution)/shard_map/ppermute | solution.py:26
  45.7 1.5 %spread.1 = (bf16[2,1280,96]{2,1,0:T(8,128)(2,1)S(1)}, bf16[256,96]{1,0:T(8,128)(2,1)S(1)}, s32[2,4]{1,0:T(2,128)S(1)}) custom-call(s32[1]{0:T(128)} %bitcast.at, s32[2,2]{1,0:T(2,128)S(1)} %get-tuple-element.67.own_offsets, f32[2,12,1024]{2,1,0:T(8,128)S(1)} %get-tuple-element.68.coupling, f32[2,288,128]{2,1,0:T(8,128)S(1)} %collective-permute-done.from_near, ...), custom_call_target="tpu_custom_call" | custom-call | tf_op jit(solution)/shard_map/spread/pallas_call | solution.py:518
  47.8 4.0 %collective-permute-done.11.refs_13_ = f32[2,256,128]{2,1,0:T(8,128)S(1)} collective-permute-done((f32[2,256,128]{2,1,0:T(8,128)S(1)}, f32[2,256,128]{2,1,0:T(8,128)S(1)}, u32[]{:S(2)}, u32[]{:S(2)}) %collective-permute-start.11) | collective-permute-done | bytes 262176 | tf_op jit(solution)/shard_map/ppermute | solution.py:26
  51.8 4.4 %step0.1 = (f32[2,256,128]{2,1,0:T(8,128)S(1)}, f32[2,256,128]{2,1,0:T(8,128)S(1)}, f32[2,2,256,128]{3,2,1,0:T(8,128)S(1)}, f32[256,128]{1,0:T(8,128)S(1)}, f32[...) custom-call(s32[2,4]{1,0:T(2,128)S(1)} %get-tuple-element.71.refs_0_, ...), custom_call_target="tpu_custom_call" | custom-call | flops 1610612736 | bytes 8388608 | tf_op jit(solution)/shard_map/step0/pallas_call | solution.py:613
  56.3 3.2 %collective-permute-start.14 = (f32[48,128]{1,0:T(8,128)S(1)}, f32[48,128]{1,0:T(8,128)S(1)}, u32[]{:S(2)}, u32[]{:S(2)}) collective-permute-start(f32[48,128]{1,0:T(8,128)S(1)} %get-tuple-element.96.refs_0_), channel_id=1, source_target_pairs={{0,24},{8,0},{16,8},{24,16},{1,25},{9,1},{17,9},{25,17},{2,26},{10... | collective-permute-start | bytes 73736 | tf_op jit(solution)/shard_map/ppermute | solution.py:26
  61.5 1.9 %collective-permute-done.13.refs_2_ = f32[48,128]{1,0:T(8,128)S(1)} collective-permute-done((f32[48,128]{1,0:T(8,128)S(1)}, f32[48,128]{1,0:T(8,128)S(1)}, u32[]{:S(2)}, u32[]{:S(2)}) %collective-permute-start.13) | collective-permute-done | bytes 24608 | tf_op jit(solution)/shard_map/ppermute | solution.py:26
  63.4 1.6 %collective-permute-done.12.refs_1_ = f32[48,128]{1,0:T(8,128)S(1)} collective-permute-done((f32[48,128]{1,0:T(8,128)S(1)}, f32[48,128]{1,0:T(8,128)S(1)}, u32[]{:S(2)}, u32[]{:S(2)}) %collective-permute-start.12) | collective-permute-done | bytes 24608 | tf_op jit(solution)/shard_map/ppermute | solution.py:26
  67.5 1.9 %collective-permute-start.15 = (f32[48,128]{1,0:T(8,128)S(1)}, f32[48,128]{1,0:T(8,128)S(1)}, u32[]{:S(2)}, u32[]{:S(2)}) collective-permute-start(f32[48,128]{1,0:T(8,128)S(1)} %get-tuple-element.99.refs_0_), channel_id=1, source_target_pairs={{0,2},{1,3},{2,4},{3,5},{4,6},{5,7},{6,0},{7,1},{8,10},{9,11},{10,... | collective-permute-start | bytes 73736 | tf_op jit(solution)/shard_map/ppermute | solution.py:26
  70.2 3.0 %collective-permute-done.16.refs_2_ = f32[48,128]{1,0:T(8,128)S(1)} collective-permute-done((f32[48,128]{1,0:T(8,128)S(1)}, f32[48,128]{1,0:T(8,128)S(1)}, u32[]{:S(2)}, u32[]{:S(2)}) %collective-permute-start.16) | collective-permute-done | bytes 24608 | tf_op jit(solution)/shard_map/ppermute | solution.py:26
  73.5 4.7 %collective-permute-start.21 = (f32[2,256,128]{2,1,0:T(8,128)S(1)}, f32[2,256,128]{2,1,0:T(8,128)S(1)}, u32[]{:S(2)}, u32[]{:S(2)}) collective-permute-start(f32[2,256,128]{2,1,0:T(8,128)S(1)} %get-tuple-element.105.refs_11_), channel_id=1, source_target_pairs={{0,8},{8,16},{16,24},{1,9},{9,17},{17,25},{2,10},{10,18},{18,26},{... | collective-permute-start | bytes 786440 | tf_op jit(solution)/shard_map/ppermute | solution.py:26
  80.2 4.4 %collective-permute-done.21.refs_13_ = f32[2,256,128]{2,1,0:T(8,128)S(1)} collective-permute-done((f32[2,256,128]{2,1,0:T(8,128)S(1)}, f32[2,256,128]{2,1,0:T(8,128)S(1)}, u32[]{:S(2)}, u32[]{:S(2)}) %collective-permute-start.21) | collective-permute-done | bytes 262176 | tf_op jit(solution)/shard_map/ppermute | solution.py:26
  84.6 4.6 %step1.1 = (f32[2,256,128]{2,1,0:T(8,128)S(1)}, f32[2,256,128]{2,1,0:T(8,128)S(1)}, f32[2,2,256,128]{3,2,1,0:T(8,128)S(1)}, f32[256,128]{1,0:T(8,128)S(1)}, f32[...) custom-call(s32[2,4]{1,0:T(2,128)S(1)} %get-tuple-element.71.refs_0_, ...), custom_call_target="tpu_custom_call" | custom-call | flops 1610612736 | bytes 8388608 | tf_op jit(solution)/shard_map/step1/pallas_call | solution.py:613
  89.2 3.2 %collective-permute-start.24 = (f32[48,128]{1,0:T(8,128)S(1)}, f32[48,128]{1,0:T(8,128)S(1)}, u32[]{:S(2)}, u32[]{:S(2)}) collective-permute-start(f32[48,128]{1,0:T(8,128)S(1)} %get-tuple-element.112.refs_0_), channel_id=1, source_target_pairs={{0,24},{8,0},{16,8},{24,16},{1,25},{9,1},{17,9},{25,17},{2,26},{10... | collective-permute-start | bytes 73736 | tf_op jit(solution)/shard_map/ppermute | solution.py:26
  94.4 1.9 %collective-permute-done.23.refs_2_ = f32[48,128]{1,0:T(8,128)S(1)} collective-permute-done((f32[48,128]{1,0:T(8,128)S(1)}, f32[48,128]{1,0:T(8,128)S(1)}, u32[]{:S(2)}, u32[]{:S(2)}) %collective-permute-start.23) | collective-permute-done | bytes 24608 | tf_op jit(solution)/shard_map/ppermute | solution.py:26
  96.2 1.6 %collective-permute-done.22.refs_1_ = f32[48,128]{1,0:T(8,128)S(1)} collective-permute-done((f32[48,128]{1,0:T(8,128)S(1)}, f32[48,128]{1,0:T(8,128)S(1)}, u32[]{:S(2)}, u32[]{:S(2)}) %collective-permute-start.22) | collective-permute-done | bytes 24608 | tf_op jit(solution)/shard_map/ppermute | solution.py:26
  104.9 2.0 %collective-permute-done.26.refs_2_ = f32[48,128]{1,0:T(8,128)S(1)} collective-permute-done((f32[48,128]{1,0:T(8,128)S(1)}, f32[48,128]{1,0:T(8,128)S(1)}, u32[]{:S(2)}, u32[]{:S(2)}) %collective-permute-start.26) | collective-permute-done | bytes 24608 | tf_op jit(solution)/shard_map/ppermute | solution.py:26
  106.9 1.4 %collective-permute-done.25.refs_1_ = f32[48,128]{1,0:T(8,128)S(1)} collective-permute-done((f32[48,128]{1,0:T(8,128)S(1)}, f32[48,128]{1,0:T(8,128)S(1)}, u32[]{:S(2)}, u32[]{:S(2)}) %collective-permute-start.25) | collective-permute-done | bytes 24608 | tf_op jit(solution)/shard_map/ppermute | solution.py:26
  108.4 1.5 %collective-permute-done.30.refs_3_ = f32[448,128]{1,0:T(8,128)S(1)} collective-permute-done((f32[448,128]{1,0:T(8,128)S(1)}, f32[448,128]{1,0:T(8,128)S(1)}, u32[]{:S(2)}, u32[]{:S(2)}) %collective-permute-start.30) | collective-permute-done | bytes 229408 | tf_op jit(solution)/shard_map/ppermute | solution.py:53
  109.9 2.1 %step2.1 = (f32[2,2,256,128]{3,2,1,0:T(8,128)}, f32[2,2,256,128]{3,2,1,0:T(8,128)}) custom-call(s32[2,4]{1,0:T(2,128)S(1)} %get-tuple-element.71.refs_0_, s32[1]{0:T(128)} %bitcast.8.side.refs_1_, f32[448,128]{1,0:T(8,128)S(1)} %get-tuple-element.120.refs_2_, f32[448,128]{1,0:T(8,128)S(1)} %collective-permute-done.30.refs_3_, ...), custom_call_target="tpu_custom_call" | custom-call | tf_op jit(solution)/shard_map/step2/pallas_call | solution.py:613
  (61 shorter events, 26.0 us)
Async XLA Ops:
  6.1 11.3 %collective-permute-start = (f32[2,288,128]{2,1,0:T(8,128)S(1)}, f32[2,288,128]{2,1,0:T(8,128)S(1)}, u32[]{:S(2)}, u32[]{:S(2)}) collective-permute-start(f32[2,288,128]{2,1,0:T(8,128)S(1)} %get-tuple-element.69), channel_id=1, source_target_pairs={{0,8},{8,16},{16,24},{1,9},{9,17},{17,25},{2,10},{10,18},{18,26},{... | collective-permute-start | bytes 884744 | tf_op jit(solution)/shard_map/ppermute | solution.py:26
  11.0 6.4 %collective-permute-start.1 = (f32[288,128]{1,0:T(8,128)S(1)}, f32[288,128]{1,0:T(8,128)S(1)}, u32[]{:S(2)}, u32[]{:S(2)}) collective-permute-start(f32[288,128]{1,0:T(8,128)S(1)} %get-tuple-element.70), channel_id=1, source_target_pairs={{0,1},{1,2},{2,3},{3,4},{4,5},{5,6},{6,7},{7,0},{8,9},{9,10},{10,1... | collective-permute-start | bytes 442376 | tf_op jit(solution)/shard_map/ppermute | solution.py:26
  15.7 29.9 %copy-start.3 = (bf16[6,32,96]{2,1,0:T(8,128)(2,1)S(1)}, bf16[6,32,96]{2,1,0:T(8,128)(2,1)}, u32[]{:S(2)}) copy-start(bf16[6,32,96]{2,1,0:T(8,128)(2,1)} %constant.23.clone.table) | copy-start | bytes 110596
  19.4 4.9 %collective-permute-start.4 = (f32[96,128]{1,0:T(8,128)S(1)}, f32[96,128]{1,0:T(8,128)S(1)}, u32[]{:S(2)}, u32[]{:S(2)}) collective-permute-start(f32[96,128]{1,0:T(8,128)S(1)} %get-tuple-element.76.refs_0_), channel_id=1, source_target_pairs={{0,24},{8,0},{16,8},{24,16},{1,25},{9,1},{17,9},{25,17},{2,26},{10... | collective-permute-start | bytes 147464 | tf_op jit(solution)/shard_map/ppermute | solution.py:26
  22.3 4.1 %collective-permute-start.3 = (f32[96,128]{1,0:T(8,128)S(1)}, f32[96,128]{1,0:T(8,128)S(1)}, u32[]{:S(2)}, u32[]{:S(2)}) collective-permute-start(f32[96,128]{1,0:T(8,128)S(1)} %get-tuple-element.76.refs_0_), channel_id=1, source_target_pairs={{0,16},{8,24},{16,0},{24,8},{1,17},{9,25},{17,1},{25,9},{2,18},{10... | collective-permute-start | bytes 147464 | tf_op jit(solution)/shard_map/ppermute | solution.py:26
  22.8 5.3 %collective-permute-start.2 = (f32[96,128]{1,0:T(8,128)S(1)}, f32[96,128]{1,0:T(8,128)S(1)}, u32[]{:S(2)}, u32[]{:S(2)}) collective-permute-start(f32[96,128]{1,0:T(8,128)S(1)} %get-tuple-element.76.refs_0_), channel_id=1, source_target_pairs={{0,8},{8,16},{16,24},{24,0},{1,9},{9,17},{17,25},{25,1},{2,10},{10... | collective-permute-start | bytes 147464 | tf_op jit(solution)/shard_map/ppermute | solution.py:26
  28.1 12.9 %collective-permute-start.9 = (f32[2,288,128]{2,1,0:T(8,128)S(1)}, f32[2,288,128]{2,1,0:T(8,128)S(1)}, u32[]{:S(2)}, u32[]{:S(2)}) collective-permute-start(f32[2,288,128]{2,1,0:T(8,128)S(1)} %get-tuple-element.83.refs_10_), channel_id=1, source_target_pairs={{8,0},{16,8},{24,16},{9,1},{17,9},{25,17},{10,2},{18,10},{26,18},{... | collective-permute-start | bytes 884744 | tf_op jit(solution)/shard_map/ppermute | solution.py:26
  29.4 11.6 %collective-permute-start.8 = (f32[288,128]{1,0:T(8,128)S(1)}, f32[288,128]{1,0:T(8,128)S(1)}, u32[]{:S(2)}, u32[]{:S(2)}) collective-permute-start(f32[288,128]{1,0:T(8,128)S(1)} %get-tuple-element.82), channel_id=1, source_target_pairs={{0,7},{1,2},{2,1},{3,4},{4,3},{5,6},{6,5},{7,0},{8,15},{9,10},{10,... | collective-permute-start | bytes 442376 | tf_op jit(solution)/shard_map/ppermute | solution.py:49
  30.8 5.6 %collective-permute-start.7 = (f32[96,128]{1,0:T(8,128)S(1)}, f32[96,128]{1,0:T(8,128)S(1)}, u32[]{:S(2)}, u32[]{:S(2)}) collective-permute-start(f32[96,128]{1,0:T(8,128)S(1)} %get-tuple-element.79.refs_0_), channel_id=1, source_target_pairs={{0,6},{1,7},{2,0},{3,1},{4,2},{5,3},{6,4},{7,5},{8,14},{9,15},{10,... | collective-permute-start | bytes 147464 | tf_op jit(solution)/shard_map/ppermute | solution.py:26
  33.0 8.0 %collective-permute-start.6 = (f32[96,128]{1,0:T(8,128)S(1)}, f32[96,128]{1,0:T(8,128)S(1)}, u32[]{:S(2)}, u32[]{:S(2)}) collective-permute-start(f32[96,128]{1,0:T(8,128)S(1)} %get-tuple-element.79.refs_0_), channel_id=1, source_target_pairs={{0,4},{1,5},{2,6},{3,7},{4,0},{5,1},{6,2},{7,3},{8,12},{9,13},{10,... | collective-permute-start | bytes 147464 | tf_op jit(solution)/shard_map/ppermute | solution.py:26
  33.0 8.0 %collective-permute-start.5 = (f32[96,128]{1,0:T(8,128)S(1)}, f32[96,128]{1,0:T(8,128)S(1)}, u32[]{:S(2)}, u32[]{:S(2)}) collective-permute-start(f32[96,128]{1,0:T(8,128)S(1)} %get-tuple-element.79.refs_0_), channel_id=1, source_target_pairs={{0,2},{1,3},{2,4},{3,5},{4,6},{5,7},{6,0},{7,1},{8,10},{9,11},{10,... | collective-permute-start | bytes 147464 | tf_op jit(solution)/shard_map/ppermute | solution.py:26
  41.0 6.2 %collective-permute-start.10 = (f32[672,128]{1,0:T(8,128)S(1)}, f32[672,128]{1,0:T(8,128)S(1)}, u32[]{:S(2)}, u32[]{:S(2)}) collective-permute-start(f32[672,128]{1,0:T(8,128)S(1)} %get-tuple-element.84.mine.refs_2_), channel_id=1, source_target_pairs={{0,1},{1,0},{2,3},{3,2},{4,5},{5,4},{6,7},{7,6},{8,9},{9,8},{10,11... | collective-permute-start | bytes 1032200 | tf_op jit(solution)/shard_map/ppermute | solution.py:53
  41.1 10.8 %collective-permute-start.11 = (f32[2,256,128]{2,1,0:T(8,128)S(1)}, f32[2,256,128]{2,1,0:T(8,128)S(1)}, u32[]{:S(2)}, u32[]{:S(2)}) collective-permute-start(f32[2,256,128]{2,1,0:T(8,128)S(1)} %get-tuple-element.93.refs_11_), channel_id=1, source_target_pairs={{0,8},{8,16},{16,24},{1,9},{9,17},{17,25},{2,10},{10,18},{18,26},{... | collective-permute-start | bytes 786440 | tf_op jit(solution)/shard_map/ppermute | solution.py:26
  56.3 5.2 %collective-permute-start.14 = (f32[48,128]{1,0:T(8,128)S(1)}, f32[48,128]{1,0:T(8,128)S(1)}, u32[]{:S(2)}, u32[]{:S(2)}) collective-permute-start(f32[48,128]{1,0:T(8,128)S(1)} %get-tuple-element.96.refs_0_), channel_id=1, source_target_pairs={{0,24},{8,0},{16,8},{24,16},{1,25},{9,1},{17,9},{25,17},{2,26},{10... | collective-permute-start | bytes 73736 | tf_op jit(solution)/shard_map/ppermute | solution.py:26
  59.5 3.9 %collective-permute-start.13 = (f32[48,128]{1,0:T(8,128)S(1)}, f32[48,128]{1,0:T(8,128)S(1)}, u32[]{:S(2)}, u32[]{:S(2)}) collective-permute-start(f32[48,128]{1,0:T(8,128)S(1)} %get-tuple-element.96.refs_0_), channel_id=1, source_target_pairs={{0,16},{8,24},{16,0},{24,8},{1,17},{9,25},{17,1},{25,9},{2,18},{10... | collective-permute-start | bytes 73736 | tf_op jit(solution)/shard_map/ppermute | solution.py:26
  60.3 4.7 %collective-permute-start.12 = (f32[48,128]{1,0:T(8,128)S(1)}, f32[48,128]{1,0:T(8,128)S(1)}, u32[]{:S(2)}, u32[]{:S(2)}) collective-permute-start(f32[48,128]{1,0:T(8,128)S(1)} %get-tuple-element.96.refs_0_), channel_id=1, source_target_pairs={{0,8},{8,16},{16,24},{24,0},{1,9},{9,17},{17,25},{25,1},{2,10},{10... | collective-permute-start | bytes 73736 | tf_op jit(solution)/shard_map/ppermute | solution.py:26
  65.0 8.4 %collective-permute-start.19 = (f32[2,256,128]{2,1,0:T(8,128)S(1)}, f32[2,256,128]{2,1,0:T(8,128)S(1)}, u32[]{:S(2)}, u32[]{:S(2)}) collective-permute-start(f32[2,256,128]{2,1,0:T(8,128)S(1)} %get-tuple-element.103.refs_10_), channel_id=1, source_target_pairs={{8,0},{16,8},{24,16},{9,1},{17,9},{25,17},{10,2},{18,10},{26,18},{... | collective-permute-start | bytes 786440 | tf_op jit(solution)/shard_map/ppermute | solution.py:26
  66.3 7.1 %collective-permute-start.18 = (f32[256,128]{1,0:T(8,128)S(1)}, f32[256,128]{1,0:T(8,128)S(1)}, u32[]{:S(2)}, u32[]{:S(2)}) collective-permute-start(f32[256,128]{1,0:T(8,128)S(1)} %get-tuple-element.102), channel_id=1, source_target_pairs={{0,7},{1,2},{2,1},{3,4},{4,3},{5,6},{6,5},{7,0},{8,15},{9,10},{10,... | collective-permute-start | bytes 393224 | tf_op jit(solution)/shard_map/ppermute | solution.py:49
  66.4 3.9 %collective-permute-start.17 = (f32[48,128]{1,0:T(8,128)S(1)}, f32[48,128]{1,0:T(8,128)S(1)}, u32[]{:S(2)}, u32[]{:S(2)}) collective-permute-start(f32[48,128]{1,0:T(8,128)S(1)} %get-tuple-element.99.refs_0_), channel_id=1, source_target_pairs={{0,6},{1,7},{2,0},{3,1},{4,2},{5,3},{6,4},{7,5},{8,14},{9,15},{10,... | collective-permute-start | bytes 73736 | tf_op jit(solution)/shard_map/ppermute | solution.py:26
  67.5 5.7 %collective-permute-start.16 = (f32[48,128]{1,0:T(8,128)S(1)}, f32[48,128]{1,0:T(8,128)S(1)}, u32[]{:S(2)}, u32[]{:S(2)}) collective-permute-start(f32[48,128]{1,0:T(8,128)S(1)} %get-tuple-element.99.refs_0_), channel_id=1, source_target_pairs={{0,4},{1,5},{2,6},{3,7},{4,0},{5,1},{6,2},{7,3},{8,12},{9,13},{10,... | collective-permute-start | bytes 73736 | tf_op jit(solution)/shard_map/ppermute | solution.py:26
  67.5 5.9 %collective-permute-start.15 = (f32[48,128]{1,0:T(8,128)S(1)}, f32[48,128]{1,0:T(8,128)S(1)}, u32[]{:S(2)}, u32[]{:S(2)}) collective-permute-start(f32[48,128]{1,0:T(8,128)S(1)} %get-tuple-element.99.refs_0_), channel_id=1, source_target_pairs={{0,2},{1,3},{2,4},{3,5},{4,6},{5,7},{6,0},{7,1},{8,10},{9,11},{10,... | collective-permute-start | bytes 73736 | tf_op jit(solution)/shard_map/ppermute | solution.py:26
  73.5 11.1 %collective-permute-start.21 = (f32[2,256,128]{2,1,0:T(8,128)S(1)}, f32[2,256,128]{2,1,0:T(8,128)S(1)}, u32[]{:S(2)}, u32[]{:S(2)}) collective-permute-start(f32[2,256,128]{2,1,0:T(8,128)S(1)} %get-tuple-element.105.refs_11_), channel_id=1, source_target_pairs={{0,8},{8,16},{16,24},{1,9},{9,17},{17,25},{2,10},{10,18},{18,26},{... | collective-permute-start | bytes 786440 | tf_op jit(solution)/shard_map/ppermute | solution.py:26
  78.2 2.0 %collective-permute-start.20 = (f32[448,128]{1,0:T(8,128)S(1)}, f32[448,128]{1,0:T(8,128)S(1)}, u32[]{:S(2)}, u32[]{:S(2)}) collective-permute-start(f32[448,128]{1,0:T(8,128)S(1)} %get-tuple-element.104.refs_2_), channel_id=1, source_target_pairs={{0,1},{1,0},{2,3},{3,2},{4,5},{5,4},{6,7},{7,6},{8,9},{9,8},{10,11... | collective-permute-start | bytes 688136 | tf_op jit(solution)/shard_map/ppermute | solution.py:53
  89.2 5.2 %collective-permute-start.24 = (f32[48,128]{1,0:T(8,128)S(1)}, f32[48,128]{1,0:T(8,128)S(1)}, u32[]{:S(2)}, u32[]{:S(2)}) collective-permute-start(f32[48,128]{1,0:T(8,128)S(1)} %get-tuple-element.112.refs_0_), channel_id=1, source_target_pairs={{0,24},{8,0},{16,8},{24,16},{1,25},{9,1},{17,9},{25,17},{2,26},{10... | collective-permute-start | bytes 73736 | tf_op jit(solution)/shard_map/ppermute | solution.py:26
  92.4 3.8 %collective-permute-start.23 = (f32[48,128]{1,0:T(8,128)S(1)}, f32[48,128]{1,0:T(8,128)S(1)}, u32[]{:S(2)}, u32[]{:S(2)}) collective-permute-start(f32[48,128]{1,0:T(8,128)S(1)} %get-tuple-element.112.refs_0_), channel_id=1, source_target_pairs={{0,16},{8,24},{16,0},{24,8},{1,17},{9,25},{17,1},{25,9},{2,18},{10... | collective-permute-start | bytes 73736 | tf_op jit(solution)/shard_map/ppermute | solution.py:26
  93.2 4.7 %collective-permute-start.22 = (f32[48,128]{1,0:T(8,128)S(1)}, f32[48,128]{1,0:T(8,128)S(1)}, u32[]{:S(2)}, u32[]{:S(2)}) collective-permute-start(f32[48,128]{1,0:T(8,128)S(1)} %get-tuple-element.112.refs_0_), channel_id=1, source_target_pairs={{0,8},{8,16},{16,24},{24,0},{1,9},{9,17},{17,25},{25,1},{2,10},{10... | collective-permute-start | bytes 73736 | tf_op jit(solution)/shard_map/ppermute | solution.py:26
  97.9 10.4 %collective-permute-start.29 = (f32[2,256,128]{2,1,0:T(8,128)S(1)}, f32[2,256,128]{2,1,0:T(8,128)S(1)}, u32[]{:S(2)}, u32[]{:S(2)}) collective-permute-start(f32[2,256,128]{2,1,0:T(8,128)S(1)} %get-tuple-element.119.refs_10_), channel_id=1, source_target_pairs={{8,0},{16,8},{24,16},{9,1},{17,9},{25,17},{10,2},{18,10},{26,18},{... | collective-permute-start | bytes 786440 | tf_op jit(solution)/shard_map/ppermute | solution.py:26
  99.2 9.1 %collective-permute-start.28 = (f32[256,128]{1,0:T(8,128)S(1)}, f32[256,128]{1,0:T(8,128)S(1)}, u32[]{:S(2)}, u32[]{:S(2)}) collective-permute-start(f32[256,128]{1,0:T(8,128)S(1)} %get-tuple-element.118), channel_id=1, source_target_pairs={{0,7},{2,1},{4,3},{6,5},{8,15},{10,9},{12,11},{14,13},{16,23},{18,... | collective-permute-start | bytes 393224 | tf_op jit(solution)/shard_map/ppermute | solution.py:49
  100.5 4.4 %collective-permute-start.27 = (f32[48,128]{1,0:T(8,128)S(1)}, f32[48,128]{1,0:T(8,128)S(1)}, u32[]{:S(2)}, u32[]{:S(2)}) collective-permute-start(f32[48,128]{1,0:T(8,128)S(1)} %get-tuple-element.115.refs_0_), channel_id=1, source_target_pairs={{0,6},{1,7},{2,0},{3,1},{4,2},{5,3},{6,4},{7,5},{8,14},{9,15},{10,... | collective-permute-start | bytes 73736 | tf_op jit(solution)/shard_map/ppermute | solution.py:26
  101.9 5.0 %collective-permute-start.26 = (f32[48,128]{1,0:T(8,128)S(1)}, f32[48,128]{1,0:T(8,128)S(1)}, u32[]{:S(2)}, u32[]{:S(2)}) collective-permute-start(f32[48,128]{1,0:T(8,128)S(1)} %get-tuple-element.115.refs_0_), channel_id=1, source_target_pairs={{0,4},{1,5},{2,6},{3,7},{4,0},{5,1},{6,2},{7,3},{8,12},{9,13},{10,... | collective-permute-start | bytes 73736 | tf_op jit(solution)/shard_map/ppermute | solution.py:26
  102.7 5.6 %collective-permute-start.25 = (f32[48,128]{1,0:T(8,128)S(1)}, f32[48,128]{1,0:T(8,128)S(1)}, u32[]{:S(2)}, u32[]{:S(2)}) collective-permute-start(f32[48,128]{1,0:T(8,128)S(1)} %get-tuple-element.115.refs_0_), channel_id=1, source_target_pairs={{0,2},{1,3},{2,4},{3,5},{4,6},{5,7},{6,0},{7,1},{8,10},{9,11},{10,... | collective-permute-start | bytes 73736 | tf_op jit(solution)/shard_map/ppermute | solution.py:26
  108.3 1.6 %collective-permute-start.30 = (f32[448,128]{1,0:T(8,128)S(1)}, f32[448,128]{1,0:T(8,128)S(1)}, u32[]{:S(2)}, u32[]{:S(2)}) collective-permute-start(f32[448,128]{1,0:T(8,128)S(1)} %get-tuple-element.120.refs_2_), channel_id=1, source_target_pairs={{0,1},{1,0},{2,3},{3,2},{4,5},{5,4},{6,7},{7,6},{8,9},{9,8},{10,11... | collective-permute-start | bytes 688136 | tf_op jit(solution)/shard_map/ppermute | solution.py:53
  (7 other events, 10.8 us)
